TPU v7x, 256 devices: a whole 4x4x8 slice. The times are simulated.
256 devices in a mesh: expert: 32 (over y, x, core), dp: 8 (over z).
Axes of the slice: x: 4, y: 4, z: 8, core: 2. Of those that a mesh axis runs over, the one named last changes fastest.
Arguments:
- tokens: bfloat16 [12288, 2048], P(('expert', 'dp')), may hold values from -6 to 6
- routes: int32 [12288, 8], P(('expert', 'dp')), may hold values from 0 to 31, all different within a row; in each aligned block of 48 rows (0 to 47, 48 to 95, ...) at most 16 rows name the same one
- gate_weights: float32 [12288, 8], P(('expert', 'dp')), may hold values from 0.05 to 0.3
- w_gate: bfloat16 [32, 2048, 768], P('expert'), may hold values from -0.125 to 0.125
- w_up: bfloat16 [32, 2048, 768], P('expert'), may hold values from -0.125 to 0.125
- w_down: bfloat16 [32, 768, 2048], P('expert'), may hold values from -0.21875 to 0.21875
- out_grad: bfloat16 [12288, 2048], P(('expert', 'dp')), may hold values from -6 to 6
Outputs:
- layer_out: bfloat16 [12288, 2048], P(('expert', 'dp'))
- token_grad: bfloat16 [12288, 2048], P(('expert', 'dp'))
- gate_weights_grad: float32 [12288, 8], P(('expert', 'dp'))
- w_gate_grad: float32 [32, 2048, 768], P('expert', 'dp')
- w_up_grad: float32 [32, 2048, 768], P('expert', 'dp')
- w_down_grad: float32 [32, 768, 2048], P('expert', None, 'dp')
Inputs may be any that keep to these rules, and one draw needn't show every extreme that they name: `routes`: each token names 8 different experts; within the rows of one device (aligned blocks of 48 rows) no expert is named more than 16 times, a bound that some block reaches.
All inputs are finite; a program needn't handle non-finite values.
Results may differ from a plain program's by a relative error of at most 0.015.
Values may be sent and summed in bfloat16 or wider, within the bound.
No kernel may reach another device: no remote copies, remote signals or barrier semaphores. Data moves between devices by JAX's collectives and lax.ppermute only.
A program may use at most 128 MiB of HBM per device.

v0:
```python
import functools

import jax
import jax.numpy as jnp
from jax import lax
from jax.experimental import pallas as pl
from jax.experimental.pallas import tpu as pltpu
from jax.sharding import PartitionSpec as P

BF16 = jnp.bfloat16
F32 = jnp.float32
LAST = (((1,), (1,)), ((), ()))
FIRST = (((0,), (0,)), ((), ()))
VMEM_LIMIT = 56 * 2**20


def params():
    return pltpu.CompilerParams(vmem_limit_bytes=VMEM_LIMIT)


def cost(flops, nbytes, exps=0):
    return pl.CostEstimate(flops=flops, bytes_accessed=nbytes, transcendentals=exps)


def dot(a, b, dims=(((1,), (0,)), ((), ()))):
    return lax.dot_general(a, b, dims, preferred_element_type=F32)


def slot_masks(routes_t, slots, capacity):
    tokens = routes_t.shape[1]
    expert = lax.broadcasted_iota(jnp.int32, (slots, tokens), 0) // capacity
    return [expert == routes_t[k : k + 1, :] for k in range(routes_t.shape[0])]


def dispatch_kernel(capacity, routes_ref, gates_ref, tokens_ref, grads_ref, rows_ref, scaled_ref, place_ref):
    routes_t, gates_t = routes_ref[...], gates_ref[...]
    slots, tokens = place_ref.shape
    masks = slot_masks(routes_t, slots, capacity)
    hit = jnp.zeros((slots, tokens), F32)
    weight = jnp.zeros((slots, tokens), F32)
    for k, mask in enumerate(masks):
        hit = jnp.where(mask, 1.0, hit)
        weight = jnp.where(mask, gates_t[k : k + 1, :], weight)
    before = (
        lax.broadcasted_iota(jnp.int32, (tokens, tokens), 0)
        < lax.broadcasted_iota(jnp.int32, (tokens, tokens), 1)
    ).astype(F32).astype(BF16)
    rank = dot(hit.astype(BF16), before)
    mine = (lax.broadcasted_iota(jnp.int32, (slots, tokens), 0) % capacity).astype(F32)
    place = jnp.where(rank == mine, hit, 0.0)
    slot_weight = jnp.sum(place * weight, axis=1, keepdims=True)
    place_low = place.astype(BF16)
    place_ref[...] = place_low
    rows_ref[...] = dot(place_low, tokens_ref[...]).astype(BF16)
    scaled_ref[...] = (slot_weight * dot(place_low, grads_ref[...])).astype(BF16)


def forward_kernel(rows_ref, gate_ref, up_ref, hidden_ref, gate_slope_ref, up_slope_ref):
    rows = rows_ref[...]
    pre_gate = dot(rows, gate_ref[...])
    pre_up = dot(rows, up_ref[...])
    sig = jax.nn.sigmoid(pre_gate)
    silu = pre_gate * sig
    hidden_ref[...] = (silu * pre_up).astype(BF16)
    gate_slope_ref[...] = pre_up * sig * (1.0 + pre_gate * (1.0 - sig))
    up_slope_ref[...] = silu


def partial_kernel(
    rows_ref, grads_ref, hidden_ref, gate_slope_ref, up_slope_ref, down_ref,
    part_ref, gate_pre_ref, up_pre_ref, score_ref, hidden_t,
):
    chunk = pl.program_id(0)
    width = rows_ref.shape[1]
    blocks = gate_pre_ref.shape[1] // width

    @pl.when(chunk == 0)
    def _():
        hidden_grad = dot(grads_ref[...], down_ref[...], LAST)
        hidden = hidden_ref[...]
        gate_pre_ref[...] = (hidden_grad * gate_slope_ref[...]).astype(BF16)
        up_pre_ref[...] = (hidden_grad * up_slope_ref[...]).astype(BF16)
        score = jnp.sum(hidden_grad * hidden.astype(F32), axis=1, keepdims=True)
        score_ref[...] = jnp.broadcast_to(score, score_ref.shape)
        hidden_t[...] = hidden.T

    rows_t = rows_ref[...].T
    for j in range(blocks):
        cols = slice(j * width, (j + 1) * width)
        part_ref[j] = dot(rows_t, gate_pre_ref[:, cols]).astype(BF16)
        part_ref[blocks + j] = dot(rows_t, up_pre_ref[:, cols]).astype(BF16)
    grads = grads_ref[:, pl.ds(pl.multiple_of(chunk * width, width), width)]
    for j in range(blocks):
        part_ref[2 * blocks + j] = dot(hidden_t[j * width : (j + 1) * width, :], grads).astype(BF16)


def return_kernel(hidden_ref, gate_pre_ref, up_pre_ref, down_ref, gate_ref, up_ref, out_ref, row_grad_ref):
    out_ref[...] = dot(hidden_ref[...], down_ref[...]).astype(BF16)
    row_grad_ref[...] = (
        dot(gate_pre_ref[...], gate_ref[...], LAST) + dot(up_pre_ref[...], up_ref[...], LAST)
    ).astype(BF16)


def combine_kernel(
    capacity, routes_ref, gates_ref, place_ref, score_ref, back_ref, back_grad_ref,
    out_ref, grad_ref, gates_grad_ref, high, low,
):
    @pl.when(pl.program_id(0) == 0)
    def _():
        routes_t, gates_t = routes_ref[...], gates_ref[...]
        place = place_ref[...].astype(F32)
        score = score_ref[:, 0:1] * place
        weight = jnp.zeros(place.shape, F32)
        for k, mask in enumerate(slot_masks(routes_t, place.shape[0], capacity)):
            weight = jnp.where(mask, gates_t[k : k + 1, :], weight)
            gates_grad_ref[k : k + 1, :] = (
                jnp.sum(jnp.where(mask, score, 0.0), axis=0, keepdims=True) / gates_t[k : k + 1, :]
            )
        weight = weight * place
        high[...] = weight.astype(BF16)
        low[...] = (weight - weight.astype(BF16).astype(F32)).astype(BF16)

    back = back_ref[...]
    out_ref[...] = (dot(high[...], back, FIRST) + dot(low[...], back, FIRST)).astype(BF16)
    grad_ref[...] = dot(place_ref[...], back_grad_ref[...], FIRST).astype(BF16)


def widen_kernel(part_ref, gate_ref, up_ref, down_ref):
    width = part_ref.shape[2]
    blocks = part_ref.shape[0] // 3
    for j in range(blocks):
        gate_ref[:, j * width : (j + 1) * width] = part_ref[j].astype(F32)
        up_ref[:, j * width : (j + 1) * width] = part_ref[blocks + j].astype(F32)
        down_ref[j * width : (j + 1) * width, :] = part_ref[2 * blocks + j].astype(F32)


def shape(dims, dtype=BF16):
    return jax.ShapeDtypeStruct(dims, dtype)


def whole(dims):
    return pl.BlockSpec(dims, lambda i: (0,) * len(dims))


def local(tokens, routes, gate_weights, w_gate, w_up, w_down, out_grad):
    count, top = routes.shape
    model = tokens.shape[1]
    experts = w_gate.shape[0] * lax.axis_size("expert")
    groups = lax.axis_size("dp")
    capacity = max(2, 4 * count * top // (3 * experts))
    slots = experts * capacity
    hid = w_gate.shape[2]
    width = model // groups
    blocks = hid // width
    w_gate, w_up, w_down = w_gate[0], w_up[0], w_down[0]
    routes_t, gates_t = routes.T, gate_weights.T

    send_rows, send_grads, place = pl.pallas_call(
        functools.partial(dispatch_kernel, capacity),
        out_shape=(shape((slots, model)), shape((slots, model)), shape((slots, count))),
        compiler_params=params(),
        cost_estimate=cost(4 * slots * count * model, 4 * slots * model),
        name="dispatch",
    )(routes_t, gates_t, tokens, out_grad)

    def exchange(array):
        wide = array.reshape(experts, capacity, array.shape[1])
        return lax.all_to_all(wide, "expert", 0, 0, tiled=True).reshape(array.shape)

    rows = exchange(send_rows)
    grads = exchange(send_grads)

    hidden, gate_slope, up_slope = pl.pallas_call(
        forward_kernel,
        grid=(blocks,),
        in_specs=[
            whole((slots, model)),
            pl.BlockSpec((model, width), lambda i: (0, i)),
            pl.BlockSpec((model, width), lambda i: (0, i)),
        ],
        out_specs=[pl.BlockSpec((slots, width), lambda i: (0, i))] * 3,
        out_shape=(shape((slots, hid)), shape((slots, hid), F32), shape((slots, hid), F32)),
        compiler_params=params(),
        cost_estimate=cost(4 * slots * model * hid, 2 * slots * model + 4 * model * hid + 10 * slots * hid),
        name="forward",
    )(rows, w_gate, w_up)

    part, gate_pre, up_pre, score = pl.pallas_call(
        partial_kernel,
        grid=(groups,),
        in_specs=[
            pl.BlockSpec((slots, width), lambda i: (0, i)),
            whole((slots, model)),
            whole((slots, hid)),
            whole((slots, hid)),
            whole((slots, hid)),
            whole((hid, model)),
        ],
        out_specs=[
            pl.BlockSpec((3 * blocks, width, width), lambda i: (i, 0, 0)),
            whole((slots, hid)),
            whole((slots, hid)),
            whole((slots, 128)),
        ],
        out_shape=(
            shape((groups * 3 * blocks, width, width)),
            shape((slots, hid)),
            shape((slots, hid)),
            shape((slots, 128), F32),
        ),
        scratch_shapes=[pltpu.VMEM((hid, slots), BF16)],
        compiler_params=params(),
        cost_estimate=cost(8 * slots * model * hid, 4 * slots * model + 8 * model * hid + 14 * slots * hid),
        name="partials",
    )(rows, grads, hidden, gate_slope, up_slope, w_down)

    summed = lax.psum_scatter(part, "dp", scatter_dimension=0, tiled=True)

    output, row_grad = pl.pallas_call(
        return_kernel,
        grid=(groups,),
        in_specs=[
            whole((slots, hid)),
            whole((slots, hid)),
            whole((slots, hid)),
            pl.BlockSpec((hid, width), lambda i: (0, i)),
            pl.BlockSpec((width, hid), lambda i: (i, 0)),
            pl.BlockSpec((width, hid), lambda i: (i, 0)),
        ],
        out_specs=[pl.BlockSpec((slots, width), lambda i: (0, i))] * 2,
        out_shape=(shape((slots, model)), shape((slots, model))),
        compiler_params=params(),
        cost_estimate=cost(6 * slots * model * hid, 4 * slots * model + 6 * model * hid + 6 * slots * hid),
        name="rows_back",
    )(hidden, gate_pre, up_pre, w_down, w_gate, w_up)

    back = exchange(output)
    back_grad = exchange(row_grad)
    back_score = exchange(score)

    half = model // 2
    layer_out, token_grad, gates_grad_t = pl.pallas_call(
        functools.partial(combine_kernel, capacity),
        grid=(2,),
        in_specs=[
            whole((top, count)),
            whole((top, count)),
            whole((slots, count)),
            whole((slots, 128)),
            pl.BlockSpec((slots, half), lambda i: (0, i)),
            pl.BlockSpec((slots, half), lambda i: (0, i)),
        ],
        out_specs=[
            pl.BlockSpec((count, half), lambda i: (0, i)),
            pl.BlockSpec((count, half), lambda i: (0, i)),
            whole((top, count)),
        ],
        out_shape=(shape((count, model)), shape((count, model)), shape((top, count), F32)),
        scratch_shapes=[pltpu.VMEM((slots, count), BF16)] * 2,
        compiler_params=params(),
        cost_estimate=cost(6 * slots * count * model, 4 * slots * model),
        name="combine",
    )(routes_t, gates_t, place, back_score, back, back_grad)

    gate_grad, up_grad, down_grad = pl.pallas_call(
        widen_kernel,
        out_shape=(shape((width, hid), F32), shape((width, hid), F32), shape((hid, width), F32)),
        compiler_params=params(),
        cost_estimate=cost(3 * width * hid, 18 * width * hid),
        name="widen",
    )(summed)
    return (layer_out, token_grad, gates_grad_t.T, gate_grad[None], up_grad[None], down_grad[None])


def solution(mesh):
    rows = P(("expert", "dp"), None)
    weights = P("expert", None, None)
    return jax.shard_map(
        local,
        mesh=mesh,
        in_specs=(rows, rows, rows, weights, weights, weights, rows),
        out_specs=(rows, rows, rows, P("expert", "dp", None), P("expert", "dp", None), P("expert", None, "dp")),
        check_vma=False,
    )
```

profile of v0, /device:TPU:2, one launch (start us, length us, event | category | flops | bytes accessed | tf_op | source)
XLA Modules:
  0.0 210.6 jit_solution(17668368616252440313)
XLA Ops:
  7.2 4.0 %dispatch.1 = (bf16[512,2048]{1,0:T(8,128)(2,1)}, bf16[512,2048]{1,0:T(8,128)(2,1)}, bf16[512,48]{1,0:T(8,128)(2,1)}) custom-call(s32[8,48]{1,0:T(8,128)} %bitcast.29, f32[8,48]{1,0:T(8,128)} %bitcast.31, bf16[48,2048]{1,0:T(8,128)(2,1)} %tokens_ref.1, bf16[48,2048]{1,0:T(8,128)(2,1)} %grads_ref.1), custom_call_target="tpu_custom_call" | custom-call | flops 201326592 | bytes 4194304 | tf_op jit(solution)/shard_map/dispatch/pallas_call | solution.py:158
  11.2 35.1 %all_to_all.25 = bf16[32,16,2048]{2,1,0:T(8,128)(2,1)} all-to-all(bf16[32,16,2048]{2,1,0:T(8,128)(2,1)} %bitcast.27), channel_id=1, replica_groups=mesh['expert'=32,'dp'=8] {'expert'}, dimensions={0} | all-to-all | bytes 4194304 | tf_op jit(solution)/shard_map/all_to_all | solution.py:168
  46.3 5.1 %all-to-all-start.1 = ((bf16[32,16,2048]{2,1,0:T(8,128)(2,1)}), bf16[32,16,2048]{2,1,0:T(8,128)(2,1)S(1)}, u32[]{:S(2)}, u32[]{:S(2)}) async-start(bf16[32,16,2048]{2,1,0:T(8,128)(2,1)} %bitcast.24), calls=%async_computation.1 | async-start | bytes 4194304 | tf_op jit(solution)/shard_map/all_to_all | solution.py:168
  51.4 0.0 reduce-scatter.2.cloned.1.call-start
  51.4 8.1 %forward.1 = (bf16[512,768]{1,0:T(8,128)(2,1)}, f32[512,768]{1,0:T(8,128)}, f32[512,768]{1,0:T(8,128)}) custom-call(bf16[512,2048]{1,0:T(8,128)(2,1)} %bitcast.21, bf16[2048,768]{1,0:T(8,128)(2,1)} %bitcast.33, bf16[2048,768]{1,0:T(8,128)(2,1)} %bitcast.35), custom_call_target="tpu_custom_call" | custom-call | flops 3221225472 | bytes 12320768 | tf_op jit(solution)/shard_map/forward/pallas_call | solution.py:173
  59.5 19.8 %all-to-all-done.1 = bf16[32,16,2048]{2,1,0:T(8,128)(2,1)S(1)} async-done(((bf16[32,16,2048]{2,1,0:T(8,128)(2,1)}), bf16[32,16,2048]{2,1,0:T(8,128)(2,1)S(1)}, u32[]{:S(2)}, u32[]{:S(2)}) %all-to-all-start.1) | async-done | bytes 2097184 | tf_op jit(solution)/shard_map/all_to_all | solution.py:168
  79.4 0.0 copy-start
  79.4 1.4 copy-done
  80.8 14.8 %partials.1 = (bf16[72,256,256]{2,1,0:T(8,128)(2,1)}, bf16[512,768]{1,0:T(8,128)(2,1)}, bf16[512,768]{1,0:T(8,128)(2,1)}, f32[512,128]{1,0:T(8,128)}) custom-call(bf16[512,2048]{1,0:T(8,128)(2,1)} %bitcast.22, bf16[512,2048]{1,0:T(8,128)(2,1)} %bitcast.23, bf16[512,768]{1,0:T(8,128)(2,1)} %get-tuple-element.27.hidden_ref, ...), custom_call_target="tpu_custom_call" | custom-call | flops 6442450944 | bytes 22282240 | tf_op jit(solution)/shard_map/partials/pallas_call | solution.py:188
  95.6 0.0 reduce-scatter.2.cloned.1.call-update
  95.6 5.9 %all-to-all-start.2 = ((f32[32,16,128]{2,1,0:T(8,128)}), f32[32,16,128]{2,1,0:T(8,128)S(1)}, u32[]{:S(2)}, u32[]{:S(2)}) async-start(f32[32,16,128]{2,1,0:T(8,128)} %bitcast.9), calls=%async_computation.2 | async-start | bytes 524288 | tf_op jit(solution)/shard_map/all_to_all | solution.py:168
  101.5 11.5 %rows_back.1 = (bf16[512,2048]{1,0:T(8,128)(2,1)}, bf16[512,2048]{1,0:T(8,128)(2,1)}) custom-call(bf16[512,768]{1,0:T(8,128)(2,1)} %get-tuple-element.27.hidden_ref, bf16[512,768]{1,0:T(8,128)(2,1)} %get-tuple-element.31.gate_pre_ref, bf16[512,768]{1,0:T(8,128)(2,1)} %get-tuple-element.32.up_pre_ref, bf16[768,2048]{1,0:T(8,128)(2,1)} %bitcast.38, ...), custom_call_target="tpu_custom_call" | custom-call | flops 4831838208 | bytes 15990784 | tf_op jit(solution)/shard_map/rows_back/pallas_call | solution.py:219
  113.0 0.0 all-to-all-done.2
  113.0 0.0 copy-start.2
  113.0 0.0 copy-start.1
  113.0 35.1 %all_to_all.26 = bf16[32,16,2048]{2,1,0:T(8,128)(2,1)} all-to-all(bf16[32,16,2048]{2,1,0:T(8,128)(2,1)} %bitcast.26), channel_id=1, replica_groups=mesh['expert'=32,'dp'=8] {'expert'}, dimensions={0} | all-to-all | bytes 4194304 | tf_op jit(solution)/shard_map/all_to_all | solution.py:168
  148.1 0.0 copy-done.2
  148.1 0.0 copy-done.1
  148.1 32.2 %all_to_all.27 = bf16[32,16,2048]{2,1,0:T(8,128)(2,1)} all-to-all(bf16[32,16,2048]{2,1,0:T(8,128)(2,1)S(1)} %bitcast.25), channel_id=1, replica_groups=mesh['expert'=32,'dp'=8] {'expert'}, dimensions={0} | all-to-all | bytes 4194304 | tf_op jit(solution)/shard_map/all_to_all | solution.py:168
  180.3 4.2 %combine.1 = (bf16[48,2048]{1,0:T(8,128)(2,1)}, bf16[48,2048]{1,0:T(8,128)(2,1)}, f32[8,48]{1,0:T(8,128)}) custom-call(s32[8,48]{1,0:T(8,128)} %bitcast.30, f32[8,48]{1,0:T(8,128)} %bitcast.32, bf16[512,48]{1,0:T(8,128)(2,1)} %get-tuple-element.24.place_ref, f32[512,128]{1,0:T(8,128)} %bitcast.28, bf16[512,2048]{1,0:T(8,128)(2,1)} %bitcast.20, ...), custom_call_target="tpu_custom_call" | custom-call | flops 301989888 | bytes 4194304 | tf_op jit(solution)/shard_map/combine/pallas_call | solution.py:242
  184.5 16.5 %reduce-scatter.2.cloned.1.call-done.part_ref = bf16[9,256,256]{2,1,0:T(8,128)(2,1)} async-done(((bf16[72,256,256]{2,1,0:T(8,128)(2,1)}), bf16[9,256,256]{2,1,0:T(8,128)(2,1)}) %reduce-scatter.2.cloned.1.call-update) | async-done | bytes 1179664 | tf_op jit(solution)/shard_map/reduce_scatter | solution.py:217
  201.0 2.7 %widen.1 = (f32[256,768]{1,0:T(8,128)}, f32[256,768]{1,0:T(8,128)}, f32[768,256]{1,0:T(8,128)}) custom-call(bf16[9,256,256]{2,1,0:T(8,128)(2,1)} %reduce-scatter.2.cloned.1.call-done.part_ref), custom_call_target="tpu_custom_call" | custom-call | flops 589824 | bytes 3538944 | tf_op jit(solution)/shard_map/widen/pallas_call | solution.py:265
Async XLA Ops:
  46.3 33.1 %all-to-all-start.1 = ((bf16[32,16,2048]{2,1,0:T(8,128)(2,1)}), bf16[32,16,2048]{2,1,0:T(8,128)(2,1)S(1)}, u32[]{:S(2)}, u32[]{:S(2)}) async-start(bf16[32,16,2048]{2,1,0:T(8,128)(2,1)} %bitcast.24), calls=%async_computation.1 | async-start | bytes 4194304 | tf_op jit(solution)/shard_map/all_to_all | solution.py:168
  51.4 149.6 %reduce-scatter.2.cloned.1.call-start = ((), (), s32[]{:S(2)}) async-start(), calls=%async_computation.6 | async-start | bytes 10616832 | tf_op jit(solution)/shard_map/reduce_scatter | solution.py:217
  79.4 1.4 copy-start
  95.6 17.4 %all-to-all-start.2 = ((f32[32,16,128]{2,1,0:T(8,128)}), f32[32,16,128]{2,1,0:T(8,128)S(1)}, u32[]{:S(2)}, u32[]{:S(2)}) async-start(f32[32,16,128]{2,1,0:T(8,128)} %bitcast.9), calls=%async_computation.2 | async-start | bytes 524288 | tf_op jit(solution)/shard_map/all_to_all | solution.py:168
  113.0 35.1 %copy-start.2 = (f32[32,16,128]{2,1,0:T(8,128)}, f32[32,16,128]{2,1,0:T(8,128)S(1)}, u32[]{:S(2)}) copy-start(f32[32,16,128]{2,1,0:T(8,128)S(1)} %all-to-all-done.2) | copy-start | bytes 786436
  113.0 35.1 %copy-start.1 = (bf16[512,2048]{1,0:T(8,128)(2,1)S(1)}, bf16[512,2048]{1,0:T(8,128)(2,1)}, u32[]{:S(2)}) copy-start(bf16[512,2048]{1,0:T(8,128)(2,1)} %get-tuple-element.33) | copy-start | bytes 6291460
Sparse Core Ops, SparseCore 0:
  95.7 105.2 reduce-scatter.1
where the time goes:
time: 212 us; the launch traced here: 211 us
  blocking collectives  102 us (48%)
  Pallas kernels  45.2 us (21%)
  waiting for transfers between devices  36.4 us (17%)
  between operations  14.1 us (7%)
  starting transfers between devices  11.1 us (5%)
    all_to_all x3, blocking collectives, exchange(): return lax.all_to_all(wide, 'expert', 0, 0, tiled=True).reshape(array.shape)  102 us
    all_to_all x2, waiting for transfers between devices, exchange(): return lax.all_to_all(wide, 'expert', 0, 0, tiled=True).reshape(array.shape)  19.8 us
    reduce_scatter x1, waiting for transfers between devices, local(): summed = lax.psum_scatter(part, 'dp', scatter_dimension=0, tiled=True)  16.5 us
    pallas_call x1, Pallas kernels, local(): pl.pallas_call(partial_kernel, grid=(groups,), in_specs=[pl.BlockSpec((sl...  14.8 us
    pallas_call x1, Pallas kernels, local(): pl.pallas_call(return_kernel, grid=(groups,), in_specs=[whole((slots, hid...  11.5 us
    all_to_all x2, starting transfers between devices, exchange(): return lax.all_to_all(wide, 'expert', 0, 0, tiled=True).reshape(array.shape)  11 us
    pallas_call x1, Pallas kernels, local(): pl.pallas_call(forward_kernel, grid=(blocks,), in_specs=[whole((slots, mo...  8.08 us
  transfers between devices with their start and end apart: 3, of which 2 were waited for; matrix products, arithmetic and copies ran while one was open for 0% of the time, Pallas kernels for 11%

commit v1 on v0

v1 whole, which is shorter than its diff:
```python
import functools

import jax
import jax.numpy as jnp
from jax import lax
from jax.experimental import pallas as pl
from jax.experimental.pallas import tpu as pltpu
from jax.sharding import PartitionSpec as P

BF16 = jnp.bfloat16
F32 = jnp.float32
LAST = (((1,), (1,)), ((), ()))
FIRST = (((0,), (0,)), ((), ()))
VMEM_LIMIT = 60 * 2**20


def params():
    return pltpu.CompilerParams(vmem_limit_bytes=VMEM_LIMIT)


def cost(flops, nbytes, exps=0):
    return pl.CostEstimate(flops=flops, bytes_accessed=nbytes, transcendentals=exps)


def dot(a, b, dims=(((1,), (0,)), ((), ()))):
    return lax.dot_general(a, b, dims, preferred_element_type=F32)


def slot_masks(routes_t, slots, capacity):
    tokens = routes_t.shape[1]
    expert = lax.broadcasted_iota(jnp.int32, (slots, tokens), 0) // capacity
    return [expert == routes_t[k : k + 1, :] for k in range(routes_t.shape[0])]


def dispatch_kernel(capacity, routes_ref, gates_ref, tokens_ref, grads_ref, rows_ref, scaled_ref, place_ref):
    routes_t, gates_t = routes_ref[...], gates_ref[...]
    slots, tokens = place_ref.shape
    masks = slot_masks(routes_t, slots, capacity)
    hit = jnp.zeros((slots, tokens), F32)
    weight = jnp.zeros((slots, tokens), F32)
    for k, mask in enumerate(masks):
        hit = jnp.where(mask, 1.0, hit)
        weight = jnp.where(mask, gates_t[k : k + 1, :], weight)
    before = (
        lax.broadcasted_iota(jnp.int32, (tokens, tokens), 0)
        < lax.broadcasted_iota(jnp.int32, (tokens, tokens), 1)
    ).astype(F32).astype(BF16)
    rank = dot(hit.astype(BF16), before)
    mine = (lax.broadcasted_iota(jnp.int32, (slots, tokens), 0) % capacity).astype(F32)
    place = jnp.where(rank == mine, hit, 0.0)
    slot_weight = jnp.sum(place * weight, axis=1, keepdims=True)
    place_low = place.astype(BF16)
    place_ref[...] = place_low
    rows_ref[...] = dot(place_low, tokens_ref[...]).astype(BF16)
    scaled_ref[...] = (slot_weight * dot(place_low, grads_ref[...])).astype(BF16)


def forward_kernel(rows_ref, gate_ref, up_ref, hidden_ref, gate_slope_ref, up_slope_ref):
    rows = rows_ref[...]
    pre_gate = dot(rows, gate_ref[...])
    pre_up = dot(rows, up_ref[...])
    sig = jax.nn.sigmoid(pre_gate)
    silu = pre_gate * sig
    hidden_ref[...] = (silu * pre_up).astype(BF16)
    gate_slope_ref[...] = pre_up * sig * (1.0 + pre_gate * (1.0 - sig))
    up_slope_ref[...] = silu


def backward_kernel(
    grads_ref, hidden_ref, gate_slope_ref, up_slope_ref, down_ref, _, gate_pre_ref, up_pre_ref, hidden_t_ref
):
    hidden_grad = dot(grads_ref[...], down_ref[...], LAST)
    gate_pre_ref[...] = (hidden_grad * gate_slope_ref[...]).astype(BF16)
    up_pre_ref[...] = (hidden_grad * up_slope_ref[...]).astype(BF16)
    hidden_t_ref[...] = hidden_ref[...].T


def chunk_sums(rows_a, rows_b, grads_b, gate_pre, up_pre, hidden_t, held_a, held_b):
    width = rows_a.shape[1]
    blocks = gate_pre.shape[1] // width
    turned_a, turned_b = rows_a[...].T, rows_b[...].T
    grads = grads_b[...]
    for j in range(blocks + 1):
        source = gate_pre[:, j * width : (j + 1) * width] if j < blocks else up_pre[:, :width]
        total = dot(turned_a, source)
        for held in held_a:
            total = total + held[j].astype(F32)
        yield "a", j, total
    for j in range(2 * blocks - 1):
        if j < blocks - 1:
            total = dot(turned_b, up_pre[:, (j + 1) * width : (j + 2) * width])
        else:
            i = j - blocks + 1
            total = dot(hidden_t[i * width : (i + 1) * width, :], grads)
        for held in held_b:
            total = total + held[j].astype(F32)
        yield "b", j, total


def link_kernel(arrived, _, rows_a, rows_b, grads_b, gate_pre, up_pre, hidden_t, *refs):
    held_a, held_b = ([refs[0]], [refs[1]]) if arrived else ([], [])
    out = {"a": refs[-2], "b": refs[-1]}
    for part, j, total in chunk_sums(rows_a, rows_b, grads_b, gate_pre, up_pre, hidden_t, held_a, held_b):
        out[part][j] = total.astype(BF16)


def last_kernel(_, rows_a, rows_b, grads_b, gate_pre, up_pre, hidden_t, a0, a1, b0, b1, gate_ref, up_ref, down_ref):
    width = rows_a.shape[1]
    blocks = gate_pre.shape[1] // width
    for part, j, total in chunk_sums(rows_a, rows_b, grads_b, gate_pre, up_pre, hidden_t, [a0, a1], [b0, b1]):
        if part == "a" and j < blocks:
            gate_ref[:, j * width : (j + 1) * width] = total
        elif part == "a":
            up_ref[:, :width] = total
        elif j < blocks - 1:
            up_ref[:, (j + 1) * width : (j + 2) * width] = total
        else:
            i = j - blocks + 1
            down_ref[i * width : (i + 1) * width, :] = total


def output_kernel(hidden_ref, down_ref, out_ref):
    out_ref[...] = dot(hidden_ref[...], down_ref[...]).astype(BF16)


def row_grad_kernel(gate_pre_ref, up_pre_ref, gate_ref, up_ref, _, after, row_grad_ref):
    row_grad_ref[...] = (
        dot(gate_pre_ref[...], gate_ref[...], LAST) + dot(up_pre_ref[...], up_ref[...], LAST)
    ).astype(BF16)


def combine_kernel(
    capacity, routes_ref, gates_ref, place_ref, grads_ref, back_ref, back_grad_ref,
    out_ref, grad_ref, gates_grad_ref, high, low, score,
):
    step = pl.program_id(0)

    @pl.when(step == 0)
    def _():
        gates_t = gates_ref[...]
        weight = jnp.zeros(place_ref.shape, F32)
        for k, mask in enumerate(slot_masks(routes_ref[...], place_ref.shape[0], capacity)):
            weight = jnp.where(mask, gates_t[k : k + 1, :], weight)
        weight = weight * place_ref[...].astype(F32)
        high[...] = weight.astype(BF16)
        low[...] = (weight - weight.astype(BF16).astype(F32)).astype(BF16)
        score[...] = jnp.zeros_like(score)

    back = back_ref[...]
    out_ref[...] = (dot(high[...], back, FIRST) + dot(low[...], back, FIRST)).astype(BF16)
    grad_ref[...] = dot(place_ref[...], back_grad_ref[...], FIRST).astype(BF16)
    slot_grads = dot(place_ref[...], grads_ref[...])
    score[...] += jnp.sum(slot_grads * back.astype(F32), axis=1, keepdims=True)

    @pl.when(step == pl.num_programs(0) - 1)
    def _():
        placed = score[...] * place_ref[...].astype(F32)
        for k, mask in enumerate(slot_masks(routes_ref[...], place_ref.shape[0], capacity)):
            gates_grad_ref[k : k + 1, :] = jnp.sum(jnp.where(mask, placed, 0.0), axis=0, keepdims=True)


def shape(dims, dtype=BF16):
    return jax.ShapeDtypeStruct(dims, dtype)


def whole(dims):
    return pl.BlockSpec(dims, lambda i: (0,) * len(dims))


def local(tokens, routes, gate_weights, w_gate, w_up, w_down, out_grad):
    count, top = routes.shape
    model = tokens.shape[1]
    experts = w_gate.shape[0] * lax.axis_size("expert")
    groups = lax.axis_size("dp")
    capacity = max(2, 4 * count * top // (3 * experts))
    slots = experts * capacity
    hid = w_gate.shape[2]
    width = model // groups
    blocks = hid // width
    w_gate, w_up, w_down = w_gate[0], w_up[0], w_down[0]
    routes_t, gates_t = routes.T, gate_weights.T

    send_rows, send_grads, place = pl.pallas_call(
        functools.partial(dispatch_kernel, capacity),
        out_shape=(shape((slots, model)), shape((slots, model)), shape((slots, count))),
        compiler_params=params(),
        cost_estimate=cost(4 * slots * count * model, 4 * slots * model),
        name="dispatch",
    )(routes_t, gates_t, tokens, out_grad)

    def exchange(array):
        wide = array.reshape(experts, capacity, array.shape[1])
        return lax.all_to_all(wide, "expert", 0, 0, tiled=True).reshape(array.shape)

    rows = exchange(send_rows)
    grads = exchange(send_grads)

    hidden, gate_slope, up_slope = pl.pallas_call(
        forward_kernel,
        grid=(blocks,),
        in_specs=[
            whole((slots, model)),
            pl.BlockSpec((model, width), lambda i: (0, i)),
            pl.BlockSpec((model, width), lambda i: (0, i)),
        ],
        out_specs=[pl.BlockSpec((slots, width), lambda i: (0, i))] * 3,
        out_shape=(shape((slots, hid)), shape((slots, hid), F32), shape((slots, hid), F32)),
        compiler_params=params(),
        cost_estimate=cost(4 * slots * model * hid, 2 * slots * model + 4 * model * hid + 10 * slots * hid),
        name="forward",
    )(rows, w_gate, w_up)

    going_back = pl.pallas_call(
        output_kernel,
        grid=(groups,),
        in_specs=[whole((slots, hid)), pl.BlockSpec((hid, width), lambda i: (0, i))],
        out_specs=pl.BlockSpec((slots, width), lambda i: (0, i)),
        out_shape=shape((slots, 2 * model)),
        compiler_params=params(),
        cost_estimate=cost(2 * slots * model * hid, 2 * slots * model + 2 * model * hid + 2 * slots * hid),
        name="outputs",
    )(hidden, w_down)

    tile = pl.BlockSpec((slots, width), lambda i: (0, i))
    anywhere = pl.BlockSpec(memory_space=pl.ANY)
    gate_pre, up_pre, hidden_t = pl.pallas_call(
        backward_kernel,
        grid=(blocks,),
        in_specs=[whole((slots, model)), tile, tile, tile, pl.BlockSpec((width, model), lambda i: (i, 0)), anywhere],
        out_specs=[tile, tile, pl.BlockSpec((width, slots), lambda i: (i, 0))],
        out_shape=(shape((slots, hid)), shape((slots, hid)), shape((hid, slots))),
        compiler_params=params(),
        cost_estimate=cost(2 * slots * model * hid, 2 * slots * model + 2 * model * hid + 14 * slots * hid),
        name="backward",
    )(grads, hidden, gate_slope, up_slope, w_down, going_back)

    me = lax.axis_index("dp")
    place_of = me.reshape(1).astype(jnp.int32)

    def chain_call(kernel, step_a, step_b, out_shape, held, name, kept=(), after=()):
        size = lambda n: pl.BlockSpec((n, width, width), lambda i, p: (0, 0, 0))
        fixed = lambda dims: pl.BlockSpec(dims, lambda i, p: (0, 0))
        return pl.pallas_call(
            kernel,
            grid_spec=pltpu.PrefetchScalarGridSpec(
                num_scalar_prefetch=1,
                grid=(1,),
                in_specs=[
                    pl.BlockSpec((slots, width), lambda i, p: (0, lax.rem(p[0] + step_a, groups))),
                    pl.BlockSpec((slots, width), lambda i, p: (0, lax.rem(p[0] + step_b, groups))),
                    pl.BlockSpec((slots, width), lambda i, p: (0, lax.rem(p[0] + step_b, groups))),
                    fixed((slots, hid)),
                    fixed((slots, hid)),
                    fixed((hid, slots)),
                    *[size(h.shape[0]) for h in held],
                    *[anywhere for _ in (*kept, *after)],
                ],
                out_specs=[
                    *[anywhere for _ in kept],
                    *[pl.BlockSpec(o.shape, lambda i, p, n=len(o.shape): (0,) * n) for o in out_shape],
                ],
            ),
            out_shape=(*[shape(x.shape, x.dtype) for x in kept], *out_shape),
            input_output_aliases={7 + len(held) + i: i for i in range(len(kept))},
            compiler_params=params(),
            cost_estimate=cost(20 * 10**9, 60 * 2**20),
            name=name,
        )(place_of, rows, rows, grads, gate_pre, up_pre, hidden_t, *held, *kept, *after)

    up_ring = [(i, (i + 1) % groups) for i in range(groups)]
    down_ring = [(i, (i - 1) % groups) for i in range(groups)]
    part_shapes = (shape((blocks + 1, width, width)), shape((2 * blocks - 1, width, width)))
    half_way = groups // 2
    slots_of_ring = [(half_way, 0)] + [(k, s) for k in range(half_way - 1, 0, -1) for s in (1, 0)]
    def row_grads(after):
        return pl.pallas_call(
            row_grad_kernel,
            grid=(groups,),
            in_specs=[
                whole((slots, hid)),
                whole((slots, hid)),
                pl.BlockSpec((width, hid), lambda i: (i, 0)),
                pl.BlockSpec((width, hid), lambda i: (i, 0)),
                anywhere,
                anywhere,
            ],
            out_specs=pl.BlockSpec((slots, width), lambda i: (0, groups + i)),
            out_shape=shape((slots, 2 * model)),
            input_output_aliases={4: 0},
            compiler_params=params(),
            cost_estimate=cost(20 * 10**9, 60 * 2**20),
            name="row_grads",
        )(gate_pre, up_pre, w_gate, w_up, going_back, after)

    came, after = {}, ()
    for number, (k, swapped) in enumerate(slots_of_ring):
        step_a, step_b = (groups - k, k) if swapped else (k, groups - k)
        held = came.get((k, swapped), ())
        kept = (going_back,) if number == 2 else ()
        *kept, part_a, part_b = chain_call(
            functools.partial(link_kernel, bool(held)),
            step_a, step_b, part_shapes, held, f"chain_sum_{number}", kept, after,
        )
        after = (part_a,)
        if number == 1:
            going_back = row_grads(part_a)
            after = ()
        elif number == 2:
            [going_back] = kept
        ring_a, ring_b = (down_ring, up_ring) if swapped else (up_ring, down_ring)
        came[k - 1, swapped] = (lax.ppermute(part_a, "dp", ring_a), lax.ppermute(part_b, "dp", ring_b))

    back = exchange(going_back)

    half = model // 2
    layer_out, token_grad, gates_grad_t = pl.pallas_call(
        functools.partial(combine_kernel, capacity),
        grid=(2,),
        in_specs=[
            whole((top, count)),
            whole((top, count)),
            whole((slots, count)),
            pl.BlockSpec((count, half), lambda i: (0, i)),
            pl.BlockSpec((slots, half), lambda i: (0, i)),
            pl.BlockSpec((slots, half), lambda i: (0, 2 + i)),
        ],
        out_specs=[
            pl.BlockSpec((count, half), lambda i: (0, i)),
            pl.BlockSpec((count, half), lambda i: (0, i)),
            whole((top, count)),
        ],
        out_shape=(shape((count, model)), shape((count, model)), shape((top, count), F32)),
        scratch_shapes=[pltpu.VMEM((slots, count), BF16)] * 2 + [pltpu.VMEM((slots, 1), F32)],
        compiler_params=params(),
        cost_estimate=cost(8 * slots * count * model, 4 * slots * model),
        name="combine",
    )(routes_t, gates_t, place, out_grad, back, back)

    (a0, b0), (a1, b1) = came[0, 0], came[0, 1]
    gate_grad, up_grad, down_grad = chain_call(
        last_kernel,
        0,
        0,
        (shape((width, hid), F32), shape((width, hid), F32), shape((hid, width), F32)),
        (a0, a1, b0, b1),
        "chain_sum_last",
    )
    return (layer_out, token_grad, gates_grad_t.T, gate_grad[None], up_grad[None], down_grad[None])


def solution(mesh):
    rows = P(("expert", "dp"), None)
    weights = P("expert", None, None)
    return jax.shard_map(
        local,
        mesh=mesh,
        in_specs=(rows, rows, rows, weights, weights, weights, rows),
        out_specs=(rows, rows, rows, P("expert", "dp", None), P("expert", "dp", None), P("expert", None, "dp")),
        check_vma=False,
    )
```

time: 212 us -> 212 us (level)
  blocking collectives: 102 us -> 35.1 us
  Pallas kernels: 45.2 us -> 72.5 us
  starting transfers between devices: 11.1 us -> 38.4 us
  waiting for transfers between devices: 36.4 us -> 55.6 us
  between operations: 14.1 us -> 0.86 us
  local copies, waits for them, and re-layouts: 1.45 us -> 8.15 us
    all_to_all x3 -> x1, blocking collectives: 102 us -> 35.1 us  [exchange(): return lax.all_to_all(wide, 'expert', 0, 0, tiled=True).reshape(array.shape)]
    ppermute x0 -> x14, waiting for transfers between devices: none -> 43.2 us  [the longest x7 35 us: local(): lax.ppermute(part_a, 'dp', ring_a)]
    ppermute x0 -> x14, starting transfers between devices: none -> 26.4 us  [the longest x7 15.1 us: local(): lax.ppermute(part_b, 'dp', ring_b)]
    pallas_call x3 -> x11, Pallas kernels: 29 us -> 54.9 us  [the longest x8 30.8 us: chain_call(): pl.pallas_call(kernel, grid_spec=pltpu.PrefetchScalarGridSpec(num_scalar_...]
    reduce_scatter x1 -> x0, waiting for transfers between devices: 16.5 us -> none  [local(): summed = lax.psum_scatter(part, 'dp', scatter_dimension=0, tiled=True)]
    all_to_all x2, waiting for transfers between devices: 19.8 us -> 12.4 us  [exchange(): return lax.all_to_all(wide, 'expert', 0, 0, tiled=True).reshape(array.shape)]
    unnamed x6 -> x38, local copies, waits for them, and re-layouts: 1.45 us -> 8.15 us
  transfers between devices with their start and end apart: 3 -> 16, of which waited for: 2 -> 9; matrix products, arithmetic and copies ran while one was open for 0% -> 0% of each run, Pallas kernels for 11% -> 25%
where the time goes in v1:
time: 212 us; the launch traced here: 211 us
  Pallas kernels  72.5 us (34%)
  waiting for transfers between devices  55.6 us (26%)
  starting transfers between devices  38.4 us (18%)
  blocking collectives  35.1 us (17%)
  local copies, waits for them, and re-layouts  8.15 us (4%)
    all_to_all x1, blocking collectives, exchange(): return lax.all_to_all(wide, 'expert', 0, 0, tiled=True).reshape(array.shape)  35.1 us
    ppermute x7, waiting for transfers between devices, local(): lax.ppermute(part_a, 'dp', ring_a)  35 us
    pallas_call x8, Pallas kernels, chain_call(): pl.pallas_call(kernel, grid_spec=pltpu.PrefetchScalarGridSpec(num_scalar_...  30.8 us
    ppermute x7, starting transfers between devices, local(): lax.ppermute(part_b, 'dp', ring_b)  15.1 us
    all_to_all x2, waiting for transfers between devices, exchange(): return lax.all_to_all(wide, 'expert', 0, 0, tiled=True).reshape(array.shape)  12.4 us
    all_to_all x2, starting transfers between devices, exchange(): return lax.all_to_all(wide, 'expert', 0, 0, tiled=True).reshape(array.shape)  12.1 us
    ppermute x7, starting transfers between devices, local(): lax.ppermute(part_a, 'dp', ring_a)  11.3 us
    pallas_call x1, Pallas kernels, row_grads(): pl.pallas_call(row_grad_kernel, grid=(groups,), in_specs=[whole((slots, h...  9.37 us
  transfers between devices with their start and end apart: 16, of which 9 were waited for; matrix products, arithmetic and copies ran while one was open for 0% of the time, Pallas kernels for 25%

profile of v1, /device:TPU:2, one launch (start us, length us, event | category | flops | bytes accessed | tf_op | source)
XLA Modules:
  0.0 210.6 jit_solution(12053877312178917026)
XLA Ops:
  0.6 4.1 %dispatch.1 = (bf16[512,2048]{1,0:T(8,128)(2,1)}, bf16[512,2048]{1,0:T(8,128)(2,1)}, bf16[512,48]{1,0:T(8,128)(2,1)}) custom-call(s32[8,48]{1,0:T(8,128)} %bitcast.47, f32[8,48]{1,0:T(8,128)} %bitcast.49, bf16[48,2048]{1,0:T(8,128)(2,1)} %tokens_ref.1, bf16[48,2048]{1,0:T(8,128)(2,1)} %grads_ref.3), custom_call_target="tpu_custom_call" | custom-call | flops 201326592 | bytes 4194304 | tf_op jit(solution)/shard_map/dispatch/pallas_call | solution.py:183
  4.7 35.1 %all_to_all.15 = bf16[32,16,2048]{2,1,0:T(8,128)(2,1)} all-to-all(bf16[32,16,2048]{2,1,0:T(8,128)(2,1)} %bitcast.46), channel_id=1, replica_groups=mesh['expert'=32,'dp'=8] {'expert'}, dimensions={0} | all-to-all | bytes 4194304 | tf_op jit(solution)/shard_map/all_to_all | solution.py:193
  39.8 5.1 %all-to-all-start.1 = ((bf16[32,16,2048]{2,1,0:T(8,128)(2,1)}), bf16[32,16,2048]{2,1,0:T(8,128)(2,1)S(1)}, u32[]{:S(2)}, u32[]{:S(2)}) async-start(bf16[32,16,2048]{2,1,0:T(8,128)(2,1)} %bitcast.45), calls=%async_computation.1 | async-start | bytes 4194304 | tf_op jit(solution)/shard_map/all_to_all | solution.py:193
  45.0 8.1 %forward.1 = (bf16[512,768]{1,0:T(8,128)(2,1)}, f32[512,768]{1,0:T(8,128)}, f32[512,768]{1,0:T(8,128)}) custom-call(bf16[512,2048]{1,0:T(8,128)(2,1)} %bitcast.28, bf16[2048,768]{1,0:T(8,128)(2,1)} %bitcast.51, bf16[2048,768]{1,0:T(8,128)(2,1)} %bitcast.53), custom_call_target="tpu_custom_call" | custom-call | flops 3221225472 | bytes 12320768 | tf_op jit(solution)/shard_map/forward/pallas_call | solution.py:198
  53.0 7.5 %outputs.1._ = bf16[512,4096]{1,0:T(8,128)(2,1)} custom-call(bf16[512,768]{1,0:T(8,128)(2,1)} %get-tuple-element.39.hidden_ref, bf16[768,2048]{1,0:T(8,128)(2,1)} %bitcast.17), custom_call_target="tpu_custom_call" | custom-call | flops 1610612736 | bytes 6029312 | tf_op jit(solution)/shard_map/outputs/pallas_call | solution.py:213
  60.5 12.4 %all-to-all-done.1 = bf16[32,16,2048]{2,1,0:T(8,128)(2,1)S(1)} async-done(((bf16[32,16,2048]{2,1,0:T(8,128)(2,1)}), bf16[32,16,2048]{2,1,0:T(8,128)(2,1)S(1)}, u32[]{:S(2)}, u32[]{:S(2)}) %all-to-all-start.1) | async-done | bytes 2097184 | tf_op jit(solution)/shard_map/all_to_all | solution.py:193
  72.9 1.4 copy-done
  74.3 7.2 %backward.1 = (bf16[512,768]{1,0:T(8,128)(2,1)}, bf16[512,768]{1,0:T(8,128)(2,1)}, bf16[768,512]{1,0:T(8,128)(2,1)}) custom-call(bf16[512,2048]{1,0:T(8,128)(2,1)} %bitcast.19, bf16[512,768]{1,0:T(8,128)(2,1)} %get-tuple-element.39.hidden_ref, f32[512,768]{1,0:T(8,128)} %get-tuple-element.40.gate_slope_ref, f32[512,768]{1,0:T(8,128)} %get-tuple-element.41.up_slope_ref, ...), custom_call_target="tpu_custom_call" | custom-call | flops 1610612736 | bytes 10747904 | tf_op jit(solution)/shard_map/backward/pallas_call | solution.py:226
  81.5 3.5 %chain_sum_0.1 = (bf16[4,256,256]{2,1,0:T(8,128)(2,1)}, bf16[5,256,256]{2,1,0:T(8,128)(2,1)}) custom-call(s32[1]{0:T(128)} %bitcast.2._, bf16[512,2048]{1,0:T(8,128)(2,1)} %bitcast.29, bf16[512,2048]{1,0:T(8,128)(2,1)} %bitcast.30, bf16[512,2048]{1,0:T(8,128)(2,1)} %bitcast.20, bf16[512,768]{1,0:T(8,128)(2,1)} %get-tuple-element.42.gate_pre.gate_pre_ref, ...), custom_call_target="tpu_custom_call" | custom-call | flops 20000000000 | bytes 62914560 | tf_op jit(solution)/shard_map/chain_sum_0/pallas_call | solution.py:243
  85.0 1.9 collective-permute-start
  87.0 3.5 %chain_sum_1.1 = (bf16[4,256,256]{2,1,0:T(8,128)(2,1)}, bf16[5,256,256]{2,1,0:T(8,128)(2,1)}) custom-call(s32[1]{0:T(128)} %bitcast.2._, bf16[512,2048]{1,0:T(8,128)(2,1)} %bitcast.31, bf16[512,2048]{1,0:T(8,128)(2,1)} %bitcast.32, bf16[512,2048]{1,0:T(8,128)(2,1)} %bitcast.21, bf16[512,768]{1,0:T(8,128)(2,1)} %get-tuple-element.42.gate_pre.gate_pre_ref, ...), custom_call_target="tpu_custom_call" | custom-call | flops 20000000000 | bytes 62914560 | tf_op jit(solution)/shard_map/chain_sum_1/pallas_call | solution.py:243
  90.5 0.0 copy-done.9
  90.5 4.0 %collective-permute-start.1 = (bf16[5,256,256]{2,1,0:T(8,128)(2,1)S(1)}, bf16[5,256,256]{2,1,0:T(8,128)(2,1)S(1)}, u32[]{:S(2)}, u32[]{:S(2)}) collective-permute-start(bf16[5,256,256]{2,1,0:T(8,128)(2,1)S(1)} %copy-done.9), channel_id=1, source_target_pairs={{0,7},{1,0},{2,1},{3,2},{4,3},{5,4},{6,5},{7,6},{8,15},{9,8},{10,9... | collective-permute-start | bytes 1966088 | tf_op jit(solution)/shard_map/ppermute | solution.py:311
  94.5 9.4 %row_grads.1.refs_2_ = bf16[512,4096]{1,0:T(8,128)(2,1)} custom-call(bf16[512,768]{1,0:T(8,128)(2,1)} %get-tuple-element.42.gate_pre.gate_pre_ref, bf16[512,768]{1,0:T(8,128)(2,1)} %get-tuple-element.43.up_pre.up_pre_ref, bf16[2048,768]{1,0:T(8,128)(2,1)} %bitcast.52, bf16[2048,768]{1,0:T(8,128)(2,1)} %bitcast.54, ...), custom_call_target="tpu_custom_call", output_to_operand_aliasing={{}: (4, {})} | custom-call | flops 20000000000 | bytes 62914560 | tf_op jit(solution)/shard_map/row_grads/pallas_call | solution.py:276
  103.9 0.0 copy-done.11
  103.9 2.0 collective-permute-start.4
  105.8 0.0 copy-done.2
  105.8 0.1 collective-permute-start.5
  105.9 0.0 collective-permute-done.refs_0_
  105.9 3.8 %collective-permute-done.1.refs_1_ = bf16[5,256,256]{2,1,0:T(8,128)(2,1)S(1)} collective-permute-done((bf16[5,256,256]{2,1,0:T(8,128)(2,1)S(1)}, bf16[5,256,256]{2,1,0:T(8,128)(2,1)S(1)}, u32[]{:S(2)}, u32[]{:S(2)}) %collective-permute-start.1) | collective-permute-done | bytes 655392 | tf_op jit(solution)/shard_map/ppermute | solution.py:311
  109.7 0.0 copy-done.17
  109.7 0.8 copy-done.10
  110.5 3.9 %chain_sum_2.1 = (bf16[512,4096]{1,0:T(8,128)(2,1)}, bf16[4,256,256]{2,1,0:T(8,128)(2,1)}, bf16[5,256,256]{2,1,0:T(8,128)(2,1)}) custom-call(s32[1]{0:T(128)} %bitcast.2._, bf16[512,2048]{1,0:T(8,128)(2,1)} %bitcast.33, bf16[512,2048]{1,0:T(8,128)(2,1)} %bitcast.34, bf16[512,2048]{1,0:T(8,128)(2,1)} %bitcast.22, ...), custom_call_target="tpu_custom_call", output_to_operand_aliasing={{0}: (9, {})} | custom-call | flops 20000000000 | bytes 62914560 | tf_op jit(solution)/shard_map/chain_sum_2/pallas_call | solution.py:243
  114.4 6.9 %all-to-all-start.2 = ((bf16[32,16,4096]{2,1,0:T(8,128)(2,1)}), bf16[32,16,4096]{2,1,0:T(8,128)(2,1)}, u32[]{:S(2)}, u32[]{:S(2)}) async-start(bf16[32,16,4096]{2,1,0:T(8,128)(2,1)} %bitcast.16), calls=%async_computation.2 | async-start | bytes 8388608 | tf_op jit(solution)/shard_map/all_to_all | solution.py:193
  121.3 0.5 collective-permute-start.2
  121.8 0.0 copy-done.3
  121.8 3.5 %collective-permute-start.3 = (bf16[5,256,256]{2,1,0:T(8,128)(2,1)S(1)}, bf16[5,256,256]{2,1,0:T(8,128)(2,1)S(1)}, u32[]{:S(2)}, u32[]{:S(2)}) collective-permute-start(bf16[5,256,256]{2,1,0:T(8,128)(2,1)S(1)} %copy-done.3), channel_id=1, source_target_pairs={{0,7},{1,0},{2,1},{3,2},{4,3},{5,4},{6,5},{7,6},{8,15},{9,8},{10,9... | collective-permute-start | bytes 1966088 | tf_op jit(solution)/shard_map/ppermute | solution.py:311
  125.4 0.0 collective-permute-done.4.refs_0_
  125.4 0.0 collective-permute-done.5.refs_1_
  125.4 0.8 copy-done.4
  126.2 3.9 %chain_sum_3.1 = (bf16[4,256,256]{2,1,0:T(8,128)(2,1)}, bf16[5,256,256]{2,1,0:T(8,128)(2,1)}) custom-call(s32[1]{0:T(128)} %bitcast.2._, bf16[512,2048]{1,0:T(8,128)(2,1)} %bitcast.35, bf16[512,2048]{1,0:T(8,128)(2,1)} %bitcast.36, bf16[512,2048]{1,0:T(8,128)(2,1)} %bitcast.23, bf16[512,768]{1,0:T(8,128)(2,1)} %get-tuple-element.42.gate_pre.gate_pre_ref, ...), custom_call_target="tpu_custom_call" | custom-call | flops 20000000000 | bytes 62914560 | tf_op jit(solution)/shard_map/chain_sum_3/pallas_call | solution.py:243
  130.1 1.7 collective-permute-start.8
  131.8 0.3 collective-permute-start.9
  132.1 5.9 %collective-permute-done.2.refs_0_ = bf16[4,256,256]{2,1,0:T(8,128)(2,1)S(1)} collective-permute-done((bf16[4,256,256]{2,1,0:T(8,128)(2,1)}, bf16[4,256,256]{2,1,0:T(8,128)(2,1)S(1)}, u32[]{:S(2)}, u32[]{:S(2)}) %collective-permute-start.2) | collective-permute-done | bytes 524320 | tf_op jit(solution)/shard_map/ppermute | solution.py:311
  138.0 2.5 %collective-permute-done.3.refs_1_ = bf16[5,256,256]{2,1,0:T(8,128)(2,1)S(1)} collective-permute-done((bf16[5,256,256]{2,1,0:T(8,128)(2,1)S(1)}, bf16[5,256,256]{2,1,0:T(8,128)(2,1)S(1)}, u32[]{:S(2)}, u32[]{:S(2)}) %collective-permute-start.3) | collective-permute-done | bytes 655392 | tf_op jit(solution)/shard_map/ppermute | solution.py:311
  140.5 0.0 copy-done.12
  140.5 0.8 copy-done.6
  141.3 3.9 %chain_sum_4.1 = (bf16[4,256,256]{2,1,0:T(8,128)(2,1)}, bf16[5,256,256]{2,1,0:T(8,128)(2,1)}) custom-call(s32[1]{0:T(128)} %bitcast.2._, bf16[512,2048]{1,0:T(8,128)(2,1)} %bitcast.37, bf16[512,2048]{1,0:T(8,128)(2,1)} %bitcast.38, bf16[512,2048]{1,0:T(8,128)(2,1)} %bitcast.24, bf16[512,768]{1,0:T(8,128)(2,1)} %get-tuple-element.42.gate_pre.gate_pre_ref, ...), custom_call_target="tpu_custom_call" | custom-call | flops 20000000000 | bytes 62914560 | tf_op jit(solution)/shard_map/chain_sum_4/pallas_call | solution.py:243
  145.2 3.1 %collective-permute-start.6 = (bf16[4,256,256]{2,1,0:T(8,128)(2,1)}, bf16[4,256,256]{2,1,0:T(8,128)(2,1)S(1)}, u32[]{:S(2)}, u32[]{:S(2)}) collective-permute-start(bf16[4,256,256]{2,1,0:T(8,128)(2,1)} %get-tuple-element.56.refs_2_), channel_id=1, source_target_pairs={{0,1},{1,2},{2,3},{3,4},{4,5},{5,6},{6,7},{7,0},{8,9},{9,10},{10,1... | collective-permute-start | bytes 1572872 | tf_op jit(solution)/shard_map/ppermute | solution.py:311
  148.3 0.5 collective-permute-start.7
  148.9 2.9 %collective-permute-done.8.refs_0_ = bf16[4,256,256]{2,1,0:T(8,128)(2,1)S(1)} collective-permute-done((bf16[4,256,256]{2,1,0:T(8,128)(2,1)}, bf16[4,256,256]{2,1,0:T(8,128)(2,1)S(1)}, u32[]{:S(2)}, u32[]{:S(2)}) %collective-permute-start.8) | collective-permute-done | bytes 524320 | tf_op jit(solution)/shard_map/ppermute | solution.py:311
  151.8 0.2 collective-permute-done.9.refs_1_
  152.1 0.6 copy-done.13
  152.6 0.8 copy-done.7
  153.5 3.9 %chain_sum_5.1 = (bf16[4,256,256]{2,1,0:T(8,128)(2,1)}, bf16[5,256,256]{2,1,0:T(8,128)(2,1)}) custom-call(s32[1]{0:T(128)} %bitcast.2._, bf16[512,2048]{1,0:T(8,128)(2,1)} %bitcast.39, bf16[512,2048]{1,0:T(8,128)(2,1)} %bitcast.40, bf16[512,2048]{1,0:T(8,128)(2,1)} %bitcast.25, bf16[512,768]{1,0:T(8,128)(2,1)} %get-tuple-element.42.gate_pre.gate_pre_ref, ...), custom_call_target="tpu_custom_call" | custom-call | flops 20000000000 | bytes 62914560 | tf_op jit(solution)/shard_map/chain_sum_5/pallas_call | solution.py:243
  157.3 3.0 %collective-permute-start.13 = (bf16[5,256,256]{2,1,0:T(8,128)(2,1)}, bf16[5,256,256]{2,1,0:T(8,128)(2,1)S(1)}, u32[]{:S(2)}, u32[]{:S(2)}) collective-permute-start(bf16[5,256,256]{2,1,0:T(8,128)(2,1)} %get-tuple-element.62), channel_id=1, source_target_pairs={{0,1},{1,2},{2,3},{3,4},{4,5},{5,6},{6,7},{7,0},{8,9},{9,10},{10,1... | collective-permute-start | bytes 1966088 | tf_op jit(solution)/shard_map/ppermute | solution.py:311
  160.4 2.9 %collective-permute-done.6.refs_0_ = bf16[4,256,256]{2,1,0:T(8,128)(2,1)S(1)} collective-permute-done((bf16[4,256,256]{2,1,0:T(8,128)(2,1)}, bf16[4,256,256]{2,1,0:T(8,128)(2,1)S(1)}, u32[]{:S(2)}, u32[]{:S(2)}) %collective-permute-start.6) | collective-permute-done | bytes 524320 | tf_op jit(solution)/shard_map/ppermute | solution.py:311
  163.3 1.8 collective-permute-done.7.refs_1_
  165.1 0.8 copy-done.8
  165.9 3.9 %chain_sum_6.1 = (bf16[4,256,256]{2,1,0:T(8,128)(2,1)}, bf16[5,256,256]{2,1,0:T(8,128)(2,1)}) custom-call(s32[1]{0:T(128)} %bitcast.2._, bf16[512,2048]{1,0:T(8,128)(2,1)} %bitcast.41, bf16[512,2048]{1,0:T(8,128)(2,1)} %bitcast.42, bf16[512,2048]{1,0:T(8,128)(2,1)} %bitcast.26, bf16[512,768]{1,0:T(8,128)(2,1)} %get-tuple-element.42.gate_pre.gate_pre_ref, ...), custom_call_target="tpu_custom_call" | custom-call | flops 20000000000 | bytes 62914560 | tf_op jit(solution)/shard_map/chain_sum_6/pallas_call | solution.py:243
  169.8 3.6 %collective-permute-start.12 = (bf16[5,256,256]{2,1,0:T(8,128)(2,1)}, bf16[5,256,256]{2,1,0:T(8,128)(2,1)S(1)}, u32[]{:S(2)}, u32[]{:S(2)}) collective-permute-start(bf16[5,256,256]{2,1,0:T(8,128)(2,1)} %get-tuple-element.61), channel_id=1, source_target_pairs={{0,7},{1,0},{2,1},{3,2},{4,3},{5,4},{6,5},{7,6},{8,15},{9,8},{10,9... | collective-permute-start | bytes 1966088 | tf_op jit(solution)/shard_map/ppermute | solution.py:311
  173.4 0.3 collective-permute-start.11
  173.7 1.8 collective-permute-start.10
  175.4 23.2 %collective-permute-done.11.a1 = bf16[4,256,256]{2,1,0:T(8,128)(2,1)S(1)} collective-permute-done((bf16[4,256,256]{2,1,0:T(8,128)(2,1)S(1)}, bf16[4,256,256]{2,1,0:T(8,128)(2,1)S(1)}, u32[]{:S(2)}, u32[]{:S(2)}) %collective-permute-start.11) | collective-permute-done | bytes 524320 | tf_op jit(solution)/shard_map/ppermute | solution.py:311
  198.6 0.0 collective-permute-done.13.b1
  198.6 0.0 collective-permute-done.10.a0
  198.7 0.0 collective-permute-done.12.b0
  198.7 0.8 copy-done.16
  199.5 0.2 copy-done.1
  199.7 0.2 copy-done.18
  199.8 0.8 copy-done.5
  200.7 4.4 %chain_sum_last.1 = (f32[256,768]{1,0:T(8,128)}, f32[256,768]{1,0:T(8,128)}, f32[768,256]{1,0:T(8,128)}) custom-call(s32[1]{0:T(128)} %bitcast.2._, bf16[512,2048]{1,0:T(8,128)(2,1)} %bitcast.43, bf16[512,2048]{1,0:T(8,128)(2,1)} %bitcast.44, bf16[512,2048]{1,0:T(8,128)(2,1)} %bitcast.27, bf16[512,768]{1,0:T(8,128)(2,1)} %get-tuple-element.42.gate_pre.gate_pre_ref, ...), custom_call_target="tpu_custom_call" | custom-call | flops 20000000000 | bytes 62914560 | tf_op jit(solution)/shard_map/chain_sum_last/pallas_call | solution.py:243
  205.1 0.0 all-to-all-done.2
  205.1 5.4 %combine.1 = (bf16[48,2048]{1,0:T(8,128)(2,1)}, bf16[48,2048]{1,0:T(8,128)(2,1)}, f32[8,48]{1,0:T(8,128)}) custom-call(s32[8,48]{1,0:T(8,128)} %bitcast.48, f32[8,48]{1,0:T(8,128)} %bitcast.50, bf16[512,48]{1,0:T(8,128)(2,1)} %get-tuple-element.36.place_ref, bf16[48,2048]{1,0:T(8,128)(2,1)} %grads_ref.3, bf16[512,4096]{1,0:T(8,128)(2,1)} %bitcast.11.back_ref.back_grad_ref, ...), custom_call_target="tpu_custom_call" | custom-call | flops 402653184 | bytes 4194304 | tf_op jit(solution)/shard_map/combine/pallas_call | solution.py:316
  (21 shorter events, 0.0 us)
Async XLA Ops:
  39.8 33.1 %all-to-all-start.1 = ((bf16[32,16,2048]{2,1,0:T(8,128)(2,1)}), bf16[32,16,2048]{2,1,0:T(8,128)(2,1)S(1)}, u32[]{:S(2)}, u32[]{:S(2)}) async-start(bf16[32,16,2048]{2,1,0:T(8,128)(2,1)} %bitcast.45), calls=%async_computation.1 | async-start | bytes 4194304 | tf_op jit(solution)/shard_map/all_to_all | solution.py:193
  72.9 1.4 copy-start
  85.0 5.5 %copy-start.9 = (bf16[5,256,256]{2,1,0:T(8,128)(2,1)S(1)}, bf16[5,256,256]{2,1,0:T(8,128)(2,1)}, u32[]{:S(2)}) copy-start(bf16[5,256,256]{2,1,0:T(8,128)(2,1)} %get-tuple-element.46) | copy-start | bytes 1966084
  85.0 20.9 %collective-permute-start = (bf16[4,256,256]{2,1,0:T(8,128)(2,1)}, bf16[4,256,256]{2,1,0:T(8,128)(2,1)S(1)}, u32[]{:S(2)}, u32[]{:S(2)}) collective-permute-start(bf16[4,256,256]{2,1,0:T(8,128)(2,1)} %get-tuple-element.45.refs_0_), channel_id=1, source_target_pairs={{0,1},{1,2},{2,3},{3,4},{4,5},{5,6},{6,7},{7,0},{8,9},{9,10},{10,1... | collective-permute-start | bytes 1572872 | tf_op jit(solution)/shard_map/ppermute | solution.py:311
  90.5 19.2 %collective-permute-start.1 = (bf16[5,256,256]{2,1,0:T(8,128)(2,1)S(1)}, bf16[5,256,256]{2,1,0:T(8,128)(2,1)S(1)}, u32[]{:S(2)}, u32[]{:S(2)}) collective-permute-start(bf16[5,256,256]{2,1,0:T(8,128)(2,1)S(1)} %copy-done.9), channel_id=1, source_target_pairs={{0,7},{1,0},{2,1},{3,2},{4,3},{5,4},{6,5},{7,6},{8,15},{9,8},{10,9... | collective-permute-start | bytes 1966088 | tf_op jit(solution)/shard_map/ppermute | solution.py:311
  94.5 9.4 %copy-start.11 = (bf16[4,256,256]{2,1,0:T(8,128)(2,1)S(1)}, bf16[4,256,256]{2,1,0:T(8,128)(2,1)}, u32[]{:S(2)}) copy-start(bf16[4,256,256]{2,1,0:T(8,128)(2,1)} %get-tuple-element.47.after) | copy-start | bytes 1572868
  94.5 11.3 %copy-start.2 = (bf16[5,256,256]{2,1,0:T(8,128)(2,1)S(1)}, bf16[5,256,256]{2,1,0:T(8,128)(2,1)}, u32[]{:S(2)}) copy-start(bf16[5,256,256]{2,1,0:T(8,128)(2,1)} %get-tuple-element.54) | copy-start | bytes 1966084
  103.9 21.5 %collective-permute-start.4 = (bf16[4,256,256]{2,1,0:T(8,128)(2,1)S(1)}, bf16[4,256,256]{2,1,0:T(8,128)(2,1)}, u32[]{:S(2)}, u32[]{:S(2)}) collective-permute-start(bf16[4,256,256]{2,1,0:T(8,128)(2,1)S(1)} %copy-done.11), channel_id=1, source_target_pairs={{0,7},{1,0},{2,1},{3,2},{4,3},{5,4},{6,5},{7,6},{8,15},{9,8},{10,9... | collective-permute-start | bytes 1572872 | tf_op jit(solution)/shard_map/ppermute | solution.py:311
  105.8 19.5 %collective-permute-start.5 = (bf16[5,256,256]{2,1,0:T(8,128)(2,1)S(1)}, bf16[5,256,256]{2,1,0:T(8,128)(2,1)S(1)}, u32[]{:S(2)}, u32[]{:S(2)}) collective-permute-start(bf16[5,256,256]{2,1,0:T(8,128)(2,1)S(1)} %copy-done.2), channel_id=1, source_target_pairs={{0,1},{1,2},{2,3},{3,4},{4,5},{5,6},{6,7},{7,0},{8,9},{9,10},{10,1... | collective-permute-start | bytes 1966088 | tf_op jit(solution)/shard_map/ppermute | solution.py:311
  105.9 3.8 %copy-start.17 = (bf16[4,256,256]{2,1,0:T(8,128)(2,1)}, bf16[4,256,256]{2,1,0:T(8,128)(2,1)S(1)}, u32[]{:S(2)}) copy-start(bf16[4,256,256]{2,1,0:T(8,128)(2,1)S(1)} %collective-permute-done.refs_0_) | copy-start | bytes 1572868
  109.7 0.8 copy-start.10
  114.4 7.4 %copy-start.3 = (bf16[5,256,256]{2,1,0:T(8,128)(2,1)S(1)}, bf16[5,256,256]{2,1,0:T(8,128)(2,1)}, u32[]{:S(2)}) copy-start(bf16[5,256,256]{2,1,0:T(8,128)(2,1)} %get-tuple-element.53) | copy-start | bytes 1966084
  114.4 90.7 %all-to-all-start.2 = ((bf16[32,16,4096]{2,1,0:T(8,128)(2,1)}), bf16[32,16,4096]{2,1,0:T(8,128)(2,1)}, u32[]{:S(2)}, u32[]{:S(2)}) async-start(bf16[32,16,4096]{2,1,0:T(8,128)(2,1)} %bitcast.16), calls=%async_computation.2 | async-start | bytes 8388608 | tf_op jit(solution)/shard_map/all_to_all | solution.py:193
  121.3 16.7 %collective-permute-start.2 = (bf16[4,256,256]{2,1,0:T(8,128)(2,1)}, bf16[4,256,256]{2,1,0:T(8,128)(2,1)S(1)}, u32[]{:S(2)}, u32[]{:S(2)}) collective-permute-start(bf16[4,256,256]{2,1,0:T(8,128)(2,1)} %get-tuple-element.52.refs_2_), channel_id=1, source_target_pairs={{0,1},{1,2},{2,3},{3,4},{4,5},{5,6},{6,7},{7,0},{8,9},{9,10},{10,1... | collective-permute-start | bytes 1572872 | tf_op jit(solution)/shard_map/ppermute | solution.py:311
  121.8 18.6 %collective-permute-start.3 = (bf16[5,256,256]{2,1,0:T(8,128)(2,1)S(1)}, bf16[5,256,256]{2,1,0:T(8,128)(2,1)S(1)}, u32[]{:S(2)}, u32[]{:S(2)}) collective-permute-start(bf16[5,256,256]{2,1,0:T(8,128)(2,1)S(1)} %copy-done.3), channel_id=1, source_target_pairs={{0,7},{1,0},{2,1},{3,2},{4,3},{5,4},{6,5},{7,6},{8,15},{9,8},{10,9... | collective-permute-start | bytes 1966088 | tf_op jit(solution)/shard_map/ppermute | solution.py:311
  125.4 0.8 copy-start.4
  130.1 21.7 %collective-permute-start.8 = (bf16[4,256,256]{2,1,0:T(8,128)(2,1)}, bf16[4,256,256]{2,1,0:T(8,128)(2,1)S(1)}, u32[]{:S(2)}, u32[]{:S(2)}) collective-permute-start(bf16[4,256,256]{2,1,0:T(8,128)(2,1)} %get-tuple-element.55.refs_2_), channel_id=1, source_target_pairs={{0,7},{1,0},{2,1},{3,2},{4,3},{5,4},{6,5},{7,6},{8,15},{9,8},{10,9... | collective-permute-start | bytes 1572872 | tf_op jit(solution)/shard_map/ppermute | solution.py:311
  131.8 20.2 %collective-permute-start.9 = (bf16[5,256,256]{2,1,0:T(8,128)(2,1)}, bf16[5,256,256]{2,1,0:T(8,128)(2,1)S(1)}, u32[]{:S(2)}, u32[]{:S(2)}) collective-permute-start(bf16[5,256,256]{2,1,0:T(8,128)(2,1)} %get-tuple-element.58), channel_id=1, source_target_pairs={{0,1},{1,2},{2,3},{3,4},{4,5},{5,6},{6,7},{7,0},{8,9},{9,10},{10,1... | collective-permute-start | bytes 1966088 | tf_op jit(solution)/shard_map/ppermute | solution.py:311
  138.0 2.5 %copy-start.12 = (bf16[4,256,256]{2,1,0:T(8,128)(2,1)}, bf16[4,256,256]{2,1,0:T(8,128)(2,1)S(1)}, u32[]{:S(2)}) copy-start(bf16[4,256,256]{2,1,0:T(8,128)(2,1)S(1)} %collective-permute-done.2.refs_0_) | copy-start | bytes 1572868
  140.5 0.8 copy-start.6
  145.2 18.1 %collective-permute-start.6 = (bf16[4,256,256]{2,1,0:T(8,128)(2,1)}, bf16[4,256,256]{2,1,0:T(8,128)(2,1)S(1)}, u32[]{:S(2)}, u32[]{:S(2)}) collective-permute-start(bf16[4,256,256]{2,1,0:T(8,128)(2,1)} %get-tuple-element.56.refs_2_), channel_id=1, source_target_pairs={{0,1},{1,2},{2,3},{3,4},{4,5},{5,6},{6,7},{7,0},{8,9},{9,10},{10,1... | collective-permute-start | bytes 1572872 | tf_op jit(solution)/shard_map/ppermute | solution.py:311
  148.3 16.7 %collective-permute-start.7 = (bf16[5,256,256]{2,1,0:T(8,128)(2,1)}, bf16[5,256,256]{2,1,0:T(8,128)(2,1)S(1)}, u32[]{:S(2)}, u32[]{:S(2)}) collective-permute-start(bf16[5,256,256]{2,1,0:T(8,128)(2,1)} %get-tuple-element.57), channel_id=1, source_target_pairs={{0,7},{1,0},{2,1},{3,2},{4,3},{5,4},{6,5},{7,6},{8,15},{9,8},{10,9... | collective-permute-start | bytes 1966088 | tf_op jit(solution)/shard_map/ppermute | solution.py:311
  151.8 0.8 copy-start.13
  152.6 0.8 copy-start.7
  157.3 41.3 %collective-permute-start.13 = (bf16[5,256,256]{2,1,0:T(8,128)(2,1)}, bf16[5,256,256]{2,1,0:T(8,128)(2,1)S(1)}, u32[]{:S(2)}, u32[]{:S(2)}) collective-permute-start(bf16[5,256,256]{2,1,0:T(8,128)(2,1)} %get-tuple-element.62), channel_id=1, source_target_pairs={{0,1},{1,2},{2,3},{3,4},{4,5},{5,6},{6,7},{7,0},{8,9},{9,10},{10,1... | collective-permute-start | bytes 1966088 | tf_op jit(solution)/shard_map/ppermute | solution.py:311
  163.3 1.8 copy-start.14
  165.1 0.8 copy-start.8
  165.9 7.5 %copy-start.15 = (bf16[4,256,256]{2,1,0:T(8,128)(2,1)S(1)}, bf16[4,256,256]{2,1,0:T(8,128)(2,1)}, u32[]{:S(2)}) copy-start(bf16[4,256,256]{2,1,0:T(8,128)(2,1)} %get-tuple-element.59.refs_2_) | copy-start | bytes 1572868
  169.8 28.8 %collective-permute-start.12 = (bf16[5,256,256]{2,1,0:T(8,128)(2,1)}, bf16[5,256,256]{2,1,0:T(8,128)(2,1)S(1)}, u32[]{:S(2)}, u32[]{:S(2)}) collective-permute-start(bf16[5,256,256]{2,1,0:T(8,128)(2,1)} %get-tuple-element.61), channel_id=1, source_target_pairs={{0,7},{1,0},{2,1},{3,2},{4,3},{5,4},{6,5},{7,6},{8,15},{9,8},{10,9... | collective-permute-start | bytes 1966088 | tf_op jit(solution)/shard_map/ppermute | solution.py:311
  173.4 25.2 %collective-permute-start.11 = (bf16[4,256,256]{2,1,0:T(8,128)(2,1)S(1)}, bf16[4,256,256]{2,1,0:T(8,128)(2,1)S(1)}, u32[]{:S(2)}, u32[]{:S(2)}) collective-permute-start(bf16[4,256,256]{2,1,0:T(8,128)(2,1)S(1)} %copy-done.15), channel_id=1, source_target_pairs={{0,7},{1,0},{2,1},{3,2},{4,3},{5,4},{6,5},{7,6},{8,15},{9,8},{10,9... | collective-permute-start | bytes 1572872 | tf_op jit(solution)/shard_map/ppermute | solution.py:311
  173.7 25.0 %collective-permute-start.10 = (bf16[4,256,256]{2,1,0:T(8,128)(2,1)}, bf16[4,256,256]{2,1,0:T(8,128)(2,1)S(1)}, u32[]{:S(2)}, u32[]{:S(2)}) collective-permute-start(bf16[4,256,256]{2,1,0:T(8,128)(2,1)} %get-tuple-element.60), channel_id=1, source_target_pairs={{0,1},{1,2},{2,3},{3,4},{4,5},{5,6},{6,7},{7,0},{8,9},{9,10},{10,1... | collective-permute-start | bytes 1572872 | tf_op jit(solution)/shard_map/ppermute | solution.py:311
  198.6 0.8 copy-start.16
  198.6 1.0 copy-start.1
  198.6 1.2 copy-start.18
  199.8 0.8 copy-start.5

commit v2 on v1

--- a/solution.py
+++ b/solution.py
@@ -11,15 +11,18 @@
 F32 = jnp.float32
 LAST = (((1,), (1,)), ((), ()))
 FIRST = (((0,), (0,)), ((), ()))
-VMEM_LIMIT = 60 * 2**20
-
-
-def params():
-    return pltpu.CompilerParams(vmem_limit_bytes=VMEM_LIMIT)
+
+
+def params(mib=56):
+    return pltpu.CompilerParams(vmem_limit_bytes=mib * 2**20)
 
 
 def cost(flops, nbytes, exps=0):
     return pl.CostEstimate(flops=flops, bytes_accessed=nbytes, transcendentals=exps)
+
+
+LONG = cost(20 * 10**9, 60 * 2**20)
+SHORT = cost(1, 1)
 
 
 def dot(a, b, dims=(((1,), (0,)), ((), ()))):
@@ -75,55 +78,59 @@
     hidden_t_ref[...] = hidden_ref[...].T
 
 
-def chunk_sums(rows_a, rows_b, grads_b, gate_pre, up_pre, hidden_t, held_a, held_b):
-    width = rows_a.shape[1]
+def chunk_sums(step_a, step_b, groups, me_ref, rows, grads, gate_pre, up_pre, hidden_t, held_a=(), held_b=()):
+    width = rows.shape[1] // groups
     blocks = gate_pre.shape[1] // width
-    turned_a, turned_b = rows_a[...].T, rows_b[...].T
-    grads = grads_b[...]
+    me = me_ref[0]
+
+    def columns(step):
+        return pl.ds(pl.multiple_of(lax.rem(me + step, groups) * width, width), width)
+
+    turned_a = rows[:, columns(step_a)].T
     for j in range(blocks + 1):
         source = gate_pre[:, j * width : (j + 1) * width] if j < blocks else up_pre[:, :width]
         total = dot(turned_a, source)
         for held in held_a:
             total = total + held[j].astype(F32)
         yield "a", j, total
+    turned_b = turned_a if step_a == step_b else rows[:, columns(step_b)].T
+    grads_b = grads[:, columns(step_b)]
     for j in range(2 * blocks - 1):
         if j < blocks - 1:
             total = dot(turned_b, up_pre[:, (j + 1) * width : (j + 2) * width])
         else:
             i = j - blocks + 1
-            total = dot(hidden_t[i * width : (i + 1) * width, :], grads)
+            total = dot(hidden_t[i * width : (i + 1) * width, :], grads_b)
         for held in held_b:
             total = total + held[j].astype(F32)
         yield "b", j, total
 
 
-def link_kernel(arrived, _, rows_a, rows_b, grads_b, gate_pre, up_pre, hidden_t, *refs):
-    held_a, held_b = ([refs[0]], [refs[1]]) if arrived else ([], [])
+def link_kernel(step_a, step_b, groups, arrived, me_ref, *refs):
+    held = [[refs[5]], [refs[6]]] if arrived else []
     out = {"a": refs[-2], "b": refs[-1]}
-    for part, j, total in chunk_sums(rows_a, rows_b, grads_b, gate_pre, up_pre, hidden_t, held_a, held_b):
-        out[part][j] = total.astype(BF16)
-
-
-def last_kernel(_, rows_a, rows_b, grads_b, gate_pre, up_pre, hidden_t, a0, a1, b0, b1, gate_ref, up_ref, down_ref):
-    width = rows_a.shape[1]
-    blocks = gate_pre.shape[1] // width
-    for part, j, total in chunk_sums(rows_a, rows_b, grads_b, gate_pre, up_pre, hidden_t, [a0, a1], [b0, b1]):
-        if part == "a" and j < blocks:
-            gate_ref[:, j * width : (j + 1) * width] = total
-        elif part == "a":
-            up_ref[:, :width] = total
-        elif j < blocks - 1:
-            up_ref[:, (j + 1) * width : (j + 2) * width] = total
-        else:
-            i = j - blocks + 1
-            down_ref[i * width : (i + 1) * width, :] = total
-
-
-def output_kernel(hidden_ref, down_ref, out_ref):
+    for part, j, total in chunk_sums(step_a, step_b, groups, me_ref, *refs[:5], *held):
+        out[part][j] = total.astype(out[part].dtype)
+
+
+def last_kernel(own_a, own_b, a0, b0, _, gate_ref, up_ref, down_ref):
+    width = own_a.shape[1]
+    blocks = own_a.shape[0] - 1
+    for j in range(blocks):
+        gate_ref[:, j * width : (j + 1) * width] = own_a[j] + a0[j].astype(F32)
+        down_ref[j * width : (j + 1) * width, :] = own_b[blocks - 1 + j] + b0[blocks - 1 + j].astype(F32)
+    up_ref[:, :width] = own_a[blocks] + a0[blocks].astype(F32)
+    for j in range(blocks - 1):
+        up_ref[:, (j + 1) * width : (j + 2) * width] = own_b[j] + b0[j].astype(F32)
+
+
+def output_kernel(hidden_ref, down_ref, out_ref, token_ref):
+    token_ref[...] = jnp.zeros_like(token_ref)
     out_ref[...] = dot(hidden_ref[...], down_ref[...]).astype(BF16)
 
 
-def row_grad_kernel(gate_pre_ref, up_pre_ref, gate_ref, up_ref, _, after, row_grad_ref):
+def row_grad_kernel(gate_pre_ref, up_pre_ref, gate_ref, up_ref, _, after, row_grad_ref, token_ref):
+    token_ref[...] = jnp.zeros_like(token_ref)
     row_grad_ref[...] = (
         dot(gate_pre_ref[...], gate_ref[...], LAST) + dot(up_pre_ref[...], up_ref[...], LAST)
     ).astype(BF16)
@@ -210,66 +217,53 @@
         name="forward",
     )(rows, w_gate, w_up)
 
-    going_back = pl.pallas_call(
+    going_back, token = pl.pallas_call(
         output_kernel,
         grid=(groups,),
         in_specs=[whole((slots, hid)), pl.BlockSpec((hid, width), lambda i: (0, i))],
-        out_specs=pl.BlockSpec((slots, width), lambda i: (0, i)),
-        out_shape=shape((slots, 2 * model)),
+        out_specs=[pl.BlockSpec((slots, width), lambda i: (0, i)), whole((8, 128))],
+        out_shape=(shape((slots, 2 * model)), shape((8, 128), F32)),
         compiler_params=params(),
         cost_estimate=cost(2 * slots * model * hid, 2 * slots * model + 2 * model * hid + 2 * slots * hid),
         name="outputs",
     )(hidden, w_down)
 
     tile = pl.BlockSpec((slots, width), lambda i: (0, i))
-    anywhere = pl.BlockSpec(memory_space=pl.ANY)
+    anywhere = pl.BlockSpec(memory_space=pltpu.HBM)
     gate_pre, up_pre, hidden_t = pl.pallas_call(
         backward_kernel,
         grid=(blocks,),
-        in_specs=[whole((slots, model)), tile, tile, tile, pl.BlockSpec((width, model), lambda i: (i, 0)), anywhere],
+        in_specs=[pl.BlockSpec(memory_space=pltpu.VMEM), tile, tile, tile, pl.BlockSpec((width, model), lambda i: (i, 0)), anywhere],
         out_specs=[tile, tile, pl.BlockSpec((width, slots), lambda i: (i, 0))],
         out_shape=(shape((slots, hid)), shape((slots, hid)), shape((hid, slots))),
-        compiler_params=params(),
+        compiler_params=params(36),
         cost_estimate=cost(2 * slots * model * hid, 2 * slots * model + 2 * model * hid + 14 * slots * hid),
         name="backward",
-    )(grads, hidden, gate_slope, up_slope, w_down, going_back)
+    )(grads, hidden, gate_slope, up_slope, w_down, token)
 
     me = lax.axis_index("dp")
     place_of = me.reshape(1).astype(jnp.int32)
 
-    def chain_call(kernel, step_a, step_b, out_shape, held, name, kept=(), after=()):
-        size = lambda n: pl.BlockSpec((n, width, width), lambda i, p: (0, 0, 0))
-        fixed = lambda dims: pl.BlockSpec(dims, lambda i, p: (0, 0))
+    resident = pl.BlockSpec(memory_space=pltpu.VMEM)
+
+    def chain_call(step_a, step_b, dtype, held, name, after):
+        parts = (shape((blocks + 1, width, width), dtype), shape((2 * blocks - 1, width, width), dtype))
         return pl.pallas_call(
-            kernel,
-            grid_spec=pltpu.PrefetchScalarGridSpec(
-                num_scalar_prefetch=1,
-                grid=(1,),
-                in_specs=[
-                    pl.BlockSpec((slots, width), lambda i, p: (0, lax.rem(p[0] + step_a, groups))),
-                    pl.BlockSpec((slots, width), lambda i, p: (0, lax.rem(p[0] + step_b, groups))),
-                    pl.BlockSpec((slots, width), lambda i, p: (0, lax.rem(p[0] + step_b, groups))),
-                    fixed((slots, hid)),
-                    fixed((slots, hid)),
-                    fixed((hid, slots)),
-                    *[size(h.shape[0]) for h in held],
-                    *[anywhere for _ in (*kept, *after)],
-                ],
-                out_specs=[
-                    *[anywhere for _ in kept],
-                    *[pl.BlockSpec(o.shape, lambda i, p, n=len(o.shape): (0,) * n) for o in out_shape],
-                ],
-            ),
-            out_shape=(*[shape(x.shape, x.dtype) for x in kept], *out_shape),
-            input_output_aliases={7 + len(held) + i: i for i in range(len(kept))},
-            compiler_params=params(),
-            cost_estimate=cost(20 * 10**9, 60 * 2**20),
+            functools.partial(link_kernel, step_a, step_b, groups, bool(held)),
+            in_specs=[
+                pl.BlockSpec(memory_space=pltpu.SMEM),
+                *[resident] * (5 + len(held)),
+                *[anywhere] * len(after),
+            ],
+            out_specs=[resident, resident],
+            out_shape=parts,
+            compiler_params=params(16),
+            cost_estimate=LONG,
             name=name,
-        )(place_of, rows, rows, grads, gate_pre, up_pre, hidden_t, *held, *kept, *after)
+        )(place_of, rows, grads, gate_pre, up_pre, hidden_t, *held, *after)
 
     up_ring = [(i, (i + 1) % groups) for i in range(groups)]
     down_ring = [(i, (i - 1) % groups) for i in range(groups)]
-    part_shapes = (shape((blocks + 1, width, width)), shape((2 * blocks - 1, width, width)))
     half_way = groups // 2
     slots_of_ring = [(half_way, 0)] + [(k, s) for k in range(half_way - 1, 0, -1) for s in (1, 0)]
     def row_grads(after):
@@ -284,11 +278,11 @@
                 anywhere,
                 anywhere,
             ],
-            out_specs=pl.BlockSpec((slots, width), lambda i: (0, groups + i)),
-            out_shape=shape((slots, 2 * model)),
+            out_specs=[pl.BlockSpec((slots, width), lambda i: (0, groups + i)), whole((8, 128))],
+            out_shape=(shape((slots, 2 * model)), shape((8, 128), F32)),
             input_output_aliases={4: 0},
-            compiler_params=params(),
-            cost_estimate=cost(20 * 10**9, 60 * 2**20),
+            compiler_params=params(52),
+            cost_estimate=SHORT,
             name="row_grads",
         )(gate_pre, up_pre, w_gate, w_up, going_back, after)
 
@@ -296,17 +290,11 @@
     for number, (k, swapped) in enumerate(slots_of_ring):
         step_a, step_b = (groups - k, k) if swapped else (k, groups - k)
         held = came.get((k, swapped), ())
-        kept = (going_back,) if number == 2 else ()
-        *kept, part_a, part_b = chain_call(
-            functools.partial(link_kernel, bool(held)),
-            step_a, step_b, part_shapes, held, f"chain_sum_{number}", kept, after,
-        )
+        part_a, part_b = chain_call(step_a, step_b, BF16, held, f"chain_sum_{number}", after)
         after = (part_a,)
         if number == 1:
-            going_back = row_grads(part_a)
-            after = ()
-        elif number == 2:
-            [going_back] = kept
+            going_back, token = row_grads(part_a)
+            after = (token,)
         ring_a, ring_b = (down_ring, up_ring) if swapped else (up_ring, down_ring)
         came[k - 1, swapped] = (lax.ppermute(part_a, "dp", ring_a), lax.ppermute(part_b, "dp", ring_b))
 
@@ -336,15 +324,15 @@
         name="combine",
     )(routes_t, gates_t, place, out_grad, back, back)
 
-    (a0, b0), (a1, b1) = came[0, 0], came[0, 1]
-    gate_grad, up_grad, down_grad = chain_call(
+    own_a, own_b = chain_call(0, 0, F32, came[0, 1], "chain_sum_own", after)
+    gate_grad, up_grad, down_grad = pl.pallas_call(
         last_kernel,
-        0,
-        0,
-        (shape((width, hid), F32), shape((width, hid), F32), shape((hid, width), F32)),
-        (a0, a1, b0, b1),
-        "chain_sum_last",
-    )
+        in_specs=[*[resident] * 4, anywhere],
+        out_shape=(shape((width, hid), F32), shape((width, hid), F32), shape((hid, width), F32)),
+        compiler_params=params(16),
+        cost_estimate=SHORT,
+        name="chain_sum_last",
+    )(own_a, own_b, *came[0, 0], token_grad)
     return (layer_out, token_grad, gates_grad_t.T, gate_grad[None], up_grad[None], down_grad[None])
 
 

time: 212 us -> 190 us (0.90)
  Pallas kernels: 72.5 us -> 51.7 us
  local copies, waits for them, and re-layouts: 8.15 us -> 13.4 us
  waiting for transfers between devices: 55.6 us -> 51.6 us
    pallas_call x9 -> x10, Pallas kernels: 38 us -> 17.5 us  [the longest x8 12 us: chain_call(): pl.pallas_call(functools.partial(link_kernel, step_a, step_b, groups, boo...]
    unnamed x38 -> x36, local copies, waits for them, and re-layouts: 8.15 us -> 13.4 us
    ppermute x7, waiting for transfers between devices: 35 us -> 31.1 us  [local(): lax.ppermute(part_a, 'dp', ring_a)]
  transfers between devices with their start and end apart: 16 -> 16, of which waited for: 9 -> 9; matrix products, arithmetic and copies ran while one was open for 0% -> 0% of each run, Pallas kernels for 25% -> 21%
where the time goes in v2:
time: 190 us; the launch traced here: 189 us
  Pallas kernels  51.7 us (27%)
  waiting for transfers between devices  51.6 us (27%)
  starting transfers between devices  36.5 us (19%)
  blocking collectives  35.1 us (18%)
  local copies, waits for them, and re-layouts  13.4 us (7%)
    all_to_all x1, blocking collectives, exchange(): return lax.all_to_all(wide, 'expert', 0, 0, tiled=True).reshape(array.shape)  35.1 us
    ppermute x7, waiting for transfers between devices, local(): lax.ppermute(part_a, 'dp', ring_a)  31.1 us
    ppermute x7, starting transfers between devices, local(): lax.ppermute(part_b, 'dp', ring_b)  14.9 us
    unnamed x36, local copies, waits for them, and re-layouts  13.4 us
    all_to_all x2, waiting for transfers between devices, exchange(): return lax.all_to_all(wide, 'expert', 0, 0, tiled=True).reshape(array.shape)  12.4 us
    pallas_call x8, Pallas kernels, chain_call(): pl.pallas_call(functools.partial(link_kernel, step_a, step_b, groups, boo...  12 us
    all_to_all x2, starting transfers between devices, exchange(): return lax.all_to_all(wide, 'expert', 0, 0, tiled=True).reshape(array.shape)  11.9 us
    ppermute x7, starting transfers between devices, local(): lax.ppermute(part_a, 'dp', ring_a)  9.67 us
  transfers between devices with their start and end apart: 16, of which 9 were waited for; matrix products, arithmetic and copies ran while one was open for 0% of the time, Pallas kernels for 21%

profile of v2, /device:TPU:2, one launch (start us, length us, event | category | flops | bytes accessed | tf_op | source)
XLA Modules:
  0.0 189.2 jit_solution(412391181800621784)
XLA Ops:
  0.6 4.1 %dispatch.1 = (bf16[512,2048]{1,0:T(8,128)(2,1)}, bf16[512,2048]{1,0:T(8,128)(2,1)}, bf16[512,48]{1,0:T(8,128)(2,1)}) custom-call(s32[8,48]{1,0:T(8,128)} %bitcast.43, f32[8,48]{1,0:T(8,128)} %bitcast.45, bf16[48,2048]{1,0:T(8,128)(2,1)} %tokens_ref.1, bf16[48,2048]{1,0:T(8,128)(2,1)} %grads_ref.3), custom_call_target="tpu_custom_call" | custom-call | flops 201326592 | bytes 4194304 | tf_op jit(solution)/shard_map/dispatch/pallas_call | solution.py:190
  4.7 35.1 %all_to_all.15 = bf16[32,16,2048]{2,1,0:T(8,128)(2,1)} all-to-all(bf16[32,16,2048]{2,1,0:T(8,128)(2,1)} %bitcast.42), channel_id=1, replica_groups=mesh['expert'=32,'dp'=8] {'expert'}, dimensions={0} | all-to-all | bytes 4194304 | tf_op jit(solution)/shard_map/all_to_all | solution.py:200
  39.8 5.1 %all-to-all-start = ((bf16[32,16,2048]{2,1,0:T(8,128)(2,1)}), bf16[32,16,2048]{2,1,0:T(8,128)(2,1)S(1)}, u32[]{:S(2)}, u32[]{:S(2)}) async-start(bf16[32,16,2048]{2,1,0:T(8,128)(2,1)} %bitcast.41), calls=%async_computation | async-start | bytes 4194304 | tf_op jit(solution)/shard_map/all_to_all | solution.py:200
  44.9 8.1 %forward.1 = (bf16[512,768]{1,0:T(8,128)(2,1)}, f32[512,768]{1,0:T(8,128)}, f32[512,768]{1,0:T(8,128)}) custom-call(bf16[512,2048]{1,0:T(8,128)(2,1)} %bitcast.27, bf16[2048,768]{1,0:T(8,128)(2,1)} %bitcast.37, bf16[2048,768]{1,0:T(8,128)(2,1)} %bitcast.39), custom_call_target="tpu_custom_call" | custom-call | flops 3221225472 | bytes 12320768 | tf_op jit(solution)/shard_map/forward/pallas_call | solution.py:205
  53.0 7.5 %outputs.1 = (bf16[512,4096]{1,0:T(8,128)(2,1)}, f32[8,128]{1,0:T(8,128)}) custom-call(bf16[512,768]{1,0:T(8,128)(2,1)} %get-tuple-element.44.hidden_ref, bf16[768,2048]{1,0:T(8,128)(2,1)} %bitcast.25), custom_call_target="tpu_custom_call" | custom-call | flops 1610612736 | bytes 6029312 | tf_op jit(solution)/shard_map/outputs/pallas_call | solution.py:220
  60.6 12.4 %all-to-all-done = bf16[32,16,2048]{2,1,0:T(8,128)(2,1)S(1)} async-done(((bf16[32,16,2048]{2,1,0:T(8,128)(2,1)}), bf16[32,16,2048]{2,1,0:T(8,128)(2,1)S(1)}, u32[]{:S(2)}, u32[]{:S(2)}) %all-to-all-start) | async-done | bytes 2097184 | tf_op jit(solution)/shard_map/all_to_all | solution.py:200
  72.9 1.9 copy-done
  74.8 1.4 copy-done.3
  76.2 1.4 copy-done.4
  77.6 1.1 copy-done.12
  78.8 0.7 copy-done.14
  79.4 2.7 %backward.1 = (bf16[512,768]{1,0:T(8,128)(2,1)S(1)}, bf16[512,768]{1,0:T(8,128)(2,1)S(1)}, bf16[768,512]{1,0:T(8,128)(2,1)S(1)}) custom-call(bf16[512,2048]{1,0:T(8,128)(2,1)S(1)} %bitcast.16, bf16[512,768]{1,0:T(8,128)(2,1)S(1)} %copy-done.12, f32[512,768]{1,0:T(8,128)S(1)} %copy-done.3, f32[512,768]{1,0:T(8,128)S(1)} %copy-done.4, ...), custom_call_target="tpu_custom_call" | custom-call | flops 1610612736 | bytes 10747904 | tf_op jit(solution)/shard_map/backward/pallas_call | solution.py:233
  82.1 0.0 copy-start.9
  82.1 0.0 copy-start.15
  82.1 0.0 copy-start.7
  82.2 1.8 chain_sum_0.1
  83.9 5.9 %collective-permute-start.3 = (bf16[5,256,256]{2,1,0:T(8,128)(2,1)}, bf16[5,256,256]{2,1,0:T(8,128)(2,1)}, u32[]{:S(2)}, u32[]{:S(2)}) collective-permute-start(bf16[5,256,256]{2,1,0:T(8,128)(2,1)} %get-tuple-element.59), channel_id=1, source_target_pairs={{0,7},{1,0},{2,1},{3,2},{4,3},{5,4},{6,5},{7,6},{8,15},{9,8},{10,9... | collective-permute-start | bytes 1966088 | tf_op jit(solution)/shard_map/ppermute | solution.py:299
  89.8 0.0 collective-permute-start.2
  89.8 1.7 chain_sum_1.1
  91.5 3.2 %collective-permute-start = (bf16[4,256,256]{2,1,0:T(8,128)(2,1)S(1)}, bf16[4,256,256]{2,1,0:T(8,128)(2,1)}, u32[]{:S(2)}, u32[]{:S(2)}) collective-permute-start(bf16[4,256,256]{2,1,0:T(8,128)(2,1)S(1)} %get-tuple-element.53.after), channel_id=1, source_target_pairs={{0,7},{1,0},{2,1},{3,2},{4,3},{5,4},{6,5},{7,6},{8,15},{9,8},{10,9... | collective-permute-start | bytes 1572872 | tf_op jit(solution)/shard_map/ppermute | solution.py:299
  94.7 9.0 %row_grads.1 = (bf16[512,4096]{1,0:T(8,128)(2,1)}, f32[8,128]{1,0:T(8,128)S(1)}) custom-call(bf16[512,768]{1,0:T(8,128)(2,1)S(1)} %get-tuple-element.48.refs_2_.gate_pre_ref, bf16[512,768]{1,0:T(8,128)(2,1)} %copy-done.9, bf16[2048,768]{1,0:T(8,128)(2,1)} %bitcast.38, bf16[2048,768]{1,0:T(8,128)(2,1)} %bitcast.40, ...), custom_call_target="tpu_custom_call", output_to_operand_aliasing={{0}: (4, {})} | custom-call | flops 1 | bytes 1 | tf_op jit(solution)/shard_map/row_grads/pallas_call | solution.py:270
  103.7 0.0 collective-permute-start.1
  103.7 6.8 %all-to-all-start.2 = ((bf16[32,16,4096]{2,1,0:T(8,128)(2,1)}), bf16[32,16,4096]{2,1,0:T(8,128)(2,1)}, u32[]{:S(2)}, u32[]{:S(2)}) async-start(bf16[32,16,4096]{2,1,0:T(8,128)(2,1)} %bitcast.36), calls=%async_computation.2 | async-start | bytes 8388608 | tf_op jit(solution)/shard_map/all_to_all | solution.py:200
  110.5 0.0 collective-permute-done.2.refs_5_
  110.5 0.0 collective-permute-done.3.refs_6_
  110.6 1.6 copy-done.2
  112.1 1.1 copy-done.10
  113.3 1.1 copy-done.16
  114.4 2.1 %chain_sum_2.1 = (bf16[4,256,256]{2,1,0:T(8,128)(2,1)S(1)}, bf16[5,256,256]{2,1,0:T(8,128)(2,1)S(1)}) custom-call(s32[1]{0:T(128)} %bitcast.9.me_ref, bf16[512,2048]{1,0:T(8,128)(2,1)S(1)} %bitcast.30, bf16[512,2048]{1,0:T(8,128)(2,1)S(1)} %bitcast.19, bf16[512,768]{1,0:T(8,128)(2,1)S(1)} %get-tuple-element.48.refs_2_.gate_pre_ref, ...), custom_call_target="tpu_custom_call" | custom-call | flops 20000000000 | bytes 62914560 | tf_op jit(solution)/shard_map/chain_sum_2/pallas_call | solution.py:251
  116.5 3.3 %collective-permute-start.7 = (bf16[5,256,256]{2,1,0:T(8,128)(2,1)S(1)}, bf16[5,256,256]{2,1,0:T(8,128)(2,1)S(1)}, u32[]{:S(2)}, u32[]{:S(2)}) collective-permute-start(bf16[5,256,256]{2,1,0:T(8,128)(2,1)S(1)} %get-tuple-element.64), channel_id=1, source_target_pairs={{0,7},{1,0},{2,1},{3,2},{4,3},{5,4},{6,5},{7,6},{8,15},{9,8},{10,9... | collective-permute-start | bytes 1966088 | tf_op jit(solution)/shard_map/ppermute | solution.py:299
  119.8 0.0 collective-permute-start.6
  119.8 0.0 collective-permute-done.refs_5_
  119.8 0.7 collective-permute-done.1.refs_6_
  120.5 2.1 %chain_sum_3.1 = (bf16[4,256,256]{2,1,0:T(8,128)(2,1)S(1)}, bf16[5,256,256]{2,1,0:T(8,128)(2,1)S(1)}) custom-call(s32[1]{0:T(128)} %bitcast.9.me_ref, bf16[512,2048]{1,0:T(8,128)(2,1)S(1)} %bitcast.31, bf16[512,2048]{1,0:T(8,128)(2,1)S(1)} %bitcast.20, bf16[512,768]{1,0:T(8,128)(2,1)S(1)} %get-tuple-element.48.refs_2_.gate_pre_ref, ...), custom_call_target="tpu_custom_call" | custom-call | flops 20000000000 | bytes 62914560 | tf_op jit(solution)/shard_map/chain_sum_3/pallas_call | solution.py:251
  122.6 0.1 collective-permute-start.5
  122.7 3.2 %collective-permute-start.4 = (bf16[4,256,256]{2,1,0:T(8,128)(2,1)S(1)}, bf16[4,256,256]{2,1,0:T(8,128)(2,1)S(1)}, u32[]{:S(2)}, u32[]{:S(2)}) collective-permute-start(bf16[4,256,256]{2,1,0:T(8,128)(2,1)S(1)} %get-tuple-element.62.refs_7_), channel_id=1, source_target_pairs={{0,7},{1,0},{2,1},{3,2},{4,3},{5,4},{6,5},{7,6},{8,15},{9,8},{10,9... | collective-permute-start | bytes 1572872 | tf_op jit(solution)/shard_map/ppermute | solution.py:299
  125.9 9.9 %collective-permute-done.6.refs_5_ = bf16[4,256,256]{2,1,0:T(8,128)(2,1)S(1)} collective-permute-done((bf16[4,256,256]{2,1,0:T(8,128)(2,1)S(1)}, bf16[4,256,256]{2,1,0:T(8,128)(2,1)S(1)}, u32[]{:S(2)}, u32[]{:S(2)}) %collective-permute-start.6) | collective-permute-done | bytes 524320 | tf_op jit(solution)/shard_map/ppermute | solution.py:299
  135.8 0.0 collective-permute-done.7.refs_6_
  135.8 0.9 chain_sum_4.1
  136.7 2.8 %collective-permute-start.11 = (bf16[5,256,256]{2,1,0:T(8,128)(2,1)S(1)}, bf16[5,256,256]{2,1,0:T(8,128)(2,1)S(1)}, u32[]{:S(2)}, u32[]{:S(2)}) collective-permute-start(bf16[5,256,256]{2,1,0:T(8,128)(2,1)S(1)} %get-tuple-element.68), channel_id=1, source_target_pairs={{0,7},{1,0},{2,1},{3,2},{4,3},{5,4},{6,5},{7,6},{8,15},{9,8},{10,9... | collective-permute-start | bytes 1966088 | tf_op jit(solution)/shard_map/ppermute | solution.py:299
  139.6 0.0 collective-permute-start.10
  139.6 6.6 %collective-permute-done.4.refs_5_ = bf16[4,256,256]{2,1,0:T(8,128)(2,1)S(1)} collective-permute-done((bf16[4,256,256]{2,1,0:T(8,128)(2,1)S(1)}, bf16[4,256,256]{2,1,0:T(8,128)(2,1)S(1)}, u32[]{:S(2)}, u32[]{:S(2)}) %collective-permute-start.4) | collective-permute-done | bytes 524320 | tf_op jit(solution)/shard_map/ppermute | solution.py:299
  146.1 3.7 %collective-permute-done.5.refs_6_ = bf16[5,256,256]{2,1,0:T(8,128)(2,1)S(1)} collective-permute-done((bf16[5,256,256]{2,1,0:T(8,128)(2,1)S(1)}, bf16[5,256,256]{2,1,0:T(8,128)(2,1)S(1)}, u32[]{:S(2)}, u32[]{:S(2)}) %collective-permute-start.5) | collective-permute-done | bytes 655392 | tf_op jit(solution)/shard_map/ppermute | solution.py:299
  149.9 0.9 chain_sum_5.1
  150.8 0.1 collective-permute-start.9
  150.8 0.0 copy-start.11
  150.9 0.0 copy-start.17
  150.9 3.2 %collective-permute-start.8 = (bf16[4,256,256]{2,1,0:T(8,128)(2,1)S(1)}, bf16[4,256,256]{2,1,0:T(8,128)(2,1)S(1)}, u32[]{:S(2)}, u32[]{:S(2)}) collective-permute-start(bf16[4,256,256]{2,1,0:T(8,128)(2,1)S(1)} %get-tuple-element.66.refs_7_), channel_id=1, source_target_pairs={{0,7},{1,0},{2,1},{3,2},{4,3},{5,4},{6,5},{7,6},{8,15},{9,8},{10,9... | collective-permute-start | bytes 1572872 | tf_op jit(solution)/shard_map/ppermute | solution.py:299
  154.1 7.0 %collective-permute-done.10.refs_5_ = bf16[4,256,256]{2,1,0:T(8,128)(2,1)S(1)} collective-permute-done((bf16[4,256,256]{2,1,0:T(8,128)(2,1)S(1)}, bf16[4,256,256]{2,1,0:T(8,128)(2,1)S(1)}, u32[]{:S(2)}, u32[]{:S(2)}) %collective-permute-start.10) | collective-permute-done | bytes 524320 | tf_op jit(solution)/shard_map/ppermute | solution.py:299
  161.1 0.0 collective-permute-done.11.refs_6_
  161.1 1.8 chain_sum_6.1
  162.9 2.8 %collective-permute-start.13 = (bf16[5,256,256]{2,1,0:T(8,128)(2,1)}, bf16[5,256,256]{2,1,0:T(8,128)(2,1)}, u32[]{:S(2)}, u32[]{:S(2)}) collective-permute-start(bf16[5,256,256]{2,1,0:T(8,128)(2,1)} %get-tuple-element.72), channel_id=1, source_target_pairs={{0,7},{1,0},{2,1},{3,2},{4,3},{5,4},{6,5},{7,6},{8,15},{9,8},{10,9... | collective-permute-start | bytes 1966088 | tf_op jit(solution)/shard_map/ppermute | solution.py:299
  165.7 0.0 collective-permute-start.12
  165.7 5.8 %collective-permute-done.8.refs_5_ = bf16[4,256,256]{2,1,0:T(8,128)(2,1)S(1)} collective-permute-done((bf16[4,256,256]{2,1,0:T(8,128)(2,1)S(1)}, bf16[4,256,256]{2,1,0:T(8,128)(2,1)S(1)}, u32[]{:S(2)}, u32[]{:S(2)}) %collective-permute-start.8) | collective-permute-done | bytes 524320 | tf_op jit(solution)/shard_map/ppermute | solution.py:299
  171.4 3.7 %collective-permute-done.9.refs_6_ = bf16[5,256,256]{2,1,0:T(8,128)(2,1)S(1)} collective-permute-done((bf16[5,256,256]{2,1,0:T(8,128)(2,1)S(1)}, bf16[5,256,256]{2,1,0:T(8,128)(2,1)S(1)}, u32[]{:S(2)}, u32[]{:S(2)}) %collective-permute-start.9) | collective-permute-done | bytes 655392 | tf_op jit(solution)/shard_map/ppermute | solution.py:299
  175.2 1.1 copy-done.8
  176.3 0.8 chain_sum_own.1
  177.2 1.0 copy-done.5
  178.1 0.0 all-to-all-done.2
  178.1 5.5 %combine.1 = (bf16[48,2048]{1,0:T(8,128)(2,1)}, bf16[48,2048]{1,0:T(8,128)(2,1)}, f32[8,48]{1,0:T(8,128)}) custom-call(s32[8,48]{1,0:T(8,128)} %bitcast.44, f32[8,48]{1,0:T(8,128)} %bitcast.46, bf16[512,48]{1,0:T(8,128)(2,1)} %get-tuple-element.41.place_ref, bf16[48,2048]{1,0:T(8,128)(2,1)} %grads_ref.3, bf16[512,4096]{1,0:T(8,128)(2,1)} %bitcast.11.back_ref.back_grad_ref, ...), custom_call_target="tpu_custom_call" | custom-call | flops 402653184 | bytes 4194304 | tf_op jit(solution)/shard_map/combine/pallas_call | solution.py:304
  183.6 1.8 collective-permute-done.12.a0
  185.4 0.0 collective-permute-done.13.b0
  185.4 0.9 copy-done.13
  186.3 2.8 %chain_sum_last.1 = (f32[256,768]{1,0:T(8,128)}, f32[256,768]{1,0:T(8,128)}, f32[768,256]{1,0:T(8,128)}) custom-call(f32[4,256,256]{2,1,0:T(8,128)S(1)} %copy-done.6, f32[5,256,256]{2,1,0:T(8,128)S(1)} %get-tuple-element.71.own_b, bf16[4,256,256]{2,1,0:T(8,128)(2,1)} %collective-permute-done.12.a0, bf16[5,256,256]{2,1,0:T(8,128)(2,1)} %collective-permute-done.13.b0, ...), custom_call_target="tpu_custom_call" | custom-call | flops 1 | bytes 1 | tf_op jit(solution)/shard_map/chain_sum_last/pallas_call | solution.py:328
  (20 shorter events, 0.0 us)
Async XLA Ops:
  39.8 33.1 %all-to-all-start = ((bf16[32,16,2048]{2,1,0:T(8,128)(2,1)}), bf16[32,16,2048]{2,1,0:T(8,128)(2,1)S(1)}, u32[]{:S(2)}, u32[]{:S(2)}) async-start(bf16[32,16,2048]{2,1,0:T(8,128)(2,1)} %bitcast.41), calls=%async_computation | async-start | bytes 4194304 | tf_op jit(solution)/shard_map/all_to_all | solution.py:200
  72.9 1.9 copy-start
  74.8 1.4 copy-start.3
  76.2 1.4 copy-start.4
  77.6 1.1 copy-start.12
  78.8 0.7 copy-start.14
  79.4 2.7 %copy-start.1 = (bf16[32,16,2048]{2,1,0:T(8,128)(2,1)S(1)}, bf16[32,16,2048]{2,1,0:T(8,128)(2,1)}, u32[]{:S(2)}) copy-start(bf16[32,16,2048]{2,1,0:T(8,128)(2,1)} %all_to_all.15) | copy-start | bytes 6291460
  82.1 7.7 %copy-start.9 = (bf16[512,768]{1,0:T(8,128)(2,1)}, bf16[512,768]{1,0:T(8,128)(2,1)S(1)}, u32[]{:S(2)}) copy-start(bf16[512,768]{1,0:T(8,128)(2,1)S(1)} %get-tuple-element.49.refs_3_.up_pre_ref) | copy-start | bytes 2359300
  82.1 7.7 %copy-start.15 = (bf16[768,512]{1,0:T(8,128)(2,1)}, bf16[768,512]{1,0:T(8,128)(2,1)S(1)}, u32[]{:S(2)}) copy-start(bf16[768,512]{1,0:T(8,128)(2,1)S(1)} %get-tuple-element.51.refs_4_) | copy-start | bytes 2359300
  82.1 79.0 %copy-start.7 = (bf16[512,768]{1,0:T(8,128)(2,1)}, bf16[512,768]{1,0:T(8,128)(2,1)S(1)}, u32[]{:S(2)}) copy-start(bf16[512,768]{1,0:T(8,128)(2,1)S(1)} %get-tuple-element.48.refs_2_.gate_pre_ref) | copy-start | bytes 2359300
  83.9 26.6 %collective-permute-start.3 = (bf16[5,256,256]{2,1,0:T(8,128)(2,1)}, bf16[5,256,256]{2,1,0:T(8,128)(2,1)}, u32[]{:S(2)}, u32[]{:S(2)}) collective-permute-start(bf16[5,256,256]{2,1,0:T(8,128)(2,1)} %get-tuple-element.59), channel_id=1, source_target_pairs={{0,7},{1,0},{2,1},{3,2},{4,3},{5,4},{6,5},{7,6},{8,15},{9,8},{10,9... | collective-permute-start | bytes 1966088 | tf_op jit(solution)/shard_map/ppermute | solution.py:299
  89.8 20.8 %collective-permute-start.2 = (bf16[4,256,256]{2,1,0:T(8,128)(2,1)}, bf16[4,256,256]{2,1,0:T(8,128)(2,1)}, u32[]{:S(2)}, u32[]{:S(2)}) collective-permute-start(bf16[4,256,256]{2,1,0:T(8,128)(2,1)} %get-tuple-element.52.refs_5_), channel_id=1, source_target_pairs={{0,1},{1,2},{2,3},{3,4},{4,5},{5,6},{6,7},{7,0},{8,9},{9,10},{10,1... | collective-permute-start | bytes 1572872 | tf_op jit(solution)/shard_map/ppermute | solution.py:299
  91.5 28.3 %collective-permute-start = (bf16[4,256,256]{2,1,0:T(8,128)(2,1)S(1)}, bf16[4,256,256]{2,1,0:T(8,128)(2,1)}, u32[]{:S(2)}, u32[]{:S(2)}) collective-permute-start(bf16[4,256,256]{2,1,0:T(8,128)(2,1)S(1)} %get-tuple-element.53.after), channel_id=1, source_target_pairs={{0,7},{1,0},{2,1},{3,2},{4,3},{5,4},{6,5},{7,6},{8,15},{9,8},{10,9... | collective-permute-start | bytes 1572872 | tf_op jit(solution)/shard_map/ppermute | solution.py:299
  103.7 16.8 %collective-permute-start.1 = (bf16[5,256,256]{2,1,0:T(8,128)(2,1)}, bf16[5,256,256]{2,1,0:T(8,128)(2,1)}, u32[]{:S(2)}, u32[]{:S(2)}) collective-permute-start(bf16[5,256,256]{2,1,0:T(8,128)(2,1)} %get-tuple-element.58), channel_id=1, source_target_pairs={{0,1},{1,2},{2,3},{3,4},{4,5},{5,6},{6,7},{7,0},{8,9},{9,10},{10,1... | collective-permute-start | bytes 1966088 | tf_op jit(solution)/shard_map/ppermute | solution.py:299
  103.7 74.4 %all-to-all-start.2 = ((bf16[32,16,4096]{2,1,0:T(8,128)(2,1)}), bf16[32,16,4096]{2,1,0:T(8,128)(2,1)}, u32[]{:S(2)}, u32[]{:S(2)}) async-start(bf16[32,16,4096]{2,1,0:T(8,128)(2,1)} %bitcast.36), calls=%async_computation.2 | async-start | bytes 8388608 | tf_op jit(solution)/shard_map/all_to_all | solution.py:200
  110.6 1.6 copy-start.2
  112.1 1.1 copy-start.10
  113.3 1.1 copy-start.16
  116.5 19.3 %collective-permute-start.7 = (bf16[5,256,256]{2,1,0:T(8,128)(2,1)S(1)}, bf16[5,256,256]{2,1,0:T(8,128)(2,1)S(1)}, u32[]{:S(2)}, u32[]{:S(2)}) collective-permute-start(bf16[5,256,256]{2,1,0:T(8,128)(2,1)S(1)} %get-tuple-element.64), channel_id=1, source_target_pairs={{0,7},{1,0},{2,1},{3,2},{4,3},{5,4},{6,5},{7,6},{8,15},{9,8},{10,9... | collective-permute-start | bytes 1966088 | tf_op jit(solution)/shard_map/ppermute | solution.py:299
  119.8 16.0 %collective-permute-start.6 = (bf16[4,256,256]{2,1,0:T(8,128)(2,1)S(1)}, bf16[4,256,256]{2,1,0:T(8,128)(2,1)S(1)}, u32[]{:S(2)}, u32[]{:S(2)}) collective-permute-start(bf16[4,256,256]{2,1,0:T(8,128)(2,1)S(1)} %get-tuple-element.61.refs_7_), channel_id=1, source_target_pairs={{0,1},{1,2},{2,3},{3,4},{4,5},{5,6},{6,7},{7,0},{8,9},{9,10},{10,1... | collective-permute-start | bytes 1572872 | tf_op jit(solution)/shard_map/ppermute | solution.py:299
  122.6 27.2 %collective-permute-start.5 = (bf16[5,256,256]{2,1,0:T(8,128)(2,1)S(1)}, bf16[5,256,256]{2,1,0:T(8,128)(2,1)S(1)}, u32[]{:S(2)}, u32[]{:S(2)}) collective-permute-start(bf16[5,256,256]{2,1,0:T(8,128)(2,1)S(1)} %get-tuple-element.63), channel_id=1, source_target_pairs={{0,1},{1,2},{2,3},{3,4},{4,5},{5,6},{6,7},{7,0},{8,9},{9,10},{10,1... | collective-permute-start | bytes 1966088 | tf_op jit(solution)/shard_map/ppermute | solution.py:299
  122.7 23.4 %collective-permute-start.4 = (bf16[4,256,256]{2,1,0:T(8,128)(2,1)S(1)}, bf16[4,256,256]{2,1,0:T(8,128)(2,1)S(1)}, u32[]{:S(2)}, u32[]{:S(2)}) collective-permute-start(bf16[4,256,256]{2,1,0:T(8,128)(2,1)S(1)} %get-tuple-element.62.refs_7_), channel_id=1, source_target_pairs={{0,7},{1,0},{2,1},{3,2},{4,3},{5,4},{6,5},{7,6},{8,15},{9,8},{10,9... | collective-permute-start | bytes 1572872 | tf_op jit(solution)/shard_map/ppermute | solution.py:299
  136.7 24.4 %collective-permute-start.11 = (bf16[5,256,256]{2,1,0:T(8,128)(2,1)S(1)}, bf16[5,256,256]{2,1,0:T(8,128)(2,1)S(1)}, u32[]{:S(2)}, u32[]{:S(2)}) collective-permute-start(bf16[5,256,256]{2,1,0:T(8,128)(2,1)S(1)} %get-tuple-element.68), channel_id=1, source_target_pairs={{0,7},{1,0},{2,1},{3,2},{4,3},{5,4},{6,5},{7,6},{8,15},{9,8},{10,9... | collective-permute-start | bytes 1966088 | tf_op jit(solution)/shard_map/ppermute | solution.py:299
  139.6 21.6 %collective-permute-start.10 = (bf16[4,256,256]{2,1,0:T(8,128)(2,1)S(1)}, bf16[4,256,256]{2,1,0:T(8,128)(2,1)S(1)}, u32[]{:S(2)}, u32[]{:S(2)}) collective-permute-start(bf16[4,256,256]{2,1,0:T(8,128)(2,1)S(1)} %get-tuple-element.65.refs_7_), channel_id=1, source_target_pairs={{0,1},{1,2},{2,3},{3,4},{4,5},{5,6},{6,7},{7,0},{8,9},{9,10},{10,1... | collective-permute-start | bytes 1572872 | tf_op jit(solution)/shard_map/ppermute | solution.py:299
  150.8 24.4 %collective-permute-start.9 = (bf16[5,256,256]{2,1,0:T(8,128)(2,1)S(1)}, bf16[5,256,256]{2,1,0:T(8,128)(2,1)S(1)}, u32[]{:S(2)}, u32[]{:S(2)}) collective-permute-start(bf16[5,256,256]{2,1,0:T(8,128)(2,1)S(1)} %get-tuple-element.67), channel_id=1, source_target_pairs={{0,1},{1,2},{2,3},{3,4},{4,5},{5,6},{6,7},{7,0},{8,9},{9,10},{10,1... | collective-permute-start | bytes 1966088 | tf_op jit(solution)/shard_map/ppermute | solution.py:299
  150.8 24.3 %copy-start.11 = (bf16[512,768]{1,0:T(8,128)(2,1)S(1)}, bf16[512,768]{1,0:T(8,128)(2,1)}, u32[]{:S(2)}) copy-start(bf16[512,768]{1,0:T(8,128)(2,1)} %copy-done.9) | copy-start | bytes 2359300
  150.9 24.3 %copy-start.17 = (bf16[768,512]{1,0:T(8,128)(2,1)S(1)}, bf16[768,512]{1,0:T(8,128)(2,1)}, u32[]{:S(2)}) copy-start(bf16[768,512]{1,0:T(8,128)(2,1)} %copy-done.15) | copy-start | bytes 2359300
  150.9 20.6 %collective-permute-start.8 = (bf16[4,256,256]{2,1,0:T(8,128)(2,1)S(1)}, bf16[4,256,256]{2,1,0:T(8,128)(2,1)S(1)}, u32[]{:S(2)}, u32[]{:S(2)}) collective-permute-start(bf16[4,256,256]{2,1,0:T(8,128)(2,1)S(1)} %get-tuple-element.66.refs_7_), channel_id=1, source_target_pairs={{0,7},{1,0},{2,1},{3,2},{4,3},{5,4},{6,5},{7,6},{8,15},{9,8},{10,9... | collective-permute-start | bytes 1572872 | tf_op jit(solution)/shard_map/ppermute | solution.py:299
  162.9 22.5 %collective-permute-start.13 = (bf16[5,256,256]{2,1,0:T(8,128)(2,1)}, bf16[5,256,256]{2,1,0:T(8,128)(2,1)}, u32[]{:S(2)}, u32[]{:S(2)}) collective-permute-start(bf16[5,256,256]{2,1,0:T(8,128)(2,1)} %get-tuple-element.72), channel_id=1, source_target_pairs={{0,7},{1,0},{2,1},{3,2},{4,3},{5,4},{6,5},{7,6},{8,15},{9,8},{10,9... | collective-permute-start | bytes 1966088 | tf_op jit(solution)/shard_map/ppermute | solution.py:299
  165.7 19.7 %collective-permute-start.12 = (bf16[4,256,256]{2,1,0:T(8,128)(2,1)}, bf16[4,256,256]{2,1,0:T(8,128)(2,1)}, u32[]{:S(2)}, u32[]{:S(2)}) collective-permute-start(bf16[4,256,256]{2,1,0:T(8,128)(2,1)} %get-tuple-element.69.refs_7_), channel_id=1, source_target_pairs={{0,1},{1,2},{2,3},{3,4},{4,5},{5,6},{6,7},{7,0},{8,9},{9,10},{10,1... | collective-permute-start | bytes 1572872 | tf_op jit(solution)/shard_map/ppermute | solution.py:299
  175.2 1.1 copy-start.8
  177.2 1.0 copy-start.5
  178.1 7.3 %copy-start.6 = (f32[4,256,256]{2,1,0:T(8,128)S(1)}, f32[4,256,256]{2,1,0:T(8,128)}, u32[]{:S(2)}) copy-start(f32[4,256,256]{2,1,0:T(8,128)} %copy-done.5) | copy-start | bytes 3145732
  185.4 0.9 copy-start.13

commit v3 on v2

v3 whole, which is shorter than its diff:
```python
import functools

import jax
import jax.numpy as jnp
from jax import lax
from jax.experimental import pallas as pl
from jax.experimental.pallas import tpu as pltpu
from jax.sharding import PartitionSpec as P

BF16 = jnp.bfloat16
F32 = jnp.float32
LAST = (((1,), (1,)), ((), ()))
FIRST = (((0,), (0,)), ((), ()))


def params(mib=16):
    return pltpu.CompilerParams(vmem_limit_bytes=mib * 2**20)


def cost(flops, nbytes, exps=0):
    return pl.CostEstimate(flops=flops, bytes_accessed=nbytes, transcendentals=exps)


LONG = cost(20 * 10**9, 60 * 2**20)
SHORT = cost(1, 1)


def dot(a, b, dims=(((1,), (0,)), ((), ()))):
    return lax.dot_general(a, b, dims, preferred_element_type=F32)


def slot_masks(routes_t, slots, capacity):
    tokens = routes_t.shape[1]
    expert = lax.broadcasted_iota(jnp.int32, (slots, tokens), 0) // capacity
    return [expert == routes_t[k : k + 1, :] for k in range(routes_t.shape[0])]


def dispatch_kernel(capacity, routes_ref, gates_ref, tokens_ref, grads_ref, wide_ref, place_ref):
    routes_t, gates_t = routes_ref[...], gates_ref[...]
    slots, tokens = place_ref.shape
    masks = slot_masks(routes_t, slots, capacity)
    hit = jnp.zeros((slots, tokens), F32)
    weight = jnp.zeros((slots, tokens), F32)
    for k, mask in enumerate(masks):
        hit = jnp.where(mask, 1.0, hit)
        weight = jnp.where(mask, gates_t[k : k + 1, :], weight)
    before = (
        lax.broadcasted_iota(jnp.int32, (tokens, tokens), 0)
        < lax.broadcasted_iota(jnp.int32, (tokens, tokens), 1)
    ).astype(F32).astype(BF16)
    rank = dot(hit.astype(BF16), before)
    mine = (lax.broadcasted_iota(jnp.int32, (slots, tokens), 0) % capacity).astype(F32)
    place = jnp.where(rank == mine, hit, 0.0)
    slot_weight = jnp.sum(place * weight, axis=1, keepdims=True)
    place_low = place.astype(BF16)
    place_ref[...] = place_low
    model = tokens_ref.shape[1]
    wide_ref[:, :model] = dot(place_low, tokens_ref[...]).astype(BF16)
    wide_ref[:, model:] = (slot_weight * dot(place_low, grads_ref[...])).astype(BF16)


def expert_kernel(width, wide_ref, gate_ref, up_ref, down_ref, hidden_ref, hidden_t_ref, gate_pre_ref, up_pre_ref):
    model, hid = gate_ref.shape
    for j in range(hid // width):
        cols = slice(j * width, (j + 1) * width)
        pre_gate = dot(wide_ref[:, :model], gate_ref[:, cols])
        pre_up = dot(wide_ref[:, :model], up_ref[:, cols])
        hidden_grad = dot(wide_ref[:, model:], down_ref[cols, :], LAST)
        sig = jax.nn.sigmoid(pre_gate)
        silu = pre_gate * sig
        hidden = (silu * pre_up).astype(BF16)
        hidden_ref[:, cols] = hidden
        hidden_t_ref[cols, :] = hidden.T
        gate_pre_ref[:, cols] = (hidden_grad * pre_up * sig * (1.0 + pre_gate * (1.0 - sig))).astype(BF16)
        up_pre_ref[:, cols] = (hidden_grad * silu).astype(BF16)


def chunk_sums(step_a, step_b, groups, me_ref, wide, gate_pre, up_pre, hidden_t, held_a=(), held_b=()):
    model = wide.shape[1] // 2
    width = model // groups
    blocks = gate_pre.shape[1] // width
    me = me_ref[0]

    def columns(step, first=0):
        return pl.ds(pl.multiple_of(first + lax.rem(me + step, groups) * width, width), width)

    turned_a = wide[:, columns(step_a)].T
    for j in range(blocks + 1):
        source = gate_pre[:, j * width : (j + 1) * width] if j < blocks else up_pre[:, :width]
        total = dot(turned_a, source)
        for held in held_a:
            total = total + held[j].astype(F32)
        yield "a", j, total
    turned_b = turned_a if step_a == step_b else wide[:, columns(step_b)].T
    grads_b = wide[:, columns(step_b, model)]
    for j in range(2 * blocks - 1):
        if j < blocks - 1:
            total = dot(turned_b, up_pre[:, (j + 1) * width : (j + 2) * width])
        else:
            i = j - blocks + 1
            total = dot(hidden_t[i * width : (i + 1) * width, :], grads_b)
        for held in held_b:
            total = total + held[j].astype(F32)
        yield "b", j, total


def link_kernel(step_a, step_b, groups, arrived, me_ref, *refs):
    held = [[refs[4]], [refs[5]]] if arrived else []
    out = {"a": refs[-2], "b": refs[-1]}
    for part, j, total in chunk_sums(step_a, step_b, groups, me_ref, *refs[:4], *held):
        out[part][j] = total.astype(out[part].dtype)


def last_kernel(own_a, own_b, a0, b0, gate_ref, up_ref, down_ref):
    width = own_a.shape[1]
    blocks = own_a.shape[0] - 1
    for j in range(blocks):
        gate_ref[:, j * width : (j + 1) * width] = own_a[j] + a0[j].astype(F32)
        down_ref[j * width : (j + 1) * width, :] = own_b[blocks - 1 + j] + b0[blocks - 1 + j].astype(F32)
    up_ref[:, :width] = own_a[blocks] + a0[blocks].astype(F32)
    for j in range(blocks - 1):
        up_ref[:, (j + 1) * width : (j + 2) * width] = own_b[j] + b0[j].astype(F32)


def back_kernel(width, hidden_ref, gate_pre_ref, up_pre_ref, down_ref, gate_ref, up_ref, _, back_ref, token_ref):
    token_ref[...] = jnp.zeros_like(token_ref)
    model = down_ref.shape[1]
    for j in range(model // width):
        cols = slice(j * width, (j + 1) * width)
        back_ref[:, cols] = dot(hidden_ref[...], down_ref[:, cols]).astype(BF16)
        row_grad = dot(gate_pre_ref[...], gate_ref[cols, :], LAST) + dot(up_pre_ref[...], up_ref[cols, :], LAST)
        back_ref[:, model + j * width : model + (j + 1) * width] = row_grad.astype(BF16)


def combine_kernel(
    capacity, routes_ref, gates_ref, place_ref, grads_ref, back_ref, back_grad_ref,
    out_ref, grad_ref, gates_grad_ref, high, low, score,
):
    step = pl.program_id(0)

    @pl.when(step == 0)
    def _():
        gates_t = gates_ref[...]
        weight = jnp.zeros(place_ref.shape, F32)
        for k, mask in enumerate(slot_masks(routes_ref[...], place_ref.shape[0], capacity)):
            weight = jnp.where(mask, gates_t[k : k + 1, :], weight)
        weight = weight * place_ref[...].astype(F32)
        high[...] = weight.astype(BF16)
        low[...] = (weight - weight.astype(BF16).astype(F32)).astype(BF16)
        score[...] = jnp.zeros_like(score)

    back = back_ref[...]
    out_ref[...] = (dot(high[...], back, FIRST) + dot(low[...], back, FIRST)).astype(BF16)
    grad_ref[...] = dot(place_ref[...], back_grad_ref[...], FIRST).astype(BF16)
    slot_grads = dot(place_ref[...], grads_ref[...])
    score[...] += jnp.sum(slot_grads * back.astype(F32), axis=1, keepdims=True)

    @pl.when(step == pl.num_programs(0) - 1)
    def _():
        placed = score[...] * place_ref[...].astype(F32)
        for k, mask in enumerate(slot_masks(routes_ref[...], place_ref.shape[0], capacity)):
            gates_grad_ref[k : k + 1, :] = jnp.sum(jnp.where(mask, placed, 0.0), axis=0, keepdims=True)


def shape(dims, dtype=BF16):
    return jax.ShapeDtypeStruct(dims, dtype)


def whole(dims):
    return pl.BlockSpec(dims, lambda i: (0,) * len(dims))


def local(tokens, routes, gate_weights, w_gate, w_up, w_down, out_grad):
    count, top = routes.shape
    model = tokens.shape[1]
    experts = w_gate.shape[0] * lax.axis_size("expert")
    groups = lax.axis_size("dp")
    capacity = max(2, 4 * count * top // (3 * experts))
    slots = experts * capacity
    hid = w_gate.shape[2]
    width = model // groups
    blocks = hid // width
    w_gate, w_up, w_down = w_gate[0], w_up[0], w_down[0]
    routes_t, gates_t = routes.T, gate_weights.T

    resident = pl.BlockSpec(memory_space=pltpu.VMEM)
    anywhere = pl.BlockSpec(memory_space=pl.ANY)
    send, place = pl.pallas_call(
        functools.partial(dispatch_kernel, capacity),
        in_specs=[resident] * 4,
        out_specs=[resident] * 2,
        out_shape=(shape((slots, 2 * model)), shape((slots, count))),
        compiler_params=params(),
        cost_estimate=cost(4 * slots * count * model, 4 * slots * model),
        name="dispatch",
    )(routes_t, gates_t, tokens, out_grad)

    def exchange(array):
        wide = array.reshape(experts, capacity, array.shape[1])
        return lax.all_to_all(wide, "expert", 0, 0, tiled=True).reshape(array.shape)

    wide = exchange(send)
    hidden, hidden_t, gate_pre, up_pre = pl.pallas_call(
        functools.partial(expert_kernel, width),
        in_specs=[resident] * 4,
        out_specs=[resident] * 4,
        out_shape=(shape((slots, hid)), shape((hid, slots)), shape((slots, hid)), shape((slots, hid))),
        compiler_params=params(),
        cost_estimate=cost(6 * slots * model * hid, 4 * slots * model + 6 * model * hid + 8 * slots * hid),
        name="expert",
    )(wide, w_gate, w_up, w_down)

    me = lax.axis_index("dp")
    place_of = me.reshape(1).astype(jnp.int32)

    def chain_call(step_a, step_b, dtype, held, name, after):
        parts = (shape((blocks + 1, width, width), dtype), shape((2 * blocks - 1, width, width), dtype))
        return pl.pallas_call(
            functools.partial(link_kernel, step_a, step_b, groups, bool(held)),
            in_specs=[
                pl.BlockSpec(memory_space=pltpu.SMEM),
                *[resident] * (4 + len(held)),
                *[anywhere] * len(after),
            ],
            out_specs=[resident, resident],
            out_shape=parts,
            compiler_params=params(),
            cost_estimate=LONG,
            name=name,
        )(place_of, wide, gate_pre, up_pre, hidden_t, *held, *after)

    up_ring = [(i, (i + 1) % groups) for i in range(groups)]
    down_ring = [(i, (i - 1) % groups) for i in range(groups)]
    half_way = groups // 2
    slots_of_ring = [(half_way, 0)] + [(k, s) for k in range(half_way - 1, 0, -1) for s in (1, 0)]
    def rows_back(after):
        return pl.pallas_call(
            functools.partial(back_kernel, width),
            in_specs=[*[resident] * 6, anywhere],
            out_specs=[resident] * 2,
            out_shape=(shape((slots, 2 * model)), shape((8, 128), F32)),
            compiler_params=params(),
            cost_estimate=SHORT,
            name="rows_back",
        )(hidden, gate_pre, up_pre, w_down, w_gate, w_up, after)

    came, after = {}, ()
    for number, (k, swapped) in enumerate(slots_of_ring):
        step_a, step_b = (groups - k, k) if swapped else (k, groups - k)
        held = came.get((k, swapped), ())
        part_a, part_b = chain_call(step_a, step_b, BF16, held, f"chain_sum_{number}", after)
        after = (part_a,)
        if number == 1:
            going_back, token = rows_back(part_a)
            after = (token,)
        ring_a, ring_b = (down_ring, up_ring) if swapped else (up_ring, down_ring)
        came[k - 1, swapped] = (lax.ppermute(part_a, "dp", ring_a), lax.ppermute(part_b, "dp", ring_b))

    back = exchange(going_back)

    half = model // 2
    layer_out, token_grad, gates_grad_t = pl.pallas_call(
        functools.partial(combine_kernel, capacity),
        grid=(2,),
        in_specs=[
            whole((top, count)),
            whole((top, count)),
            whole((slots, count)),
            pl.BlockSpec((count, half), lambda i: (0, i)),
            pl.BlockSpec((slots, half), lambda i: (0, i)),
            pl.BlockSpec((slots, half), lambda i: (0, 2 + i)),
        ],
        out_specs=[
            pl.BlockSpec((count, half), lambda i: (0, i)),
            pl.BlockSpec((count, half), lambda i: (0, i)),
            whole((top, count)),
        ],
        out_shape=(shape((count, model)), shape((count, model)), shape((top, count), F32)),
        scratch_shapes=[pltpu.VMEM((slots, count), BF16)] * 2 + [pltpu.VMEM((slots, 1), F32)],
        compiler_params=params(),
        cost_estimate=cost(8 * slots * count * model, 4 * slots * model),
        name="combine",
    )(routes_t, gates_t, place, out_grad, back, back)

    own_a, own_b = chain_call(0, 0, F32, came[0, 1], "chain_sum_own", (*after, token_grad))
    gate_grad, up_grad, down_grad = pl.pallas_call(
        last_kernel,
        in_specs=[resident] * 4,
        out_shape=(shape((width, hid), F32), shape((width, hid), F32), shape((hid, width), F32)),
        compiler_params=params(),
        cost_estimate=SHORT,
        name="chain_sum_last",
    )(own_a, own_b, *came[0, 0])
    return (layer_out, token_grad, gates_grad_t.T, gate_grad[None], up_grad[None], down_grad[None])


def solution(mesh):
    rows = P(("expert", "dp"), None)
    weights = P("expert", None, None)
    return jax.shard_map(
        local,
        mesh=mesh,
        in_specs=(rows, rows, rows, weights, weights, weights, rows),
        out_specs=(rows, rows, rows, P("expert", "dp", None), P("expert", "dp", None), P("expert", None, "dp")),
        check_vma=False,
    )
```

time: 190 us -> 183 us (0.963)
  blocking collectives: 35.1 us -> 0 us
  waiting for transfers between devices: 51.6 us -> 79.6 us
  starting transfers between devices: 36.5 us -> 39.2 us
    all_to_all x2, waiting for transfers between devices: 12.4 us -> 51.4 us  [exchange(): return lax.all_to_all(wide, 'expert', 0, 0, tiled=True).reshape(array.shape)]
    all_to_all x1 -> x0, blocking collectives: 35.1 us -> none  [exchange(): return lax.all_to_all(wide, 'expert', 0, 0, tiled=True).reshape(array.shape)]
    pallas_call x6 -> x4, Pallas kernels: 34.2 us -> 15.6 us  [the longest x1 7.46 us: local(): pl.pallas_call(functools.partial(expert_kernel, width), in_specs=[residen...]
    pallas_call x8, Pallas kernels: 12 us -> 29.7 us  [chain_call(): pl.pallas_call(functools.partial(link_kernel, step_a, step_b, groups, boo...]
    ppermute x7, waiting for transfers between devices: 31.1 us -> 20.7 us  [local(): lax.ppermute(part_a, 'dp', ring_a)]
    ppermute x7, starting transfers between devices: 14.9 us -> 11.9 us  [local(): lax.ppermute(part_b, 'dp', ring_b)]
    all_to_all x2, starting transfers between devices: 11.9 us -> 14.9 us  [exchange(): return lax.all_to_all(wide, 'expert', 0, 0, tiled=True).reshape(array.shape)]
    ppermute x7, starting transfers between devices: 9.67 us -> 12.4 us  [local(): lax.ppermute(part_a, 'dp', ring_a)]
  transfers between devices with their start and end apart: 16 -> 16, of which waited for: 9 -> 10; matrix products, arithmetic and copies ran while one was open for 0% -> 0% of each run, Pallas kernels for 21% -> 19%
where the time goes in v3:
time: 183 us; the launch traced here: 182 us
  waiting for transfers between devices  79.6 us (43%)
  Pallas kernels  50.4 us (28%)
  starting transfers between devices  39.2 us (21%)
  local copies, waits for them, and re-layouts  12.1 us (7%)
    all_to_all x2, waiting for transfers between devices, exchange(): return lax.all_to_all(wide, 'expert', 0, 0, tiled=True).reshape(array.shape)  51.4 us
    pallas_call x8, Pallas kernels, chain_call(): pl.pallas_call(functools.partial(link_kernel, step_a, step_b, groups, boo...  29.7 us
    ppermute x7, waiting for transfers between devices, local(): lax.ppermute(part_a, 'dp', ring_a)  20.7 us
    all_to_all x2, starting transfers between devices, exchange(): return lax.all_to_all(wide, 'expert', 0, 0, tiled=True).reshape(array.shape)  14.9 us
    ppermute x7, starting transfers between devices, local(): lax.ppermute(part_a, 'dp', ring_a)  12.4 us
    unnamed x46, local copies, waits for them, and re-layouts  12.1 us
    ppermute x7, starting transfers between devices, local(): lax.ppermute(part_b, 'dp', ring_b)  11.9 us
    ppermute x7, waiting for transfers between devices, local(): lax.ppermute(part_b, 'dp', ring_b)  7.51 us
  transfers between devices with their start and end apart: 16, of which 10 were waited for; matrix products, arithmetic and copies ran while one was open for 0% of the time, Pallas kernels for 19%

profile of v3, /device:TPU:2, one launch (start us, length us, event | category | flops | bytes accessed | tf_op | source)
XLA Modules:
  0.0 182.1 jit_solution(6112969804118912177)
XLA Ops:
  0.6 0.0 copy-start.11
  0.6 0.9 copy-done.11
  1.6 0.7 copy-done.13
  2.3 0.7 copy-done.15
  2.9 0.9 copy-done.17
  3.9 1.5 dispatch.1
  5.4 2.0 %copy-done.1 = bf16[512,4096]{1,0:T(8,128)(2,1)} copy-done((bf16[512,4096]{1,0:T(8,128)(2,1)}, bf16[512,4096]{1,0:T(8,128)(2,1)S(1)}, u32[]{:S(2)}) %copy-start.1) | copy-done | bytes 4194328
  7.4 7.9 %all-to-all-start = ((bf16[32,16,4096]{2,1,0:T(8,128)(2,1)}), bf16[32,16,4096]{2,1,0:T(8,128)(2,1)}, u32[]{:S(2)}, u32[]{:S(2)}) async-start(bf16[32,16,4096]{2,1,0:T(8,128)(2,1)} %bitcast.15), calls=%async_computation | async-start | bytes 8388608 | tf_op jit(solution)/shard_map/all_to_all | solution.py:200
  15.4 51.4 %all-to-all-done = bf16[32,16,4096]{2,1,0:T(8,128)(2,1)} async-done(((bf16[32,16,4096]{2,1,0:T(8,128)(2,1)}), bf16[32,16,4096]{2,1,0:T(8,128)(2,1)}, u32[]{:S(2)}, u32[]{:S(2)}) %all-to-all-start) | async-done | bytes 4194336 | tf_op jit(solution)/shard_map/all_to_all | solution.py:200
  66.7 1.9 %copy-done.3 = bf16[1,2048,768]{2,1,0:T(8,128)(2,1)S(1)} copy-done((bf16[1,2048,768]{2,1,0:T(8,128)(2,1)S(1)}, bf16[1,2048,768]{2,1,0:T(8,128)(2,1)}, u32[]{:S(2)}) %copy-start.3) | copy-done | bytes 3145752
  68.6 1.9 %copy-done.5 = bf16[1,768,2048]{2,1,0:T(8,128)(2,1)S(1)} copy-done((bf16[1,768,2048]{2,1,0:T(8,128)(2,1)S(1)}, bf16[1,768,2048]{2,1,0:T(8,128)(2,1)}, u32[]{:S(2)}) %copy-start.5) | copy-done | bytes 3145752
  70.5 7.5 %expert.1 = (bf16[512,768]{1,0:T(8,128)(2,1)S(1)}, bf16[768,512]{1,0:T(8,128)(2,1)S(1)}, bf16[512,768]{1,0:T(8,128)(2,1)S(1)}, bf16[512,768]{1,0:T(8,128)(2,1)S(1)}) custom-call(bf16[512,4096]{1,0:T(8,128)(2,1)} %bitcast.3.wide_ref.refs_0_, bf16[2048,768]{1,0:T(8,128)(2,1)S(1)} %bitcast.16, bf16[2048,768]{1,0:T(8,128)(2,1)S(1)} %bitcast.18, ...), custom_call_target="tpu_custom_call" | custom-call | flops 4831838208 | bytes 16777216 | tf_op jit(solution)/shard_map/expert/pallas_call | solution.py:203
  78.0 0.0 copy-start.19
  78.0 0.0 copy-start.7
  78.0 0.0 copy-start.9
  78.0 4.7 %chain_sum_0.1 = (bf16[4,256,256]{2,1,0:T(8,128)(2,1)}, bf16[5,256,256]{2,1,0:T(8,128)(2,1)}) custom-call(s32[1]{0:T(128)} %bitcast.7.me_ref, bf16[512,4096]{1,0:T(8,128)(2,1)} %bitcast.3.wide_ref.refs_0_, bf16[512,768]{1,0:T(8,128)(2,1)S(1)} %get-tuple-element.39.refs_1_.gate_pre_ref, bf16[512,768]{1,0:T(8,128)(2,1)S(1)} %get-tuple-element.40.refs_2_.up_pre_ref, ...), custom_call_target="tpu_custom_call" | custom-call | flops 20000000000 | bytes 62914560 | tf_op jit(solution)/shard_map/chain_sum_0/pallas_call | solution.py:218
  82.7 1.9 %collective-permute-start.2 = (bf16[4,256,256]{2,1,0:T(8,128)(2,1)}, bf16[4,256,256]{2,1,0:T(8,128)(2,1)}, u32[]{:S(2)}, u32[]{:S(2)}) collective-permute-start(bf16[4,256,256]{2,1,0:T(8,128)(2,1)} %get-tuple-element.42.refs_4_), channel_id=1, source_target_pairs={{0,1},{1,2},{2,3},{3,4},{4,5},{5,6},{6,7},{7,0},{8,9},{9,10},{10,1... | collective-permute-start | bytes 1572872 | tf_op jit(solution)/shard_map/ppermute | solution.py:257
  84.6 4.0 %collective-permute-start.3 = (bf16[5,256,256]{2,1,0:T(8,128)(2,1)}, bf16[5,256,256]{2,1,0:T(8,128)(2,1)}, u32[]{:S(2)}, u32[]{:S(2)}) collective-permute-start(bf16[5,256,256]{2,1,0:T(8,128)(2,1)} %get-tuple-element.49), channel_id=1, source_target_pairs={{0,7},{1,0},{2,1},{3,2},{4,3},{5,4},{6,5},{7,6},{8,15},{9,8},{10,9... | collective-permute-start | bytes 1966088 | tf_op jit(solution)/shard_map/ppermute | solution.py:257
  88.7 3.9 %chain_sum_1.1 = (bf16[4,256,256]{2,1,0:T(8,128)(2,1)}, bf16[5,256,256]{2,1,0:T(8,128)(2,1)}) custom-call(s32[1]{0:T(128)} %bitcast.7.me_ref, bf16[512,4096]{1,0:T(8,128)(2,1)} %bitcast.3.wide_ref.refs_0_, bf16[512,768]{1,0:T(8,128)(2,1)S(1)} %get-tuple-element.39.refs_1_.gate_pre_ref, bf16[512,768]{1,0:T(8,128)(2,1)S(1)} %get-tuple-element.40.refs_2_.up_pre_ref, ...), custom_call_target="tpu_custom_call" | custom-call | flops 20000000000 | bytes 62914560 | tf_op jit(solution)/shard_map/chain_sum_1/pallas_call | solution.py:218
  92.6 1.9 %collective-permute-start = (bf16[4,256,256]{2,1,0:T(8,128)(2,1)}, bf16[4,256,256]{2,1,0:T(8,128)(2,1)}, u32[]{:S(2)}, u32[]{:S(2)}) collective-permute-start(bf16[4,256,256]{2,1,0:T(8,128)(2,1)} %get-tuple-element.43._), channel_id=1, source_target_pairs={{0,7},{1,0},{2,1},{3,2},{4,3},{5,4},{6,5},{7,6},{8,15},{9,8},{10,9... | collective-permute-start | bytes 1572872 | tf_op jit(solution)/shard_map/ppermute | solution.py:257
  94.5 0.1 collective-permute-start.1
  94.6 0.0 copy-done.7
  94.6 5.0 %rows_back.1 = (bf16[512,4096]{1,0:T(8,128)(2,1)S(1)}, f32[8,128]{1,0:T(8,128)S(1)}) custom-call(bf16[512,768]{1,0:T(8,128)(2,1)S(1)} %get-tuple-element.38.hidden_ref, bf16[512,768]{1,0:T(8,128)(2,1)S(1)} %get-tuple-element.39.refs_1_.gate_pre_ref, bf16[512,768]{1,0:T(8,128)(2,1)S(1)} %get-tuple-element.40.refs_2_.up_pre_ref, ...), custom_call_target="tpu_custom_call" | custom-call | flops 1 | bytes 1 | tf_op jit(solution)/shard_map/rows_back/pallas_call | solution.py:237
  99.7 0.0 copy-start
  99.7 2.1 %copy-done = bf16[512,4096]{1,0:T(8,128)(2,1)} copy-done((bf16[512,4096]{1,0:T(8,128)(2,1)}, bf16[512,4096]{1,0:T(8,128)(2,1)S(1)}, u32[]{:S(2)}) %copy-start) | copy-done | bytes 4194328
  101.7 7.0 %all-to-all-start.1 = ((bf16[32,16,4096]{2,1,0:T(8,128)(2,1)}), bf16[32,16,4096]{2,1,0:T(8,128)(2,1)}, u32[]{:S(2)}, u32[]{:S(2)}) async-start(bf16[32,16,4096]{2,1,0:T(8,128)(2,1)} %bitcast.14), calls=%async_computation.1 | async-start | bytes 8388608 | tf_op jit(solution)/shard_map/all_to_all | solution.py:200
  108.7 0.0 collective-permute-done.2.refs_4_
  108.7 0.0 collective-permute-done.3.refs_5_
  108.8 0.0 copy-done.8
  108.8 0.0 copy-done.10
  108.8 0.0 copy-start.21
  108.8 3.4 %chain_sum_2.1 = (bf16[4,256,256]{2,1,0:T(8,128)(2,1)S(1)}, bf16[5,256,256]{2,1,0:T(8,128)(2,1)S(1)}) custom-call(s32[1]{0:T(128)} %bitcast.7.me_ref, bf16[512,4096]{1,0:T(8,128)(2,1)} %bitcast.3.wide_ref.refs_0_, bf16[512,768]{1,0:T(8,128)(2,1)S(1)} %copy-done.8, bf16[512,768]{1,0:T(8,128)(2,1)S(1)} %copy-done.10, bf16[768,512]{1,0:T(8,128)(2,1)S(1)} %copy-done.20, ...), custom_call_target="tpu_custom_call" | custom-call | flops 20000000000 | bytes 62914560 | tf_op jit(solution)/shard_map/chain_sum_2/pallas_call | solution.py:218
  112.2 0.1 collective-permute-start.6
  112.3 3.2 %collective-permute-start.7 = (bf16[5,256,256]{2,1,0:T(8,128)(2,1)S(1)}, bf16[5,256,256]{2,1,0:T(8,128)(2,1)S(1)}, u32[]{:S(2)}, u32[]{:S(2)}) collective-permute-start(bf16[5,256,256]{2,1,0:T(8,128)(2,1)S(1)} %get-tuple-element.54), channel_id=1, source_target_pairs={{0,7},{1,0},{2,1},{3,2},{4,3},{5,4},{6,5},{7,6},{8,15},{9,8},{10,9... | collective-permute-start | bytes 1966088 | tf_op jit(solution)/shard_map/ppermute | solution.py:257
  115.6 0.0 collective-permute-done.refs_4_
  115.6 0.0 collective-permute-done.1.refs_5_
  115.6 3.4 %chain_sum_3.1 = (bf16[4,256,256]{2,1,0:T(8,128)(2,1)S(1)}, bf16[5,256,256]{2,1,0:T(8,128)(2,1)S(1)}) custom-call(s32[1]{0:T(128)} %bitcast.7.me_ref, bf16[512,4096]{1,0:T(8,128)(2,1)} %bitcast.3.wide_ref.refs_0_, bf16[512,768]{1,0:T(8,128)(2,1)S(1)} %copy-done.8, bf16[512,768]{1,0:T(8,128)(2,1)S(1)} %copy-done.10, bf16[768,512]{1,0:T(8,128)(2,1)S(1)} %copy-done.21, ...), custom_call_target="tpu_custom_call" | custom-call | flops 20000000000 | bytes 62914560 | tf_op jit(solution)/shard_map/chain_sum_3/pallas_call | solution.py:218
  119.0 2.1 %collective-permute-start.4 = (bf16[4,256,256]{2,1,0:T(8,128)(2,1)S(1)}, bf16[4,256,256]{2,1,0:T(8,128)(2,1)S(1)}, u32[]{:S(2)}, u32[]{:S(2)}) collective-permute-start(bf16[4,256,256]{2,1,0:T(8,128)(2,1)S(1)} %get-tuple-element.52.refs_6_), channel_id=1, source_target_pairs={{0,7},{1,0},{2,1},{3,2},{4,3},{5,4},{6,5},{7,6},{8,15},{9,8},{10,9... | collective-permute-start | bytes 1572872 | tf_op jit(solution)/shard_map/ppermute | solution.py:257
  121.1 0.0 collective-permute-start.5
  121.1 7.2 %collective-permute-done.6.refs_4_ = bf16[4,256,256]{2,1,0:T(8,128)(2,1)S(1)} collective-permute-done((bf16[4,256,256]{2,1,0:T(8,128)(2,1)S(1)}, bf16[4,256,256]{2,1,0:T(8,128)(2,1)S(1)}, u32[]{:S(2)}, u32[]{:S(2)}) %collective-permute-start.6) | collective-permute-done | bytes 524320 | tf_op jit(solution)/shard_map/ppermute | solution.py:257
  128.3 2.4 %collective-permute-done.7.refs_5_ = bf16[5,256,256]{2,1,0:T(8,128)(2,1)S(1)} collective-permute-done((bf16[5,256,256]{2,1,0:T(8,128)(2,1)S(1)}, bf16[5,256,256]{2,1,0:T(8,128)(2,1)S(1)}, u32[]{:S(2)}, u32[]{:S(2)}) %collective-permute-start.7) | collective-permute-done | bytes 655392 | tf_op jit(solution)/shard_map/ppermute | solution.py:257
  130.7 3.1 %chain_sum_4.1 = (bf16[4,256,256]{2,1,0:T(8,128)(2,1)S(1)}, bf16[5,256,256]{2,1,0:T(8,128)(2,1)S(1)}) custom-call(s32[1]{0:T(128)} %bitcast.7.me_ref, bf16[512,4096]{1,0:T(8,128)(2,1)} %bitcast.3.wide_ref.refs_0_, bf16[512,768]{1,0:T(8,128)(2,1)S(1)} %copy-done.8, bf16[512,768]{1,0:T(8,128)(2,1)S(1)} %copy-done.10, bf16[768,512]{1,0:T(8,128)(2,1)S(1)} %copy-done.21, ...), custom_call_target="tpu_custom_call" | custom-call | flops 20000000000 | bytes 62914560 | tf_op jit(solution)/shard_map/chain_sum_4/pallas_call | solution.py:218
  133.7 1.6 collective-permute-start.10
  135.3 2.3 %collective-permute-start.11 = (bf16[5,256,256]{2,1,0:T(8,128)(2,1)S(1)}, bf16[5,256,256]{2,1,0:T(8,128)(2,1)S(1)}, u32[]{:S(2)}, u32[]{:S(2)}) collective-permute-start(bf16[5,256,256]{2,1,0:T(8,128)(2,1)S(1)} %get-tuple-element.58), channel_id=1, source_target_pairs={{0,7},{1,0},{2,1},{3,2},{4,3},{5,4},{6,5},{7,6},{8,15},{9,8},{10,9... | collective-permute-start | bytes 1966088 | tf_op jit(solution)/shard_map/ppermute | solution.py:257
  137.6 4.3 %collective-permute-done.4.refs_4_ = bf16[4,256,256]{2,1,0:T(8,128)(2,1)S(1)} collective-permute-done((bf16[4,256,256]{2,1,0:T(8,128)(2,1)S(1)}, bf16[4,256,256]{2,1,0:T(8,128)(2,1)S(1)}, u32[]{:S(2)}, u32[]{:S(2)}) %collective-permute-start.4) | collective-permute-done | bytes 524320 | tf_op jit(solution)/shard_map/ppermute | solution.py:257
  141.9 0.4 collective-permute-done.5.refs_5_
  142.3 3.9 %chain_sum_5.1 = (bf16[4,256,256]{2,1,0:T(8,128)(2,1)}, bf16[5,256,256]{2,1,0:T(8,128)(2,1)}) custom-call(s32[1]{0:T(128)} %bitcast.7.me_ref, bf16[512,4096]{1,0:T(8,128)(2,1)} %bitcast.3.wide_ref.refs_0_, bf16[512,768]{1,0:T(8,128)(2,1)S(1)} %copy-done.8, bf16[512,768]{1,0:T(8,128)(2,1)S(1)} %copy-done.10, bf16[768,512]{1,0:T(8,128)(2,1)S(1)} %copy-done.21, ...), custom_call_target="tpu_custom_call" | custom-call | flops 20000000000 | bytes 62914560 | tf_op jit(solution)/shard_map/chain_sum_5/pallas_call | solution.py:218
  146.2 3.3 %collective-permute-start.8 = (bf16[4,256,256]{2,1,0:T(8,128)(2,1)}, bf16[4,256,256]{2,1,0:T(8,128)(2,1)}, u32[]{:S(2)}, u32[]{:S(2)}) collective-permute-start(bf16[4,256,256]{2,1,0:T(8,128)(2,1)} %get-tuple-element.56.refs_6_), channel_id=1, source_target_pairs={{0,7},{1,0},{2,1},{3,2},{4,3},{5,4},{6,5},{7,6},{8,15},{9,8},{10,9... | collective-permute-start | bytes 1572872 | tf_op jit(solution)/shard_map/ppermute | solution.py:257
  149.5 0.0 collective-permute-start.9
  149.5 4.0 %collective-permute-done.10.refs_4_ = bf16[4,256,256]{2,1,0:T(8,128)(2,1)S(1)} collective-permute-done((bf16[4,256,256]{2,1,0:T(8,128)(2,1)S(1)}, bf16[4,256,256]{2,1,0:T(8,128)(2,1)S(1)}, u32[]{:S(2)}, u32[]{:S(2)}) %collective-permute-start.10) | collective-permute-done | bytes 524320 | tf_op jit(solution)/shard_map/ppermute | solution.py:257
  153.5 2.4 %collective-permute-done.11.refs_5_ = bf16[5,256,256]{2,1,0:T(8,128)(2,1)S(1)} collective-permute-done((bf16[5,256,256]{2,1,0:T(8,128)(2,1)S(1)}, bf16[5,256,256]{2,1,0:T(8,128)(2,1)S(1)}, u32[]{:S(2)}, u32[]{:S(2)}) %collective-permute-start.11) | collective-permute-done | bytes 655392 | tf_op jit(solution)/shard_map/ppermute | solution.py:257
  155.9 3.9 %chain_sum_6.1 = (bf16[4,256,256]{2,1,0:T(8,128)(2,1)}, bf16[5,256,256]{2,1,0:T(8,128)(2,1)}) custom-call(s32[1]{0:T(128)} %bitcast.7.me_ref, bf16[512,4096]{1,0:T(8,128)(2,1)} %bitcast.3.wide_ref.refs_0_, bf16[512,768]{1,0:T(8,128)(2,1)S(1)} %copy-done.8, bf16[512,768]{1,0:T(8,128)(2,1)S(1)} %copy-done.10, bf16[768,512]{1,0:T(8,128)(2,1)S(1)} %copy-done.21, ...), custom_call_target="tpu_custom_call" | custom-call | flops 20000000000 | bytes 62914560 | tf_op jit(solution)/shard_map/chain_sum_6/pallas_call | solution.py:218
  159.9 1.5 collective-permute-start.12
  161.3 2.2 %collective-permute-start.13 = (bf16[5,256,256]{2,1,0:T(8,128)(2,1)}, bf16[5,256,256]{2,1,0:T(8,128)(2,1)S(1)}, u32[]{:S(2)}, u32[]{:S(2)}) collective-permute-start(bf16[5,256,256]{2,1,0:T(8,128)(2,1)} %get-tuple-element.62), channel_id=1, source_target_pairs={{0,7},{1,0},{2,1},{3,2},{4,3},{5,4},{6,5},{7,6},{8,15},{9,8},{10,9... | collective-permute-start | bytes 1966088 | tf_op jit(solution)/shard_map/ppermute | solution.py:257
  163.6 0.0 all-to-all-done.1
  163.6 0.0 copy-start.22
  163.6 5.1 %combine.1 = (bf16[48,2048]{1,0:T(8,128)(2,1)}, bf16[48,2048]{1,0:T(8,128)(2,1)}, f32[8,48]{1,0:T(8,128)}) custom-call(s32[8,48]{1,0:T(8,128)S(1)} %bitcast.23, f32[8,48]{1,0:T(8,128)S(1)} %bitcast.25, bf16[512,48]{1,0:T(8,128)(2,1)S(1)} %get-tuple-element.36.place_ref, bf16[48,2048]{1,0:T(8,128)(2,1)S(1)} %copy-done.12, ...), custom_call_target="tpu_custom_call" | custom-call | flops 402653184 | bytes 4194304 | tf_op jit(solution)/shard_map/combine/pallas_call | solution.py:262
  168.7 0.0 collective-permute-done.8.refs_4_
  168.7 0.1 collective-permute-done.9.refs_5_
  168.7 0.9 copy-done.18
  169.6 3.4 %chain_sum_own.1 = (f32[4,256,256]{2,1,0:T(8,128)S(1)}, f32[5,256,256]{2,1,0:T(8,128)S(1)}) custom-call(s32[1]{0:T(128)} %bitcast.7.me_ref, bf16[512,4096]{1,0:T(8,128)(2,1)} %bitcast.3.wide_ref.refs_0_, bf16[512,768]{1,0:T(8,128)(2,1)S(1)} %copy-done.8, bf16[512,768]{1,0:T(8,128)(2,1)S(1)} %copy-done.10, bf16[768,512]{1,0:T(8,128)(2,1)S(1)} %copy-done.22, ...), custom_call_target="tpu_custom_call" | custom-call | flops 20000000000 | bytes 62914560 | tf_op jit(solution)/shard_map/chain_sum_own/pallas_call | solution.py:218
  173.0 5.2 %collective-permute-done.12.a0 = bf16[4,256,256]{2,1,0:T(8,128)(2,1)S(1)} collective-permute-done((bf16[4,256,256]{2,1,0:T(8,128)(2,1)}, bf16[4,256,256]{2,1,0:T(8,128)(2,1)S(1)}, u32[]{:S(2)}, u32[]{:S(2)}) %collective-permute-start.12) | collective-permute-done | bytes 524320 | tf_op jit(solution)/shard_map/ppermute | solution.py:257
  178.2 2.3 %collective-permute-done.13.b0 = bf16[5,256,256]{2,1,0:T(8,128)(2,1)S(1)} collective-permute-done((bf16[5,256,256]{2,1,0:T(8,128)(2,1)}, bf16[5,256,256]{2,1,0:T(8,128)(2,1)S(1)}, u32[]{:S(2)}, u32[]{:S(2)}) %collective-permute-start.13) | collective-permute-done | bytes 655392 | tf_op jit(solution)/shard_map/ppermute | solution.py:257
  180.5 1.6 chain_sum_last.1
  (27 shorter events, 0.0 us)
Async XLA Ops:
  0.6 0.9 copy-start.11
  1.6 0.7 copy-start.13
  2.2 0.7 copy-start.15
  2.9 0.9 copy-start.17
  5.4 2.0 %copy-start.1 = (bf16[512,4096]{1,0:T(8,128)(2,1)}, bf16[512,4096]{1,0:T(8,128)(2,1)S(1)}, u32[]{:S(2)}) copy-start(bf16[512,4096]{1,0:T(8,128)(2,1)S(1)} %get-tuple-element.37) | copy-start | bytes 12582916
  7.4 59.3 %copy-start.2 = (bf16[1,2048,768]{2,1,0:T(8,128)(2,1)S(1)}, bf16[1,2048,768]{2,1,0:T(8,128)(2,1)}, u32[]{:S(2)}) copy-start(bf16[1,2048,768]{2,1,0:T(8,128)(2,1)} %param.10) | copy-start | bytes 9437188
  7.4 59.3 %all-to-all-start = ((bf16[32,16,4096]{2,1,0:T(8,128)(2,1)}), bf16[32,16,4096]{2,1,0:T(8,128)(2,1)}, u32[]{:S(2)}, u32[]{:S(2)}) async-start(bf16[32,16,4096]{2,1,0:T(8,128)(2,1)} %bitcast.15), calls=%async_computation | async-start | bytes 8388608 | tf_op jit(solution)/shard_map/all_to_all | solution.py:200
  66.7 1.9 %copy-start.3 = (bf16[1,2048,768]{2,1,0:T(8,128)(2,1)S(1)}, bf16[1,2048,768]{2,1,0:T(8,128)(2,1)}, u32[]{:S(2)}) copy-start(bf16[1,2048,768]{2,1,0:T(8,128)(2,1)} %param.11) | copy-start | bytes 9437188
  68.6 1.9 %copy-start.5 = (bf16[1,768,2048]{2,1,0:T(8,128)(2,1)S(1)}, bf16[1,768,2048]{2,1,0:T(8,128)(2,1)}, u32[]{:S(2)}) copy-start(bf16[1,768,2048]{2,1,0:T(8,128)(2,1)} %param.12) | copy-start | bytes 9437188
  78.0 10.7 %copy-start.19 = (bf16[768,512]{1,0:T(8,128)(2,1)}, bf16[768,512]{1,0:T(8,128)(2,1)S(1)}, u32[]{:S(2)}) copy-start(bf16[768,512]{1,0:T(8,128)(2,1)S(1)} %get-tuple-element.41.refs_3_) | copy-start | bytes 2359300
  78.0 16.6 %copy-start.7 = (bf16[512,768]{1,0:T(8,128)(2,1)}, bf16[512,768]{1,0:T(8,128)(2,1)S(1)}, u32[]{:S(2)}) copy-start(bf16[512,768]{1,0:T(8,128)(2,1)S(1)} %get-tuple-element.39.refs_1_.gate_pre_ref) | copy-start | bytes 2359300
  78.0 16.6 %copy-start.9 = (bf16[512,768]{1,0:T(8,128)(2,1)}, bf16[512,768]{1,0:T(8,128)(2,1)S(1)}, u32[]{:S(2)}) copy-start(bf16[512,768]{1,0:T(8,128)(2,1)S(1)} %get-tuple-element.40.refs_2_.up_pre_ref) | copy-start | bytes 2359300
  82.7 26.0 %collective-permute-start.2 = (bf16[4,256,256]{2,1,0:T(8,128)(2,1)}, bf16[4,256,256]{2,1,0:T(8,128)(2,1)}, u32[]{:S(2)}, u32[]{:S(2)}) collective-permute-start(bf16[4,256,256]{2,1,0:T(8,128)(2,1)} %get-tuple-element.42.refs_4_), channel_id=1, source_target_pairs={{0,1},{1,2},{2,3},{3,4},{4,5},{5,6},{6,7},{7,0},{8,9},{9,10},{10,1... | collective-permute-start | bytes 1572872 | tf_op jit(solution)/shard_map/ppermute | solution.py:257
  84.6 10.0 %copy-start.4 = (bf16[1,2048,768]{2,1,0:T(8,128)(2,1)S(1)}, bf16[1,2048,768]{2,1,0:T(8,128)(2,1)}, u32[]{:S(2)}) copy-start(bf16[1,2048,768]{2,1,0:T(8,128)(2,1)} %param.11) | copy-start | bytes 9437188
  84.6 10.0 %copy-start.6 = (bf16[1,768,2048]{2,1,0:T(8,128)(2,1)S(1)}, bf16[1,768,2048]{2,1,0:T(8,128)(2,1)}, u32[]{:S(2)}) copy-start(bf16[1,768,2048]{2,1,0:T(8,128)(2,1)} %param.12) | copy-start | bytes 9437188
  84.6 24.1 %collective-permute-start.3 = (bf16[5,256,256]{2,1,0:T(8,128)(2,1)}, bf16[5,256,256]{2,1,0:T(8,128)(2,1)}, u32[]{:S(2)}, u32[]{:S(2)}) collective-permute-start(bf16[5,256,256]{2,1,0:T(8,128)(2,1)} %get-tuple-element.49), channel_id=1, source_target_pairs={{0,7},{1,0},{2,1},{3,2},{4,3},{5,4},{6,5},{7,6},{8,15},{9,8},{10,9... | collective-permute-start | bytes 1966088 | tf_op jit(solution)/shard_map/ppermute | solution.py:257
  92.6 23.0 %collective-permute-start = (bf16[4,256,256]{2,1,0:T(8,128)(2,1)}, bf16[4,256,256]{2,1,0:T(8,128)(2,1)}, u32[]{:S(2)}, u32[]{:S(2)}) collective-permute-start(bf16[4,256,256]{2,1,0:T(8,128)(2,1)} %get-tuple-element.43._), channel_id=1, source_target_pairs={{0,7},{1,0},{2,1},{3,2},{4,3},{5,4},{6,5},{7,6},{8,15},{9,8},{10,9... | collective-permute-start | bytes 1572872 | tf_op jit(solution)/shard_map/ppermute | solution.py:257
  94.5 21.1 %collective-permute-start.1 = (bf16[5,256,256]{2,1,0:T(8,128)(2,1)}, bf16[5,256,256]{2,1,0:T(8,128)(2,1)}, u32[]{:S(2)}, u32[]{:S(2)}) collective-permute-start(bf16[5,256,256]{2,1,0:T(8,128)(2,1)} %get-tuple-element.48), channel_id=1, source_target_pairs={{0,1},{1,2},{2,3},{3,4},{4,5},{5,6},{6,7},{7,0},{8,9},{9,10},{10,1... | collective-permute-start | bytes 1966088 | tf_op jit(solution)/shard_map/ppermute | solution.py:257
  99.7 2.1 %copy-start = (bf16[512,4096]{1,0:T(8,128)(2,1)}, bf16[512,4096]{1,0:T(8,128)(2,1)S(1)}, u32[]{:S(2)}) copy-start(bf16[512,4096]{1,0:T(8,128)(2,1)S(1)} %get-tuple-element.44) | copy-start | bytes 12582916
  101.7 7.0 %copy-start.8 = (bf16[512,768]{1,0:T(8,128)(2,1)S(1)}, bf16[512,768]{1,0:T(8,128)(2,1)}, u32[]{:S(2)}) copy-start(bf16[512,768]{1,0:T(8,128)(2,1)} %copy-done.7) | copy-start | bytes 2359300
  101.7 7.0 %copy-start.10 = (bf16[512,768]{1,0:T(8,128)(2,1)S(1)}, bf16[512,768]{1,0:T(8,128)(2,1)}, u32[]{:S(2)}) copy-start(bf16[512,768]{1,0:T(8,128)(2,1)} %copy-done.9) | copy-start | bytes 2359300
  101.7 7.0 %copy-start.20 = (bf16[768,512]{1,0:T(8,128)(2,1)S(1)}, bf16[768,512]{1,0:T(8,128)(2,1)}, u32[]{:S(2)}) copy-start(bf16[768,512]{1,0:T(8,128)(2,1)} %copy-done.19) | copy-start | bytes 2359300
  101.7 61.8 %all-to-all-start.1 = ((bf16[32,16,4096]{2,1,0:T(8,128)(2,1)}), bf16[32,16,4096]{2,1,0:T(8,128)(2,1)}, u32[]{:S(2)}, u32[]{:S(2)}) async-start(bf16[32,16,4096]{2,1,0:T(8,128)(2,1)} %bitcast.14), calls=%async_computation.1 | async-start | bytes 8388608 | tf_op jit(solution)/shard_map/all_to_all | solution.py:200
  108.8 6.8 %copy-start.21 = (bf16[768,512]{1,0:T(8,128)(2,1)S(1)}, bf16[768,512]{1,0:T(8,128)(2,1)}, u32[]{:S(2)}) copy-start(bf16[768,512]{1,0:T(8,128)(2,1)} %copy-done.19) | copy-start | bytes 2359300
  112.2 16.0 %collective-permute-start.6 = (bf16[4,256,256]{2,1,0:T(8,128)(2,1)S(1)}, bf16[4,256,256]{2,1,0:T(8,128)(2,1)S(1)}, u32[]{:S(2)}, u32[]{:S(2)}) collective-permute-start(bf16[4,256,256]{2,1,0:T(8,128)(2,1)S(1)} %get-tuple-element.51.refs_6_), channel_id=1, source_target_pairs={{0,1},{1,2},{2,3},{3,4},{4,5},{5,6},{6,7},{7,0},{8,9},{9,10},{10,1... | collective-permute-start | bytes 1572872 | tf_op jit(solution)/shard_map/ppermute | solution.py:257
  112.3 18.3 %collective-permute-start.7 = (bf16[5,256,256]{2,1,0:T(8,128)(2,1)S(1)}, bf16[5,256,256]{2,1,0:T(8,128)(2,1)S(1)}, u32[]{:S(2)}, u32[]{:S(2)}) collective-permute-start(bf16[5,256,256]{2,1,0:T(8,128)(2,1)S(1)} %get-tuple-element.54), channel_id=1, source_target_pairs={{0,7},{1,0},{2,1},{3,2},{4,3},{5,4},{6,5},{7,6},{8,15},{9,8},{10,9... | collective-permute-start | bytes 1966088 | tf_op jit(solution)/shard_map/ppermute | solution.py:257
  119.0 22.9 %collective-permute-start.4 = (bf16[4,256,256]{2,1,0:T(8,128)(2,1)S(1)}, bf16[4,256,256]{2,1,0:T(8,128)(2,1)S(1)}, u32[]{:S(2)}, u32[]{:S(2)}) collective-permute-start(bf16[4,256,256]{2,1,0:T(8,128)(2,1)S(1)} %get-tuple-element.52.refs_6_), channel_id=1, source_target_pairs={{0,7},{1,0},{2,1},{3,2},{4,3},{5,4},{6,5},{7,6},{8,15},{9,8},{10,9... | collective-permute-start | bytes 1572872 | tf_op jit(solution)/shard_map/ppermute | solution.py:257
  121.1 21.2 %collective-permute-start.5 = (bf16[5,256,256]{2,1,0:T(8,128)(2,1)S(1)}, bf16[5,256,256]{2,1,0:T(8,128)(2,1)S(1)}, u32[]{:S(2)}, u32[]{:S(2)}) collective-permute-start(bf16[5,256,256]{2,1,0:T(8,128)(2,1)S(1)} %get-tuple-element.53), channel_id=1, source_target_pairs={{0,1},{1,2},{2,3},{3,4},{4,5},{5,6},{6,7},{7,0},{8,9},{9,10},{10,1... | collective-permute-start | bytes 1966088 | tf_op jit(solution)/shard_map/ppermute | solution.py:257
  133.7 19.8 %collective-permute-start.10 = (bf16[4,256,256]{2,1,0:T(8,128)(2,1)S(1)}, bf16[4,256,256]{2,1,0:T(8,128)(2,1)S(1)}, u32[]{:S(2)}, u32[]{:S(2)}) collective-permute-start(bf16[4,256,256]{2,1,0:T(8,128)(2,1)S(1)} %get-tuple-element.55.refs_6_), channel_id=1, source_target_pairs={{0,1},{1,2},{2,3},{3,4},{4,5},{5,6},{6,7},{7,0},{8,9},{9,10},{10,1... | collective-permute-start | bytes 1572872 | tf_op jit(solution)/shard_map/ppermute | solution.py:257
  135.3 20.6 %collective-permute-start.11 = (bf16[5,256,256]{2,1,0:T(8,128)(2,1)S(1)}, bf16[5,256,256]{2,1,0:T(8,128)(2,1)S(1)}, u32[]{:S(2)}, u32[]{:S(2)}) collective-permute-start(bf16[5,256,256]{2,1,0:T(8,128)(2,1)S(1)} %get-tuple-element.58), channel_id=1, source_target_pairs={{0,7},{1,0},{2,1},{3,2},{4,3},{5,4},{6,5},{7,6},{8,15},{9,8},{10,9... | collective-permute-start | bytes 1966088 | tf_op jit(solution)/shard_map/ppermute | solution.py:257
  146.2 22.4 %collective-permute-start.8 = (bf16[4,256,256]{2,1,0:T(8,128)(2,1)}, bf16[4,256,256]{2,1,0:T(8,128)(2,1)}, u32[]{:S(2)}, u32[]{:S(2)}) collective-permute-start(bf16[4,256,256]{2,1,0:T(8,128)(2,1)} %get-tuple-element.56.refs_6_), channel_id=1, source_target_pairs={{0,7},{1,0},{2,1},{3,2},{4,3},{5,4},{6,5},{7,6},{8,15},{9,8},{10,9... | collective-permute-start | bytes 1572872 | tf_op jit(solution)/shard_map/ppermute | solution.py:257
  149.5 14.1 %copy-start.12 = (bf16[48,2048]{1,0:T(8,128)(2,1)S(1)}, bf16[48,2048]{1,0:T(8,128)(2,1)}, u32[]{:S(2)}) copy-start(bf16[48,2048]{1,0:T(8,128)(2,1)} %grads_ref.3) | copy-start | bytes 589828
  149.5 14.1 %copy-start.14 = (s32[48,8]{0,1:T(8,128)S(1)}, s32[48,8]{0,1:T(8,128)}, u32[]{:S(2)}) copy-start(s32[48,8]{0,1:T(8,128)} %param.8) | copy-start | bytes 4612
  149.5 14.1 %copy-start.16 = (f32[48,8]{0,1:T(8,128)S(1)}, f32[48,8]{0,1:T(8,128)}, u32[]{:S(2)}) copy-start(f32[48,8]{0,1:T(8,128)} %param.9) | copy-start | bytes 4612
  149.5 19.2 %collective-permute-start.9 = (bf16[5,256,256]{2,1,0:T(8,128)(2,1)}, bf16[5,256,256]{2,1,0:T(8,128)(2,1)}, u32[]{:S(2)}, u32[]{:S(2)}) collective-permute-start(bf16[5,256,256]{2,1,0:T(8,128)(2,1)} %get-tuple-element.57), channel_id=1, source_target_pairs={{0,1},{1,2},{2,3},{3,4},{4,5},{5,6},{6,7},{7,0},{8,9},{9,10},{10,1... | collective-permute-start | bytes 1966088 | tf_op jit(solution)/shard_map/ppermute | solution.py:257
  159.9 18.4 %collective-permute-start.12 = (bf16[4,256,256]{2,1,0:T(8,128)(2,1)}, bf16[4,256,256]{2,1,0:T(8,128)(2,1)S(1)}, u32[]{:S(2)}, u32[]{:S(2)}) collective-permute-start(bf16[4,256,256]{2,1,0:T(8,128)(2,1)} %get-tuple-element.59.refs_6_), channel_id=1, source_target_pairs={{0,1},{1,2},{2,3},{3,4},{4,5},{5,6},{6,7},{7,0},{8,9},{9,10},{10,1... | collective-permute-start | bytes 1572872 | tf_op jit(solution)/shard_map/ppermute | solution.py:257
  161.3 19.2 %collective-permute-start.13 = (bf16[5,256,256]{2,1,0:T(8,128)(2,1)}, bf16[5,256,256]{2,1,0:T(8,128)(2,1)S(1)}, u32[]{:S(2)}, u32[]{:S(2)}) collective-permute-start(bf16[5,256,256]{2,1,0:T(8,128)(2,1)} %get-tuple-element.62), channel_id=1, source_target_pairs={{0,7},{1,0},{2,1},{3,2},{4,3},{5,4},{6,5},{7,6},{8,15},{9,8},{10,9... | collective-permute-start | bytes 1966088 | tf_op jit(solution)/shard_map/ppermute | solution.py:257
  163.6 5.1 %copy-start.22 = (bf16[768,512]{1,0:T(8,128)(2,1)S(1)}, bf16[768,512]{1,0:T(8,128)(2,1)}, u32[]{:S(2)}) copy-start(bf16[768,512]{1,0:T(8,128)(2,1)} %copy-done.19) | copy-start | bytes 2359300
  168.7 0.9 copy-start.18

commit v4 on v3

--- a/solution.py
+++ b/solution.py
@@ -35,79 +35,76 @@
     return [expert == routes_t[k : k + 1, :] for k in range(routes_t.shape[0])]
 
 
-def dispatch_kernel(capacity, routes_ref, gates_ref, tokens_ref, grads_ref, wide_ref, place_ref):
-    routes_t, gates_t = routes_ref[...], gates_ref[...]
-    slots, tokens = place_ref.shape
-    masks = slot_masks(routes_t, slots, capacity)
-    hit = jnp.zeros((slots, tokens), F32)
-    weight = jnp.zeros((slots, tokens), F32)
-    for k, mask in enumerate(masks):
-        hit = jnp.where(mask, 1.0, hit)
-        weight = jnp.where(mask, gates_t[k : k + 1, :], weight)
-    before = (
-        lax.broadcasted_iota(jnp.int32, (tokens, tokens), 0)
-        < lax.broadcasted_iota(jnp.int32, (tokens, tokens), 1)
-    ).astype(F32).astype(BF16)
-    rank = dot(hit.astype(BF16), before)
-    mine = (lax.broadcasted_iota(jnp.int32, (slots, tokens), 0) % capacity).astype(F32)
-    place = jnp.where(rank == mine, hit, 0.0)
-    slot_weight = jnp.sum(place * weight, axis=1, keepdims=True)
-    place_low = place.astype(BF16)
-    place_ref[...] = place_low
-    model = tokens_ref.shape[1]
-    wide_ref[:, :model] = dot(place_low, tokens_ref[...]).astype(BF16)
-    wide_ref[:, model:] = (slot_weight * dot(place_low, grads_ref[...])).astype(BF16)
-
-
-def expert_kernel(width, wide_ref, gate_ref, up_ref, down_ref, hidden_ref, hidden_t_ref, gate_pre_ref, up_pre_ref):
-    model, hid = gate_ref.shape
-    for j in range(hid // width):
-        cols = slice(j * width, (j + 1) * width)
-        pre_gate = dot(wide_ref[:, :model], gate_ref[:, cols])
-        pre_up = dot(wide_ref[:, :model], up_ref[:, cols])
-        hidden_grad = dot(wide_ref[:, model:], down_ref[cols, :], LAST)
-        sig = jax.nn.sigmoid(pre_gate)
-        silu = pre_gate * sig
-        hidden = (silu * pre_up).astype(BF16)
-        hidden_ref[:, cols] = hidden
-        hidden_t_ref[cols, :] = hidden.T
-        gate_pre_ref[:, cols] = (hidden_grad * pre_up * sig * (1.0 + pre_gate * (1.0 - sig))).astype(BF16)
-        up_pre_ref[:, cols] = (hidden_grad * silu).astype(BF16)
-
-
-def chunk_sums(step_a, step_b, groups, me_ref, wide, gate_pre, up_pre, hidden_t, held_a=(), held_b=()):
-    model = wide.shape[1] // 2
-    width = model // groups
+def dispatch_kernel(capacity, routes_ref, gates_ref, tokens_ref, grads_ref, wide_ref, place_ref, slot_weight):
+    step, half = pl.program_id(0), pl.num_programs(0) // 2
+
+    @pl.when(step == 0)
+    def _():
+        slots, tokens = place_ref.shape
+        hit = jnp.zeros((slots, tokens), F32)
+        weight = jnp.zeros((slots, tokens), F32)
+        gates_t = gates_ref[...]
+        for k, mask in enumerate(slot_masks(routes_ref[...], slots, capacity)):
+            hit = jnp.where(mask, 1.0, hit)
+            weight = jnp.where(mask, gates_t[k : k + 1, :], weight)
+        before = (
+            lax.broadcasted_iota(jnp.int32, (tokens, tokens), 0)
+            < lax.broadcasted_iota(jnp.int32, (tokens, tokens), 1)
+        ).astype(F32).astype(BF16)
+        rank = dot(hit.astype(BF16), before)
+        mine = (lax.broadcasted_iota(jnp.int32, (slots, tokens), 0) % capacity).astype(F32)
+        place = jnp.where(rank == mine, hit, 0.0)
+        slot_weight[...] = jnp.sum(place * weight, axis=1, keepdims=True)
+        place_ref[...] = place.astype(BF16)
+
+    @pl.when(step < half)
+    def _():
+        wide_ref[...] = dot(place_ref[...], tokens_ref[...]).astype(BF16)
+
+    @pl.when(step >= half)
+    def _():
+        wide_ref[...] = (slot_weight[...] * dot(place_ref[...], grads_ref[...])).astype(BF16)
+
+
+def expert_kernel(rows_ref, grads_ref, gate_ref, up_ref, down_ref, hidden_ref, hidden_t_ref, gate_pre_ref, up_pre_ref):
+    rows = rows_ref[...]
+    pre_gate = dot(rows, gate_ref[...])
+    pre_up = dot(rows, up_ref[...])
+    hidden_grad = dot(grads_ref[...], down_ref[...], LAST)
+    sig = jax.nn.sigmoid(pre_gate)
+    silu = pre_gate * sig
+    hidden = (silu * pre_up).astype(BF16)
+    hidden_ref[...] = hidden
+    hidden_t_ref[...] = hidden.T
+    gate_pre_ref[...] = (hidden_grad * pre_up * sig * (1.0 + pre_gate * (1.0 - sig))).astype(BF16)
+    up_pre_ref[...] = (hidden_grad * silu).astype(BF16)
+
+
+def chunk_sums(rows_a, rows_b, grads_b, gate_pre, up_pre, hidden_t, held_a=(), held_b=()):
+    width = rows_a.shape[1]
     blocks = gate_pre.shape[1] // width
-    me = me_ref[0]
-
-    def columns(step, first=0):
-        return pl.ds(pl.multiple_of(first + lax.rem(me + step, groups) * width, width), width)
-
-    turned_a = wide[:, columns(step_a)].T
+    turned_a, turned_b, grads = rows_a[...].T, rows_b[...].T, grads_b[...]
     for j in range(blocks + 1):
         source = gate_pre[:, j * width : (j + 1) * width] if j < blocks else up_pre[:, :width]
         total = dot(turned_a, source)
         for held in held_a:
             total = total + held[j].astype(F32)
         yield "a", j, total
-    turned_b = turned_a if step_a == step_b else wide[:, columns(step_b)].T
-    grads_b = wide[:, columns(step_b, model)]
     for j in range(2 * blocks - 1):
         if j < blocks - 1:
             total = dot(turned_b, up_pre[:, (j + 1) * width : (j + 2) * width])
         else:
             i = j - blocks + 1
-            total = dot(hidden_t[i * width : (i + 1) * width, :], grads_b)
+            total = dot(hidden_t[i * width : (i + 1) * width, :], grads)
         for held in held_b:
             total = total + held[j].astype(F32)
         yield "b", j, total
 
 
-def link_kernel(step_a, step_b, groups, arrived, me_ref, *refs):
-    held = [[refs[4]], [refs[5]]] if arrived else []
+def link_kernel(arrived, _, *refs):
+    held = [[refs[6]], [refs[7]]] if arrived else []
     out = {"a": refs[-2], "b": refs[-1]}
-    for part, j, total in chunk_sums(step_a, step_b, groups, me_ref, *refs[:4], *held):
+    for part, j, total in chunk_sums(*refs[:6], *held):
         out[part][j] = total.astype(out[part].dtype)
 
 
@@ -185,12 +182,20 @@
 
     resident = pl.BlockSpec(memory_space=pltpu.VMEM)
     anywhere = pl.BlockSpec(memory_space=pl.ANY)
+    half = model // 2
     send, place = pl.pallas_call(
         functools.partial(dispatch_kernel, capacity),
-        in_specs=[resident] * 4,
-        out_specs=[resident] * 2,
+        grid=(4,),
+        in_specs=[
+            whole((top, count)),
+            whole((top, count)),
+            pl.BlockSpec((count, half), lambda i: (0, jnp.minimum(i, 1))),
+            pl.BlockSpec((count, half), lambda i: (0, jnp.maximum(i - 2, 0))),
+        ],
+        out_specs=[pl.BlockSpec((slots, half), lambda i: (0, i)), whole((slots, count))],
         out_shape=(shape((slots, 2 * model)), shape((slots, count))),
-        compiler_params=params(),
+        scratch_shapes=[pltpu.VMEM((slots, 1), F32)],
+        compiler_params=params(58),
         cost_estimate=cost(4 * slots * count * model, 4 * slots * model),
         name="dispatch",
     )(routes_t, gates_t, tokens, out_grad)
@@ -200,15 +205,23 @@
         return lax.all_to_all(wide, "expert", 0, 0, tiled=True).reshape(array.shape)
 
     wide = exchange(send)
+    tile = pl.BlockSpec((slots, width), lambda i: (0, i))
     hidden, hidden_t, gate_pre, up_pre = pl.pallas_call(
-        functools.partial(expert_kernel, width),
-        in_specs=[resident] * 4,
-        out_specs=[resident] * 4,
+        expert_kernel,
+        grid=(blocks,),
+        in_specs=[
+            pl.BlockSpec((slots, model), lambda i: (0, 0)),
+            pl.BlockSpec((slots, model), lambda i: (0, 1)),
+            pl.BlockSpec((model, width), lambda i: (0, i)),
+            pl.BlockSpec((model, width), lambda i: (0, i)),
+            pl.BlockSpec((width, model), lambda i: (i, 0)),
+        ],
+        out_specs=[tile, pl.BlockSpec((width, slots), lambda i: (i, 0)), tile, tile],
         out_shape=(shape((slots, hid)), shape((hid, slots)), shape((slots, hid)), shape((slots, hid))),
-        compiler_params=params(),
+        compiler_params=params(54),
         cost_estimate=cost(6 * slots * model * hid, 4 * slots * model + 6 * model * hid + 8 * slots * hid),
         name="expert",
-    )(wide, w_gate, w_up, w_down)
+    )(wide, wide, w_gate, w_up, w_down)
 
     me = lax.axis_index("dp")
     place_of = me.reshape(1).astype(jnp.int32)
@@ -216,18 +229,24 @@
     def chain_call(step_a, step_b, dtype, held, name, after):
         parts = (shape((blocks + 1, width, width), dtype), shape((2 * blocks - 1, width, width), dtype))
         return pl.pallas_call(
-            functools.partial(link_kernel, step_a, step_b, groups, bool(held)),
-            in_specs=[
-                pl.BlockSpec(memory_space=pltpu.SMEM),
-                *[resident] * (4 + len(held)),
-                *[anywhere] * len(after),
-            ],
-            out_specs=[resident, resident],
+            functools.partial(link_kernel, bool(held)),
+            grid_spec=pltpu.PrefetchScalarGridSpec(
+                num_scalar_prefetch=1,
+                grid=(1,),
+                in_specs=[
+                    pl.BlockSpec((slots, width), lambda i, p: (0, lax.rem(p[0] + step_a, groups))),
+                    pl.BlockSpec((slots, width), lambda i, p: (0, lax.rem(p[0] + step_b, groups))),
+                    pl.BlockSpec((slots, width), lambda i, p: (0, groups + lax.rem(p[0] + step_b, groups))),
+                    *[resident] * (3 + len(held)),
+                    *[anywhere] * len(after),
+                ],
+                out_specs=[resident, resident],
+            ),
             out_shape=parts,
             compiler_params=params(),
             cost_estimate=LONG,
             name=name,
-        )(place_of, wide, gate_pre, up_pre, hidden_t, *held, *after)
+        )(place_of, wide, wide, wide, gate_pre, up_pre, hidden_t, *held, *after)
 
     up_ring = [(i, (i + 1) % groups) for i in range(groups)]
     down_ring = [(i, (i - 1) % groups) for i in range(groups)]
@@ -258,7 +277,6 @@
 
     back = exchange(going_back)
 
-    half = model // 2
     layer_out, token_grad, gates_grad_t = pl.pallas_call(
         functools.partial(combine_kernel, capacity),
         grid=(2,),

time: 183 us -> 181 us (0.989)
  waiting for transfers between devices: 79.6 us -> 84.2 us
  local copies, waits for them, and re-layouts: 12.1 us -> 7.53 us
  Pallas kernels: 50.4 us -> 46.5 us
  starting transfers between devices: 39.2 us -> 41.1 us
    unnamed x46 -> x34, local copies, waits for them, and re-layouts: 12.1 us -> 7.53 us
    ppermute x7, waiting for transfers between devices: 20.7 us -> 25.2 us  [local(): lax.ppermute(part_a, 'dp', ring_a)]
    pallas_call x10, Pallas kernels: 38.7 us -> 34.8 us  [the longest x8 19 us: chain_call(): pl.pallas_call(functools.partial(link_kernel, bool(held)), grid_spec=pltp...]
  transfers between devices with their start and end apart: 16 -> 16, of which waited for: 10 -> 10; matrix products, arithmetic and copies ran while one was open for 0% -> 0% of each run, Pallas kernels for 19% -> 15%
where the time goes in v4:
time: 181 us; the launch traced here: 180 us
  waiting for transfers between devices  84.2 us (47%)
  Pallas kernels  46.5 us (26%)
  starting transfers between devices  41.1 us (23%)
  local copies, waits for them, and re-layouts  7.53 us (4%)
    all_to_all x2, waiting for transfers between devices, exchange(): return lax.all_to_all(wide, 'expert', 0, 0, tiled=True).reshape(array.shape)  51.4 us
    ppermute x7, waiting for transfers between devices, local(): lax.ppermute(part_a, 'dp', ring_a)  25.2 us
    pallas_call x8, Pallas kernels, chain_call(): pl.pallas_call(functools.partial(link_kernel, bool(held)), grid_spec=pltp...  19 us
    all_to_all x2, starting transfers between devices, exchange(): return lax.all_to_all(wide, 'expert', 0, 0, tiled=True).reshape(array.shape)  14.7 us
    ppermute x7, starting transfers between devices, local(): lax.ppermute(part_a, 'dp', ring_a)  14.1 us
    ppermute x7, starting transfers between devices, local(): lax.ppermute(part_b, 'dp', ring_b)  12.3 us
    pallas_call x1, Pallas kernels, local(): pl.pallas_call(expert_kernel, grid=(blocks,), in_specs=[pl.BlockSpec((slo...  10.5 us
    ppermute x7, waiting for transfers between devices, local(): lax.ppermute(part_b, 'dp', ring_b)  7.69 us
  transfers between devices with their start and end apart: 16, of which 10 were waited for; matrix products, arithmetic and copies ran while one was open for 0% of the time, Pallas kernels for 15%

profile of v4, /device:TPU:2, one launch (start us, length us, event | category | flops | bytes accessed | tf_op | source)
XLA Modules:
  0.0 180.2 jit_solution(552287114377618182)
XLA Ops:
  0.6 5.4 %dispatch.1 = (bf16[512,4096]{1,0:T(8,128)(2,1)}, bf16[512,48]{1,0:T(8,128)(2,1)}) custom-call(s32[8,48]{1,0:T(8,128)} %bitcast.21, f32[8,48]{1,0:T(8,128)} %bitcast.23, bf16[48,2048]{1,0:T(8,128)(2,1)} %tokens_ref.1, bf16[48,2048]{1,0:T(8,128)(2,1)} %grads_ref.3), custom_call_target="tpu_custom_call" | custom-call | flops 201326592 | bytes 4194304 | tf_op jit(solution)/shard_map/dispatch/pallas_call | solution.py:186
  6.0 7.7 %all-to-all-start = ((bf16[32,16,4096]{2,1,0:T(8,128)(2,1)}), bf16[32,16,4096]{2,1,0:T(8,128)(2,1)}, u32[]{:S(2)}, u32[]{:S(2)}) async-start(bf16[32,16,4096]{2,1,0:T(8,128)(2,1)} %bitcast.25), calls=%async_computation | async-start | bytes 8388608 | tf_op jit(solution)/shard_map/all_to_all | solution.py:205
  13.7 51.4 %all-to-all-done = bf16[32,16,4096]{2,1,0:T(8,128)(2,1)} async-done(((bf16[32,16,4096]{2,1,0:T(8,128)(2,1)}), bf16[32,16,4096]{2,1,0:T(8,128)(2,1)}, u32[]{:S(2)}, u32[]{:S(2)}) %all-to-all-start) | async-done | bytes 4194336 | tf_op jit(solution)/shard_map/all_to_all | solution.py:205
  65.1 10.5 %expert.1 = (bf16[512,768]{1,0:T(8,128)(2,1)}, bf16[768,512]{1,0:T(8,128)(2,1)}, bf16[512,768]{1,0:T(8,128)(2,1)}, bf16[512,768]{1,0:T(8,128)(2,1)}) custom-call(bf16[512,4096]{1,0:T(8,128)(2,1)} %bitcast.3.rows_ref.grads_ref.refs_0_.refs_1_.refs_2_, bf16[512,4096]{1,0:T(8,128)(2,1)} %bitcast.3.rows_ref.grads_ref.refs_0_.refs_1_.refs_2_, ...), custom_call_target="tpu_custom_call" | custom-call | flops 4831838208 | bytes 16777216 | tf_op jit(solution)/shard_map/expert/pallas_call | solution.py:209
  75.5 1.1 copy-done.4
  76.6 1.1 copy-done.6
  77.8 1.1 copy-done.14
  78.9 2.8 %chain_sum_0.1 = (bf16[4,256,256]{2,1,0:T(8,128)(2,1)}, bf16[5,256,256]{2,1,0:T(8,128)(2,1)}) custom-call(s32[1]{0:T(128)} %bitcast.7._, bf16[512,4096]{1,0:T(8,128)(2,1)} %bitcast.3.rows_ref.grads_ref.refs_0_.refs_1_.refs_2_, bf16[512,4096]{1,0:T(8,128)(2,1)} %bitcast.3.rows_ref.grads_ref.refs_0_.refs_1_.refs_2_, ...), custom_call_target="tpu_custom_call" | custom-call | flops 20000000000 | bytes 62914560 | tf_op jit(solution)/shard_map/chain_sum_0/pallas_call | solution.py:231
  81.7 1.9 %collective-permute-start.2 = (bf16[4,256,256]{2,1,0:T(8,128)(2,1)}, bf16[4,256,256]{2,1,0:T(8,128)(2,1)}, u32[]{:S(2)}, u32[]{:S(2)}) collective-permute-start(bf16[4,256,256]{2,1,0:T(8,128)(2,1)} %get-tuple-element.42.refs_6_), channel_id=1, source_target_pairs={{0,1},{1,2},{2,3},{3,4},{4,5},{5,6},{6,7},{7,0},{8,9},{9,10},{10,1... | collective-permute-start | bytes 1572872 | tf_op jit(solution)/shard_map/ppermute | solution.py:276
  83.6 4.1 %collective-permute-start.3 = (bf16[5,256,256]{2,1,0:T(8,128)(2,1)}, bf16[5,256,256]{2,1,0:T(8,128)(2,1)}, u32[]{:S(2)}, u32[]{:S(2)}) collective-permute-start(bf16[5,256,256]{2,1,0:T(8,128)(2,1)} %get-tuple-element.49), channel_id=1, source_target_pairs={{0,7},{1,0},{2,1},{3,2},{4,3},{5,4},{6,5},{7,6},{8,15},{9,8},{10,9... | collective-permute-start | bytes 1966088 | tf_op jit(solution)/shard_map/ppermute | solution.py:276
  87.7 1.9 %chain_sum_1.1 = (bf16[4,256,256]{2,1,0:T(8,128)(2,1)S(1)}, bf16[5,256,256]{2,1,0:T(8,128)(2,1)S(1)}) custom-call(s32[1]{0:T(128)} %bitcast.7._, bf16[512,4096]{1,0:T(8,128)(2,1)} %bitcast.3.rows_ref.grads_ref.refs_0_.refs_1_.refs_2_, bf16[512,4096]{1,0:T(8,128)(2,1)} %bitcast.3.rows_ref.grads_ref.refs_0_.refs_1_.refs_2_, ...), custom_call_target="tpu_custom_call" | custom-call | flops 20000000000 | bytes 62914560 | tf_op jit(solution)/shard_map/chain_sum_1/pallas_call | solution.py:231
  89.6 2.9 %collective-permute-start = (bf16[4,256,256]{2,1,0:T(8,128)(2,1)S(1)}, bf16[4,256,256]{2,1,0:T(8,128)(2,1)}, u32[]{:S(2)}, u32[]{:S(2)}) collective-permute-start(bf16[4,256,256]{2,1,0:T(8,128)(2,1)S(1)} %get-tuple-element.43._), channel_id=1, source_target_pairs={{0,7},{1,0},{2,1},{3,2},{4,3},{5,4},{6,5},{7,6},{8,15},{9,8},{10,9... | collective-permute-start | bytes 1572872 | tf_op jit(solution)/shard_map/ppermute | solution.py:276
  92.5 0.0 collective-permute-start.1
  92.5 0.0 copy-done.1
  92.5 0.0 copy-done.2
  92.5 0.0 copy-done.3
  92.5 0.0 copy-done.8
  92.5 5.0 %rows_back.1 = (bf16[512,4096]{1,0:T(8,128)(2,1)S(1)}, f32[8,128]{1,0:T(8,128)S(1)}) custom-call(bf16[512,768]{1,0:T(8,128)(2,1)S(1)} %copy-done.8, bf16[512,768]{1,0:T(8,128)(2,1)S(1)} %copy-done.4, bf16[512,768]{1,0:T(8,128)(2,1)S(1)} %copy-done.6, bf16[768,2048]{1,0:T(8,128)(2,1)S(1)} %bitcast.20, bf16[2048,768]{1,0:T(8,128)(2,1)S(1)} %bitcast.16, ...), custom_call_target="tpu_custom_call" | custom-call | flops 1 | bytes 1 | tf_op jit(solution)/shard_map/rows_back/pallas_call | solution.py:256
  97.6 0.0 copy-start
  97.6 2.0 %copy-done = bf16[512,4096]{1,0:T(8,128)(2,1)} copy-done((bf16[512,4096]{1,0:T(8,128)(2,1)}, bf16[512,4096]{1,0:T(8,128)(2,1)S(1)}, u32[]{:S(2)}) %copy-start) | copy-done | bytes 4194328
  99.6 7.0 %all-to-all-start.1 = ((bf16[32,16,4096]{2,1,0:T(8,128)(2,1)}), bf16[32,16,4096]{2,1,0:T(8,128)(2,1)}, u32[]{:S(2)}, u32[]{:S(2)}) async-start(bf16[32,16,4096]{2,1,0:T(8,128)(2,1)} %bitcast.14), calls=%async_computation.1 | async-start | bytes 8388608 | tf_op jit(solution)/shard_map/all_to_all | solution.py:205
  106.6 0.0 collective-permute-done.2.refs_6_
  106.6 0.0 collective-permute-done.3.refs_7_
  106.6 0.0 copy-done.5
  106.6 0.0 copy-done.7
  106.6 0.0 copy-start.15
  106.6 1.1 copy-done.15
  107.8 2.3 %chain_sum_2.1 = (bf16[4,256,256]{2,1,0:T(8,128)(2,1)S(1)}, bf16[5,256,256]{2,1,0:T(8,128)(2,1)S(1)}) custom-call(s32[1]{0:T(128)} %bitcast.7._, bf16[512,4096]{1,0:T(8,128)(2,1)} %bitcast.3.rows_ref.grads_ref.refs_0_.refs_1_.refs_2_, bf16[512,4096]{1,0:T(8,128)(2,1)} %bitcast.3.rows_ref.grads_ref.refs_0_.refs_1_.refs_2_, ...), custom_call_target="tpu_custom_call" | custom-call | flops 20000000000 | bytes 62914560 | tf_op jit(solution)/shard_map/chain_sum_2/pallas_call | solution.py:231
  110.1 0.3 collective-permute-start.6
  110.4 3.3 %collective-permute-start.7 = (bf16[5,256,256]{2,1,0:T(8,128)(2,1)S(1)}, bf16[5,256,256]{2,1,0:T(8,128)(2,1)S(1)}, u32[]{:S(2)}, u32[]{:S(2)}) collective-permute-start(bf16[5,256,256]{2,1,0:T(8,128)(2,1)S(1)} %get-tuple-element.54), channel_id=1, source_target_pairs={{0,7},{1,0},{2,1},{3,2},{4,3},{5,4},{6,5},{7,6},{8,15},{9,8},{10,9... | collective-permute-start | bytes 1966088 | tf_op jit(solution)/shard_map/ppermute | solution.py:276
  113.7 0.0 collective-permute-done.refs_6_
  113.7 0.0 collective-permute-done.1.refs_7_
  113.7 2.1 %chain_sum_3.1 = (bf16[4,256,256]{2,1,0:T(8,128)(2,1)S(1)}, bf16[5,256,256]{2,1,0:T(8,128)(2,1)S(1)}) custom-call(s32[1]{0:T(128)} %bitcast.7._, bf16[512,4096]{1,0:T(8,128)(2,1)} %bitcast.3.rows_ref.grads_ref.refs_0_.refs_1_.refs_2_, bf16[512,4096]{1,0:T(8,128)(2,1)} %bitcast.3.rows_ref.grads_ref.refs_0_.refs_1_.refs_2_, ...), custom_call_target="tpu_custom_call" | custom-call | flops 20000000000 | bytes 62914560 | tf_op jit(solution)/shard_map/chain_sum_3/pallas_call | solution.py:231
  115.8 3.1 %collective-permute-start.4 = (bf16[4,256,256]{2,1,0:T(8,128)(2,1)S(1)}, bf16[4,256,256]{2,1,0:T(8,128)(2,1)S(1)}, u32[]{:S(2)}, u32[]{:S(2)}) collective-permute-start(bf16[4,256,256]{2,1,0:T(8,128)(2,1)S(1)} %get-tuple-element.52.refs_8_), channel_id=1, source_target_pairs={{0,7},{1,0},{2,1},{3,2},{4,3},{5,4},{6,5},{7,6},{8,15},{9,8},{10,9... | collective-permute-start | bytes 1572872 | tf_op jit(solution)/shard_map/ppermute | solution.py:276
  118.8 0.0 collective-permute-start.5
  118.8 7.5 %collective-permute-done.6.refs_6_ = bf16[4,256,256]{2,1,0:T(8,128)(2,1)S(1)} collective-permute-done((bf16[4,256,256]{2,1,0:T(8,128)(2,1)S(1)}, bf16[4,256,256]{2,1,0:T(8,128)(2,1)S(1)}, u32[]{:S(2)}, u32[]{:S(2)}) %collective-permute-start.6) | collective-permute-done | bytes 524320 | tf_op jit(solution)/shard_map/ppermute | solution.py:276
  126.3 2.5 %collective-permute-done.7.refs_7_ = bf16[5,256,256]{2,1,0:T(8,128)(2,1)S(1)} collective-permute-done((bf16[5,256,256]{2,1,0:T(8,128)(2,1)S(1)}, bf16[5,256,256]{2,1,0:T(8,128)(2,1)S(1)}, u32[]{:S(2)}, u32[]{:S(2)}) %collective-permute-start.7) | collective-permute-done | bytes 655392 | tf_op jit(solution)/shard_map/ppermute | solution.py:276
  128.8 1.9 %chain_sum_4.1 = (bf16[4,256,256]{2,1,0:T(8,128)(2,1)S(1)}, bf16[5,256,256]{2,1,0:T(8,128)(2,1)S(1)}) custom-call(s32[1]{0:T(128)} %bitcast.7._, bf16[512,4096]{1,0:T(8,128)(2,1)} %bitcast.3.rows_ref.grads_ref.refs_0_.refs_1_.refs_2_, bf16[512,4096]{1,0:T(8,128)(2,1)} %bitcast.3.rows_ref.grads_ref.refs_0_.refs_1_.refs_2_, ...), custom_call_target="tpu_custom_call" | custom-call | flops 20000000000 | bytes 62914560 | tf_op jit(solution)/shard_map/chain_sum_4/pallas_call | solution.py:231
  130.7 1.4 collective-permute-start.10
  132.1 2.5 %collective-permute-start.11 = (bf16[5,256,256]{2,1,0:T(8,128)(2,1)S(1)}, bf16[5,256,256]{2,1,0:T(8,128)(2,1)S(1)}, u32[]{:S(2)}, u32[]{:S(2)}) collective-permute-start(bf16[5,256,256]{2,1,0:T(8,128)(2,1)S(1)} %get-tuple-element.58), channel_id=1, source_target_pairs={{0,7},{1,0},{2,1},{3,2},{4,3},{5,4},{6,5},{7,6},{8,15},{9,8},{10,9... | collective-permute-start | bytes 1966088 | tf_op jit(solution)/shard_map/ppermute | solution.py:276
  134.6 5.4 %collective-permute-done.4.refs_6_ = bf16[4,256,256]{2,1,0:T(8,128)(2,1)S(1)} collective-permute-done((bf16[4,256,256]{2,1,0:T(8,128)(2,1)S(1)}, bf16[4,256,256]{2,1,0:T(8,128)(2,1)S(1)}, u32[]{:S(2)}, u32[]{:S(2)}) %collective-permute-start.4) | collective-permute-done | bytes 524320 | tf_op jit(solution)/shard_map/ppermute | solution.py:276
  140.0 0.3 collective-permute-done.5.refs_7_
  140.3 2.8 %chain_sum_5.1 = (bf16[4,256,256]{2,1,0:T(8,128)(2,1)}, bf16[5,256,256]{2,1,0:T(8,128)(2,1)}) custom-call(s32[1]{0:T(128)} %bitcast.7._, bf16[512,4096]{1,0:T(8,128)(2,1)} %bitcast.3.rows_ref.grads_ref.refs_0_.refs_1_.refs_2_, bf16[512,4096]{1,0:T(8,128)(2,1)} %bitcast.3.rows_ref.grads_ref.refs_0_.refs_1_.refs_2_, ...), custom_call_target="tpu_custom_call" | custom-call | flops 20000000000 | bytes 62914560 | tf_op jit(solution)/shard_map/chain_sum_5/pallas_call | solution.py:231
  143.2 3.3 %collective-permute-start.8 = (bf16[4,256,256]{2,1,0:T(8,128)(2,1)}, bf16[4,256,256]{2,1,0:T(8,128)(2,1)}, u32[]{:S(2)}, u32[]{:S(2)}) collective-permute-start(bf16[4,256,256]{2,1,0:T(8,128)(2,1)} %get-tuple-element.56.refs_8_), channel_id=1, source_target_pairs={{0,7},{1,0},{2,1},{3,2},{4,3},{5,4},{6,5},{7,6},{8,15},{9,8},{10,9... | collective-permute-start | bytes 1572872 | tf_op jit(solution)/shard_map/ppermute | solution.py:276
  146.5 0.1 collective-permute-start.9
  146.6 5.0 %collective-permute-done.10.refs_6_ = bf16[4,256,256]{2,1,0:T(8,128)(2,1)S(1)} collective-permute-done((bf16[4,256,256]{2,1,0:T(8,128)(2,1)S(1)}, bf16[4,256,256]{2,1,0:T(8,128)(2,1)S(1)}, u32[]{:S(2)}, u32[]{:S(2)}) %collective-permute-start.10) | collective-permute-done | bytes 524320 | tf_op jit(solution)/shard_map/ppermute | solution.py:276
  151.6 2.5 %collective-permute-done.11.refs_7_ = bf16[5,256,256]{2,1,0:T(8,128)(2,1)S(1)} collective-permute-done((bf16[5,256,256]{2,1,0:T(8,128)(2,1)S(1)}, bf16[5,256,256]{2,1,0:T(8,128)(2,1)S(1)}, u32[]{:S(2)}, u32[]{:S(2)}) %collective-permute-start.11) | collective-permute-done | bytes 655392 | tf_op jit(solution)/shard_map/ppermute | solution.py:276
  154.0 2.8 %chain_sum_6.1 = (bf16[4,256,256]{2,1,0:T(8,128)(2,1)}, bf16[5,256,256]{2,1,0:T(8,128)(2,1)}) custom-call(s32[1]{0:T(128)} %bitcast.7._, bf16[512,4096]{1,0:T(8,128)(2,1)} %bitcast.3.rows_ref.grads_ref.refs_0_.refs_1_.refs_2_, bf16[512,4096]{1,0:T(8,128)(2,1)} %bitcast.3.rows_ref.grads_ref.refs_0_.refs_1_.refs_2_, ...), custom_call_target="tpu_custom_call" | custom-call | flops 20000000000 | bytes 62914560 | tf_op jit(solution)/shard_map/chain_sum_6/pallas_call | solution.py:231
  156.8 1.3 collective-permute-start.12
  158.2 2.4 %collective-permute-start.13 = (bf16[5,256,256]{2,1,0:T(8,128)(2,1)}, bf16[5,256,256]{2,1,0:T(8,128)(2,1)S(1)}, u32[]{:S(2)}, u32[]{:S(2)}) collective-permute-start(bf16[5,256,256]{2,1,0:T(8,128)(2,1)} %get-tuple-element.62), channel_id=1, source_target_pairs={{0,7},{1,0},{2,1},{3,2},{4,3},{5,4},{6,5},{7,6},{8,15},{9,8},{10,9... | collective-permute-start | bytes 1966088 | tf_op jit(solution)/shard_map/ppermute | solution.py:276
  160.5 0.0 all-to-all-done.1
  160.5 0.0 copy-done.9
  160.5 0.0 copy-done.10
  160.5 0.0 copy-done.11
  160.6 0.0 copy-start.16
  160.6 5.1 %combine.1 = (bf16[48,2048]{1,0:T(8,128)(2,1)}, bf16[48,2048]{1,0:T(8,128)(2,1)}, f32[8,48]{1,0:T(8,128)}) custom-call(s32[8,48]{1,0:T(8,128)S(1)} %bitcast.22, f32[8,48]{1,0:T(8,128)S(1)} %bitcast.24, bf16[512,48]{1,0:T(8,128)(2,1)S(1)} %copy-done.10, bf16[48,2048]{1,0:T(8,128)(2,1)S(1)} %copy-done.9, bf16[512,4096]{1,0:T(8,128)(2,1)} %bitcast.9.back_ref.back_grad_ref, ...), custom_call_target="tpu_custom_call" | custom-call | flops 402653184 | bytes 4194304 | tf_op jit(solution)/shard_map/combine/pallas_call | solution.py:280
  165.6 0.0 collective-permute-done.8.refs_6_
  165.6 0.2 collective-permute-done.9.refs_7_
  165.8 0.0 copy-done.16
  165.8 0.9 copy-done.13
  166.7 2.3 %chain_sum_own.1 = (f32[4,256,256]{2,1,0:T(8,128)S(1)}, f32[5,256,256]{2,1,0:T(8,128)S(1)}) custom-call(s32[1]{0:T(128)} %bitcast.7._, bf16[512,4096]{1,0:T(8,128)(2,1)} %bitcast.3.rows_ref.grads_ref.refs_0_.refs_1_.refs_2_, bf16[512,4096]{1,0:T(8,128)(2,1)} %bitcast.3.rows_ref.grads_ref.refs_0_.refs_1_.refs_2_, ...), custom_call_target="tpu_custom_call" | custom-call | flops 20000000000 | bytes 62914560 | tf_op jit(solution)/shard_map/chain_sum_own/pallas_call | solution.py:231
  169.1 7.3 %collective-permute-done.12.a0 = bf16[4,256,256]{2,1,0:T(8,128)(2,1)S(1)} collective-permute-done((bf16[4,256,256]{2,1,0:T(8,128)(2,1)}, bf16[4,256,256]{2,1,0:T(8,128)(2,1)S(1)}, u32[]{:S(2)}, u32[]{:S(2)}) %collective-permute-start.12) | collective-permute-done | bytes 524320 | tf_op jit(solution)/shard_map/ppermute | solution.py:276
  176.4 2.3 %collective-permute-done.13.b0 = bf16[5,256,256]{2,1,0:T(8,128)(2,1)S(1)} collective-permute-done((bf16[5,256,256]{2,1,0:T(8,128)(2,1)}, bf16[5,256,256]{2,1,0:T(8,128)(2,1)S(1)}, u32[]{:S(2)}, u32[]{:S(2)}) %collective-permute-start.13) | collective-permute-done | bytes 655392 | tf_op jit(solution)/shard_map/ppermute | solution.py:276
  178.6 1.6 chain_sum_last.1
  (15 shorter events, 0.0 us)
Async XLA Ops:
  6.0 59.1 %all-to-all-start = ((bf16[32,16,4096]{2,1,0:T(8,128)(2,1)}), bf16[32,16,4096]{2,1,0:T(8,128)(2,1)}, u32[]{:S(2)}, u32[]{:S(2)}) async-start(bf16[32,16,4096]{2,1,0:T(8,128)(2,1)} %bitcast.25), calls=%async_computation | async-start | bytes 8388608 | tf_op jit(solution)/shard_map/all_to_all | solution.py:205
  75.5 1.1 copy-start.4
  76.6 1.1 copy-start.6
  77.8 1.1 copy-start.14
  81.7 24.9 %collective-permute-start.2 = (bf16[4,256,256]{2,1,0:T(8,128)(2,1)}, bf16[4,256,256]{2,1,0:T(8,128)(2,1)}, u32[]{:S(2)}, u32[]{:S(2)}) collective-permute-start(bf16[4,256,256]{2,1,0:T(8,128)(2,1)} %get-tuple-element.42.refs_6_), channel_id=1, source_target_pairs={{0,1},{1,2},{2,3},{3,4},{4,5},{5,6},{6,7},{7,0},{8,9},{9,10},{10,1... | collective-permute-start | bytes 1572872 | tf_op jit(solution)/shard_map/ppermute | solution.py:276
  83.6 8.9 %copy-start.1 = (bf16[1,2048,768]{2,1,0:T(8,128)(2,1)S(1)}, bf16[1,2048,768]{2,1,0:T(8,128)(2,1)}, u32[]{:S(2)}) copy-start(bf16[1,2048,768]{2,1,0:T(8,128)(2,1)} %param.10) | copy-start | bytes 9437188
  83.6 8.9 %copy-start.2 = (bf16[1,2048,768]{2,1,0:T(8,128)(2,1)S(1)}, bf16[1,2048,768]{2,1,0:T(8,128)(2,1)}, u32[]{:S(2)}) copy-start(bf16[1,2048,768]{2,1,0:T(8,128)(2,1)} %param.11) | copy-start | bytes 9437188
  83.6 8.9 %copy-start.3 = (bf16[1,768,2048]{2,1,0:T(8,128)(2,1)S(1)}, bf16[1,768,2048]{2,1,0:T(8,128)(2,1)}, u32[]{:S(2)}) copy-start(bf16[1,768,2048]{2,1,0:T(8,128)(2,1)} %param.12) | copy-start | bytes 9437188
  83.6 8.9 %copy-start.8 = (bf16[512,768]{1,0:T(8,128)(2,1)S(1)}, bf16[512,768]{1,0:T(8,128)(2,1)}, u32[]{:S(2)}) copy-start(bf16[512,768]{1,0:T(8,128)(2,1)} %get-tuple-element.38.hidden_ref) | copy-start | bytes 2359300
  83.6 23.0 %collective-permute-start.3 = (bf16[5,256,256]{2,1,0:T(8,128)(2,1)}, bf16[5,256,256]{2,1,0:T(8,128)(2,1)}, u32[]{:S(2)}, u32[]{:S(2)}) collective-permute-start(bf16[5,256,256]{2,1,0:T(8,128)(2,1)} %get-tuple-element.49), channel_id=1, source_target_pairs={{0,7},{1,0},{2,1},{3,2},{4,3},{5,4},{6,5},{7,6},{8,15},{9,8},{10,9... | collective-permute-start | bytes 1966088 | tf_op jit(solution)/shard_map/ppermute | solution.py:276
  89.6 24.0 %collective-permute-start = (bf16[4,256,256]{2,1,0:T(8,128)(2,1)S(1)}, bf16[4,256,256]{2,1,0:T(8,128)(2,1)}, u32[]{:S(2)}, u32[]{:S(2)}) collective-permute-start(bf16[4,256,256]{2,1,0:T(8,128)(2,1)S(1)} %get-tuple-element.43._), channel_id=1, source_target_pairs={{0,7},{1,0},{2,1},{3,2},{4,3},{5,4},{6,5},{7,6},{8,15},{9,8},{10,9... | collective-permute-start | bytes 1572872 | tf_op jit(solution)/shard_map/ppermute | solution.py:276
  92.5 21.2 %collective-permute-start.1 = (bf16[5,256,256]{2,1,0:T(8,128)(2,1)S(1)}, bf16[5,256,256]{2,1,0:T(8,128)(2,1)S(1)}, u32[]{:S(2)}, u32[]{:S(2)}) collective-permute-start(bf16[5,256,256]{2,1,0:T(8,128)(2,1)S(1)} %get-tuple-element.48), channel_id=1, source_target_pairs={{0,1},{1,2},{2,3},{3,4},{4,5},{5,6},{6,7},{7,0},{8,9},{9,10},{10,1... | collective-permute-start | bytes 1966088 | tf_op jit(solution)/shard_map/ppermute | solution.py:276
  97.6 2.0 %copy-start = (bf16[512,4096]{1,0:T(8,128)(2,1)}, bf16[512,4096]{1,0:T(8,128)(2,1)S(1)}, u32[]{:S(2)}) copy-start(bf16[512,4096]{1,0:T(8,128)(2,1)S(1)} %get-tuple-element.44) | copy-start | bytes 12582916
  99.6 7.0 %copy-start.5 = (bf16[512,768]{1,0:T(8,128)(2,1)S(1)}, bf16[512,768]{1,0:T(8,128)(2,1)}, u32[]{:S(2)}) copy-start(bf16[512,768]{1,0:T(8,128)(2,1)} %get-tuple-element.39.refs_3_.gate_pre_ref) | copy-start | bytes 2359300
  99.6 7.0 %copy-start.7 = (bf16[512,768]{1,0:T(8,128)(2,1)S(1)}, bf16[512,768]{1,0:T(8,128)(2,1)}, u32[]{:S(2)}) copy-start(bf16[512,768]{1,0:T(8,128)(2,1)} %get-tuple-element.40.refs_4_.up_pre_ref) | copy-start | bytes 2359300
  99.6 60.9 %all-to-all-start.1 = ((bf16[32,16,4096]{2,1,0:T(8,128)(2,1)}), bf16[32,16,4096]{2,1,0:T(8,128)(2,1)}, u32[]{:S(2)}, u32[]{:S(2)}) async-start(bf16[32,16,4096]{2,1,0:T(8,128)(2,1)} %bitcast.14), calls=%async_computation.1 | async-start | bytes 8388608 | tf_op jit(solution)/shard_map/all_to_all | solution.py:205
  106.6 1.1 copy-start.15
  110.1 16.2 %collective-permute-start.6 = (bf16[4,256,256]{2,1,0:T(8,128)(2,1)S(1)}, bf16[4,256,256]{2,1,0:T(8,128)(2,1)S(1)}, u32[]{:S(2)}, u32[]{:S(2)}) collective-permute-start(bf16[4,256,256]{2,1,0:T(8,128)(2,1)S(1)} %get-tuple-element.51.refs_8_), channel_id=1, source_target_pairs={{0,1},{1,2},{2,3},{3,4},{4,5},{5,6},{6,7},{7,0},{8,9},{9,10},{10,1... | collective-permute-start | bytes 1572872 | tf_op jit(solution)/shard_map/ppermute | solution.py:276
  110.4 18.4 %collective-permute-start.7 = (bf16[5,256,256]{2,1,0:T(8,128)(2,1)S(1)}, bf16[5,256,256]{2,1,0:T(8,128)(2,1)S(1)}, u32[]{:S(2)}, u32[]{:S(2)}) collective-permute-start(bf16[5,256,256]{2,1,0:T(8,128)(2,1)S(1)} %get-tuple-element.54), channel_id=1, source_target_pairs={{0,7},{1,0},{2,1},{3,2},{4,3},{5,4},{6,5},{7,6},{8,15},{9,8},{10,9... | collective-permute-start | bytes 1966088 | tf_op jit(solution)/shard_map/ppermute | solution.py:276
  115.8 24.2 %collective-permute-start.4 = (bf16[4,256,256]{2,1,0:T(8,128)(2,1)S(1)}, bf16[4,256,256]{2,1,0:T(8,128)(2,1)S(1)}, u32[]{:S(2)}, u32[]{:S(2)}) collective-permute-start(bf16[4,256,256]{2,1,0:T(8,128)(2,1)S(1)} %get-tuple-element.52.refs_8_), channel_id=1, source_target_pairs={{0,7},{1,0},{2,1},{3,2},{4,3},{5,4},{6,5},{7,6},{8,15},{9,8},{10,9... | collective-permute-start | bytes 1572872 | tf_op jit(solution)/shard_map/ppermute | solution.py:276
  118.8 21.5 %collective-permute-start.5 = (bf16[5,256,256]{2,1,0:T(8,128)(2,1)S(1)}, bf16[5,256,256]{2,1,0:T(8,128)(2,1)S(1)}, u32[]{:S(2)}, u32[]{:S(2)}) collective-permute-start(bf16[5,256,256]{2,1,0:T(8,128)(2,1)S(1)} %get-tuple-element.53), channel_id=1, source_target_pairs={{0,1},{1,2},{2,3},{3,4},{4,5},{5,6},{6,7},{7,0},{8,9},{9,10},{10,1... | collective-permute-start | bytes 1966088 | tf_op jit(solution)/shard_map/ppermute | solution.py:276
  130.7 20.9 %collective-permute-start.10 = (bf16[4,256,256]{2,1,0:T(8,128)(2,1)S(1)}, bf16[4,256,256]{2,1,0:T(8,128)(2,1)S(1)}, u32[]{:S(2)}, u32[]{:S(2)}) collective-permute-start(bf16[4,256,256]{2,1,0:T(8,128)(2,1)S(1)} %get-tuple-element.55.refs_8_), channel_id=1, source_target_pairs={{0,1},{1,2},{2,3},{3,4},{4,5},{5,6},{6,7},{7,0},{8,9},{9,10},{10,1... | collective-permute-start | bytes 1572872 | tf_op jit(solution)/shard_map/ppermute | solution.py:276
  132.1 21.9 %collective-permute-start.11 = (bf16[5,256,256]{2,1,0:T(8,128)(2,1)S(1)}, bf16[5,256,256]{2,1,0:T(8,128)(2,1)S(1)}, u32[]{:S(2)}, u32[]{:S(2)}) collective-permute-start(bf16[5,256,256]{2,1,0:T(8,128)(2,1)S(1)} %get-tuple-element.58), channel_id=1, source_target_pairs={{0,7},{1,0},{2,1},{3,2},{4,3},{5,4},{6,5},{7,6},{8,15},{9,8},{10,9... | collective-permute-start | bytes 1966088 | tf_op jit(solution)/shard_map/ppermute | solution.py:276
  143.2 22.5 %collective-permute-start.8 = (bf16[4,256,256]{2,1,0:T(8,128)(2,1)}, bf16[4,256,256]{2,1,0:T(8,128)(2,1)}, u32[]{:S(2)}, u32[]{:S(2)}) collective-permute-start(bf16[4,256,256]{2,1,0:T(8,128)(2,1)} %get-tuple-element.56.refs_8_), channel_id=1, source_target_pairs={{0,7},{1,0},{2,1},{3,2},{4,3},{5,4},{6,5},{7,6},{8,15},{9,8},{10,9... | collective-permute-start | bytes 1572872 | tf_op jit(solution)/shard_map/ppermute | solution.py:276
  146.5 14.0 %copy-start.9 = (bf16[48,2048]{1,0:T(8,128)(2,1)S(1)}, bf16[48,2048]{1,0:T(8,128)(2,1)}, u32[]{:S(2)}) copy-start(bf16[48,2048]{1,0:T(8,128)(2,1)} %grads_ref.3) | copy-start | bytes 589828
  146.5 14.0 %copy-start.10 = (bf16[512,48]{1,0:T(8,128)(2,1)S(1)}, bf16[512,48]{1,0:T(8,128)(2,1)}, u32[]{:S(2)}) copy-start(bf16[512,48]{1,0:T(8,128)(2,1)} %get-tuple-element.36.place_ref) | copy-start | bytes 147460
  146.5 14.0 %copy-start.11 = (s32[48,8]{0,1:T(8,128)S(1)}, s32[48,8]{0,1:T(8,128)}, u32[]{:S(2)}) copy-start(s32[48,8]{0,1:T(8,128)} %param.8) | copy-start | bytes 4612
  146.5 14.0 %copy-start.12 = (f32[48,8]{0,1:T(8,128)S(1)}, f32[48,8]{0,1:T(8,128)}, u32[]{:S(2)}) copy-start(f32[48,8]{0,1:T(8,128)} %param.9) | copy-start | bytes 4612
  146.5 19.3 %collective-permute-start.9 = (bf16[5,256,256]{2,1,0:T(8,128)(2,1)}, bf16[5,256,256]{2,1,0:T(8,128)(2,1)}, u32[]{:S(2)}, u32[]{:S(2)}) collective-permute-start(bf16[5,256,256]{2,1,0:T(8,128)(2,1)} %get-tuple-element.57), channel_id=1, source_target_pairs={{0,1},{1,2},{2,3},{3,4},{4,5},{5,6},{6,7},{7,0},{8,9},{9,10},{10,1... | collective-permute-start | bytes 1966088 | tf_op jit(solution)/shard_map/ppermute | solution.py:276
  156.8 19.5 %collective-permute-start.12 = (bf16[4,256,256]{2,1,0:T(8,128)(2,1)}, bf16[4,256,256]{2,1,0:T(8,128)(2,1)S(1)}, u32[]{:S(2)}, u32[]{:S(2)}) collective-permute-start(bf16[4,256,256]{2,1,0:T(8,128)(2,1)} %get-tuple-element.59.refs_8_), channel_id=1, source_target_pairs={{0,1},{1,2},{2,3},{3,4},{4,5},{5,6},{6,7},{7,0},{8,9},{9,10},{10,1... | collective-permute-start | bytes 1572872 | tf_op jit(solution)/shard_map/ppermute | solution.py:276
  158.2 20.5 %collective-permute-start.13 = (bf16[5,256,256]{2,1,0:T(8,128)(2,1)}, bf16[5,256,256]{2,1,0:T(8,128)(2,1)S(1)}, u32[]{:S(2)}, u32[]{:S(2)}) collective-permute-start(bf16[5,256,256]{2,1,0:T(8,128)(2,1)} %get-tuple-element.62), channel_id=1, source_target_pairs={{0,7},{1,0},{2,1},{3,2},{4,3},{5,4},{6,5},{7,6},{8,15},{9,8},{10,9... | collective-permute-start | bytes 1966088 | tf_op jit(solution)/shard_map/ppermute | solution.py:276
  160.6 5.2 %copy-start.16 = (bf16[768,512]{1,0:T(8,128)(2,1)S(1)}, bf16[768,512]{1,0:T(8,128)(2,1)}, u32[]{:S(2)}) copy-start(bf16[768,512]{1,0:T(8,128)(2,1)} %get-tuple-element.41.refs_5_) | copy-start | bytes 2359300
  165.8 0.9 copy-start.13

commit v5 on v4

--- a/solution.py
+++ b/solution.py
@@ -67,6 +67,8 @@
 
 
 def expert_kernel(rows_ref, grads_ref, gate_ref, up_ref, down_ref, hidden_ref, hidden_t_ref, gate_pre_ref, up_pre_ref):
+    width = gate_ref.shape[1]
+    mine = pl.ds(pl.multiple_of(pl.program_id(0) * width, width), width)
     rows = rows_ref[...]
     pre_gate = dot(rows, gate_ref[...])
     pre_up = dot(rows, up_ref[...])
@@ -74,10 +76,10 @@
     sig = jax.nn.sigmoid(pre_gate)
     silu = pre_gate * sig
     hidden = (silu * pre_up).astype(BF16)
-    hidden_ref[...] = hidden
-    hidden_t_ref[...] = hidden.T
-    gate_pre_ref[...] = (hidden_grad * pre_up * sig * (1.0 + pre_gate * (1.0 - sig))).astype(BF16)
-    up_pre_ref[...] = (hidden_grad * silu).astype(BF16)
+    hidden_ref[:, mine] = hidden
+    hidden_t_ref[mine, :] = hidden.T
+    gate_pre_ref[:, mine] = (hidden_grad * pre_up * sig * (1.0 + pre_gate * (1.0 - sig))).astype(BF16)
+    up_pre_ref[:, mine] = (hidden_grad * silu).astype(BF16)
 
 
 def chunk_sums(rows_a, rows_b, grads_b, gate_pre, up_pre, hidden_t, held_a=(), held_b=()):
@@ -205,7 +207,6 @@
         return lax.all_to_all(wide, "expert", 0, 0, tiled=True).reshape(array.shape)
 
     wide = exchange(send)
-    tile = pl.BlockSpec((slots, width), lambda i: (0, i))
     hidden, hidden_t, gate_pre, up_pre = pl.pallas_call(
         expert_kernel,
         grid=(blocks,),
@@ -216,9 +217,9 @@
             pl.BlockSpec((model, width), lambda i: (0, i)),
             pl.BlockSpec((width, model), lambda i: (i, 0)),
         ],
-        out_specs=[tile, pl.BlockSpec((width, slots), lambda i: (i, 0)), tile, tile],
+        out_specs=[resident] * 4,
         out_shape=(shape((slots, hid)), shape((hid, slots)), shape((slots, hid)), shape((slots, hid))),
-        compiler_params=params(54),
+        compiler_params=params(50),
         cost_estimate=cost(6 * slots * model * hid, 4 * slots * model + 6 * model * hid + 8 * slots * hid),
         name="expert",
     )(wide, wide, w_gate, w_up, w_down)
@@ -269,7 +270,7 @@
         held = came.get((k, swapped), ())
         part_a, part_b = chain_call(step_a, step_b, BF16, held, f"chain_sum_{number}", after)
         after = (part_a,)
-        if number == 1:
+        if number == 2:
             going_back, token = rows_back(part_a)
             after = (token,)
         ring_a, ring_b = (down_ring, up_ring) if swapped else (up_ring, down_ring)

time: 181 us -> 180 us (level)
  waiting for transfers between devices: 84.2 us -> 91.2 us
  starting transfers between devices: 41.1 us -> 37.4 us
  local copies, waits for them, and re-layouts: 7.53 us -> 4.12 us
    all_to_all x2, waiting for transfers between devices: 51.4 us -> 61.4 us  [exchange(): return lax.all_to_all(wide, 'expert', 0, 0, tiled=True).reshape(array.shape)]
    ppermute x7, starting transfers between devices: 14.1 us -> 7.02 us  [local(): lax.ppermute(part_a, 'dp', ring_a)]
    ppermute x7, waiting for transfers between devices: 25.2 us -> 21.5 us  [local(): lax.ppermute(part_a, 'dp', ring_a)]
    ppermute x7, starting transfers between devices: 12.3 us -> 15.8 us  [local(): lax.ppermute(part_b, 'dp', ring_b)]
    unnamed x34 -> x24, local copies, waits for them, and re-layouts: 7.53 us -> 4.12 us
  transfers between devices with their start and end apart: 16 -> 16, of which waited for: 10 -> 7; matrix products, arithmetic and copies ran while one was open for 0% -> 0% of each run, Pallas kernels for 15% -> 15%
where the time goes in v5:
time: 180 us; the launch traced here: 179 us
  waiting for transfers between devices  91.2 us (51%)
  Pallas kernels  45.6 us (25%)
  starting transfers between devices  37.4 us (21%)
  local copies, waits for them, and re-layouts  4.12 us (2%)
    all_to_all x2, waiting for transfers between devices, exchange(): return lax.all_to_all(wide, 'expert', 0, 0, tiled=True).reshape(array.shape)  61.4 us
    ppermute x7, waiting for transfers between devices, local(): lax.ppermute(part_a, 'dp', ring_a)  21.5 us
    pallas_call x8, Pallas kernels, chain_call(): pl.pallas_call(functools.partial(link_kernel, bool(held)), grid_spec=pltp...  19.3 us
    ppermute x7, starting transfers between devices, local(): lax.ppermute(part_b, 'dp', ring_b)  15.8 us
    all_to_all x2, starting transfers between devices, exchange(): return lax.all_to_all(wide, 'expert', 0, 0, tiled=True).reshape(array.shape)  14.5 us
    pallas_call x1, Pallas kernels, local(): pl.pallas_call(expert_kernel, grid=(blocks,), in_specs=[pl.BlockSpec((slo...  9.28 us
    ppermute x7, waiting for transfers between devices, local(): lax.ppermute(part_b, 'dp', ring_b)  8.3 us
    ppermute x7, starting transfers between devices, local(): lax.ppermute(part_a, 'dp', ring_a)  7.02 us
  transfers between devices with their start and end apart: 16, of which 7 were waited for; matrix products, arithmetic and copies ran while one was open for 0% of the time, Pallas kernels for 15%

profile of v5, /device:TPU:2, one launch (start us, length us, event | category | flops | bytes accessed | tf_op | source)
XLA Modules:
  0.0 179.1 jit_solution(17780460037782907224)
XLA Ops:
  0.6 5.3 %dispatch.1 = (bf16[512,4096]{1,0:T(8,128)(2,1)}, bf16[512,48]{1,0:T(8,128)(2,1)}) custom-call(s32[8,48]{1,0:T(8,128)} %bitcast.21, f32[8,48]{1,0:T(8,128)} %bitcast.23, bf16[48,2048]{1,0:T(8,128)(2,1)} %tokens_ref.1, bf16[48,2048]{1,0:T(8,128)(2,1)} %grads_ref.3), custom_call_target="tpu_custom_call" | custom-call | flops 201326592 | bytes 4194304 | tf_op jit(solution)/shard_map/dispatch/pallas_call | solution.py:188
  6.0 7.7 %all-to-all-start = ((bf16[32,16,4096]{2,1,0:T(8,128)(2,1)}), bf16[32,16,4096]{2,1,0:T(8,128)(2,1)}, u32[]{:S(2)}, u32[]{:S(2)}) async-start(bf16[32,16,4096]{2,1,0:T(8,128)(2,1)} %bitcast.25), calls=%async_computation | async-start | bytes 8388608 | tf_op jit(solution)/shard_map/all_to_all | solution.py:207
  13.6 51.4 %all-to-all-done = bf16[32,16,4096]{2,1,0:T(8,128)(2,1)} async-done(((bf16[32,16,4096]{2,1,0:T(8,128)(2,1)}), bf16[32,16,4096]{2,1,0:T(8,128)(2,1)}, u32[]{:S(2)}, u32[]{:S(2)}) %all-to-all-start) | async-done | bytes 4194336 | tf_op jit(solution)/shard_map/all_to_all | solution.py:207
  65.0 9.3 %expert.1 = (bf16[512,768]{1,0:T(8,128)(2,1)S(1)}, bf16[768,512]{1,0:T(8,128)(2,1)S(1)}, bf16[512,768]{1,0:T(8,128)(2,1)S(1)}, bf16[512,768]{1,0:T(8,128)(2,1)S(1)}) custom-call(bf16[512,4096]{1,0:T(8,128)(2,1)} %bitcast.3.rows_ref.grads_ref.refs_0_.refs_1_.refs_2_, bf16[512,4096]{1,0:T(8,128)(2,1)} %bitcast.3.rows_ref.grads_ref.refs_0_.refs_1_.refs_2_, ...), custom_call_target="tpu_custom_call" | custom-call | flops 4831838208 | bytes 16777216 | tf_op jit(solution)/shard_map/expert/pallas_call | solution.py:210
  74.3 0.0 copy-start.9
  74.3 2.2 %chain_sum_0.1 = (bf16[4,256,256]{2,1,0:T(8,128)(2,1)S(1)}, bf16[5,256,256]{2,1,0:T(8,128)(2,1)S(1)}) custom-call(s32[1]{0:T(128)} %bitcast.7._, bf16[512,4096]{1,0:T(8,128)(2,1)} %bitcast.3.rows_ref.grads_ref.refs_0_.refs_1_.refs_2_, bf16[512,4096]{1,0:T(8,128)(2,1)} %bitcast.3.rows_ref.grads_ref.refs_0_.refs_1_.refs_2_, ...), custom_call_target="tpu_custom_call" | custom-call | flops 20000000000 | bytes 62914560 | tf_op jit(solution)/shard_map/chain_sum_0/pallas_call | solution.py:232
  76.5 2.0 %collective-permute-start = (bf16[4,256,256]{2,1,0:T(8,128)(2,1)S(1)}, bf16[4,256,256]{2,1,0:T(8,128)(2,1)S(1)}, u32[]{:S(2)}, u32[]{:S(2)}) collective-permute-start(bf16[4,256,256]{2,1,0:T(8,128)(2,1)S(1)} %get-tuple-element.42.refs_6_), channel_id=1, source_target_pairs={{0,1},{1,2},{2,3},{3,4},{4,5},{5,6},{6,7},{7,0},{8,9},{9,10},{10,1... | collective-permute-start | bytes 1572872 | tf_op jit(solution)/shard_map/ppermute | solution.py:277
  78.5 4.0 %collective-permute-start.1 = (bf16[5,256,256]{2,1,0:T(8,128)(2,1)S(1)}, bf16[5,256,256]{2,1,0:T(8,128)(2,1)S(1)}, u32[]{:S(2)}, u32[]{:S(2)}) collective-permute-start(bf16[5,256,256]{2,1,0:T(8,128)(2,1)S(1)} %get-tuple-element.43), channel_id=1, source_target_pairs={{0,7},{1,0},{2,1},{3,2},{4,3},{5,4},{6,5},{7,6},{8,15},{9,8},{10,9... | collective-permute-start | bytes 1966088 | tf_op jit(solution)/shard_map/ppermute | solution.py:277
  82.6 2.8 %chain_sum_1.1 = (bf16[4,256,256]{2,1,0:T(8,128)(2,1)}, bf16[5,256,256]{2,1,0:T(8,128)(2,1)}) custom-call(s32[1]{0:T(128)} %bitcast.7._, bf16[512,4096]{1,0:T(8,128)(2,1)} %bitcast.3.rows_ref.grads_ref.refs_0_.refs_1_.refs_2_, bf16[512,4096]{1,0:T(8,128)(2,1)} %bitcast.3.rows_ref.grads_ref.refs_0_.refs_1_.refs_2_, ...), custom_call_target="tpu_custom_call" | custom-call | flops 20000000000 | bytes 62914560 | tf_op jit(solution)/shard_map/chain_sum_1/pallas_call | solution.py:232
  85.3 1.9 %collective-permute-start.2 = (bf16[4,256,256]{2,1,0:T(8,128)(2,1)}, bf16[4,256,256]{2,1,0:T(8,128)(2,1)}, u32[]{:S(2)}, u32[]{:S(2)}) collective-permute-start(bf16[4,256,256]{2,1,0:T(8,128)(2,1)} %get-tuple-element.44.refs_8_), channel_id=1, source_target_pairs={{0,7},{1,0},{2,1},{3,2},{4,3},{5,4},{6,5},{7,6},{8,15},{9,8},{10,9... | collective-permute-start | bytes 1572872 | tf_op jit(solution)/shard_map/ppermute | solution.py:277
  87.3 0.1 collective-permute-start.3
  87.4 7.9 %collective-permute-done.refs_6_ = bf16[4,256,256]{2,1,0:T(8,128)(2,1)S(1)} collective-permute-done((bf16[4,256,256]{2,1,0:T(8,128)(2,1)S(1)}, bf16[4,256,256]{2,1,0:T(8,128)(2,1)S(1)}, u32[]{:S(2)}, u32[]{:S(2)}) %collective-permute-start) | collective-permute-done | bytes 524320 | tf_op jit(solution)/shard_map/ppermute | solution.py:277
  95.3 2.5 %collective-permute-done.1.refs_7_ = bf16[5,256,256]{2,1,0:T(8,128)(2,1)S(1)} collective-permute-done((bf16[5,256,256]{2,1,0:T(8,128)(2,1)S(1)}, bf16[5,256,256]{2,1,0:T(8,128)(2,1)S(1)}, u32[]{:S(2)}, u32[]{:S(2)}) %collective-permute-start.1) | collective-permute-done | bytes 655392 | tf_op jit(solution)/shard_map/ppermute | solution.py:277
  97.7 0.0 copy-done.9
  97.7 1.9 %chain_sum_2.1 = (bf16[4,256,256]{2,1,0:T(8,128)(2,1)S(1)}, bf16[5,256,256]{2,1,0:T(8,128)(2,1)S(1)}) custom-call(s32[1]{0:T(128)} %bitcast.7._, bf16[512,4096]{1,0:T(8,128)(2,1)} %bitcast.3.rows_ref.grads_ref.refs_0_.refs_1_.refs_2_, bf16[512,4096]{1,0:T(8,128)(2,1)} %bitcast.3.rows_ref.grads_ref.refs_0_.refs_1_.refs_2_, ...), custom_call_target="tpu_custom_call" | custom-call | flops 20000000000 | bytes 62914560 | tf_op jit(solution)/shard_map/chain_sum_2/pallas_call | solution.py:232
  99.7 0.4 collective-permute-start.6
  100.1 3.6 %collective-permute-start.7 = (bf16[5,256,256]{2,1,0:T(8,128)(2,1)S(1)}, bf16[5,256,256]{2,1,0:T(8,128)(2,1)S(1)}, u32[]{:S(2)}, u32[]{:S(2)}) collective-permute-start(bf16[5,256,256]{2,1,0:T(8,128)(2,1)S(1)} %get-tuple-element.54), channel_id=1, source_target_pairs={{0,7},{1,0},{2,1},{3,2},{4,3},{5,4},{6,5},{7,6},{8,15},{9,8},{10,9... | collective-permute-start | bytes 1966088 | tf_op jit(solution)/shard_map/ppermute | solution.py:277
  103.7 0.0 copy-done.1
  103.7 0.0 copy-done.2
  103.7 0.0 copy-done.3
  103.7 5.0 %rows_back.1 = (bf16[512,4096]{1,0:T(8,128)(2,1)S(1)}, f32[8,128]{1,0:T(8,128)S(1)}) custom-call(bf16[512,768]{1,0:T(8,128)(2,1)S(1)} %get-tuple-element.38.hidden_ref, bf16[512,768]{1,0:T(8,128)(2,1)S(1)} %get-tuple-element.39.refs_3_.gate_pre_ref, bf16[512,768]{1,0:T(8,128)(2,1)S(1)} %get-tuple-element.40.refs_4_.up_pre_ref, ...), custom_call_target="tpu_custom_call" | custom-call | flops 1 | bytes 1 | tf_op jit(solution)/shard_map/rows_back/pallas_call | solution.py:257
  108.8 0.0 copy-start
  108.8 2.0 %copy-done = bf16[512,4096]{1,0:T(8,128)(2,1)} copy-done((bf16[512,4096]{1,0:T(8,128)(2,1)}, bf16[512,4096]{1,0:T(8,128)(2,1)S(1)}, u32[]{:S(2)}) %copy-start) | copy-done | bytes 4194328
  110.8 6.9 %all-to-all-start.1 = ((bf16[32,16,4096]{2,1,0:T(8,128)(2,1)}), bf16[32,16,4096]{2,1,0:T(8,128)(2,1)}, u32[]{:S(2)}, u32[]{:S(2)}) async-start(bf16[32,16,4096]{2,1,0:T(8,128)(2,1)} %bitcast.14), calls=%async_computation.1 | async-start | bytes 8388608 | tf_op jit(solution)/shard_map/all_to_all | solution.py:207
  117.7 0.0 collective-permute-done.2.refs_6_
  117.7 0.0 collective-permute-done.3.refs_7_
  117.7 0.0 copy-start.10
  117.7 1.1 copy-done.10
  118.8 2.3 %chain_sum_3.1 = (bf16[4,256,256]{2,1,0:T(8,128)(2,1)S(1)}, bf16[5,256,256]{2,1,0:T(8,128)(2,1)S(1)}) custom-call(s32[1]{0:T(128)} %bitcast.7._, bf16[512,4096]{1,0:T(8,128)(2,1)} %bitcast.3.rows_ref.grads_ref.refs_0_.refs_1_.refs_2_, bf16[512,4096]{1,0:T(8,128)(2,1)} %bitcast.3.rows_ref.grads_ref.refs_0_.refs_1_.refs_2_, ...), custom_call_target="tpu_custom_call" | custom-call | flops 20000000000 | bytes 62914560 | tf_op jit(solution)/shard_map/chain_sum_3/pallas_call | solution.py:232
  121.2 1.8 %collective-permute-start.4 = (bf16[4,256,256]{2,1,0:T(8,128)(2,1)S(1)}, bf16[4,256,256]{2,1,0:T(8,128)(2,1)S(1)}, u32[]{:S(2)}, u32[]{:S(2)}) collective-permute-start(bf16[4,256,256]{2,1,0:T(8,128)(2,1)S(1)} %get-tuple-element.52.refs_8_), channel_id=1, source_target_pairs={{0,7},{1,0},{2,1},{3,2},{4,3},{5,4},{6,5},{7,6},{8,15},{9,8},{10,9... | collective-permute-start | bytes 1572872 | tf_op jit(solution)/shard_map/ppermute | solution.py:277
  123.0 0.3 collective-permute-start.5
  123.3 0.0 collective-permute-done.6.refs_6_
  123.3 0.0 collective-permute-done.7.refs_7_
  123.3 2.1 %chain_sum_4.1 = (bf16[4,256,256]{2,1,0:T(8,128)(2,1)S(1)}, bf16[5,256,256]{2,1,0:T(8,128)(2,1)S(1)}) custom-call(s32[1]{0:T(128)} %bitcast.7._, bf16[512,4096]{1,0:T(8,128)(2,1)} %bitcast.3.rows_ref.grads_ref.refs_0_.refs_1_.refs_2_, bf16[512,4096]{1,0:T(8,128)(2,1)} %bitcast.3.rows_ref.grads_ref.refs_0_.refs_1_.refs_2_, ...), custom_call_target="tpu_custom_call" | custom-call | flops 20000000000 | bytes 62914560 | tf_op jit(solution)/shard_map/chain_sum_4/pallas_call | solution.py:232
  125.4 0.8 collective-permute-start.10
  126.2 2.5 %collective-permute-start.11 = (bf16[5,256,256]{2,1,0:T(8,128)(2,1)S(1)}, bf16[5,256,256]{2,1,0:T(8,128)(2,1)S(1)}, u32[]{:S(2)}, u32[]{:S(2)}) collective-permute-start(bf16[5,256,256]{2,1,0:T(8,128)(2,1)S(1)} %get-tuple-element.58), channel_id=1, source_target_pairs={{0,7},{1,0},{2,1},{3,2},{4,3},{5,4},{6,5},{7,6},{8,15},{9,8},{10,9... | collective-permute-start | bytes 1966088 | tf_op jit(solution)/shard_map/ppermute | solution.py:277
  128.7 7.3 %collective-permute-done.4.refs_6_ = bf16[4,256,256]{2,1,0:T(8,128)(2,1)S(1)} collective-permute-done((bf16[4,256,256]{2,1,0:T(8,128)(2,1)S(1)}, bf16[4,256,256]{2,1,0:T(8,128)(2,1)S(1)}, u32[]{:S(2)}, u32[]{:S(2)}) %collective-permute-start.4) | collective-permute-done | bytes 524320 | tf_op jit(solution)/shard_map/ppermute | solution.py:277
  136.0 5.8 %collective-permute-done.5.refs_7_ = bf16[5,256,256]{2,1,0:T(8,128)(2,1)S(1)} collective-permute-done((bf16[5,256,256]{2,1,0:T(8,128)(2,1)S(1)}, bf16[5,256,256]{2,1,0:T(8,128)(2,1)S(1)}, u32[]{:S(2)}, u32[]{:S(2)}) %collective-permute-start.5) | collective-permute-done | bytes 655392 | tf_op jit(solution)/shard_map/ppermute | solution.py:277
  141.8 2.8 %chain_sum_5.1 = (bf16[4,256,256]{2,1,0:T(8,128)(2,1)}, bf16[5,256,256]{2,1,0:T(8,128)(2,1)}) custom-call(s32[1]{0:T(128)} %bitcast.7._, bf16[512,4096]{1,0:T(8,128)(2,1)} %bitcast.3.rows_ref.grads_ref.refs_0_.refs_1_.refs_2_, bf16[512,4096]{1,0:T(8,128)(2,1)} %bitcast.3.rows_ref.grads_ref.refs_0_.refs_1_.refs_2_, ...), custom_call_target="tpu_custom_call" | custom-call | flops 20000000000 | bytes 62914560 | tf_op jit(solution)/shard_map/chain_sum_5/pallas_call | solution.py:232
  144.6 0.0 collective-permute-start.8
  144.6 0.0 copy-start.6
  144.6 0.0 copy-start.7
  144.7 2.1 %collective-permute-start.9 = (bf16[5,256,256]{2,1,0:T(8,128)(2,1)}, bf16[5,256,256]{2,1,0:T(8,128)(2,1)}, u32[]{:S(2)}, u32[]{:S(2)}) collective-permute-start(bf16[5,256,256]{2,1,0:T(8,128)(2,1)} %get-tuple-element.57), channel_id=1, source_target_pairs={{0,1},{1,2},{2,3},{3,4},{4,5},{5,6},{6,7},{7,0},{8,9},{9,10},{10,1... | collective-permute-start | bytes 1966088 | tf_op jit(solution)/shard_map/ppermute | solution.py:277
  146.7 6.3 %collective-permute-done.10.refs_6_ = bf16[4,256,256]{2,1,0:T(8,128)(2,1)S(1)} collective-permute-done((bf16[4,256,256]{2,1,0:T(8,128)(2,1)S(1)}, bf16[4,256,256]{2,1,0:T(8,128)(2,1)S(1)}, u32[]{:S(2)}, u32[]{:S(2)}) %collective-permute-start.10) | collective-permute-done | bytes 524320 | tf_op jit(solution)/shard_map/ppermute | solution.py:277
  153.1 0.0 collective-permute-done.11.refs_7_
  153.1 2.8 %chain_sum_6.1 = (bf16[4,256,256]{2,1,0:T(8,128)(2,1)}, bf16[5,256,256]{2,1,0:T(8,128)(2,1)}) custom-call(s32[1]{0:T(128)} %bitcast.7._, bf16[512,4096]{1,0:T(8,128)(2,1)} %bitcast.3.rows_ref.grads_ref.refs_0_.refs_1_.refs_2_, bf16[512,4096]{1,0:T(8,128)(2,1)} %bitcast.3.rows_ref.grads_ref.refs_0_.refs_1_.refs_2_, ...), custom_call_target="tpu_custom_call" | custom-call | flops 20000000000 | bytes 62914560 | tf_op jit(solution)/shard_map/chain_sum_6/pallas_call | solution.py:232
  155.9 0.0 collective-permute-start.12
  155.9 3.2 %collective-permute-start.13 = (bf16[5,256,256]{2,1,0:T(8,128)(2,1)}, bf16[5,256,256]{2,1,0:T(8,128)(2,1)S(1)}, u32[]{:S(2)}, u32[]{:S(2)}) collective-permute-start(bf16[5,256,256]{2,1,0:T(8,128)(2,1)} %get-tuple-element.62), channel_id=1, source_target_pairs={{0,7},{1,0},{2,1},{3,2},{4,3},{5,4},{6,5},{7,6},{8,15},{9,8},{10,9... | collective-permute-start | bytes 1966088 | tf_op jit(solution)/shard_map/ppermute | solution.py:277
  159.1 10.0 %all-to-all-done.1 = bf16[32,16,4096]{2,1,0:T(8,128)(2,1)} async-done(((bf16[32,16,4096]{2,1,0:T(8,128)(2,1)}), bf16[32,16,4096]{2,1,0:T(8,128)(2,1)}, u32[]{:S(2)}, u32[]{:S(2)}) %all-to-all-start.1) | async-done | bytes 4194336 | tf_op jit(solution)/shard_map/all_to_all | solution.py:207
  169.1 0.0 copy-done.4
  169.2 0.0 copy-done.5
  169.2 0.0 copy-done.6
  169.2 0.0 copy-done.7
  169.2 0.0 copy-start.11
  169.2 5.1 %combine.1 = (bf16[48,2048]{1,0:T(8,128)(2,1)}, bf16[48,2048]{1,0:T(8,128)(2,1)}, f32[8,48]{1,0:T(8,128)}) custom-call(s32[8,48]{1,0:T(8,128)S(1)} %bitcast.22, f32[8,48]{1,0:T(8,128)S(1)} %bitcast.24, bf16[512,48]{1,0:T(8,128)(2,1)S(1)} %copy-done.5, bf16[48,2048]{1,0:T(8,128)(2,1)S(1)} %copy-done.4, bf16[512,4096]{1,0:T(8,128)(2,1)} %bitcast.9.back_ref.back_grad_ref, ...), custom_call_target="tpu_custom_call" | custom-call | flops 402653184 | bytes 4194304 | tf_op jit(solution)/shard_map/combine/pallas_call | solution.py:281
  174.2 0.0 collective-permute-done.8.refs_6_
  174.2 0.0 collective-permute-done.9.refs_7_
  174.3 0.0 copy-done.11
  174.3 0.0 copy-start.8
  174.3 0.9 copy-done.8
  175.2 2.3 %chain_sum_own.1 = (f32[4,256,256]{2,1,0:T(8,128)S(1)}, f32[5,256,256]{2,1,0:T(8,128)S(1)}) custom-call(s32[1]{0:T(128)} %bitcast.7._, bf16[512,4096]{1,0:T(8,128)(2,1)} %bitcast.3.rows_ref.grads_ref.refs_0_.refs_1_.refs_2_, bf16[512,4096]{1,0:T(8,128)(2,1)} %bitcast.3.rows_ref.grads_ref.refs_0_.refs_1_.refs_2_, ...), custom_call_target="tpu_custom_call" | custom-call | flops 20000000000 | bytes 62914560 | tf_op jit(solution)/shard_map/chain_sum_own/pallas_call | solution.py:232
  177.5 0.0 collective-permute-done.12.a0
  177.5 0.0 collective-permute-done.13.b0
  177.5 1.6 chain_sum_last.1
  (5 shorter events, 0.0 us)
Async XLA Ops:
  6.0 59.1 %all-to-all-start = ((bf16[32,16,4096]{2,1,0:T(8,128)(2,1)}), bf16[32,16,4096]{2,1,0:T(8,128)(2,1)}, u32[]{:S(2)}, u32[]{:S(2)}) async-start(bf16[32,16,4096]{2,1,0:T(8,128)(2,1)} %bitcast.25), calls=%async_computation | async-start | bytes 8388608 | tf_op jit(solution)/shard_map/all_to_all | solution.py:207
  74.3 23.5 %copy-start.9 = (bf16[768,512]{1,0:T(8,128)(2,1)}, bf16[768,512]{1,0:T(8,128)(2,1)S(1)}, u32[]{:S(2)}) copy-start(bf16[768,512]{1,0:T(8,128)(2,1)S(1)} %get-tuple-element.41.refs_5_) | copy-start | bytes 2359300
  76.5 18.7 %collective-permute-start = (bf16[4,256,256]{2,1,0:T(8,128)(2,1)S(1)}, bf16[4,256,256]{2,1,0:T(8,128)(2,1)S(1)}, u32[]{:S(2)}, u32[]{:S(2)}) collective-permute-start(bf16[4,256,256]{2,1,0:T(8,128)(2,1)S(1)} %get-tuple-element.42.refs_6_), channel_id=1, source_target_pairs={{0,1},{1,2},{2,3},{3,4},{4,5},{5,6},{6,7},{7,0},{8,9},{9,10},{10,1... | collective-permute-start | bytes 1572872 | tf_op jit(solution)/shard_map/ppermute | solution.py:277
  78.5 19.2 %collective-permute-start.1 = (bf16[5,256,256]{2,1,0:T(8,128)(2,1)S(1)}, bf16[5,256,256]{2,1,0:T(8,128)(2,1)S(1)}, u32[]{:S(2)}, u32[]{:S(2)}) collective-permute-start(bf16[5,256,256]{2,1,0:T(8,128)(2,1)S(1)} %get-tuple-element.43), channel_id=1, source_target_pairs={{0,7},{1,0},{2,1},{3,2},{4,3},{5,4},{6,5},{7,6},{8,15},{9,8},{10,9... | collective-permute-start | bytes 1966088 | tf_op jit(solution)/shard_map/ppermute | solution.py:277
  85.3 32.3 %collective-permute-start.2 = (bf16[4,256,256]{2,1,0:T(8,128)(2,1)}, bf16[4,256,256]{2,1,0:T(8,128)(2,1)}, u32[]{:S(2)}, u32[]{:S(2)}) collective-permute-start(bf16[4,256,256]{2,1,0:T(8,128)(2,1)} %get-tuple-element.44.refs_8_), channel_id=1, source_target_pairs={{0,7},{1,0},{2,1},{3,2},{4,3},{5,4},{6,5},{7,6},{8,15},{9,8},{10,9... | collective-permute-start | bytes 1572872 | tf_op jit(solution)/shard_map/ppermute | solution.py:277
  87.3 16.5 %copy-start.1 = (bf16[1,2048,768]{2,1,0:T(8,128)(2,1)S(1)}, bf16[1,2048,768]{2,1,0:T(8,128)(2,1)}, u32[]{:S(2)}) copy-start(bf16[1,2048,768]{2,1,0:T(8,128)(2,1)} %param.10) | copy-start | bytes 9437188
  87.3 16.5 %copy-start.2 = (bf16[1,2048,768]{2,1,0:T(8,128)(2,1)S(1)}, bf16[1,2048,768]{2,1,0:T(8,128)(2,1)}, u32[]{:S(2)}) copy-start(bf16[1,2048,768]{2,1,0:T(8,128)(2,1)} %param.11) | copy-start | bytes 9437188
  87.3 16.5 %copy-start.3 = (bf16[1,768,2048]{2,1,0:T(8,128)(2,1)S(1)}, bf16[1,768,2048]{2,1,0:T(8,128)(2,1)}, u32[]{:S(2)}) copy-start(bf16[1,768,2048]{2,1,0:T(8,128)(2,1)} %param.12) | copy-start | bytes 9437188
  87.3 30.4 %collective-permute-start.3 = (bf16[5,256,256]{2,1,0:T(8,128)(2,1)}, bf16[5,256,256]{2,1,0:T(8,128)(2,1)}, u32[]{:S(2)}, u32[]{:S(2)}) collective-permute-start(bf16[5,256,256]{2,1,0:T(8,128)(2,1)} %get-tuple-element.50), channel_id=1, source_target_pairs={{0,1},{1,2},{2,3},{3,4},{4,5},{5,6},{6,7},{7,0},{8,9},{9,10},{10,1... | collective-permute-start | bytes 1966088 | tf_op jit(solution)/shard_map/ppermute | solution.py:277
  99.7 23.6 %collective-permute-start.6 = (bf16[4,256,256]{2,1,0:T(8,128)(2,1)S(1)}, bf16[4,256,256]{2,1,0:T(8,128)(2,1)}, u32[]{:S(2)}, u32[]{:S(2)}) collective-permute-start(bf16[4,256,256]{2,1,0:T(8,128)(2,1)S(1)} %get-tuple-element.45._), channel_id=1, source_target_pairs={{0,1},{1,2},{2,3},{3,4},{4,5},{5,6},{6,7},{7,0},{8,9},{9,10},{10,1... | collective-permute-start | bytes 1572872 | tf_op jit(solution)/shard_map/ppermute | solution.py:277
  100.1 23.2 %collective-permute-start.7 = (bf16[5,256,256]{2,1,0:T(8,128)(2,1)S(1)}, bf16[5,256,256]{2,1,0:T(8,128)(2,1)S(1)}, u32[]{:S(2)}, u32[]{:S(2)}) collective-permute-start(bf16[5,256,256]{2,1,0:T(8,128)(2,1)S(1)} %get-tuple-element.54), channel_id=1, source_target_pairs={{0,7},{1,0},{2,1},{3,2},{4,3},{5,4},{6,5},{7,6},{8,15},{9,8},{10,9... | collective-permute-start | bytes 1966088 | tf_op jit(solution)/shard_map/ppermute | solution.py:277
  108.8 2.0 %copy-start = (bf16[512,4096]{1,0:T(8,128)(2,1)}, bf16[512,4096]{1,0:T(8,128)(2,1)S(1)}, u32[]{:S(2)}) copy-start(bf16[512,4096]{1,0:T(8,128)(2,1)S(1)} %get-tuple-element.46) | copy-start | bytes 12582916
  110.8 58.3 %all-to-all-start.1 = ((bf16[32,16,4096]{2,1,0:T(8,128)(2,1)}), bf16[32,16,4096]{2,1,0:T(8,128)(2,1)}, u32[]{:S(2)}, u32[]{:S(2)}) async-start(bf16[32,16,4096]{2,1,0:T(8,128)(2,1)} %bitcast.14), calls=%async_computation.1 | async-start | bytes 8388608 | tf_op jit(solution)/shard_map/all_to_all | solution.py:207
  117.7 1.1 copy-start.10
  121.2 14.8 %collective-permute-start.4 = (bf16[4,256,256]{2,1,0:T(8,128)(2,1)S(1)}, bf16[4,256,256]{2,1,0:T(8,128)(2,1)S(1)}, u32[]{:S(2)}, u32[]{:S(2)}) collective-permute-start(bf16[4,256,256]{2,1,0:T(8,128)(2,1)S(1)} %get-tuple-element.52.refs_8_), channel_id=1, source_target_pairs={{0,7},{1,0},{2,1},{3,2},{4,3},{5,4},{6,5},{7,6},{8,15},{9,8},{10,9... | collective-permute-start | bytes 1572872 | tf_op jit(solution)/shard_map/ppermute | solution.py:277
  123.0 18.8 %collective-permute-start.5 = (bf16[5,256,256]{2,1,0:T(8,128)(2,1)S(1)}, bf16[5,256,256]{2,1,0:T(8,128)(2,1)S(1)}, u32[]{:S(2)}, u32[]{:S(2)}) collective-permute-start(bf16[5,256,256]{2,1,0:T(8,128)(2,1)S(1)} %get-tuple-element.53), channel_id=1, source_target_pairs={{0,1},{1,2},{2,3},{3,4},{4,5},{5,6},{6,7},{7,0},{8,9},{9,10},{10,1... | collective-permute-start | bytes 1966088 | tf_op jit(solution)/shard_map/ppermute | solution.py:277
  125.4 27.7 %collective-permute-start.10 = (bf16[4,256,256]{2,1,0:T(8,128)(2,1)S(1)}, bf16[4,256,256]{2,1,0:T(8,128)(2,1)S(1)}, u32[]{:S(2)}, u32[]{:S(2)}) collective-permute-start(bf16[4,256,256]{2,1,0:T(8,128)(2,1)S(1)} %get-tuple-element.55.refs_8_), channel_id=1, source_target_pairs={{0,1},{1,2},{2,3},{3,4},{4,5},{5,6},{6,7},{7,0},{8,9},{9,10},{10,1... | collective-permute-start | bytes 1572872 | tf_op jit(solution)/shard_map/ppermute | solution.py:277
  126.2 26.8 %collective-permute-start.11 = (bf16[5,256,256]{2,1,0:T(8,128)(2,1)S(1)}, bf16[5,256,256]{2,1,0:T(8,128)(2,1)S(1)}, u32[]{:S(2)}, u32[]{:S(2)}) collective-permute-start(bf16[5,256,256]{2,1,0:T(8,128)(2,1)S(1)} %get-tuple-element.58), channel_id=1, source_target_pairs={{0,7},{1,0},{2,1},{3,2},{4,3},{5,4},{6,5},{7,6},{8,15},{9,8},{10,9... | collective-permute-start | bytes 1966088 | tf_op jit(solution)/shard_map/ppermute | solution.py:277
  144.6 29.6 %collective-permute-start.8 = (bf16[4,256,256]{2,1,0:T(8,128)(2,1)}, bf16[4,256,256]{2,1,0:T(8,128)(2,1)}, u32[]{:S(2)}, u32[]{:S(2)}) collective-permute-start(bf16[4,256,256]{2,1,0:T(8,128)(2,1)} %get-tuple-element.56.refs_8_), channel_id=1, source_target_pairs={{0,7},{1,0},{2,1},{3,2},{4,3},{5,4},{6,5},{7,6},{8,15},{9,8},{10,9... | collective-permute-start | bytes 1572872 | tf_op jit(solution)/shard_map/ppermute | solution.py:277
  144.6 24.5 %copy-start.4 = (bf16[48,2048]{1,0:T(8,128)(2,1)S(1)}, bf16[48,2048]{1,0:T(8,128)(2,1)}, u32[]{:S(2)}) copy-start(bf16[48,2048]{1,0:T(8,128)(2,1)} %grads_ref.3) | copy-start | bytes 589828
  144.6 24.5 %copy-start.5 = (bf16[512,48]{1,0:T(8,128)(2,1)S(1)}, bf16[512,48]{1,0:T(8,128)(2,1)}, u32[]{:S(2)}) copy-start(bf16[512,48]{1,0:T(8,128)(2,1)} %get-tuple-element.36.place_ref) | copy-start | bytes 147460
  144.6 24.5 %copy-start.6 = (s32[48,8]{0,1:T(8,128)S(1)}, s32[48,8]{0,1:T(8,128)}, u32[]{:S(2)}) copy-start(s32[48,8]{0,1:T(8,128)} %param.8) | copy-start | bytes 4612
  144.6 24.5 %copy-start.7 = (f32[48,8]{0,1:T(8,128)S(1)}, f32[48,8]{0,1:T(8,128)}, u32[]{:S(2)}) copy-start(f32[48,8]{0,1:T(8,128)} %param.9) | copy-start | bytes 4612
  144.7 29.6 %collective-permute-start.9 = (bf16[5,256,256]{2,1,0:T(8,128)(2,1)}, bf16[5,256,256]{2,1,0:T(8,128)(2,1)}, u32[]{:S(2)}, u32[]{:S(2)}) collective-permute-start(bf16[5,256,256]{2,1,0:T(8,128)(2,1)} %get-tuple-element.57), channel_id=1, source_target_pairs={{0,1},{1,2},{2,3},{3,4},{4,5},{5,6},{6,7},{7,0},{8,9},{9,10},{10,1... | collective-permute-start | bytes 1966088 | tf_op jit(solution)/shard_map/ppermute | solution.py:277
  155.9 21.7 %collective-permute-start.12 = (bf16[4,256,256]{2,1,0:T(8,128)(2,1)}, bf16[4,256,256]{2,1,0:T(8,128)(2,1)S(1)}, u32[]{:S(2)}, u32[]{:S(2)}) collective-permute-start(bf16[4,256,256]{2,1,0:T(8,128)(2,1)} %get-tuple-element.59.refs_8_), channel_id=1, source_target_pairs={{0,1},{1,2},{2,3},{3,4},{4,5},{5,6},{6,7},{7,0},{8,9},{9,10},{10,1... | collective-permute-start | bytes 1572872 | tf_op jit(solution)/shard_map/ppermute | solution.py:277
  155.9 21.7 %collective-permute-start.13 = (bf16[5,256,256]{2,1,0:T(8,128)(2,1)}, bf16[5,256,256]{2,1,0:T(8,128)(2,1)S(1)}, u32[]{:S(2)}, u32[]{:S(2)}) collective-permute-start(bf16[5,256,256]{2,1,0:T(8,128)(2,1)} %get-tuple-element.62), channel_id=1, source_target_pairs={{0,7},{1,0},{2,1},{3,2},{4,3},{5,4},{6,5},{7,6},{8,15},{9,8},{10,9... | collective-permute-start | bytes 1966088 | tf_op jit(solution)/shard_map/ppermute | solution.py:277
  169.2 5.1 %copy-start.11 = (bf16[768,512]{1,0:T(8,128)(2,1)S(1)}, bf16[768,512]{1,0:T(8,128)(2,1)}, u32[]{:S(2)}) copy-start(bf16[768,512]{1,0:T(8,128)(2,1)} %copy-done.9) | copy-start | bytes 2359300
  174.3 0.9 copy-start.8

commit v6 on v5

--- a/solution.py
+++ b/solution.py
@@ -36,7 +36,7 @@
 
 
 def dispatch_kernel(capacity, routes_ref, gates_ref, tokens_ref, grads_ref, wide_ref, place_ref, slot_weight):
-    step, half = pl.program_id(0), pl.num_programs(0) // 2
+    step = pl.program_id(0)
 
     @pl.when(step == 0)
     def _():
@@ -57,11 +57,11 @@
         slot_weight[...] = jnp.sum(place * weight, axis=1, keepdims=True)
         place_ref[...] = place.astype(BF16)
 
-    @pl.when(step < half)
+    @pl.when(step == 0)
     def _():
         wide_ref[...] = dot(place_ref[...], tokens_ref[...]).astype(BF16)
 
-    @pl.when(step >= half)
+    @pl.when(step == 1)
     def _():
         wide_ref[...] = (slot_weight[...] * dot(place_ref[...], grads_ref[...])).astype(BF16)
 
@@ -110,7 +110,7 @@
         out[part][j] = total.astype(out[part].dtype)
 
 
-def last_kernel(own_a, own_b, a0, b0, gate_ref, up_ref, down_ref):
+def last_kernel(own_a, own_b, a0, b0, _, gate_ref, up_ref, down_ref):
     width = own_a.shape[1]
     blocks = own_a.shape[0] - 1
     for j in range(blocks):
@@ -121,38 +121,40 @@
         up_ref[:, (j + 1) * width : (j + 2) * width] = own_b[j] + b0[j].astype(F32)
 
 
-def back_kernel(width, hidden_ref, gate_pre_ref, up_pre_ref, down_ref, gate_ref, up_ref, _, back_ref, token_ref):
+def back_kernel(hidden_ref, gate_pre_ref, up_pre_ref, down_ref, gate_ref, up_ref, _, back_ref, token_ref):
+    width = gate_ref.shape[0]
     token_ref[...] = jnp.zeros_like(token_ref)
-    model = down_ref.shape[1]
-    for j in range(model // width):
-        cols = slice(j * width, (j + 1) * width)
-        back_ref[:, cols] = dot(hidden_ref[...], down_ref[:, cols]).astype(BF16)
-        row_grad = dot(gate_pre_ref[...], gate_ref[cols, :], LAST) + dot(up_pre_ref[...], up_ref[cols, :], LAST)
-        back_ref[:, model + j * width : model + (j + 1) * width] = row_grad.astype(BF16)
+    back_ref[:, :width] = dot(hidden_ref[...], down_ref[...]).astype(BF16)
+    row_grad = dot(gate_pre_ref[...], gate_ref[...], LAST) + dot(up_pre_ref[...], up_ref[...], LAST)
+    back_ref[:, width:] = row_grad.astype(BF16)
 
 
 def combine_kernel(
-    capacity, routes_ref, gates_ref, place_ref, grads_ref, back_ref, back_grad_ref,
-    out_ref, grad_ref, gates_grad_ref, high, low, score,
+    capacity, width, routes_ref, gates_ref, place_ref, grads_ref, back_ref,
+    out_ref, grad_ref, gates_grad_ref, high, low, place_t, score,
 ):
     step = pl.program_id(0)
 
     @pl.when(step == 0)
     def _():
         gates_t = gates_ref[...]
-        weight = jnp.zeros(place_ref.shape, F32)
-        for k, mask in enumerate(slot_masks(routes_ref[...], place_ref.shape[0], capacity)):
+        place = place_ref[...].astype(F32)
+        weight = jnp.zeros(place.shape, F32)
+        for k, mask in enumerate(slot_masks(routes_ref[...], place.shape[0], capacity)):
             weight = jnp.where(mask, gates_t[k : k + 1, :], weight)
-        weight = weight * place_ref[...].astype(F32)
+        weight = (weight * place).T
         high[...] = weight.astype(BF16)
         low[...] = (weight - weight.astype(BF16).astype(F32)).astype(BF16)
+        place_t[...] = place.T.astype(BF16)
         score[...] = jnp.zeros_like(score)
 
-    back = back_ref[...]
-    out_ref[...] = (dot(high[...], back, FIRST) + dot(low[...], back, FIRST)).astype(BF16)
-    grad_ref[...] = dot(place_ref[...], back_grad_ref[...], FIRST).astype(BF16)
-    slot_grads = dot(place_ref[...], grads_ref[...])
-    score[...] += jnp.sum(slot_grads * back.astype(F32), axis=1, keepdims=True)
+    for j in range(grads_ref.shape[1] // width):
+        cols = slice(j * width, (j + 1) * width)
+        back = back_ref[:, 2 * j * width : (2 * j + 1) * width]
+        out_ref[:, cols] = (dot(high[...], back) + dot(low[...], back)).astype(BF16)
+        grad_ref[:, cols] = dot(place_t[...], back_ref[:, (2 * j + 1) * width : (2 * j + 2) * width]).astype(BF16)
+        slot_grads = dot(place_ref[...], grads_ref[:, cols])
+        score[...] += jnp.sum(slot_grads * back.astype(F32), axis=1, keepdims=True)
 
     @pl.when(step == pl.num_programs(0) - 1)
     def _():
@@ -187,14 +189,14 @@
     half = model // 2
     send, place = pl.pallas_call(
         functools.partial(dispatch_kernel, capacity),
-        grid=(4,),
+        grid=(2,),
         in_specs=[
             whole((top, count)),
             whole((top, count)),
-            pl.BlockSpec((count, half), lambda i: (0, jnp.minimum(i, 1))),
-            pl.BlockSpec((count, half), lambda i: (0, jnp.maximum(i - 2, 0))),
+            whole((count, model)),
+            whole((count, model)),
         ],
-        out_specs=[pl.BlockSpec((slots, half), lambda i: (0, i)), whole((slots, count))],
+        out_specs=[pl.BlockSpec((slots, model), lambda i: (0, i)), whole((slots, count))],
         out_shape=(shape((slots, 2 * model)), shape((slots, count))),
         scratch_shapes=[pltpu.VMEM((slots, 1), F32)],
         compiler_params=params(58),
@@ -255,11 +257,18 @@
     slots_of_ring = [(half_way, 0)] + [(k, s) for k in range(half_way - 1, 0, -1) for s in (1, 0)]
     def rows_back(after):
         return pl.pallas_call(
-            functools.partial(back_kernel, width),
-            in_specs=[*[resident] * 6, anywhere],
-            out_specs=[resident] * 2,
+            back_kernel,
+            grid=(groups,),
+            in_specs=[
+                *[resident] * 3,
+                pl.BlockSpec((hid, width), lambda i: (0, i)),
+                pl.BlockSpec((width, hid), lambda i: (i, 0)),
+                pl.BlockSpec((width, hid), lambda i: (i, 0)),
+                anywhere,
+            ],
+            out_specs=[pl.BlockSpec((slots, 2 * width), lambda i: (0, i)), whole((8, 128))],
             out_shape=(shape((slots, 2 * model)), shape((8, 128), F32)),
-            compiler_params=params(),
+            compiler_params=params(50),
             cost_estimate=SHORT,
             name="rows_back",
         )(hidden, gate_pre, up_pre, w_down, w_gate, w_up, after)
@@ -270,7 +279,7 @@
         held = came.get((k, swapped), ())
         part_a, part_b = chain_call(step_a, step_b, BF16, held, f"chain_sum_{number}", after)
         after = (part_a,)
-        if number == 2:
+        if number == 1:
             going_back, token = rows_back(part_a)
             after = (token,)
         ring_a, ring_b = (down_ring, up_ring) if swapped else (up_ring, down_ring)
@@ -279,15 +288,14 @@
     back = exchange(going_back)
 
     layer_out, token_grad, gates_grad_t = pl.pallas_call(
-        functools.partial(combine_kernel, capacity),
+        functools.partial(combine_kernel, capacity, width),
         grid=(2,),
         in_specs=[
             whole((top, count)),
             whole((top, count)),
             whole((slots, count)),
             pl.BlockSpec((count, half), lambda i: (0, i)),
-            pl.BlockSpec((slots, half), lambda i: (0, i)),
-            pl.BlockSpec((slots, half), lambda i: (0, 2 + i)),
+            pl.BlockSpec((slots, model), lambda i: (0, i)),
         ],
         out_specs=[
             pl.BlockSpec((count, half), lambda i: (0, i)),
@@ -295,21 +303,21 @@
             whole((top, count)),
         ],
         out_shape=(shape((count, model)), shape((count, model)), shape((top, count), F32)),
-        scratch_shapes=[pltpu.VMEM((slots, count), BF16)] * 2 + [pltpu.VMEM((slots, 1), F32)],
-        compiler_params=params(),
+        scratch_shapes=[pltpu.VMEM((count, slots), BF16)] * 3 + [pltpu.VMEM((slots, 1), F32)],
+        compiler_params=params(40),
         cost_estimate=cost(8 * slots * count * model, 4 * slots * model),
         name="combine",
-    )(routes_t, gates_t, place, out_grad, back, back)
-
-    own_a, own_b = chain_call(0, 0, F32, came[0, 1], "chain_sum_own", (*after, token_grad))
+    )(routes_t, gates_t, place, out_grad, back)
+
+    own_a, own_b = chain_call(0, 0, F32, came[0, 1], "chain_sum_own", after)
     gate_grad, up_grad, down_grad = pl.pallas_call(
         last_kernel,
-        in_specs=[resident] * 4,
+        in_specs=[*[resident] * 4, anywhere],
         out_shape=(shape((width, hid), F32), shape((width, hid), F32), shape((hid, width), F32)),
         compiler_params=params(),
         cost_estimate=SHORT,
         name="chain_sum_last",
-    )(own_a, own_b, *came[0, 0])
+    )(own_a, own_b, *came[0, 0], gates_grad_t)
     return (layer_out, token_grad, gates_grad_t.T, gate_grad[None], up_grad[None], down_grad[None])
 
 

time: 180 us -> 181 us (level)
  Pallas kernels: 45.6 us -> 50.3 us
  waiting for transfers between devices: 91.2 us -> 87.7 us
    all_to_all x2, waiting for transfers between devices: 61.4 us -> 51.4 us  [exchange(): return lax.all_to_all(wide, 'expert', 0, 0, tiled=True).reshape(array.shape)]
    pallas_call x4, Pallas kernels: 17 us -> 22.5 us  [the longest x1 10.7 us: rows_back(): pl.pallas_call(back_kernel, grid=(groups,), in_specs=[*[resident] * 3, pl...]
    ppermute x7, waiting for transfers between devices: 21.5 us -> 25.9 us  [local(): lax.ppermute(part_a, 'dp', ring_a)]
    ppermute x7, starting transfers between devices: 7.02 us -> 10.5 us  [local(): lax.ppermute(part_a, 'dp', ring_a)]
    ppermute x7, starting transfers between devices: 15.8 us -> 13 us  [local(): lax.ppermute(part_b, 'dp', ring_b)]
    ppermute x7, waiting for transfers between devices: 8.3 us -> 10.5 us  [local(): lax.ppermute(part_b, 'dp', ring_b)]
    unnamed x24 -> x18, local copies, waits for them, and re-layouts: 4.12 us -> 2.98 us
  transfers between devices with their start and end apart: 16 -> 16, of which waited for: 7 -> 9; matrix products, arithmetic and copies ran while one was open for 0% -> 0% of each run, Pallas kernels for 15% -> 17%
where the time goes in v6:
time: 181 us; the launch traced here: 180 us
  waiting for transfers between devices  87.7 us (48%)
  Pallas kernels  50.3 us (28%)
  starting transfers between devices  38 us (21%)
  local copies, waits for them, and re-layouts  2.98 us (2%)
    all_to_all x2, waiting for transfers between devices, exchange(): return lax.all_to_all(wide, 'expert', 0, 0, tiled=True).reshape(array.shape)  51.4 us
    ppermute x7, waiting for transfers between devices, local(): lax.ppermute(part_a, 'dp', ring_a)  25.9 us
    pallas_call x8, Pallas kernels, chain_call(): pl.pallas_call(functools.partial(link_kernel, bool(held)), grid_spec=pltp...  18.6 us
    all_to_all x2, starting transfers between devices, exchange(): return lax.all_to_all(wide, 'expert', 0, 0, tiled=True).reshape(array.shape)  14.5 us
    ppermute x7, starting transfers between devices, local(): lax.ppermute(part_b, 'dp', ring_b)  13 us
    pallas_call x1, Pallas kernels, rows_back(): pl.pallas_call(back_kernel, grid=(groups,), in_specs=[*[resident] * 3, pl...  10.7 us
    ppermute x7, waiting for transfers between devices, local(): lax.ppermute(part_b, 'dp', ring_b)  10.5 us
    ppermute x7, starting transfers between devices, local(): lax.ppermute(part_a, 'dp', ring_a)  10.5 us
  transfers between devices with their start and end apart: 16, of which 9 were waited for; matrix products, arithmetic and copies ran while one was open for 0% of the time, Pallas kernels for 17%

profile of v6, /device:TPU:2, one launch (start us, length us, event | category | flops | bytes accessed | tf_op | source)
XLA Modules:
  0.0 179.9 jit_solution(12155567531425726016)
XLA Ops:
  0.6 4.2 %dispatch.1 = (bf16[512,4096]{1,0:T(8,128)(2,1)}, bf16[512,48]{1,0:T(8,128)(2,1)}) custom-call(s32[8,48]{1,0:T(8,128)} %bitcast.14, f32[8,48]{1,0:T(8,128)} %bitcast.16, bf16[48,2048]{1,0:T(8,128)(2,1)} %tokens_ref.1, bf16[48,2048]{1,0:T(8,128)(2,1)} %grads_ref.3), custom_call_target="tpu_custom_call" | custom-call | flops 201326592 | bytes 4194304 | tf_op jit(solution)/shard_map/dispatch/pallas_call | solution.py:190
  4.8 7.7 %all-to-all-start = ((bf16[32,16,4096]{2,1,0:T(8,128)(2,1)}), bf16[32,16,4096]{2,1,0:T(8,128)(2,1)}, u32[]{:S(2)}, u32[]{:S(2)}) async-start(bf16[32,16,4096]{2,1,0:T(8,128)(2,1)} %bitcast.20), calls=%async_computation | async-start | bytes 8388608 | tf_op jit(solution)/shard_map/all_to_all | solution.py:209
  12.5 51.4 %all-to-all-done = bf16[32,16,4096]{2,1,0:T(8,128)(2,1)} async-done(((bf16[32,16,4096]{2,1,0:T(8,128)(2,1)}), bf16[32,16,4096]{2,1,0:T(8,128)(2,1)}, u32[]{:S(2)}, u32[]{:S(2)}) %all-to-all-start) | async-done | bytes 4194336 | tf_op jit(solution)/shard_map/all_to_all | solution.py:209
  63.9 9.3 %expert.1 = (bf16[512,768]{1,0:T(8,128)(2,1)S(1)}, bf16[768,512]{1,0:T(8,128)(2,1)S(1)}, bf16[512,768]{1,0:T(8,128)(2,1)S(1)}, bf16[512,768]{1,0:T(8,128)(2,1)S(1)}) custom-call(bf16[512,4096]{1,0:T(8,128)(2,1)} %bitcast.3.rows_ref.grads_ref.refs_0_.refs_1_.refs_2_, bf16[512,4096]{1,0:T(8,128)(2,1)} %bitcast.3.rows_ref.grads_ref.refs_0_.refs_1_.refs_2_, ...), custom_call_target="tpu_custom_call" | custom-call | flops 4831838208 | bytes 16777216 | tf_op jit(solution)/shard_map/expert/pallas_call | solution.py:212
  73.2 0.0 copy-start.7
  73.2 0.0 copy-start
  73.2 3.3 %chain_sum_0.1 = (bf16[4,256,256]{2,1,0:T(8,128)(2,1)}, bf16[5,256,256]{2,1,0:T(8,128)(2,1)}) custom-call(s32[1]{0:T(128)} %bitcast.7._, bf16[512,4096]{1,0:T(8,128)(2,1)} %bitcast.3.rows_ref.grads_ref.refs_0_.refs_1_.refs_2_, bf16[512,4096]{1,0:T(8,128)(2,1)} %bitcast.3.rows_ref.grads_ref.refs_0_.refs_1_.refs_2_, ...), custom_call_target="tpu_custom_call" | custom-call | flops 20000000000 | bytes 62914560 | tf_op jit(solution)/shard_map/chain_sum_0/pallas_call | solution.py:234
  76.5 1.9 %collective-permute-start.2 = (bf16[4,256,256]{2,1,0:T(8,128)(2,1)}, bf16[4,256,256]{2,1,0:T(8,128)(2,1)}, u32[]{:S(2)}, u32[]{:S(2)}) collective-permute-start(bf16[4,256,256]{2,1,0:T(8,128)(2,1)} %get-tuple-element.42.refs_6_), channel_id=1, source_target_pairs={{0,1},{1,2},{2,3},{3,4},{4,5},{5,6},{6,7},{7,0},{8,9},{9,10},{10,1... | collective-permute-start | bytes 1572872 | tf_op jit(solution)/shard_map/ppermute | solution.py:286
  78.4 4.0 %collective-permute-start.3 = (bf16[5,256,256]{2,1,0:T(8,128)(2,1)}, bf16[5,256,256]{2,1,0:T(8,128)(2,1)}, u32[]{:S(2)}, u32[]{:S(2)}) collective-permute-start(bf16[5,256,256]{2,1,0:T(8,128)(2,1)} %get-tuple-element.49), channel_id=1, source_target_pairs={{0,7},{1,0},{2,1},{3,2},{4,3},{5,4},{6,5},{7,6},{8,15},{9,8},{10,9... | collective-permute-start | bytes 1966088 | tf_op jit(solution)/shard_map/ppermute | solution.py:286
  82.4 0.0 copy-done.7
  82.4 1.9 %chain_sum_1.1 = (bf16[4,256,256]{2,1,0:T(8,128)(2,1)S(1)}, bf16[5,256,256]{2,1,0:T(8,128)(2,1)S(1)}) custom-call(s32[1]{0:T(128)} %bitcast.7._, bf16[512,4096]{1,0:T(8,128)(2,1)} %bitcast.3.rows_ref.grads_ref.refs_0_.refs_1_.refs_2_, bf16[512,4096]{1,0:T(8,128)(2,1)} %bitcast.3.rows_ref.grads_ref.refs_0_.refs_1_.refs_2_, ...), custom_call_target="tpu_custom_call" | custom-call | flops 20000000000 | bytes 62914560 | tf_op jit(solution)/shard_map/chain_sum_1/pallas_call | solution.py:234
  84.3 2.1 %collective-permute-start = (bf16[4,256,256]{2,1,0:T(8,128)(2,1)S(1)}, bf16[4,256,256]{2,1,0:T(8,128)(2,1)}, u32[]{:S(2)}, u32[]{:S(2)}) collective-permute-start(bf16[4,256,256]{2,1,0:T(8,128)(2,1)S(1)} %get-tuple-element.43._), channel_id=1, source_target_pairs={{0,7},{1,0},{2,1},{3,2},{4,3},{5,4},{6,5},{7,6},{8,15},{9,8},{10,9... | collective-permute-start | bytes 1572872 | tf_op jit(solution)/shard_map/ppermute | solution.py:286
  86.4 10.7 %rows_back.1 = (bf16[512,4096]{1,0:T(8,128)(2,1)}, f32[8,128]{1,0:T(8,128)S(1)}) custom-call(bf16[512,768]{1,0:T(8,128)(2,1)S(1)} %get-tuple-element.38.hidden_ref, bf16[512,768]{1,0:T(8,128)(2,1)S(1)} %get-tuple-element.39.refs_3_.gate_pre_ref, bf16[512,768]{1,0:T(8,128)(2,1)S(1)} %get-tuple-element.40.refs_4_.up_pre_ref, bf16[768,2048]{1,0:T(8,128)(2,1)} %bitcast.26, ...), custom_call_target="tpu_custom_call" | custom-call | flops 1 | bytes 1 | tf_op jit(solution)/shard_map/rows_back/pallas_call | solution.py:259
  97.1 0.0 collective-permute-start.1
  97.2 6.9 %all-to-all-start.1 = ((bf16[32,16,4096]{2,1,0:T(8,128)(2,1)}), bf16[32,16,4096]{2,1,0:T(8,128)(2,1)}, u32[]{:S(2)}, u32[]{:S(2)}) async-start(bf16[32,16,4096]{2,1,0:T(8,128)(2,1)} %bitcast.19), calls=%async_computation.1 | async-start | bytes 8388608 | tf_op jit(solution)/shard_map/all_to_all | solution.py:209
  104.0 0.0 collective-permute-done.2.refs_6_
  104.0 0.0 collective-permute-done.3.refs_7_
  104.0 0.0 copy-start.8
  104.1 1.1 copy-done.8
  105.2 2.3 %chain_sum_2.1 = (bf16[4,256,256]{2,1,0:T(8,128)(2,1)S(1)}, bf16[5,256,256]{2,1,0:T(8,128)(2,1)S(1)}) custom-call(s32[1]{0:T(128)} %bitcast.7._, bf16[512,4096]{1,0:T(8,128)(2,1)} %bitcast.3.rows_ref.grads_ref.refs_0_.refs_1_.refs_2_, bf16[512,4096]{1,0:T(8,128)(2,1)} %bitcast.3.rows_ref.grads_ref.refs_0_.refs_1_.refs_2_, ...), custom_call_target="tpu_custom_call" | custom-call | flops 20000000000 | bytes 62914560 | tf_op jit(solution)/shard_map/chain_sum_2/pallas_call | solution.py:234
  107.5 3.3 %collective-permute-start.7 = (bf16[5,256,256]{2,1,0:T(8,128)(2,1)S(1)}, bf16[5,256,256]{2,1,0:T(8,128)(2,1)S(1)}, u32[]{:S(2)}, u32[]{:S(2)}) collective-permute-start(bf16[5,256,256]{2,1,0:T(8,128)(2,1)S(1)} %get-tuple-element.54), channel_id=1, source_target_pairs={{0,7},{1,0},{2,1},{3,2},{4,3},{5,4},{6,5},{7,6},{8,15},{9,8},{10,9... | collective-permute-start | bytes 1966088 | tf_op jit(solution)/shard_map/ppermute | solution.py:286
  110.8 0.0 collective-permute-start.6
  110.8 0.0 collective-permute-done.refs_6_
  110.8 3.0 %collective-permute-done.1.refs_7_ = bf16[5,256,256]{2,1,0:T(8,128)(2,1)} collective-permute-done((bf16[5,256,256]{2,1,0:T(8,128)(2,1)S(1)}, bf16[5,256,256]{2,1,0:T(8,128)(2,1)}, u32[]{:S(2)}, u32[]{:S(2)}) %collective-permute-start.1) | collective-permute-done | bytes 655392 | tf_op jit(solution)/shard_map/ppermute | solution.py:286
  113.8 2.3 %chain_sum_3.1 = (bf16[4,256,256]{2,1,0:T(8,128)(2,1)S(1)}, bf16[5,256,256]{2,1,0:T(8,128)(2,1)S(1)}) custom-call(s32[1]{0:T(128)} %bitcast.7._, bf16[512,4096]{1,0:T(8,128)(2,1)} %bitcast.3.rows_ref.grads_ref.refs_0_.refs_1_.refs_2_, bf16[512,4096]{1,0:T(8,128)(2,1)} %bitcast.3.rows_ref.grads_ref.refs_0_.refs_1_.refs_2_, ...), custom_call_target="tpu_custom_call" | custom-call | flops 20000000000 | bytes 62914560 | tf_op jit(solution)/shard_map/chain_sum_3/pallas_call | solution.py:234
  116.2 0.1 collective-permute-start.5
  116.2 3.2 %collective-permute-start.4 = (bf16[4,256,256]{2,1,0:T(8,128)(2,1)S(1)}, bf16[4,256,256]{2,1,0:T(8,128)(2,1)S(1)}, u32[]{:S(2)}, u32[]{:S(2)}) collective-permute-start(bf16[4,256,256]{2,1,0:T(8,128)(2,1)S(1)} %get-tuple-element.52.refs_8_), channel_id=1, source_target_pairs={{0,7},{1,0},{2,1},{3,2},{4,3},{5,4},{6,5},{7,6},{8,15},{9,8},{10,9... | collective-permute-start | bytes 1572872 | tf_op jit(solution)/shard_map/ppermute | solution.py:286
  119.5 7.4 %collective-permute-done.6.refs_6_ = bf16[4,256,256]{2,1,0:T(8,128)(2,1)S(1)} collective-permute-done((bf16[4,256,256]{2,1,0:T(8,128)(2,1)S(1)}, bf16[4,256,256]{2,1,0:T(8,128)(2,1)S(1)}, u32[]{:S(2)}, u32[]{:S(2)}) %collective-permute-start.6) | collective-permute-done | bytes 524320 | tf_op jit(solution)/shard_map/ppermute | solution.py:286
  126.8 0.0 collective-permute-done.7.refs_7_
  126.8 1.9 %chain_sum_4.1 = (bf16[4,256,256]{2,1,0:T(8,128)(2,1)S(1)}, bf16[5,256,256]{2,1,0:T(8,128)(2,1)S(1)}) custom-call(s32[1]{0:T(128)} %bitcast.7._, bf16[512,4096]{1,0:T(8,128)(2,1)} %bitcast.3.rows_ref.grads_ref.refs_0_.refs_1_.refs_2_, bf16[512,4096]{1,0:T(8,128)(2,1)} %bitcast.3.rows_ref.grads_ref.refs_0_.refs_1_.refs_2_, ...), custom_call_target="tpu_custom_call" | custom-call | flops 20000000000 | bytes 62914560 | tf_op jit(solution)/shard_map/chain_sum_4/pallas_call | solution.py:234
  128.8 2.8 %collective-permute-start.11 = (bf16[5,256,256]{2,1,0:T(8,128)(2,1)S(1)}, bf16[5,256,256]{2,1,0:T(8,128)(2,1)S(1)}, u32[]{:S(2)}, u32[]{:S(2)}) collective-permute-start(bf16[5,256,256]{2,1,0:T(8,128)(2,1)S(1)} %get-tuple-element.58), channel_id=1, source_target_pairs={{0,7},{1,0},{2,1},{3,2},{4,3},{5,4},{6,5},{7,6},{8,15},{9,8},{10,9... | collective-permute-start | bytes 1966088 | tf_op jit(solution)/shard_map/ppermute | solution.py:286
  131.6 0.0 collective-permute-start.10
  131.6 5.5 %collective-permute-done.4.refs_6_ = bf16[4,256,256]{2,1,0:T(8,128)(2,1)S(1)} collective-permute-done((bf16[4,256,256]{2,1,0:T(8,128)(2,1)S(1)}, bf16[4,256,256]{2,1,0:T(8,128)(2,1)S(1)}, u32[]{:S(2)}, u32[]{:S(2)}) %collective-permute-start.4) | collective-permute-done | bytes 524320 | tf_op jit(solution)/shard_map/ppermute | solution.py:286
  137.1 3.7 %collective-permute-done.5.refs_7_ = bf16[5,256,256]{2,1,0:T(8,128)(2,1)S(1)} collective-permute-done((bf16[5,256,256]{2,1,0:T(8,128)(2,1)S(1)}, bf16[5,256,256]{2,1,0:T(8,128)(2,1)S(1)}, u32[]{:S(2)}, u32[]{:S(2)}) %collective-permute-start.5) | collective-permute-done | bytes 655392 | tf_op jit(solution)/shard_map/ppermute | solution.py:286
  140.9 1.9 %chain_sum_5.1 = (bf16[4,256,256]{2,1,0:T(8,128)(2,1)S(1)}, bf16[5,256,256]{2,1,0:T(8,128)(2,1)S(1)}) custom-call(s32[1]{0:T(128)} %bitcast.7._, bf16[512,4096]{1,0:T(8,128)(2,1)} %bitcast.3.rows_ref.grads_ref.refs_0_.refs_1_.refs_2_, bf16[512,4096]{1,0:T(8,128)(2,1)} %bitcast.3.rows_ref.grads_ref.refs_0_.refs_1_.refs_2_, ...), custom_call_target="tpu_custom_call" | custom-call | flops 20000000000 | bytes 62914560 | tf_op jit(solution)/shard_map/chain_sum_5/pallas_call | solution.py:234
  142.8 0.1 collective-permute-start.9
  142.9 3.2 %collective-permute-start.8 = (bf16[4,256,256]{2,1,0:T(8,128)(2,1)S(1)}, bf16[4,256,256]{2,1,0:T(8,128)(2,1)S(1)}, u32[]{:S(2)}, u32[]{:S(2)}) collective-permute-start(bf16[4,256,256]{2,1,0:T(8,128)(2,1)S(1)} %get-tuple-element.56.refs_8_), channel_id=1, source_target_pairs={{0,7},{1,0},{2,1},{3,2},{4,3},{5,4},{6,5},{7,6},{8,15},{9,8},{10,9... | collective-permute-start | bytes 1572872 | tf_op jit(solution)/shard_map/ppermute | solution.py:286
  146.1 6.0 %collective-permute-done.10.refs_6_ = bf16[4,256,256]{2,1,0:T(8,128)(2,1)S(1)} collective-permute-done((bf16[4,256,256]{2,1,0:T(8,128)(2,1)S(1)}, bf16[4,256,256]{2,1,0:T(8,128)(2,1)S(1)}, u32[]{:S(2)}, u32[]{:S(2)}) %collective-permute-start.10) | collective-permute-done | bytes 524320 | tf_op jit(solution)/shard_map/ppermute | solution.py:286
  152.1 0.0 collective-permute-done.11.refs_7_
  152.1 0.0 copy-done
  152.1 2.8 %chain_sum_6.1 = (bf16[4,256,256]{2,1,0:T(8,128)(2,1)}, bf16[5,256,256]{2,1,0:T(8,128)(2,1)}) custom-call(s32[1]{0:T(128)} %bitcast.7._, bf16[512,4096]{1,0:T(8,128)(2,1)} %bitcast.3.rows_ref.grads_ref.refs_0_.refs_1_.refs_2_, bf16[512,4096]{1,0:T(8,128)(2,1)} %bitcast.3.rows_ref.grads_ref.refs_0_.refs_1_.refs_2_, ...), custom_call_target="tpu_custom_call" | custom-call | flops 20000000000 | bytes 62914560 | tf_op jit(solution)/shard_map/chain_sum_6/pallas_call | solution.py:234
  154.9 2.8 %collective-permute-start.13 = (bf16[5,256,256]{2,1,0:T(8,128)(2,1)}, bf16[5,256,256]{2,1,0:T(8,128)(2,1)}, u32[]{:S(2)}, u32[]{:S(2)}) collective-permute-start(bf16[5,256,256]{2,1,0:T(8,128)(2,1)} %get-tuple-element.62), channel_id=1, source_target_pairs={{0,7},{1,0},{2,1},{3,2},{4,3},{5,4},{6,5},{7,6},{8,15},{9,8},{10,9... | collective-permute-start | bytes 1966088 | tf_op jit(solution)/shard_map/ppermute | solution.py:286
  157.7 0.0 collective-permute-start.12
  157.7 4.7 %collective-permute-done.8.refs_6_ = bf16[4,256,256]{2,1,0:T(8,128)(2,1)S(1)} collective-permute-done((bf16[4,256,256]{2,1,0:T(8,128)(2,1)S(1)}, bf16[4,256,256]{2,1,0:T(8,128)(2,1)S(1)}, u32[]{:S(2)}, u32[]{:S(2)}) %collective-permute-start.8) | collective-permute-done | bytes 524320 | tf_op jit(solution)/shard_map/ppermute | solution.py:286
  162.4 3.7 %collective-permute-done.9.refs_7_ = bf16[5,256,256]{2,1,0:T(8,128)(2,1)S(1)} collective-permute-done((bf16[5,256,256]{2,1,0:T(8,128)(2,1)S(1)}, bf16[5,256,256]{2,1,0:T(8,128)(2,1)S(1)}, u32[]{:S(2)}, u32[]{:S(2)}) %collective-permute-start.9) | collective-permute-done | bytes 655392 | tf_op jit(solution)/shard_map/ppermute | solution.py:286
  166.2 0.0 copy-start.1
  166.2 1.1 copy-done.1
  167.3 0.0 copy-start.2
  167.3 0.0 copy-start.3
  167.3 0.0 copy-start.4
  167.3 0.0 copy-start.5
  167.3 2.0 %chain_sum_own.1 = (f32[4,256,256]{2,1,0:T(8,128)S(1)}, f32[5,256,256]{2,1,0:T(8,128)S(1)}) custom-call(s32[1]{0:T(128)} %bitcast.7._, bf16[512,4096]{1,0:T(8,128)(2,1)} %bitcast.3.rows_ref.grads_ref.refs_0_.refs_1_.refs_2_, bf16[512,4096]{1,0:T(8,128)(2,1)} %bitcast.3.rows_ref.grads_ref.refs_0_.refs_1_.refs_2_, ...), custom_call_target="tpu_custom_call" | custom-call | flops 20000000000 | bytes 62914560 | tf_op jit(solution)/shard_map/chain_sum_own/pallas_call | solution.py:234
  169.3 0.0 all-to-all-done.1
  169.3 0.0 copy-done.2
  169.3 0.0 copy-done.3
  169.3 0.0 copy-done.4
  169.3 0.0 copy-done.5
  169.4 4.7 %combine.1 = (bf16[48,2048]{1,0:T(8,128)(2,1)}, bf16[48,2048]{1,0:T(8,128)(2,1)}, f32[8,48]{1,0:T(8,128)}) custom-call(s32[8,48]{1,0:T(8,128)S(1)} %bitcast.15, f32[8,48]{1,0:T(8,128)S(1)} %bitcast.17, bf16[512,48]{1,0:T(8,128)(2,1)S(1)} %copy-done.3, bf16[48,2048]{1,0:T(8,128)(2,1)S(1)} %copy-done.2, bf16[512,4096]{1,0:T(8,128)(2,1)} %bitcast.9.back_ref), custom_call_target="tpu_custom_call" | custom-call | flops 402653184 | bytes 4194304 | tf_op jit(solution)/shard_map/combine/pallas_call | solution.py:290
  174.1 2.3 %collective-permute-done.12.a0 = bf16[4,256,256]{2,1,0:T(8,128)(2,1)} collective-permute-done((bf16[4,256,256]{2,1,0:T(8,128)(2,1)}, bf16[4,256,256]{2,1,0:T(8,128)(2,1)}, u32[]{:S(2)}, u32[]{:S(2)}) %collective-permute-start.12) | collective-permute-done | bytes 524320 | tf_op jit(solution)/shard_map/ppermute | solution.py:286
  176.4 0.0 collective-permute-done.13.b0
  176.4 0.0 copy-start.6
  176.4 0.7 copy-done.6
  177.1 2.8 %chain_sum_last.1 = (f32[256,768]{1,0:T(8,128)}, f32[256,768]{1,0:T(8,128)}, f32[768,256]{1,0:T(8,128)}) custom-call(f32[4,256,256]{2,1,0:T(8,128)S(1)} %get-tuple-element.60.own_a, f32[5,256,256]{2,1,0:T(8,128)S(1)} %get-tuple-element.61.own_b, bf16[4,256,256]{2,1,0:T(8,128)(2,1)} %collective-permute-done.12.a0, ...), custom_call_target="tpu_custom_call" | custom-call | flops 1 | bytes 1 | tf_op jit(solution)/shard_map/chain_sum_last/pallas_call | solution.py:313
Async XLA Ops:
  4.8 59.1 %all-to-all-start = ((bf16[32,16,4096]{2,1,0:T(8,128)(2,1)}), bf16[32,16,4096]{2,1,0:T(8,128)(2,1)}, u32[]{:S(2)}, u32[]{:S(2)}) async-start(bf16[32,16,4096]{2,1,0:T(8,128)(2,1)} %bitcast.20), calls=%async_computation | async-start | bytes 8388608 | tf_op jit(solution)/shard_map/all_to_all | solution.py:209
  73.2 9.2 %copy-start.7 = (bf16[768,512]{1,0:T(8,128)(2,1)}, bf16[768,512]{1,0:T(8,128)(2,1)S(1)}, u32[]{:S(2)}) copy-start(bf16[768,512]{1,0:T(8,128)(2,1)S(1)} %get-tuple-element.41.refs_5_) | copy-start | bytes 2359300
  73.2 78.9 %copy-start = (bf16[512,768]{1,0:T(8,128)(2,1)}, bf16[512,768]{1,0:T(8,128)(2,1)S(1)}, u32[]{:S(2)}) copy-start(bf16[512,768]{1,0:T(8,128)(2,1)S(1)} %get-tuple-element.40.refs_4_.up_pre_ref) | copy-start | bytes 2359300
  76.5 27.5 %collective-permute-start.2 = (bf16[4,256,256]{2,1,0:T(8,128)(2,1)}, bf16[4,256,256]{2,1,0:T(8,128)(2,1)}, u32[]{:S(2)}, u32[]{:S(2)}) collective-permute-start(bf16[4,256,256]{2,1,0:T(8,128)(2,1)} %get-tuple-element.42.refs_6_), channel_id=1, source_target_pairs={{0,1},{1,2},{2,3},{3,4},{4,5},{5,6},{6,7},{7,0},{8,9},{9,10},{10,1... | collective-permute-start | bytes 1572872 | tf_op jit(solution)/shard_map/ppermute | solution.py:286
  78.4 25.6 %collective-permute-start.3 = (bf16[5,256,256]{2,1,0:T(8,128)(2,1)}, bf16[5,256,256]{2,1,0:T(8,128)(2,1)}, u32[]{:S(2)}, u32[]{:S(2)}) collective-permute-start(bf16[5,256,256]{2,1,0:T(8,128)(2,1)} %get-tuple-element.49), channel_id=1, source_target_pairs={{0,7},{1,0},{2,1},{3,2},{4,3},{5,4},{6,5},{7,6},{8,15},{9,8},{10,9... | collective-permute-start | bytes 1966088 | tf_op jit(solution)/shard_map/ppermute | solution.py:286
  84.3 26.5 %collective-permute-start = (bf16[4,256,256]{2,1,0:T(8,128)(2,1)S(1)}, bf16[4,256,256]{2,1,0:T(8,128)(2,1)}, u32[]{:S(2)}, u32[]{:S(2)}) collective-permute-start(bf16[4,256,256]{2,1,0:T(8,128)(2,1)S(1)} %get-tuple-element.43._), channel_id=1, source_target_pairs={{0,7},{1,0},{2,1},{3,2},{4,3},{5,4},{6,5},{7,6},{8,15},{9,8},{10,9... | collective-permute-start | bytes 1572872 | tf_op jit(solution)/shard_map/ppermute | solution.py:286
  97.1 16.7 %collective-permute-start.1 = (bf16[5,256,256]{2,1,0:T(8,128)(2,1)S(1)}, bf16[5,256,256]{2,1,0:T(8,128)(2,1)}, u32[]{:S(2)}, u32[]{:S(2)}) collective-permute-start(bf16[5,256,256]{2,1,0:T(8,128)(2,1)S(1)} %get-tuple-element.48), channel_id=1, source_target_pairs={{0,1},{1,2},{2,3},{3,4},{4,5},{5,6},{6,7},{7,0},{8,9},{9,10},{10,1... | collective-permute-start | bytes 1966088 | tf_op jit(solution)/shard_map/ppermute | solution.py:286
  97.2 72.2 %all-to-all-start.1 = ((bf16[32,16,4096]{2,1,0:T(8,128)(2,1)}), bf16[32,16,4096]{2,1,0:T(8,128)(2,1)}, u32[]{:S(2)}, u32[]{:S(2)}) async-start(bf16[32,16,4096]{2,1,0:T(8,128)(2,1)} %bitcast.19), calls=%async_computation.1 | async-start | bytes 8388608 | tf_op jit(solution)/shard_map/all_to_all | solution.py:209
  104.0 1.1 copy-start.8
  107.5 19.3 %collective-permute-start.7 = (bf16[5,256,256]{2,1,0:T(8,128)(2,1)S(1)}, bf16[5,256,256]{2,1,0:T(8,128)(2,1)S(1)}, u32[]{:S(2)}, u32[]{:S(2)}) collective-permute-start(bf16[5,256,256]{2,1,0:T(8,128)(2,1)S(1)} %get-tuple-element.54), channel_id=1, source_target_pairs={{0,7},{1,0},{2,1},{3,2},{4,3},{5,4},{6,5},{7,6},{8,15},{9,8},{10,9... | collective-permute-start | bytes 1966088 | tf_op jit(solution)/shard_map/ppermute | solution.py:286
  110.8 16.0 %collective-permute-start.6 = (bf16[4,256,256]{2,1,0:T(8,128)(2,1)S(1)}, bf16[4,256,256]{2,1,0:T(8,128)(2,1)S(1)}, u32[]{:S(2)}, u32[]{:S(2)}) collective-permute-start(bf16[4,256,256]{2,1,0:T(8,128)(2,1)S(1)} %get-tuple-element.51.refs_8_), channel_id=1, source_target_pairs={{0,1},{1,2},{2,3},{3,4},{4,5},{5,6},{6,7},{7,0},{8,9},{9,10},{10,1... | collective-permute-start | bytes 1572872 | tf_op jit(solution)/shard_map/ppermute | solution.py:286
  116.2 24.7 %collective-permute-start.5 = (bf16[5,256,256]{2,1,0:T(8,128)(2,1)S(1)}, bf16[5,256,256]{2,1,0:T(8,128)(2,1)S(1)}, u32[]{:S(2)}, u32[]{:S(2)}) collective-permute-start(bf16[5,256,256]{2,1,0:T(8,128)(2,1)S(1)} %get-tuple-element.53), channel_id=1, source_target_pairs={{0,1},{1,2},{2,3},{3,4},{4,5},{5,6},{6,7},{7,0},{8,9},{9,10},{10,1... | collective-permute-start | bytes 1966088 | tf_op jit(solution)/shard_map/ppermute | solution.py:286
  116.2 20.9 %collective-permute-start.4 = (bf16[4,256,256]{2,1,0:T(8,128)(2,1)S(1)}, bf16[4,256,256]{2,1,0:T(8,128)(2,1)S(1)}, u32[]{:S(2)}, u32[]{:S(2)}) collective-permute-start(bf16[4,256,256]{2,1,0:T(8,128)(2,1)S(1)} %get-tuple-element.52.refs_8_), channel_id=1, source_target_pairs={{0,7},{1,0},{2,1},{3,2},{4,3},{5,4},{6,5},{7,6},{8,15},{9,8},{10,9... | collective-permute-start | bytes 1572872 | tf_op jit(solution)/shard_map/ppermute | solution.py:286
  128.8 23.3 %collective-permute-start.11 = (bf16[5,256,256]{2,1,0:T(8,128)(2,1)S(1)}, bf16[5,256,256]{2,1,0:T(8,128)(2,1)S(1)}, u32[]{:S(2)}, u32[]{:S(2)}) collective-permute-start(bf16[5,256,256]{2,1,0:T(8,128)(2,1)S(1)} %get-tuple-element.58), channel_id=1, source_target_pairs={{0,7},{1,0},{2,1},{3,2},{4,3},{5,4},{6,5},{7,6},{8,15},{9,8},{10,9... | collective-permute-start | bytes 1966088 | tf_op jit(solution)/shard_map/ppermute | solution.py:286
  131.6 20.5 %collective-permute-start.10 = (bf16[4,256,256]{2,1,0:T(8,128)(2,1)S(1)}, bf16[4,256,256]{2,1,0:T(8,128)(2,1)S(1)}, u32[]{:S(2)}, u32[]{:S(2)}) collective-permute-start(bf16[4,256,256]{2,1,0:T(8,128)(2,1)S(1)} %get-tuple-element.55.refs_8_), channel_id=1, source_target_pairs={{0,1},{1,2},{2,3},{3,4},{4,5},{5,6},{6,7},{7,0},{8,9},{9,10},{10,1... | collective-permute-start | bytes 1572872 | tf_op jit(solution)/shard_map/ppermute | solution.py:286
  142.8 23.3 %collective-permute-start.9 = (bf16[5,256,256]{2,1,0:T(8,128)(2,1)S(1)}, bf16[5,256,256]{2,1,0:T(8,128)(2,1)S(1)}, u32[]{:S(2)}, u32[]{:S(2)}) collective-permute-start(bf16[5,256,256]{2,1,0:T(8,128)(2,1)S(1)} %get-tuple-element.57), channel_id=1, source_target_pairs={{0,1},{1,2},{2,3},{3,4},{4,5},{5,6},{6,7},{7,0},{8,9},{9,10},{10,1... | collective-permute-start | bytes 1966088 | tf_op jit(solution)/shard_map/ppermute | solution.py:286
  142.9 19.5 %collective-permute-start.8 = (bf16[4,256,256]{2,1,0:T(8,128)(2,1)S(1)}, bf16[4,256,256]{2,1,0:T(8,128)(2,1)S(1)}, u32[]{:S(2)}, u32[]{:S(2)}) collective-permute-start(bf16[4,256,256]{2,1,0:T(8,128)(2,1)S(1)} %get-tuple-element.56.refs_8_), channel_id=1, source_target_pairs={{0,7},{1,0},{2,1},{3,2},{4,3},{5,4},{6,5},{7,6},{8,15},{9,8},{10,9... | collective-permute-start | bytes 1572872 | tf_op jit(solution)/shard_map/ppermute | solution.py:286
  154.9 21.5 %collective-permute-start.13 = (bf16[5,256,256]{2,1,0:T(8,128)(2,1)}, bf16[5,256,256]{2,1,0:T(8,128)(2,1)}, u32[]{:S(2)}, u32[]{:S(2)}) collective-permute-start(bf16[5,256,256]{2,1,0:T(8,128)(2,1)} %get-tuple-element.62), channel_id=1, source_target_pairs={{0,7},{1,0},{2,1},{3,2},{4,3},{5,4},{6,5},{7,6},{8,15},{9,8},{10,9... | collective-permute-start | bytes 1966088 | tf_op jit(solution)/shard_map/ppermute | solution.py:286
  157.7 18.7 %collective-permute-start.12 = (bf16[4,256,256]{2,1,0:T(8,128)(2,1)}, bf16[4,256,256]{2,1,0:T(8,128)(2,1)}, u32[]{:S(2)}, u32[]{:S(2)}) collective-permute-start(bf16[4,256,256]{2,1,0:T(8,128)(2,1)} %get-tuple-element.59.refs_8_), channel_id=1, source_target_pairs={{0,1},{1,2},{2,3},{3,4},{4,5},{5,6},{6,7},{7,0},{8,9},{9,10},{10,1... | collective-permute-start | bytes 1572872 | tf_op jit(solution)/shard_map/ppermute | solution.py:286
  166.2 1.1 copy-start.1
  167.3 2.0 %copy-start.2 = (bf16[48,2048]{1,0:T(8,128)(2,1)S(1)}, bf16[48,2048]{1,0:T(8,128)(2,1)}, u32[]{:S(2)}) copy-start(bf16[48,2048]{1,0:T(8,128)(2,1)} %grads_ref.3) | copy-start | bytes 589828
  167.3 2.0 %copy-start.3 = (bf16[512,48]{1,0:T(8,128)(2,1)S(1)}, bf16[512,48]{1,0:T(8,128)(2,1)}, u32[]{:S(2)}) copy-start(bf16[512,48]{1,0:T(8,128)(2,1)} %get-tuple-element.36.place_ref) | copy-start | bytes 147460
  167.3 2.0 %copy-start.4 = (s32[48,8]{0,1:T(8,128)S(1)}, s32[48,8]{0,1:T(8,128)}, u32[]{:S(2)}) copy-start(s32[48,8]{0,1:T(8,128)} %param.8) | copy-start | bytes 4612
  167.3 2.0 %copy-start.5 = (f32[48,8]{0,1:T(8,128)S(1)}, f32[48,8]{0,1:T(8,128)}, u32[]{:S(2)}) copy-start(f32[48,8]{0,1:T(8,128)} %param.9) | copy-start | bytes 4612
  176.4 0.7 copy-start.6

commit v7 on v6

--- a/solution.py
+++ b/solution.py
@@ -121,12 +121,15 @@
         up_ref[:, (j + 1) * width : (j + 2) * width] = own_b[j] + b0[j].astype(F32)
 
 
-def back_kernel(hidden_ref, gate_pre_ref, up_pre_ref, down_ref, gate_ref, up_ref, _, back_ref, token_ref):
-    width = gate_ref.shape[0]
+def back_kernel(width, hidden_ref, gate_pre_ref, up_pre_ref, down_ref, gate_ref, up_ref, _, back_ref, token_ref):
     token_ref[...] = jnp.zeros_like(token_ref)
-    back_ref[:, :width] = dot(hidden_ref[...], down_ref[...]).astype(BF16)
-    row_grad = dot(gate_pre_ref[...], gate_ref[...], LAST) + dot(up_pre_ref[...], up_ref[...], LAST)
-    back_ref[:, width:] = row_grad.astype(BF16)
+    for j in range(back_ref.shape[1] // (2 * width)):
+        first = pl.program_id(0) * (back_ref.shape[1] // 2) + j * width
+        mine = pl.ds(pl.multiple_of(first, width), width)
+        at = 2 * j * width
+        back_ref[:, at : at + width] = dot(hidden_ref[...], down_ref[:, mine]).astype(BF16)
+        row_grad = dot(gate_pre_ref[...], gate_ref[mine, :], LAST) + dot(up_pre_ref[...], up_ref[mine, :], LAST)
+        back_ref[:, at + width : at + 2 * width] = row_grad.astype(BF16)
 
 
 def combine_kernel(
@@ -257,18 +260,12 @@
     slots_of_ring = [(half_way, 0)] + [(k, s) for k in range(half_way - 1, 0, -1) for s in (1, 0)]
     def rows_back(after):
         return pl.pallas_call(
-            back_kernel,
-            grid=(groups,),
-            in_specs=[
-                *[resident] * 3,
-                pl.BlockSpec((hid, width), lambda i: (0, i)),
-                pl.BlockSpec((width, hid), lambda i: (i, 0)),
-                pl.BlockSpec((width, hid), lambda i: (i, 0)),
-                anywhere,
-            ],
-            out_specs=[pl.BlockSpec((slots, 2 * width), lambda i: (0, i)), whole((8, 128))],
+            functools.partial(back_kernel, width),
+            grid=(groups // 2,),
+            in_specs=[*[resident] * 6, anywhere],
+            out_specs=[pl.BlockSpec((slots, 4 * width), lambda i: (0, i)), whole((8, 128))],
             out_shape=(shape((slots, 2 * model)), shape((8, 128), F32)),
-            compiler_params=params(50),
+            compiler_params=params(40),
             cost_estimate=SHORT,
             name="rows_back",
         )(hidden, gate_pre, up_pre, w_down, w_gate, w_up, after)

time: 181 us -> 177 us (0.978)
  Pallas kernels: 50.3 us -> 46.5 us
    pallas_call x1, Pallas kernels: 10.7 us -> 6.73 us  [rows_back(): pl.pallas_call(functools.partial(back_kernel, width), grid=(groups // 2,)...]
  transfers between devices with their start and end apart: 16 -> 16, of which waited for: 9 -> 10; matrix products, arithmetic and copies ran while one was open for 0% -> 0% of each run, Pallas kernels for 17% -> 15%
where the time goes in v7:
time: 177 us
  waiting for transfers between devices  87.7 us (50%)
  Pallas kernels  46.5 us (26%)
  starting transfers between devices  38.7 us (22%)
  local copies, waits for them, and re-layouts  2.99 us (2%)
    all_to_all x2, waiting for transfers between devices, exchange(): return lax.all_to_all(wide, 'expert', 0, 0, tiled=True).reshape(array.shape)  51.4 us
    ppermute x7, waiting for transfers between devices, local(): lax.ppermute(part_a, 'dp', ring_a)  26 us
    pallas_call x8, Pallas kernels, chain_call(): pl.pallas_call(functools.partial(link_kernel, bool(held)), grid_spec=pltp...  18.6 us
    all_to_all x2, starting transfers between devices, exchange(): return lax.all_to_all(wide, 'expert', 0, 0, tiled=True).reshape(array.shape)  14.5 us
    ppermute x7, starting transfers between devices, local(): lax.ppermute(part_b, 'dp', ring_b)  13.1 us
    ppermute x7, starting transfers between devices, local(): lax.ppermute(part_a, 'dp', ring_a)  11.1 us
    ppermute x7, waiting for transfers between devices, local(): lax.ppermute(part_b, 'dp', ring_b)  10.3 us
    pallas_call x1, Pallas kernels, local(): pl.pallas_call(expert_kernel, grid=(blocks,), in_specs=[pl.BlockSpec((slo...  9.28 us
  transfers between devices with their start and end apart: 16, of which 10 were waited for; matrix products, arithmetic and copies ran while one was open for 0% of the time, Pallas kernels for 15%

profile of v7, /device:TPU:2, one launch (start us, length us, event | category | flops | bytes accessed | tf_op | source)
XLA Modules:
  0.0 176.8 jit_solution(16353715785456069632)
XLA Ops:
  0.6 4.3 %dispatch.1 = (bf16[512,4096]{1,0:T(8,128)(2,1)}, bf16[512,48]{1,0:T(8,128)(2,1)}) custom-call(s32[8,48]{1,0:T(8,128)} %bitcast.20, f32[8,48]{1,0:T(8,128)} %bitcast.22, bf16[48,2048]{1,0:T(8,128)(2,1)} %tokens_ref.1, bf16[48,2048]{1,0:T(8,128)(2,1)} %grads_ref.3), custom_call_target="tpu_custom_call" | custom-call | flops 201326592 | bytes 4194304 | tf_op jit(solution)/shard_map/dispatch/pallas_call | solution.py:193
  4.9 7.7 %all-to-all-start = ((bf16[32,16,4096]{2,1,0:T(8,128)(2,1)}), bf16[32,16,4096]{2,1,0:T(8,128)(2,1)}, u32[]{:S(2)}, u32[]{:S(2)}) async-start(bf16[32,16,4096]{2,1,0:T(8,128)(2,1)} %bitcast.26), calls=%async_computation | async-start | bytes 8388608 | tf_op jit(solution)/shard_map/all_to_all | solution.py:212
  12.6 51.4 %all-to-all-done = bf16[32,16,4096]{2,1,0:T(8,128)(2,1)} async-done(((bf16[32,16,4096]{2,1,0:T(8,128)(2,1)}), bf16[32,16,4096]{2,1,0:T(8,128)(2,1)}, u32[]{:S(2)}, u32[]{:S(2)}) %all-to-all-start) | async-done | bytes 4194336 | tf_op jit(solution)/shard_map/all_to_all | solution.py:212
  64.0 9.3 %expert.1 = (bf16[512,768]{1,0:T(8,128)(2,1)S(1)}, bf16[768,512]{1,0:T(8,128)(2,1)S(1)}, bf16[512,768]{1,0:T(8,128)(2,1)S(1)}, bf16[512,768]{1,0:T(8,128)(2,1)S(1)}) custom-call(bf16[512,4096]{1,0:T(8,128)(2,1)} %bitcast.3.rows_ref.grads_ref.refs_0_.refs_1_.refs_2_, bf16[512,4096]{1,0:T(8,128)(2,1)} %bitcast.3.rows_ref.grads_ref.refs_0_.refs_1_.refs_2_, ...), custom_call_target="tpu_custom_call" | custom-call | flops 4831838208 | bytes 16777216 | tf_op jit(solution)/shard_map/expert/pallas_call | solution.py:215
  73.3 0.0 copy-start.10
  73.3 0.0 copy-start.3
  73.3 3.3 %chain_sum_0.1 = (bf16[4,256,256]{2,1,0:T(8,128)(2,1)}, bf16[5,256,256]{2,1,0:T(8,128)(2,1)}) custom-call(s32[1]{0:T(128)} %bitcast.7._, bf16[512,4096]{1,0:T(8,128)(2,1)} %bitcast.3.rows_ref.grads_ref.refs_0_.refs_1_.refs_2_, bf16[512,4096]{1,0:T(8,128)(2,1)} %bitcast.3.rows_ref.grads_ref.refs_0_.refs_1_.refs_2_, ...), custom_call_target="tpu_custom_call" | custom-call | flops 20000000000 | bytes 62914560 | tf_op jit(solution)/shard_map/chain_sum_0/pallas_call | solution.py:237
  76.7 1.9 %collective-permute-start.2 = (bf16[4,256,256]{2,1,0:T(8,128)(2,1)}, bf16[4,256,256]{2,1,0:T(8,128)(2,1)}, u32[]{:S(2)}, u32[]{:S(2)}) collective-permute-start(bf16[4,256,256]{2,1,0:T(8,128)(2,1)} %get-tuple-element.42.refs_6_), channel_id=1, source_target_pairs={{0,1},{1,2},{2,3},{3,4},{4,5},{5,6},{6,7},{7,0},{8,9},{9,10},{10,1... | collective-permute-start | bytes 1572872 | tf_op jit(solution)/shard_map/ppermute | solution.py:283
  78.6 0.0 copy-start
  78.6 0.0 copy-start.1
  78.6 0.0 copy-start.2
  78.6 4.0 %collective-permute-start.3 = (bf16[5,256,256]{2,1,0:T(8,128)(2,1)}, bf16[5,256,256]{2,1,0:T(8,128)(2,1)}, u32[]{:S(2)}, u32[]{:S(2)}) collective-permute-start(bf16[5,256,256]{2,1,0:T(8,128)(2,1)} %get-tuple-element.49), channel_id=1, source_target_pairs={{0,7},{1,0},{2,1},{3,2},{4,3},{5,4},{6,5},{7,6},{8,15},{9,8},{10,9... | collective-permute-start | bytes 1966088 | tf_op jit(solution)/shard_map/ppermute | solution.py:283
  82.6 0.0 copy-done.10
  82.6 1.9 %chain_sum_1.1 = (bf16[4,256,256]{2,1,0:T(8,128)(2,1)S(1)}, bf16[5,256,256]{2,1,0:T(8,128)(2,1)S(1)}) custom-call(s32[1]{0:T(128)} %bitcast.7._, bf16[512,4096]{1,0:T(8,128)(2,1)} %bitcast.3.rows_ref.grads_ref.refs_0_.refs_1_.refs_2_, bf16[512,4096]{1,0:T(8,128)(2,1)} %bitcast.3.rows_ref.grads_ref.refs_0_.refs_1_.refs_2_, ...), custom_call_target="tpu_custom_call" | custom-call | flops 20000000000 | bytes 62914560 | tf_op jit(solution)/shard_map/chain_sum_1/pallas_call | solution.py:237
  84.5 2.7 %collective-permute-start = (bf16[4,256,256]{2,1,0:T(8,128)(2,1)S(1)}, bf16[4,256,256]{2,1,0:T(8,128)(2,1)}, u32[]{:S(2)}, u32[]{:S(2)}) collective-permute-start(bf16[4,256,256]{2,1,0:T(8,128)(2,1)S(1)} %get-tuple-element.43._), channel_id=1, source_target_pairs={{0,7},{1,0},{2,1},{3,2},{4,3},{5,4},{6,5},{7,6},{8,15},{9,8},{10,9... | collective-permute-start | bytes 1572872 | tf_op jit(solution)/shard_map/ppermute | solution.py:283
  87.3 0.0 copy-done
  87.3 0.0 copy-done.1
  87.3 0.0 copy-done.2
  87.3 6.7 %rows_back.1 = (bf16[512,4096]{1,0:T(8,128)(2,1)}, f32[8,128]{1,0:T(8,128)S(1)}) custom-call(bf16[512,768]{1,0:T(8,128)(2,1)S(1)} %get-tuple-element.38.hidden_ref, bf16[512,768]{1,0:T(8,128)(2,1)S(1)} %get-tuple-element.39.refs_3_.gate_pre_ref, bf16[512,768]{1,0:T(8,128)(2,1)S(1)} %get-tuple-element.40.refs_4_.up_pre_ref, bf16[768,2048]{1,0:T(8,128)(2,1)S(1)} %bitcast.19, ...), custom_call_target="tpu_custom_call" | custom-call | flops 1 | bytes 1 | tf_op jit(solution)/shard_map/rows_back/pallas_call | solution.py:262
  94.0 0.0 collective-permute-start.1
  94.0 6.9 %all-to-all-start.1 = ((bf16[32,16,4096]{2,1,0:T(8,128)(2,1)}), bf16[32,16,4096]{2,1,0:T(8,128)(2,1)}, u32[]{:S(2)}, u32[]{:S(2)}) async-start(bf16[32,16,4096]{2,1,0:T(8,128)(2,1)} %bitcast.25), calls=%async_computation.1 | async-start | bytes 8388608 | tf_op jit(solution)/shard_map/all_to_all | solution.py:212
  100.9 0.0 collective-permute-done.2.refs_6_
  100.9 0.0 collective-permute-done.3.refs_7_
  100.9 0.0 copy-start.11
  100.9 1.1 copy-done.11
  102.0 2.3 %chain_sum_2.1 = (bf16[4,256,256]{2,1,0:T(8,128)(2,1)S(1)}, bf16[5,256,256]{2,1,0:T(8,128)(2,1)S(1)}) custom-call(s32[1]{0:T(128)} %bitcast.7._, bf16[512,4096]{1,0:T(8,128)(2,1)} %bitcast.3.rows_ref.grads_ref.refs_0_.refs_1_.refs_2_, bf16[512,4096]{1,0:T(8,128)(2,1)} %bitcast.3.rows_ref.grads_ref.refs_0_.refs_1_.refs_2_, ...), custom_call_target="tpu_custom_call" | custom-call | flops 20000000000 | bytes 62914560 | tf_op jit(solution)/shard_map/chain_sum_2/pallas_call | solution.py:237
  104.4 3.3 %collective-permute-start.7 = (bf16[5,256,256]{2,1,0:T(8,128)(2,1)S(1)}, bf16[5,256,256]{2,1,0:T(8,128)(2,1)S(1)}, u32[]{:S(2)}, u32[]{:S(2)}) collective-permute-start(bf16[5,256,256]{2,1,0:T(8,128)(2,1)S(1)} %get-tuple-element.54), channel_id=1, source_target_pairs={{0,7},{1,0},{2,1},{3,2},{4,3},{5,4},{6,5},{7,6},{8,15},{9,8},{10,9... | collective-permute-start | bytes 1966088 | tf_op jit(solution)/shard_map/ppermute | solution.py:283
  107.7 0.0 collective-permute-start.6
  107.7 0.1 collective-permute-done.refs_6_
  107.8 2.9 %collective-permute-done.1.refs_7_ = bf16[5,256,256]{2,1,0:T(8,128)(2,1)} collective-permute-done((bf16[5,256,256]{2,1,0:T(8,128)(2,1)S(1)}, bf16[5,256,256]{2,1,0:T(8,128)(2,1)}, u32[]{:S(2)}, u32[]{:S(2)}) %collective-permute-start.1) | collective-permute-done | bytes 655392 | tf_op jit(solution)/shard_map/ppermute | solution.py:283
  110.6 2.3 %chain_sum_3.1 = (bf16[4,256,256]{2,1,0:T(8,128)(2,1)S(1)}, bf16[5,256,256]{2,1,0:T(8,128)(2,1)S(1)}) custom-call(s32[1]{0:T(128)} %bitcast.7._, bf16[512,4096]{1,0:T(8,128)(2,1)} %bitcast.3.rows_ref.grads_ref.refs_0_.refs_1_.refs_2_, bf16[512,4096]{1,0:T(8,128)(2,1)} %bitcast.3.rows_ref.grads_ref.refs_0_.refs_1_.refs_2_, ...), custom_call_target="tpu_custom_call" | custom-call | flops 20000000000 | bytes 62914560 | tf_op jit(solution)/shard_map/chain_sum_3/pallas_call | solution.py:237
  113.0 0.1 collective-permute-start.5
  113.0 3.2 %collective-permute-start.4 = (bf16[4,256,256]{2,1,0:T(8,128)(2,1)S(1)}, bf16[4,256,256]{2,1,0:T(8,128)(2,1)S(1)}, u32[]{:S(2)}, u32[]{:S(2)}) collective-permute-start(bf16[4,256,256]{2,1,0:T(8,128)(2,1)S(1)} %get-tuple-element.52.refs_8_), channel_id=1, source_target_pairs={{0,7},{1,0},{2,1},{3,2},{4,3},{5,4},{6,5},{7,6},{8,15},{9,8},{10,9... | collective-permute-start | bytes 1572872 | tf_op jit(solution)/shard_map/ppermute | solution.py:283
  116.3 7.4 %collective-permute-done.6.refs_6_ = bf16[4,256,256]{2,1,0:T(8,128)(2,1)S(1)} collective-permute-done((bf16[4,256,256]{2,1,0:T(8,128)(2,1)S(1)}, bf16[4,256,256]{2,1,0:T(8,128)(2,1)S(1)}, u32[]{:S(2)}, u32[]{:S(2)}) %collective-permute-start.6) | collective-permute-done | bytes 524320 | tf_op jit(solution)/shard_map/ppermute | solution.py:283
  123.7 0.0 collective-permute-done.7.refs_7_
  123.7 1.9 %chain_sum_4.1 = (bf16[4,256,256]{2,1,0:T(8,128)(2,1)S(1)}, bf16[5,256,256]{2,1,0:T(8,128)(2,1)S(1)}) custom-call(s32[1]{0:T(128)} %bitcast.7._, bf16[512,4096]{1,0:T(8,128)(2,1)} %bitcast.3.rows_ref.grads_ref.refs_0_.refs_1_.refs_2_, bf16[512,4096]{1,0:T(8,128)(2,1)} %bitcast.3.rows_ref.grads_ref.refs_0_.refs_1_.refs_2_, ...), custom_call_target="tpu_custom_call" | custom-call | flops 20000000000 | bytes 62914560 | tf_op jit(solution)/shard_map/chain_sum_4/pallas_call | solution.py:237
  125.6 2.8 %collective-permute-start.11 = (bf16[5,256,256]{2,1,0:T(8,128)(2,1)S(1)}, bf16[5,256,256]{2,1,0:T(8,128)(2,1)S(1)}, u32[]{:S(2)}, u32[]{:S(2)}) collective-permute-start(bf16[5,256,256]{2,1,0:T(8,128)(2,1)S(1)} %get-tuple-element.58), channel_id=1, source_target_pairs={{0,7},{1,0},{2,1},{3,2},{4,3},{5,4},{6,5},{7,6},{8,15},{9,8},{10,9... | collective-permute-start | bytes 1966088 | tf_op jit(solution)/shard_map/ppermute | solution.py:283
  128.5 0.0 collective-permute-start.10
  128.5 5.5 %collective-permute-done.4.refs_6_ = bf16[4,256,256]{2,1,0:T(8,128)(2,1)S(1)} collective-permute-done((bf16[4,256,256]{2,1,0:T(8,128)(2,1)S(1)}, bf16[4,256,256]{2,1,0:T(8,128)(2,1)S(1)}, u32[]{:S(2)}, u32[]{:S(2)}) %collective-permute-start.4) | collective-permute-done | bytes 524320 | tf_op jit(solution)/shard_map/ppermute | solution.py:283
  134.0 3.7 %collective-permute-done.5.refs_7_ = bf16[5,256,256]{2,1,0:T(8,128)(2,1)S(1)} collective-permute-done((bf16[5,256,256]{2,1,0:T(8,128)(2,1)S(1)}, bf16[5,256,256]{2,1,0:T(8,128)(2,1)S(1)}, u32[]{:S(2)}, u32[]{:S(2)}) %collective-permute-start.5) | collective-permute-done | bytes 655392 | tf_op jit(solution)/shard_map/ppermute | solution.py:283
  137.7 1.9 %chain_sum_5.1 = (bf16[4,256,256]{2,1,0:T(8,128)(2,1)S(1)}, bf16[5,256,256]{2,1,0:T(8,128)(2,1)S(1)}) custom-call(s32[1]{0:T(128)} %bitcast.7._, bf16[512,4096]{1,0:T(8,128)(2,1)} %bitcast.3.rows_ref.grads_ref.refs_0_.refs_1_.refs_2_, bf16[512,4096]{1,0:T(8,128)(2,1)} %bitcast.3.rows_ref.grads_ref.refs_0_.refs_1_.refs_2_, ...), custom_call_target="tpu_custom_call" | custom-call | flops 20000000000 | bytes 62914560 | tf_op jit(solution)/shard_map/chain_sum_5/pallas_call | solution.py:237
  139.7 0.1 collective-permute-start.9
  139.8 3.2 %collective-permute-start.8 = (bf16[4,256,256]{2,1,0:T(8,128)(2,1)S(1)}, bf16[4,256,256]{2,1,0:T(8,128)(2,1)S(1)}, u32[]{:S(2)}, u32[]{:S(2)}) collective-permute-start(bf16[4,256,256]{2,1,0:T(8,128)(2,1)S(1)} %get-tuple-element.56.refs_8_), channel_id=1, source_target_pairs={{0,7},{1,0},{2,1},{3,2},{4,3},{5,4},{6,5},{7,6},{8,15},{9,8},{10,9... | collective-permute-start | bytes 1572872 | tf_op jit(solution)/shard_map/ppermute | solution.py:283
  143.0 6.0 %collective-permute-done.10.refs_6_ = bf16[4,256,256]{2,1,0:T(8,128)(2,1)S(1)} collective-permute-done((bf16[4,256,256]{2,1,0:T(8,128)(2,1)S(1)}, bf16[4,256,256]{2,1,0:T(8,128)(2,1)S(1)}, u32[]{:S(2)}, u32[]{:S(2)}) %collective-permute-start.10) | collective-permute-done | bytes 524320 | tf_op jit(solution)/shard_map/ppermute | solution.py:283
  149.0 0.0 collective-permute-done.11.refs_7_
  149.0 0.0 copy-done.3
  149.0 2.8 %chain_sum_6.1 = (bf16[4,256,256]{2,1,0:T(8,128)(2,1)}, bf16[5,256,256]{2,1,0:T(8,128)(2,1)}) custom-call(s32[1]{0:T(128)} %bitcast.7._, bf16[512,4096]{1,0:T(8,128)(2,1)} %bitcast.3.rows_ref.grads_ref.refs_0_.refs_1_.refs_2_, bf16[512,4096]{1,0:T(8,128)(2,1)} %bitcast.3.rows_ref.grads_ref.refs_0_.refs_1_.refs_2_, ...), custom_call_target="tpu_custom_call" | custom-call | flops 20000000000 | bytes 62914560 | tf_op jit(solution)/shard_map/chain_sum_6/pallas_call | solution.py:237
  151.8 2.8 %collective-permute-start.13 = (bf16[5,256,256]{2,1,0:T(8,128)(2,1)}, bf16[5,256,256]{2,1,0:T(8,128)(2,1)}, u32[]{:S(2)}, u32[]{:S(2)}) collective-permute-start(bf16[5,256,256]{2,1,0:T(8,128)(2,1)} %get-tuple-element.62), channel_id=1, source_target_pairs={{0,7},{1,0},{2,1},{3,2},{4,3},{5,4},{6,5},{7,6},{8,15},{9,8},{10,9... | collective-permute-start | bytes 1966088 | tf_op jit(solution)/shard_map/ppermute | solution.py:283
  154.5 0.0 collective-permute-start.12
  154.6 4.7 %collective-permute-done.8.refs_6_ = bf16[4,256,256]{2,1,0:T(8,128)(2,1)S(1)} collective-permute-done((bf16[4,256,256]{2,1,0:T(8,128)(2,1)S(1)}, bf16[4,256,256]{2,1,0:T(8,128)(2,1)S(1)}, u32[]{:S(2)}, u32[]{:S(2)}) %collective-permute-start.8) | collective-permute-done | bytes 524320 | tf_op jit(solution)/shard_map/ppermute | solution.py:283
  159.3 3.7 %collective-permute-done.9.refs_7_ = bf16[5,256,256]{2,1,0:T(8,128)(2,1)S(1)} collective-permute-done((bf16[5,256,256]{2,1,0:T(8,128)(2,1)S(1)}, bf16[5,256,256]{2,1,0:T(8,128)(2,1)S(1)}, u32[]{:S(2)}, u32[]{:S(2)}) %collective-permute-start.9) | collective-permute-done | bytes 655392 | tf_op jit(solution)/shard_map/ppermute | solution.py:283
  163.0 0.0 copy-start.4
  163.0 1.1 copy-done.4
  164.1 2.0 %chain_sum_own.1 = (f32[4,256,256]{2,1,0:T(8,128)S(1)}, f32[5,256,256]{2,1,0:T(8,128)S(1)}) custom-call(s32[1]{0:T(128)} %bitcast.7._, bf16[512,4096]{1,0:T(8,128)(2,1)} %bitcast.3.rows_ref.grads_ref.refs_0_.refs_1_.refs_2_, bf16[512,4096]{1,0:T(8,128)(2,1)} %bitcast.3.rows_ref.grads_ref.refs_0_.refs_1_.refs_2_, ...), custom_call_target="tpu_custom_call" | custom-call | flops 20000000000 | bytes 62914560 | tf_op jit(solution)/shard_map/chain_sum_own/pallas_call | solution.py:237
  166.2 0.0 all-to-all-done.1
  166.2 0.0 copy-done.5
  166.2 0.0 copy-done.6
  166.2 0.0 copy-done.7
  166.2 0.0 copy-done.8
  166.2 4.7 %combine.1 = (bf16[48,2048]{1,0:T(8,128)(2,1)}, bf16[48,2048]{1,0:T(8,128)(2,1)}, f32[8,48]{1,0:T(8,128)}) custom-call(s32[8,48]{1,0:T(8,128)S(1)} %bitcast.21, f32[8,48]{1,0:T(8,128)S(1)} %bitcast.23, bf16[512,48]{1,0:T(8,128)(2,1)S(1)} %copy-done.6, bf16[48,2048]{1,0:T(8,128)(2,1)S(1)} %copy-done.5, bf16[512,4096]{1,0:T(8,128)(2,1)} %bitcast.9.back_ref), custom_call_target="tpu_custom_call" | custom-call | flops 402653184 | bytes 4194304 | tf_op jit(solution)/shard_map/combine/pallas_call | solution.py:287
  170.9 2.3 %collective-permute-done.12.a0 = bf16[4,256,256]{2,1,0:T(8,128)(2,1)} collective-permute-done((bf16[4,256,256]{2,1,0:T(8,128)(2,1)}, bf16[4,256,256]{2,1,0:T(8,128)(2,1)}, u32[]{:S(2)}, u32[]{:S(2)}) %collective-permute-start.12) | collective-permute-done | bytes 524320 | tf_op jit(solution)/shard_map/ppermute | solution.py:283
  173.2 0.0 collective-permute-done.13.b0
  173.2 0.7 copy-done.9
  173.9 2.8 %chain_sum_last.1 = (f32[256,768]{1,0:T(8,128)}, f32[256,768]{1,0:T(8,128)}, f32[768,256]{1,0:T(8,128)}) custom-call(f32[4,256,256]{2,1,0:T(8,128)S(1)} %get-tuple-element.60.own_a, f32[5,256,256]{2,1,0:T(8,128)S(1)} %get-tuple-element.61.own_b, bf16[4,256,256]{2,1,0:T(8,128)(2,1)} %collective-permute-done.12.a0, ...), custom_call_target="tpu_custom_call" | custom-call | flops 1 | bytes 1 | tf_op jit(solution)/shard_map/chain_sum_last/pallas_call | solution.py:310
  (5 shorter events, 0.0 us)
Async XLA Ops:
  4.9 59.1 %all-to-all-start = ((bf16[32,16,4096]{2,1,0:T(8,128)(2,1)}), bf16[32,16,4096]{2,1,0:T(8,128)(2,1)}, u32[]{:S(2)}, u32[]{:S(2)}) async-start(bf16[32,16,4096]{2,1,0:T(8,128)(2,1)} %bitcast.26), calls=%async_computation | async-start | bytes 8388608 | tf_op jit(solution)/shard_map/all_to_all | solution.py:212
  73.3 9.3 %copy-start.10 = (bf16[768,512]{1,0:T(8,128)(2,1)}, bf16[768,512]{1,0:T(8,128)(2,1)S(1)}, u32[]{:S(2)}) copy-start(bf16[768,512]{1,0:T(8,128)(2,1)S(1)} %get-tuple-element.41.refs_5_) | copy-start | bytes 2359300
  73.3 75.7 %copy-start.3 = (bf16[512,768]{1,0:T(8,128)(2,1)}, bf16[512,768]{1,0:T(8,128)(2,1)S(1)}, u32[]{:S(2)}) copy-start(bf16[512,768]{1,0:T(8,128)(2,1)S(1)} %get-tuple-element.40.refs_4_.up_pre_ref) | copy-start | bytes 2359300
  76.7 24.2 %collective-permute-start.2 = (bf16[4,256,256]{2,1,0:T(8,128)(2,1)}, bf16[4,256,256]{2,1,0:T(8,128)(2,1)}, u32[]{:S(2)}, u32[]{:S(2)}) collective-permute-start(bf16[4,256,256]{2,1,0:T(8,128)(2,1)} %get-tuple-element.42.refs_6_), channel_id=1, source_target_pairs={{0,1},{1,2},{2,3},{3,4},{4,5},{5,6},{6,7},{7,0},{8,9},{9,10},{10,1... | collective-permute-start | bytes 1572872 | tf_op jit(solution)/shard_map/ppermute | solution.py:283
  78.6 8.7 %copy-start = (bf16[1,2048,768]{2,1,0:T(8,128)(2,1)S(1)}, bf16[1,2048,768]{2,1,0:T(8,128)(2,1)}, u32[]{:S(2)}) copy-start(bf16[1,2048,768]{2,1,0:T(8,128)(2,1)} %param.10) | copy-start | bytes 9437188
  78.6 8.7 %copy-start.1 = (bf16[1,2048,768]{2,1,0:T(8,128)(2,1)S(1)}, bf16[1,2048,768]{2,1,0:T(8,128)(2,1)}, u32[]{:S(2)}) copy-start(bf16[1,2048,768]{2,1,0:T(8,128)(2,1)} %param.11) | copy-start | bytes 9437188
  78.6 8.7 %copy-start.2 = (bf16[1,768,2048]{2,1,0:T(8,128)(2,1)S(1)}, bf16[1,768,2048]{2,1,0:T(8,128)(2,1)}, u32[]{:S(2)}) copy-start(bf16[1,768,2048]{2,1,0:T(8,128)(2,1)} %param.12) | copy-start | bytes 9437188
  78.6 22.3 %collective-permute-start.3 = (bf16[5,256,256]{2,1,0:T(8,128)(2,1)}, bf16[5,256,256]{2,1,0:T(8,128)(2,1)}, u32[]{:S(2)}, u32[]{:S(2)}) collective-permute-start(bf16[5,256,256]{2,1,0:T(8,128)(2,1)} %get-tuple-element.49), channel_id=1, source_target_pairs={{0,7},{1,0},{2,1},{3,2},{4,3},{5,4},{6,5},{7,6},{8,15},{9,8},{10,9... | collective-permute-start | bytes 1966088 | tf_op jit(solution)/shard_map/ppermute | solution.py:283
  84.5 23.2 %collective-permute-start = (bf16[4,256,256]{2,1,0:T(8,128)(2,1)S(1)}, bf16[4,256,256]{2,1,0:T(8,128)(2,1)}, u32[]{:S(2)}, u32[]{:S(2)}) collective-permute-start(bf16[4,256,256]{2,1,0:T(8,128)(2,1)S(1)} %get-tuple-element.43._), channel_id=1, source_target_pairs={{0,7},{1,0},{2,1},{3,2},{4,3},{5,4},{6,5},{7,6},{8,15},{9,8},{10,9... | collective-permute-start | bytes 1572872 | tf_op jit(solution)/shard_map/ppermute | solution.py:283
  94.0 16.6 %collective-permute-start.1 = (bf16[5,256,256]{2,1,0:T(8,128)(2,1)S(1)}, bf16[5,256,256]{2,1,0:T(8,128)(2,1)}, u32[]{:S(2)}, u32[]{:S(2)}) collective-permute-start(bf16[5,256,256]{2,1,0:T(8,128)(2,1)S(1)} %get-tuple-element.48), channel_id=1, source_target_pairs={{0,1},{1,2},{2,3},{3,4},{4,5},{5,6},{6,7},{7,0},{8,9},{9,10},{10,1... | collective-permute-start | bytes 1966088 | tf_op jit(solution)/shard_map/ppermute | solution.py:283
  94.0 72.1 %all-to-all-start.1 = ((bf16[32,16,4096]{2,1,0:T(8,128)(2,1)}), bf16[32,16,4096]{2,1,0:T(8,128)(2,1)}, u32[]{:S(2)}, u32[]{:S(2)}) async-start(bf16[32,16,4096]{2,1,0:T(8,128)(2,1)} %bitcast.25), calls=%async_computation.1 | async-start | bytes 8388608 | tf_op jit(solution)/shard_map/all_to_all | solution.py:212
  100.9 1.1 copy-start.11
  104.4 19.3 %collective-permute-start.7 = (bf16[5,256,256]{2,1,0:T(8,128)(2,1)S(1)}, bf16[5,256,256]{2,1,0:T(8,128)(2,1)S(1)}, u32[]{:S(2)}, u32[]{:S(2)}) collective-permute-start(bf16[5,256,256]{2,1,0:T(8,128)(2,1)S(1)} %get-tuple-element.54), channel_id=1, source_target_pairs={{0,7},{1,0},{2,1},{3,2},{4,3},{5,4},{6,5},{7,6},{8,15},{9,8},{10,9... | collective-permute-start | bytes 1966088 | tf_op jit(solution)/shard_map/ppermute | solution.py:283
  107.7 16.0 %collective-permute-start.6 = (bf16[4,256,256]{2,1,0:T(8,128)(2,1)S(1)}, bf16[4,256,256]{2,1,0:T(8,128)(2,1)S(1)}, u32[]{:S(2)}, u32[]{:S(2)}) collective-permute-start(bf16[4,256,256]{2,1,0:T(8,128)(2,1)S(1)} %get-tuple-element.51.refs_8_), channel_id=1, source_target_pairs={{0,1},{1,2},{2,3},{3,4},{4,5},{5,6},{6,7},{7,0},{8,9},{9,10},{10,1... | collective-permute-start | bytes 1572872 | tf_op jit(solution)/shard_map/ppermute | solution.py:283
  113.0 24.8 %collective-permute-start.5 = (bf16[5,256,256]{2,1,0:T(8,128)(2,1)S(1)}, bf16[5,256,256]{2,1,0:T(8,128)(2,1)S(1)}, u32[]{:S(2)}, u32[]{:S(2)}) collective-permute-start(bf16[5,256,256]{2,1,0:T(8,128)(2,1)S(1)} %get-tuple-element.53), channel_id=1, source_target_pairs={{0,1},{1,2},{2,3},{3,4},{4,5},{5,6},{6,7},{7,0},{8,9},{9,10},{10,1... | collective-permute-start | bytes 1966088 | tf_op jit(solution)/shard_map/ppermute | solution.py:283
  113.0 20.9 %collective-permute-start.4 = (bf16[4,256,256]{2,1,0:T(8,128)(2,1)S(1)}, bf16[4,256,256]{2,1,0:T(8,128)(2,1)S(1)}, u32[]{:S(2)}, u32[]{:S(2)}) collective-permute-start(bf16[4,256,256]{2,1,0:T(8,128)(2,1)S(1)} %get-tuple-element.52.refs_8_), channel_id=1, source_target_pairs={{0,7},{1,0},{2,1},{3,2},{4,3},{5,4},{6,5},{7,6},{8,15},{9,8},{10,9... | collective-permute-start | bytes 1572872 | tf_op jit(solution)/shard_map/ppermute | solution.py:283
  125.6 23.3 %collective-permute-start.11 = (bf16[5,256,256]{2,1,0:T(8,128)(2,1)S(1)}, bf16[5,256,256]{2,1,0:T(8,128)(2,1)S(1)}, u32[]{:S(2)}, u32[]{:S(2)}) collective-permute-start(bf16[5,256,256]{2,1,0:T(8,128)(2,1)S(1)} %get-tuple-element.58), channel_id=1, source_target_pairs={{0,7},{1,0},{2,1},{3,2},{4,3},{5,4},{6,5},{7,6},{8,15},{9,8},{10,9... | collective-permute-start | bytes 1966088 | tf_op jit(solution)/shard_map/ppermute | solution.py:283
  128.5 20.5 %collective-permute-start.10 = (bf16[4,256,256]{2,1,0:T(8,128)(2,1)S(1)}, bf16[4,256,256]{2,1,0:T(8,128)(2,1)S(1)}, u32[]{:S(2)}, u32[]{:S(2)}) collective-permute-start(bf16[4,256,256]{2,1,0:T(8,128)(2,1)S(1)} %get-tuple-element.55.refs_8_), channel_id=1, source_target_pairs={{0,1},{1,2},{2,3},{3,4},{4,5},{5,6},{6,7},{7,0},{8,9},{9,10},{10,1... | collective-permute-start | bytes 1572872 | tf_op jit(solution)/shard_map/ppermute | solution.py:283
  139.7 23.3 %collective-permute-start.9 = (bf16[5,256,256]{2,1,0:T(8,128)(2,1)S(1)}, bf16[5,256,256]{2,1,0:T(8,128)(2,1)S(1)}, u32[]{:S(2)}, u32[]{:S(2)}) collective-permute-start(bf16[5,256,256]{2,1,0:T(8,128)(2,1)S(1)} %get-tuple-element.57), channel_id=1, source_target_pairs={{0,1},{1,2},{2,3},{3,4},{4,5},{5,6},{6,7},{7,0},{8,9},{9,10},{10,1... | collective-permute-start | bytes 1966088 | tf_op jit(solution)/shard_map/ppermute | solution.py:283
  139.8 19.5 %collective-permute-start.8 = (bf16[4,256,256]{2,1,0:T(8,128)(2,1)S(1)}, bf16[4,256,256]{2,1,0:T(8,128)(2,1)S(1)}, u32[]{:S(2)}, u32[]{:S(2)}) collective-permute-start(bf16[4,256,256]{2,1,0:T(8,128)(2,1)S(1)} %get-tuple-element.56.refs_8_), channel_id=1, source_target_pairs={{0,7},{1,0},{2,1},{3,2},{4,3},{5,4},{6,5},{7,6},{8,15},{9,8},{10,9... | collective-permute-start | bytes 1572872 | tf_op jit(solution)/shard_map/ppermute | solution.py:283
  151.8 21.5 %collective-permute-start.13 = (bf16[5,256,256]{2,1,0:T(8,128)(2,1)}, bf16[5,256,256]{2,1,0:T(8,128)(2,1)}, u32[]{:S(2)}, u32[]{:S(2)}) collective-permute-start(bf16[5,256,256]{2,1,0:T(8,128)(2,1)} %get-tuple-element.62), channel_id=1, source_target_pairs={{0,7},{1,0},{2,1},{3,2},{4,3},{5,4},{6,5},{7,6},{8,15},{9,8},{10,9... | collective-permute-start | bytes 1966088 | tf_op jit(solution)/shard_map/ppermute | solution.py:283
  154.5 18.7 %collective-permute-start.12 = (bf16[4,256,256]{2,1,0:T(8,128)(2,1)}, bf16[4,256,256]{2,1,0:T(8,128)(2,1)}, u32[]{:S(2)}, u32[]{:S(2)}) collective-permute-start(bf16[4,256,256]{2,1,0:T(8,128)(2,1)} %get-tuple-element.59.refs_8_), channel_id=1, source_target_pairs={{0,1},{1,2},{2,3},{3,4},{4,5},{5,6},{6,7},{7,0},{8,9},{9,10},{10,1... | collective-permute-start | bytes 1572872 | tf_op jit(solution)/shard_map/ppermute | solution.py:283
  163.0 1.1 copy-start.4
  164.1 2.0 %copy-start.5 = (bf16[48,2048]{1,0:T(8,128)(2,1)S(1)}, bf16[48,2048]{1,0:T(8,128)(2,1)}, u32[]{:S(2)}) copy-start(bf16[48,2048]{1,0:T(8,128)(2,1)} %grads_ref.3) | copy-start | bytes 589828
  164.1 2.0 %copy-start.6 = (bf16[512,48]{1,0:T(8,128)(2,1)S(1)}, bf16[512,48]{1,0:T(8,128)(2,1)}, u32[]{:S(2)}) copy-start(bf16[512,48]{1,0:T(8,128)(2,1)} %get-tuple-element.36.place_ref) | copy-start | bytes 147460
  164.1 2.0 %copy-start.7 = (s32[48,8]{0,1:T(8,128)S(1)}, s32[48,8]{0,1:T(8,128)}, u32[]{:S(2)}) copy-start(s32[48,8]{0,1:T(8,128)} %param.8) | copy-start | bytes 4612
  164.1 2.0 %copy-start.8 = (f32[48,8]{0,1:T(8,128)S(1)}, f32[48,8]{0,1:T(8,128)}, u32[]{:S(2)}) copy-start(f32[48,8]{0,1:T(8,128)} %param.9) | copy-start | bytes 4612
  173.2 0.7 copy-start.9

commit v8 on v7

--- a/solution.py
+++ b/solution.py
@@ -110,7 +110,7 @@
         out[part][j] = total.astype(out[part].dtype)
 
 
-def last_kernel(own_a, own_b, a0, b0, _, gate_ref, up_ref, down_ref):
+def last_kernel(own_a, own_b, a0, b0, gate_ref, up_ref, down_ref):
     width = own_a.shape[1]
     blocks = own_a.shape[0] - 1
     for j in range(blocks):
@@ -134,9 +134,10 @@
 
 def combine_kernel(
     capacity, width, routes_ref, gates_ref, place_ref, grads_ref, back_ref,
-    out_ref, grad_ref, gates_grad_ref, high, low, place_t, score,
+    out_ref, grad_ref, gates_grad_ref, token_ref, high, low, place_t, score,
 ):
     step = pl.program_id(0)
+    token_ref[...] = jnp.zeros_like(token_ref)
 
     @pl.when(step == 0)
     def _():
@@ -284,7 +285,7 @@
 
     back = exchange(going_back)
 
-    layer_out, token_grad, gates_grad_t = pl.pallas_call(
+    layer_out, token_grad, gates_grad_t, token = pl.pallas_call(
         functools.partial(combine_kernel, capacity, width),
         grid=(2,),
         in_specs=[
@@ -298,23 +299,24 @@
             pl.BlockSpec((count, half), lambda i: (0, i)),
             pl.BlockSpec((count, half), lambda i: (0, i)),
             whole((top, count)),
+            whole((8, 128)),
         ],
-        out_shape=(shape((count, model)), shape((count, model)), shape((top, count), F32)),
+        out_shape=(shape((count, model)), shape((count, model)), shape((top, count), F32), shape((8, 128), F32)),
         scratch_shapes=[pltpu.VMEM((count, slots), BF16)] * 3 + [pltpu.VMEM((slots, 1), F32)],
         compiler_params=params(40),
         cost_estimate=cost(8 * slots * count * model, 4 * slots * model),
         name="combine",
     )(routes_t, gates_t, place, out_grad, back)
 
-    own_a, own_b = chain_call(0, 0, F32, came[0, 1], "chain_sum_own", after)
+    own_a, own_b = chain_call(0, 0, F32, came[0, 1], "chain_sum_own", (*after, token))
     gate_grad, up_grad, down_grad = pl.pallas_call(
         last_kernel,
-        in_specs=[*[resident] * 4, anywhere],
+        in_specs=[resident] * 4,
         out_shape=(shape((width, hid), F32), shape((width, hid), F32), shape((hid, width), F32)),
         compiler_params=params(),
         cost_estimate=SHORT,
         name="chain_sum_last",
-    )(own_a, own_b, *came[0, 0], gates_grad_t)
+    )(own_a, own_b, *came[0, 0])
     return (layer_out, token_grad, gates_grad_t.T, gate_grad[None], up_grad[None], down_grad[None])
 
 

time: 177 us -> 175 us (0.989)
  waiting for transfers between devices: 87.7 us -> 85.1 us
  starting transfers between devices: 38.7 us -> 41.2 us
  local copies, waits for them, and re-layouts: 2.99 us -> 1.16 us
    ppermute x7, starting transfers between devices: 11.1 us -> 13.7 us  [local(): lax.ppermute(part_a, 'dp', ring_a)]
    unnamed x24 -> x20, local copies, waits for them, and re-layouts: 2.99 us -> 1.16 us
  transfers between devices with their start and end apart: 16 -> 16, of which waited for: 10 -> 11; matrix products, arithmetic and copies ran while one was open for 0% -> 0% of each run, Pallas kernels for 15% -> 16%
where the time goes in v8:
time: 175 us; the launch traced here: 174 us
  waiting for transfers between devices  85.1 us (49%)
  Pallas kernels  45.9 us (26%)
  starting transfers between devices  41.2 us (24%)
    all_to_all x2, waiting for transfers between devices, exchange(): return lax.all_to_all(wide, 'expert', 0, 0, tiled=True).reshape(array.shape)  51.4 us
    ppermute x7, waiting for transfers between devices, local(): lax.ppermute(part_a, 'dp', ring_a)  25 us
    pallas_call x8, Pallas kernels, chain_call(): pl.pallas_call(functools.partial(link_kernel, bool(held)), grid_spec=pltp...  19.3 us
    all_to_all x2, starting transfers between devices, exchange(): return lax.all_to_all(wide, 'expert', 0, 0, tiled=True).reshape(array.shape)  14.5 us
    ppermute x7, starting transfers between devices, local(): lax.ppermute(part_a, 'dp', ring_a)  13.7 us
    ppermute x7, starting transfers between devices, local(): lax.ppermute(part_b, 'dp', ring_b)  12.9 us
    pallas_call x1, Pallas kernels, local(): pl.pallas_call(expert_kernel, grid=(blocks,), in_specs=[pl.BlockSpec((slo...  9.26 us
    ppermute x7, waiting for transfers between devices, local(): lax.ppermute(part_b, 'dp', ring_b)  8.77 us
  transfers between devices with their start and end apart: 16, of which 11 were waited for; matrix products, arithmetic and copies ran while one was open for 0% of the time, Pallas kernels for 16%

profile of v8, /device:TPU:2, one launch (start us, length us, event | category | flops | bytes accessed | tf_op | source)
XLA Modules:
  0.0 174.2 jit_solution(6279938822718300069)
XLA Ops:
  0.6 4.3 %dispatch.1 = (bf16[512,4096]{1,0:T(8,128)(2,1)}, bf16[512,48]{1,0:T(8,128)(2,1)}) custom-call(s32[8,48]{1,0:T(8,128)} %bitcast.20, f32[8,48]{1,0:T(8,128)} %bitcast.22, bf16[48,2048]{1,0:T(8,128)(2,1)} %tokens_ref.1, bf16[48,2048]{1,0:T(8,128)(2,1)} %grads_ref.3), custom_call_target="tpu_custom_call" | custom-call | flops 201326592 | bytes 4194304 | tf_op jit(solution)/shard_map/dispatch/pallas_call | solution.py:194
  4.9 7.7 %all-to-all-start = ((bf16[32,16,4096]{2,1,0:T(8,128)(2,1)}), bf16[32,16,4096]{2,1,0:T(8,128)(2,1)}, u32[]{:S(2)}, u32[]{:S(2)}) async-start(bf16[32,16,4096]{2,1,0:T(8,128)(2,1)} %bitcast.25), calls=%async_computation | async-start | bytes 8388608 | tf_op jit(solution)/shard_map/all_to_all | solution.py:213
  12.6 51.4 %all-to-all-done = bf16[32,16,4096]{2,1,0:T(8,128)(2,1)} async-done(((bf16[32,16,4096]{2,1,0:T(8,128)(2,1)}), bf16[32,16,4096]{2,1,0:T(8,128)(2,1)}, u32[]{:S(2)}, u32[]{:S(2)}) %all-to-all-start) | async-done | bytes 4194336 | tf_op jit(solution)/shard_map/all_to_all | solution.py:213
  64.0 9.3 %expert.1 = (bf16[512,768]{1,0:T(8,128)(2,1)S(1)}, bf16[768,512]{1,0:T(8,128)(2,1)S(1)}, bf16[512,768]{1,0:T(8,128)(2,1)S(1)}, bf16[512,768]{1,0:T(8,128)(2,1)S(1)}) custom-call(bf16[512,4096]{1,0:T(8,128)(2,1)} %bitcast.3.rows_ref.grads_ref.refs_0_.refs_1_.refs_2_, bf16[512,4096]{1,0:T(8,128)(2,1)} %bitcast.3.rows_ref.grads_ref.refs_0_.refs_1_.refs_2_, ...), custom_call_target="tpu_custom_call" | custom-call | flops 4831838208 | bytes 16777216 | tf_op jit(solution)/shard_map/expert/pallas_call | solution.py:216
  73.3 0.0 copy-start.7
  73.3 3.1 %chain_sum_0.1 = (bf16[4,256,256]{2,1,0:T(8,128)(2,1)}, bf16[5,256,256]{2,1,0:T(8,128)(2,1)}) custom-call(s32[1]{0:T(128)} %bitcast.7._, bf16[512,4096]{1,0:T(8,128)(2,1)} %bitcast.3.rows_ref.grads_ref.refs_0_.refs_1_.refs_2_, bf16[512,4096]{1,0:T(8,128)(2,1)} %bitcast.3.rows_ref.grads_ref.refs_0_.refs_1_.refs_2_, ...), custom_call_target="tpu_custom_call" | custom-call | flops 20000000000 | bytes 62914560 | tf_op jit(solution)/shard_map/chain_sum_0/pallas_call | solution.py:238
  76.3 1.9 %collective-permute-start.2 = (bf16[4,256,256]{2,1,0:T(8,128)(2,1)}, bf16[4,256,256]{2,1,0:T(8,128)(2,1)}, u32[]{:S(2)}, u32[]{:S(2)}) collective-permute-start(bf16[4,256,256]{2,1,0:T(8,128)(2,1)} %get-tuple-element.43.refs_6_), channel_id=1, source_target_pairs={{0,1},{1,2},{2,3},{3,4},{4,5},{5,6},{6,7},{7,0},{8,9},{9,10},{10,1... | collective-permute-start | bytes 1572872 | tf_op jit(solution)/shard_map/ppermute | solution.py:284
  78.3 0.0 copy-start
  78.3 0.0 copy-start.1
  78.3 0.0 copy-start.2
  78.3 4.0 %collective-permute-start.3 = (bf16[5,256,256]{2,1,0:T(8,128)(2,1)}, bf16[5,256,256]{2,1,0:T(8,128)(2,1)}, u32[]{:S(2)}, u32[]{:S(2)}) collective-permute-start(bf16[5,256,256]{2,1,0:T(8,128)(2,1)} %get-tuple-element.50), channel_id=1, source_target_pairs={{0,7},{1,0},{2,1},{3,2},{4,3},{5,4},{6,5},{7,6},{8,15},{9,8},{10,9... | collective-permute-start | bytes 1966088 | tf_op jit(solution)/shard_map/ppermute | solution.py:284
  82.3 0.0 copy-done.7
  82.3 1.9 %chain_sum_1.1 = (bf16[4,256,256]{2,1,0:T(8,128)(2,1)S(1)}, bf16[5,256,256]{2,1,0:T(8,128)(2,1)S(1)}) custom-call(s32[1]{0:T(128)} %bitcast.7._, bf16[512,4096]{1,0:T(8,128)(2,1)} %bitcast.3.rows_ref.grads_ref.refs_0_.refs_1_.refs_2_, bf16[512,4096]{1,0:T(8,128)(2,1)} %bitcast.3.rows_ref.grads_ref.refs_0_.refs_1_.refs_2_, ...), custom_call_target="tpu_custom_call" | custom-call | flops 20000000000 | bytes 62914560 | tf_op jit(solution)/shard_map/chain_sum_1/pallas_call | solution.py:238
  84.2 2.7 %collective-permute-start = (bf16[4,256,256]{2,1,0:T(8,128)(2,1)S(1)}, bf16[4,256,256]{2,1,0:T(8,128)(2,1)}, u32[]{:S(2)}, u32[]{:S(2)}) collective-permute-start(bf16[4,256,256]{2,1,0:T(8,128)(2,1)S(1)} %get-tuple-element.44._), channel_id=1, source_target_pairs={{0,7},{1,0},{2,1},{3,2},{4,3},{5,4},{6,5},{7,6},{8,15},{9,8},{10,9... | collective-permute-start | bytes 1572872 | tf_op jit(solution)/shard_map/ppermute | solution.py:284
  87.0 0.0 collective-permute-start.1
  87.0 0.0 copy-done
  87.0 0.0 copy-done.1
  87.0 0.0 copy-done.2
  87.0 6.7 %rows_back.1 = (bf16[512,4096]{1,0:T(8,128)(2,1)}, f32[8,128]{1,0:T(8,128)S(1)}) custom-call(bf16[512,768]{1,0:T(8,128)(2,1)S(1)} %get-tuple-element.39.hidden_ref, bf16[512,768]{1,0:T(8,128)(2,1)S(1)} %get-tuple-element.40.refs_3_.gate_pre_ref, bf16[512,768]{1,0:T(8,128)(2,1)S(1)} %get-tuple-element.41.refs_4_.up_pre_ref, bf16[768,2048]{1,0:T(8,128)(2,1)S(1)} %bitcast.19, ...), custom_call_target="tpu_custom_call" | custom-call | flops 1 | bytes 1 | tf_op jit(solution)/shard_map/rows_back/pallas_call | solution.py:263
  93.7 6.9 %all-to-all-start.1 = ((bf16[32,16,4096]{2,1,0:T(8,128)(2,1)}), bf16[32,16,4096]{2,1,0:T(8,128)(2,1)}, u32[]{:S(2)}, u32[]{:S(2)}) async-start(bf16[32,16,4096]{2,1,0:T(8,128)(2,1)} %bitcast.24), calls=%async_computation.1 | async-start | bytes 8388608 | tf_op jit(solution)/shard_map/all_to_all | solution.py:213
  100.6 0.0 collective-permute-done.2.refs_6_
  100.6 0.0 collective-permute-done.3.refs_7_
  100.6 0.0 copy-start.8
  100.6 1.1 copy-done.8
  101.7 2.3 %chain_sum_2.1 = (bf16[4,256,256]{2,1,0:T(8,128)(2,1)S(1)}, bf16[5,256,256]{2,1,0:T(8,128)(2,1)S(1)}) custom-call(s32[1]{0:T(128)} %bitcast.7._, bf16[512,4096]{1,0:T(8,128)(2,1)} %bitcast.3.rows_ref.grads_ref.refs_0_.refs_1_.refs_2_, bf16[512,4096]{1,0:T(8,128)(2,1)} %bitcast.3.rows_ref.grads_ref.refs_0_.refs_1_.refs_2_, ...), custom_call_target="tpu_custom_call" | custom-call | flops 20000000000 | bytes 62914560 | tf_op jit(solution)/shard_map/chain_sum_2/pallas_call | solution.py:238
  104.1 0.1 collective-permute-start.6
  104.2 3.5 %collective-permute-start.7 = (bf16[5,256,256]{2,1,0:T(8,128)(2,1)S(1)}, bf16[5,256,256]{2,1,0:T(8,128)(2,1)S(1)}, u32[]{:S(2)}, u32[]{:S(2)}) collective-permute-start(bf16[5,256,256]{2,1,0:T(8,128)(2,1)S(1)} %get-tuple-element.55), channel_id=1, source_target_pairs={{0,7},{1,0},{2,1},{3,2},{4,3},{5,4},{6,5},{7,6},{8,15},{9,8},{10,9... | collective-permute-start | bytes 1966088 | tf_op jit(solution)/shard_map/ppermute | solution.py:284
  107.6 0.0 collective-permute-done.refs_6_
  107.6 0.5 collective-permute-done.1.refs_7_
  108.1 2.1 %chain_sum_3.1 = (bf16[4,256,256]{2,1,0:T(8,128)(2,1)S(1)}, bf16[5,256,256]{2,1,0:T(8,128)(2,1)S(1)}) custom-call(s32[1]{0:T(128)} %bitcast.7._, bf16[512,4096]{1,0:T(8,128)(2,1)} %bitcast.3.rows_ref.grads_ref.refs_0_.refs_1_.refs_2_, bf16[512,4096]{1,0:T(8,128)(2,1)} %bitcast.3.rows_ref.grads_ref.refs_0_.refs_1_.refs_2_, ...), custom_call_target="tpu_custom_call" | custom-call | flops 20000000000 | bytes 62914560 | tf_op jit(solution)/shard_map/chain_sum_3/pallas_call | solution.py:238
  110.2 3.2 %collective-permute-start.4 = (bf16[4,256,256]{2,1,0:T(8,128)(2,1)S(1)}, bf16[4,256,256]{2,1,0:T(8,128)(2,1)S(1)}, u32[]{:S(2)}, u32[]{:S(2)}) collective-permute-start(bf16[4,256,256]{2,1,0:T(8,128)(2,1)S(1)} %get-tuple-element.53.refs_8_), channel_id=1, source_target_pairs={{0,7},{1,0},{2,1},{3,2},{4,3},{5,4},{6,5},{7,6},{8,15},{9,8},{10,9... | collective-permute-start | bytes 1572872 | tf_op jit(solution)/shard_map/ppermute | solution.py:284
  113.5 0.0 collective-permute-start.5
  113.5 6.6 %collective-permute-done.6.refs_6_ = bf16[4,256,256]{2,1,0:T(8,128)(2,1)S(1)} collective-permute-done((bf16[4,256,256]{2,1,0:T(8,128)(2,1)S(1)}, bf16[4,256,256]{2,1,0:T(8,128)(2,1)S(1)}, u32[]{:S(2)}, u32[]{:S(2)}) %collective-permute-start.6) | collective-permute-done | bytes 524320 | tf_op jit(solution)/shard_map/ppermute | solution.py:284
  120.1 2.6 %collective-permute-done.7.refs_7_ = bf16[5,256,256]{2,1,0:T(8,128)(2,1)S(1)} collective-permute-done((bf16[5,256,256]{2,1,0:T(8,128)(2,1)S(1)}, bf16[5,256,256]{2,1,0:T(8,128)(2,1)S(1)}, u32[]{:S(2)}, u32[]{:S(2)}) %collective-permute-start.7) | collective-permute-done | bytes 655392 | tf_op jit(solution)/shard_map/ppermute | solution.py:284
  122.7 1.9 %chain_sum_4.1 = (bf16[4,256,256]{2,1,0:T(8,128)(2,1)S(1)}, bf16[5,256,256]{2,1,0:T(8,128)(2,1)S(1)}) custom-call(s32[1]{0:T(128)} %bitcast.7._, bf16[512,4096]{1,0:T(8,128)(2,1)} %bitcast.3.rows_ref.grads_ref.refs_0_.refs_1_.refs_2_, bf16[512,4096]{1,0:T(8,128)(2,1)} %bitcast.3.rows_ref.grads_ref.refs_0_.refs_1_.refs_2_, ...), custom_call_target="tpu_custom_call" | custom-call | flops 20000000000 | bytes 62914560 | tf_op jit(solution)/shard_map/chain_sum_4/pallas_call | solution.py:238
  124.7 1.2 collective-permute-start.10
  125.8 2.7 %collective-permute-start.11 = (bf16[5,256,256]{2,1,0:T(8,128)(2,1)S(1)}, bf16[5,256,256]{2,1,0:T(8,128)(2,1)S(1)}, u32[]{:S(2)}, u32[]{:S(2)}) collective-permute-start(bf16[5,256,256]{2,1,0:T(8,128)(2,1)S(1)} %get-tuple-element.59), channel_id=1, source_target_pairs={{0,7},{1,0},{2,1},{3,2},{4,3},{5,4},{6,5},{7,6},{8,15},{9,8},{10,9... | collective-permute-start | bytes 1966088 | tf_op jit(solution)/shard_map/ppermute | solution.py:284
  128.5 5.4 %collective-permute-done.4.refs_6_ = bf16[4,256,256]{2,1,0:T(8,128)(2,1)S(1)} collective-permute-done((bf16[4,256,256]{2,1,0:T(8,128)(2,1)S(1)}, bf16[4,256,256]{2,1,0:T(8,128)(2,1)S(1)}, u32[]{:S(2)}, u32[]{:S(2)}) %collective-permute-start.4) | collective-permute-done | bytes 524320 | tf_op jit(solution)/shard_map/ppermute | solution.py:284
  133.9 0.2 collective-permute-done.5.refs_7_
  134.1 2.8 %chain_sum_5.1 = (bf16[4,256,256]{2,1,0:T(8,128)(2,1)}, bf16[5,256,256]{2,1,0:T(8,128)(2,1)}) custom-call(s32[1]{0:T(128)} %bitcast.7._, bf16[512,4096]{1,0:T(8,128)(2,1)} %bitcast.3.rows_ref.grads_ref.refs_0_.refs_1_.refs_2_, bf16[512,4096]{1,0:T(8,128)(2,1)} %bitcast.3.rows_ref.grads_ref.refs_0_.refs_1_.refs_2_, ...), custom_call_target="tpu_custom_call" | custom-call | flops 20000000000 | bytes 62914560 | tf_op jit(solution)/shard_map/chain_sum_5/pallas_call | solution.py:238
  136.9 3.5 %collective-permute-start.8 = (bf16[4,256,256]{2,1,0:T(8,128)(2,1)}, bf16[4,256,256]{2,1,0:T(8,128)(2,1)}, u32[]{:S(2)}, u32[]{:S(2)}) collective-permute-start(bf16[4,256,256]{2,1,0:T(8,128)(2,1)} %get-tuple-element.57.refs_8_), channel_id=1, source_target_pairs={{0,7},{1,0},{2,1},{3,2},{4,3},{5,4},{6,5},{7,6},{8,15},{9,8},{10,9... | collective-permute-start | bytes 1572872 | tf_op jit(solution)/shard_map/ppermute | solution.py:284
  140.5 0.0 copy-start.3
  140.5 0.0 copy-start.4
  140.5 0.0 copy-start.5
  140.5 0.1 collective-permute-start.9
  140.6 4.8 %collective-permute-done.10.refs_6_ = bf16[4,256,256]{2,1,0:T(8,128)(2,1)S(1)} collective-permute-done((bf16[4,256,256]{2,1,0:T(8,128)(2,1)S(1)}, bf16[4,256,256]{2,1,0:T(8,128)(2,1)S(1)}, u32[]{:S(2)}, u32[]{:S(2)}) %collective-permute-start.10) | collective-permute-done | bytes 524320 | tf_op jit(solution)/shard_map/ppermute | solution.py:284
  145.4 2.6 %collective-permute-done.11.refs_7_ = bf16[5,256,256]{2,1,0:T(8,128)(2,1)S(1)} collective-permute-done((bf16[5,256,256]{2,1,0:T(8,128)(2,1)S(1)}, bf16[5,256,256]{2,1,0:T(8,128)(2,1)S(1)}, u32[]{:S(2)}, u32[]{:S(2)}) %collective-permute-start.11) | collective-permute-done | bytes 655392 | tf_op jit(solution)/shard_map/ppermute | solution.py:284
  148.0 2.8 %chain_sum_6.1 = (bf16[4,256,256]{2,1,0:T(8,128)(2,1)}, bf16[5,256,256]{2,1,0:T(8,128)(2,1)}) custom-call(s32[1]{0:T(128)} %bitcast.7._, bf16[512,4096]{1,0:T(8,128)(2,1)} %bitcast.3.rows_ref.grads_ref.refs_0_.refs_1_.refs_2_, bf16[512,4096]{1,0:T(8,128)(2,1)} %bitcast.3.rows_ref.grads_ref.refs_0_.refs_1_.refs_2_, ...), custom_call_target="tpu_custom_call" | custom-call | flops 20000000000 | bytes 62914560 | tf_op jit(solution)/shard_map/chain_sum_6/pallas_call | solution.py:238
  150.8 1.1 collective-permute-start.12
  151.9 2.6 %collective-permute-start.13 = (bf16[5,256,256]{2,1,0:T(8,128)(2,1)}, bf16[5,256,256]{2,1,0:T(8,128)(2,1)S(1)}, u32[]{:S(2)}, u32[]{:S(2)}) collective-permute-start(bf16[5,256,256]{2,1,0:T(8,128)(2,1)} %get-tuple-element.64), channel_id=1, source_target_pairs={{0,7},{1,0},{2,1},{3,2},{4,3},{5,4},{6,5},{7,6},{8,15},{9,8},{10,9... | collective-permute-start | bytes 1966088 | tf_op jit(solution)/shard_map/ppermute | solution.py:284
  154.5 0.0 all-to-all-done.1
  154.5 0.0 copy-start.9
  154.5 0.0 copy-done.3
  154.5 0.0 copy-done.4
  154.5 0.0 copy-done.5
  154.5 0.0 copy-done.6
  154.5 4.8 %combine.1 = (bf16[48,2048]{1,0:T(8,128)(2,1)}, bf16[48,2048]{1,0:T(8,128)(2,1)}, f32[8,48]{1,0:T(8,128)}, f32[8,128]{1,0:T(8,128)S(1)}) custom-call(s32[8,48]{1,0:T(8,128)S(1)} %bitcast.21, f32[8,48]{1,0:T(8,128)S(1)} %bitcast.23, bf16[512,48]{1,0:T(8,128)(2,1)S(1)} %copy-done.4, bf16[48,2048]{1,0:T(8,128)(2,1)S(1)} %copy-done.3, ...), custom_call_target="tpu_custom_call" | custom-call | flops 402653184 | bytes 4194304 | tf_op jit(solution)/shard_map/combine/pallas_call | solution.py:288
  159.3 0.0 collective-permute-done.8.refs_6_
  159.3 0.4 collective-permute-done.9.refs_7_
  159.7 0.0 copy-done.9
  159.7 2.3 %chain_sum_own.1 = (f32[4,256,256]{2,1,0:T(8,128)S(1)}, f32[5,256,256]{2,1,0:T(8,128)S(1)}) custom-call(s32[1]{0:T(128)} %bitcast.7._, bf16[512,4096]{1,0:T(8,128)(2,1)} %bitcast.3.rows_ref.grads_ref.refs_0_.refs_1_.refs_2_, bf16[512,4096]{1,0:T(8,128)(2,1)} %bitcast.3.rows_ref.grads_ref.refs_0_.refs_1_.refs_2_, ...), custom_call_target="tpu_custom_call" | custom-call | flops 20000000000 | bytes 62914560 | tf_op jit(solution)/shard_map/chain_sum_own/pallas_call | solution.py:238
  162.1 8.1 %collective-permute-done.12.a0 = bf16[4,256,256]{2,1,0:T(8,128)(2,1)S(1)} collective-permute-done((bf16[4,256,256]{2,1,0:T(8,128)(2,1)}, bf16[4,256,256]{2,1,0:T(8,128)(2,1)S(1)}, u32[]{:S(2)}, u32[]{:S(2)}) %collective-permute-start.12) | collective-permute-done | bytes 524320 | tf_op jit(solution)/shard_map/ppermute | solution.py:284
  170.1 2.4 %collective-permute-done.13.b0 = bf16[5,256,256]{2,1,0:T(8,128)(2,1)S(1)} collective-permute-done((bf16[5,256,256]{2,1,0:T(8,128)(2,1)}, bf16[5,256,256]{2,1,0:T(8,128)(2,1)S(1)}, u32[]{:S(2)}, u32[]{:S(2)}) %collective-permute-start.13) | collective-permute-done | bytes 655392 | tf_op jit(solution)/shard_map/ppermute | solution.py:284
  172.6 1.6 chain_sum_last.1
  (1 shorter events, 0.0 us)
Async XLA Ops:
  4.9 59.1 %all-to-all-start = ((bf16[32,16,4096]{2,1,0:T(8,128)(2,1)}), bf16[32,16,4096]{2,1,0:T(8,128)(2,1)}, u32[]{:S(2)}, u32[]{:S(2)}) async-start(bf16[32,16,4096]{2,1,0:T(8,128)(2,1)} %bitcast.25), calls=%async_computation | async-start | bytes 8388608 | tf_op jit(solution)/shard_map/all_to_all | solution.py:213
  73.3 9.0 %copy-start.7 = (bf16[768,512]{1,0:T(8,128)(2,1)}, bf16[768,512]{1,0:T(8,128)(2,1)S(1)}, u32[]{:S(2)}) copy-start(bf16[768,512]{1,0:T(8,128)(2,1)S(1)} %get-tuple-element.42.refs_5_) | copy-start | bytes 2359300
  76.3 24.2 %collective-permute-start.2 = (bf16[4,256,256]{2,1,0:T(8,128)(2,1)}, bf16[4,256,256]{2,1,0:T(8,128)(2,1)}, u32[]{:S(2)}, u32[]{:S(2)}) collective-permute-start(bf16[4,256,256]{2,1,0:T(8,128)(2,1)} %get-tuple-element.43.refs_6_), channel_id=1, source_target_pairs={{0,1},{1,2},{2,3},{3,4},{4,5},{5,6},{6,7},{7,0},{8,9},{9,10},{10,1... | collective-permute-start | bytes 1572872 | tf_op jit(solution)/shard_map/ppermute | solution.py:284
  78.3 8.7 %copy-start = (bf16[1,2048,768]{2,1,0:T(8,128)(2,1)S(1)}, bf16[1,2048,768]{2,1,0:T(8,128)(2,1)}, u32[]{:S(2)}) copy-start(bf16[1,2048,768]{2,1,0:T(8,128)(2,1)} %param.10) | copy-start | bytes 9437188
  78.3 8.7 %copy-start.1 = (bf16[1,2048,768]{2,1,0:T(8,128)(2,1)S(1)}, bf16[1,2048,768]{2,1,0:T(8,128)(2,1)}, u32[]{:S(2)}) copy-start(bf16[1,2048,768]{2,1,0:T(8,128)(2,1)} %param.11) | copy-start | bytes 9437188
  78.3 8.7 %copy-start.2 = (bf16[1,768,2048]{2,1,0:T(8,128)(2,1)S(1)}, bf16[1,768,2048]{2,1,0:T(8,128)(2,1)}, u32[]{:S(2)}) copy-start(bf16[1,768,2048]{2,1,0:T(8,128)(2,1)} %param.12) | copy-start | bytes 9437188
  78.3 22.3 %collective-permute-start.3 = (bf16[5,256,256]{2,1,0:T(8,128)(2,1)}, bf16[5,256,256]{2,1,0:T(8,128)(2,1)}, u32[]{:S(2)}, u32[]{:S(2)}) collective-permute-start(bf16[5,256,256]{2,1,0:T(8,128)(2,1)} %get-tuple-element.50), channel_id=1, source_target_pairs={{0,7},{1,0},{2,1},{3,2},{4,3},{5,4},{6,5},{7,6},{8,15},{9,8},{10,9... | collective-permute-start | bytes 1966088 | tf_op jit(solution)/shard_map/ppermute | solution.py:284
  84.2 23.4 %collective-permute-start = (bf16[4,256,256]{2,1,0:T(8,128)(2,1)S(1)}, bf16[4,256,256]{2,1,0:T(8,128)(2,1)}, u32[]{:S(2)}, u32[]{:S(2)}) collective-permute-start(bf16[4,256,256]{2,1,0:T(8,128)(2,1)S(1)} %get-tuple-element.44._), channel_id=1, source_target_pairs={{0,7},{1,0},{2,1},{3,2},{4,3},{5,4},{6,5},{7,6},{8,15},{9,8},{10,9... | collective-permute-start | bytes 1572872 | tf_op jit(solution)/shard_map/ppermute | solution.py:284
  87.0 21.1 %collective-permute-start.1 = (bf16[5,256,256]{2,1,0:T(8,128)(2,1)S(1)}, bf16[5,256,256]{2,1,0:T(8,128)(2,1)S(1)}, u32[]{:S(2)}, u32[]{:S(2)}) collective-permute-start(bf16[5,256,256]{2,1,0:T(8,128)(2,1)S(1)} %get-tuple-element.49), channel_id=1, source_target_pairs={{0,1},{1,2},{2,3},{3,4},{4,5},{5,6},{6,7},{7,0},{8,9},{9,10},{10,1... | collective-permute-start | bytes 1966088 | tf_op jit(solution)/shard_map/ppermute | solution.py:284
  93.7 60.8 %all-to-all-start.1 = ((bf16[32,16,4096]{2,1,0:T(8,128)(2,1)}), bf16[32,16,4096]{2,1,0:T(8,128)(2,1)}, u32[]{:S(2)}, u32[]{:S(2)}) async-start(bf16[32,16,4096]{2,1,0:T(8,128)(2,1)} %bitcast.24), calls=%async_computation.1 | async-start | bytes 8388608 | tf_op jit(solution)/shard_map/all_to_all | solution.py:213
  100.6 1.1 copy-start.8
  104.1 16.0 %collective-permute-start.6 = (bf16[4,256,256]{2,1,0:T(8,128)(2,1)S(1)}, bf16[4,256,256]{2,1,0:T(8,128)(2,1)S(1)}, u32[]{:S(2)}, u32[]{:S(2)}) collective-permute-start(bf16[4,256,256]{2,1,0:T(8,128)(2,1)S(1)} %get-tuple-element.52.refs_8_), channel_id=1, source_target_pairs={{0,1},{1,2},{2,3},{3,4},{4,5},{5,6},{6,7},{7,0},{8,9},{9,10},{10,1... | collective-permute-start | bytes 1572872 | tf_op jit(solution)/shard_map/ppermute | solution.py:284
  104.2 18.6 %collective-permute-start.7 = (bf16[5,256,256]{2,1,0:T(8,128)(2,1)S(1)}, bf16[5,256,256]{2,1,0:T(8,128)(2,1)S(1)}, u32[]{:S(2)}, u32[]{:S(2)}) collective-permute-start(bf16[5,256,256]{2,1,0:T(8,128)(2,1)S(1)} %get-tuple-element.55), channel_id=1, source_target_pairs={{0,7},{1,0},{2,1},{3,2},{4,3},{5,4},{6,5},{7,6},{8,15},{9,8},{10,9... | collective-permute-start | bytes 1966088 | tf_op jit(solution)/shard_map/ppermute | solution.py:284
  110.2 23.7 %collective-permute-start.4 = (bf16[4,256,256]{2,1,0:T(8,128)(2,1)S(1)}, bf16[4,256,256]{2,1,0:T(8,128)(2,1)S(1)}, u32[]{:S(2)}, u32[]{:S(2)}) collective-permute-start(bf16[4,256,256]{2,1,0:T(8,128)(2,1)S(1)} %get-tuple-element.53.refs_8_), channel_id=1, source_target_pairs={{0,7},{1,0},{2,1},{3,2},{4,3},{5,4},{6,5},{7,6},{8,15},{9,8},{10,9... | collective-permute-start | bytes 1572872 | tf_op jit(solution)/shard_map/ppermute | solution.py:284
  113.5 20.7 %collective-permute-start.5 = (bf16[5,256,256]{2,1,0:T(8,128)(2,1)S(1)}, bf16[5,256,256]{2,1,0:T(8,128)(2,1)S(1)}, u32[]{:S(2)}, u32[]{:S(2)}) collective-permute-start(bf16[5,256,256]{2,1,0:T(8,128)(2,1)S(1)} %get-tuple-element.54), channel_id=1, source_target_pairs={{0,1},{1,2},{2,3},{3,4},{4,5},{5,6},{6,7},{7,0},{8,9},{9,10},{10,1... | collective-permute-start | bytes 1966088 | tf_op jit(solution)/shard_map/ppermute | solution.py:284
  124.7 20.7 %collective-permute-start.10 = (bf16[4,256,256]{2,1,0:T(8,128)(2,1)S(1)}, bf16[4,256,256]{2,1,0:T(8,128)(2,1)S(1)}, u32[]{:S(2)}, u32[]{:S(2)}) collective-permute-start(bf16[4,256,256]{2,1,0:T(8,128)(2,1)S(1)} %get-tuple-element.56.refs_8_), channel_id=1, source_target_pairs={{0,1},{1,2},{2,3},{3,4},{4,5},{5,6},{6,7},{7,0},{8,9},{9,10},{10,1... | collective-permute-start | bytes 1572872 | tf_op jit(solution)/shard_map/ppermute | solution.py:284
  125.8 22.2 %collective-permute-start.11 = (bf16[5,256,256]{2,1,0:T(8,128)(2,1)S(1)}, bf16[5,256,256]{2,1,0:T(8,128)(2,1)S(1)}, u32[]{:S(2)}, u32[]{:S(2)}) collective-permute-start(bf16[5,256,256]{2,1,0:T(8,128)(2,1)S(1)} %get-tuple-element.59), channel_id=1, source_target_pairs={{0,7},{1,0},{2,1},{3,2},{4,3},{5,4},{6,5},{7,6},{8,15},{9,8},{10,9... | collective-permute-start | bytes 1966088 | tf_op jit(solution)/shard_map/ppermute | solution.py:284
  136.9 22.4 %collective-permute-start.8 = (bf16[4,256,256]{2,1,0:T(8,128)(2,1)}, bf16[4,256,256]{2,1,0:T(8,128)(2,1)}, u32[]{:S(2)}, u32[]{:S(2)}) collective-permute-start(bf16[4,256,256]{2,1,0:T(8,128)(2,1)} %get-tuple-element.57.refs_8_), channel_id=1, source_target_pairs={{0,7},{1,0},{2,1},{3,2},{4,3},{5,4},{6,5},{7,6},{8,15},{9,8},{10,9... | collective-permute-start | bytes 1572872 | tf_op jit(solution)/shard_map/ppermute | solution.py:284
  140.5 14.1 %copy-start.3 = (bf16[48,2048]{1,0:T(8,128)(2,1)S(1)}, bf16[48,2048]{1,0:T(8,128)(2,1)}, u32[]{:S(2)}) copy-start(bf16[48,2048]{1,0:T(8,128)(2,1)} %grads_ref.3) | copy-start | bytes 589828
  140.5 14.1 %copy-start.4 = (bf16[512,48]{1,0:T(8,128)(2,1)S(1)}, bf16[512,48]{1,0:T(8,128)(2,1)}, u32[]{:S(2)}) copy-start(bf16[512,48]{1,0:T(8,128)(2,1)} %get-tuple-element.37.place_ref) | copy-start | bytes 147460
  140.5 14.1 %copy-start.5 = (s32[48,8]{0,1:T(8,128)S(1)}, s32[48,8]{0,1:T(8,128)}, u32[]{:S(2)}) copy-start(s32[48,8]{0,1:T(8,128)} %param.8) | copy-start | bytes 4612
  140.5 14.1 %copy-start.6 = (f32[48,8]{0,1:T(8,128)S(1)}, f32[48,8]{0,1:T(8,128)}, u32[]{:S(2)}) copy-start(f32[48,8]{0,1:T(8,128)} %param.9) | copy-start | bytes 4612
  140.5 19.3 %collective-permute-start.9 = (bf16[5,256,256]{2,1,0:T(8,128)(2,1)}, bf16[5,256,256]{2,1,0:T(8,128)(2,1)}, u32[]{:S(2)}, u32[]{:S(2)}) collective-permute-start(bf16[5,256,256]{2,1,0:T(8,128)(2,1)} %get-tuple-element.58), channel_id=1, source_target_pairs={{0,1},{1,2},{2,3},{3,4},{4,5},{5,6},{6,7},{7,0},{8,9},{9,10},{10,1... | collective-permute-start | bytes 1966088 | tf_op jit(solution)/shard_map/ppermute | solution.py:284
  150.8 19.3 %collective-permute-start.12 = (bf16[4,256,256]{2,1,0:T(8,128)(2,1)}, bf16[4,256,256]{2,1,0:T(8,128)(2,1)S(1)}, u32[]{:S(2)}, u32[]{:S(2)}) collective-permute-start(bf16[4,256,256]{2,1,0:T(8,128)(2,1)} %get-tuple-element.60.refs_8_), channel_id=1, source_target_pairs={{0,1},{1,2},{2,3},{3,4},{4,5},{5,6},{6,7},{7,0},{8,9},{9,10},{10,1... | collective-permute-start | bytes 1572872 | tf_op jit(solution)/shard_map/ppermute | solution.py:284
  151.9 20.7 %collective-permute-start.13 = (bf16[5,256,256]{2,1,0:T(8,128)(2,1)}, bf16[5,256,256]{2,1,0:T(8,128)(2,1)S(1)}, u32[]{:S(2)}, u32[]{:S(2)}) collective-permute-start(bf16[5,256,256]{2,1,0:T(8,128)(2,1)} %get-tuple-element.64), channel_id=1, source_target_pairs={{0,7},{1,0},{2,1},{3,2},{4,3},{5,4},{6,5},{7,6},{8,15},{9,8},{10,9... | collective-permute-start | bytes 1966088 | tf_op jit(solution)/shard_map/ppermute | solution.py:284
  154.5 5.2 %copy-start.9 = (bf16[768,512]{1,0:T(8,128)(2,1)S(1)}, bf16[768,512]{1,0:T(8,128)(2,1)}, u32[]{:S(2)}) copy-start(bf16[768,512]{1,0:T(8,128)(2,1)} %copy-done.7) | copy-start | bytes 2359300

commit v9 on v8

--- a/solution.py
+++ b/solution.py
@@ -35,35 +35,26 @@
     return [expert == routes_t[k : k + 1, :] for k in range(routes_t.shape[0])]
 
 
-def dispatch_kernel(capacity, routes_ref, gates_ref, tokens_ref, grads_ref, wide_ref, place_ref, slot_weight):
-    step = pl.program_id(0)
-
-    @pl.when(step == 0)
-    def _():
-        slots, tokens = place_ref.shape
-        hit = jnp.zeros((slots, tokens), F32)
-        weight = jnp.zeros((slots, tokens), F32)
-        gates_t = gates_ref[...]
-        for k, mask in enumerate(slot_masks(routes_ref[...], slots, capacity)):
-            hit = jnp.where(mask, 1.0, hit)
-            weight = jnp.where(mask, gates_t[k : k + 1, :], weight)
-        before = (
-            lax.broadcasted_iota(jnp.int32, (tokens, tokens), 0)
-            < lax.broadcasted_iota(jnp.int32, (tokens, tokens), 1)
-        ).astype(F32).astype(BF16)
-        rank = dot(hit.astype(BF16), before)
-        mine = (lax.broadcasted_iota(jnp.int32, (slots, tokens), 0) % capacity).astype(F32)
-        place = jnp.where(rank == mine, hit, 0.0)
-        slot_weight[...] = jnp.sum(place * weight, axis=1, keepdims=True)
-        place_ref[...] = place.astype(BF16)
-
-    @pl.when(step == 0)
-    def _():
-        wide_ref[...] = dot(place_ref[...], tokens_ref[...]).astype(BF16)
-
-    @pl.when(step == 1)
-    def _():
-        wide_ref[...] = (slot_weight[...] * dot(place_ref[...], grads_ref[...])).astype(BF16)
+def dispatch_kernel(capacity, routes_ref, gates_ref, tokens_ref, grads_ref, wide_ref, place_ref):
+    slots, tokens = place_ref.shape
+    model = tokens_ref.shape[1]
+    hit = jnp.zeros((slots, tokens), F32)
+    weight = jnp.zeros((slots, tokens), F32)
+    gates_t = gates_ref[...]
+    for k, mask in enumerate(slot_masks(routes_ref[...], slots, capacity)):
+        hit = jnp.where(mask, 1.0, hit)
+        weight = jnp.where(mask, gates_t[k : k + 1, :], weight)
+    before = (
+        lax.broadcasted_iota(jnp.int32, (tokens, tokens), 0) < lax.broadcasted_iota(jnp.int32, (tokens, tokens), 1)
+    ).astype(F32).astype(BF16)
+    rank = dot(hit.astype(BF16), before)
+    mine = (lax.broadcasted_iota(jnp.int32, (slots, tokens), 0) % capacity).astype(F32)
+    place = jnp.where(rank == mine, hit, 0.0)
+    slot_weight = jnp.sum(place * weight, axis=1, keepdims=True)
+    place_low = place.astype(BF16)
+    place_ref[...] = place_low
+    wide_ref[:, :model] = dot(place_low, tokens_ref[...]).astype(BF16)
+    wide_ref[:, model:] = (slot_weight * dot(place_low, grads_ref[...])).astype(BF16)
 
 
 def expert_kernel(rows_ref, grads_ref, gate_ref, up_ref, down_ref, hidden_ref, hidden_t_ref, gate_pre_ref, up_pre_ref):
@@ -193,16 +184,7 @@
     half = model // 2
     send, place = pl.pallas_call(
         functools.partial(dispatch_kernel, capacity),
-        grid=(2,),
-        in_specs=[
-            whole((top, count)),
-            whole((top, count)),
-            whole((count, model)),
-            whole((count, model)),
-        ],
-        out_specs=[pl.BlockSpec((slots, model), lambda i: (0, i)), whole((slots, count))],
         out_shape=(shape((slots, 2 * model)), shape((slots, count))),
-        scratch_shapes=[pltpu.VMEM((slots, 1), F32)],
         compiler_params=params(58),
         cost_estimate=cost(4 * slots * count * model, 4 * slots * model),
         name="dispatch",

time: 175 us -> 175 us (level)
  no operation moved by 1% of the time
where the time goes in v9:
time: 175 us; the launch traced here: 174 us
  waiting for transfers between devices  85.1 us (49%)
  Pallas kernels  46.2 us (26%)
  starting transfers between devices  41.2 us (24%)
    all_to_all x2, waiting for transfers between devices, exchange(): return lax.all_to_all(wide, 'expert', 0, 0, tiled=True).reshape(array.shape)  51.4 us
    ppermute x7, waiting for transfers between devices, local(): lax.ppermute(part_a, 'dp', ring_a)  25 us
    pallas_call x8, Pallas kernels, chain_call(): pl.pallas_call(functools.partial(link_kernel, bool(held)), grid_spec=pltp...  19.3 us
    all_to_all x2, starting transfers between devices, exchange(): return lax.all_to_all(wide, 'expert', 0, 0, tiled=True).reshape(array.shape)  14.5 us
    ppermute x7, starting transfers between devices, local(): lax.ppermute(part_a, 'dp', ring_a)  13.7 us
    ppermute x7, starting transfers between devices, local(): lax.ppermute(part_b, 'dp', ring_b)  12.9 us
    pallas_call x1, Pallas kernels, local(): pl.pallas_call(expert_kernel, grid=(blocks,), in_specs=[pl.BlockSpec((slo...  9.27 us
    ppermute x7, waiting for transfers between devices, local(): lax.ppermute(part_b, 'dp', ring_b)  8.78 us
  transfers between devices with their start and end apart: 16, of which 11 were waited for; matrix products, arithmetic and copies ran while one was open for 0% of the time, Pallas kernels for 16%

profile of v9, /device:TPU:2, one launch (start us, length us, event | category | flops | bytes accessed | tf_op | source)
XLA Modules:
  0.0 174.5 jit_solution(2497382382702902512)
XLA Ops:
  0.6 4.6 %dispatch.1 = (bf16[512,4096]{1,0:T(8,128)(2,1)}, bf16[512,48]{1,0:T(8,128)(2,1)}) custom-call(s32[8,48]{1,0:T(8,128)} %bitcast.20, f32[8,48]{1,0:T(8,128)} %bitcast.22, bf16[48,2048]{1,0:T(8,128)(2,1)} %tokens_ref.1, bf16[48,2048]{1,0:T(8,128)(2,1)} %grads_ref.3), custom_call_target="tpu_custom_call" | custom-call | flops 201326592 | bytes 4194304 | tf_op jit(solution)/shard_map/dispatch/pallas_call | solution.py:185
  5.2 7.7 %all-to-all-start = ((bf16[32,16,4096]{2,1,0:T(8,128)(2,1)}), bf16[32,16,4096]{2,1,0:T(8,128)(2,1)}, u32[]{:S(2)}, u32[]{:S(2)}) async-start(bf16[32,16,4096]{2,1,0:T(8,128)(2,1)} %bitcast.25), calls=%async_computation | async-start | bytes 8388608 | tf_op jit(solution)/shard_map/all_to_all | solution.py:195
  12.9 51.4 %all-to-all-done = bf16[32,16,4096]{2,1,0:T(8,128)(2,1)} async-done(((bf16[32,16,4096]{2,1,0:T(8,128)(2,1)}), bf16[32,16,4096]{2,1,0:T(8,128)(2,1)}, u32[]{:S(2)}, u32[]{:S(2)}) %all-to-all-start) | async-done | bytes 4194336 | tf_op jit(solution)/shard_map/all_to_all | solution.py:195
  64.3 9.3 %expert.1 = (bf16[512,768]{1,0:T(8,128)(2,1)S(1)}, bf16[768,512]{1,0:T(8,128)(2,1)S(1)}, bf16[512,768]{1,0:T(8,128)(2,1)S(1)}, bf16[512,768]{1,0:T(8,128)(2,1)S(1)}) custom-call(bf16[512,4096]{1,0:T(8,128)(2,1)} %bitcast.3.rows_ref.grads_ref.refs_0_.refs_1_.refs_2_, bf16[512,4096]{1,0:T(8,128)(2,1)} %bitcast.3.rows_ref.grads_ref.refs_0_.refs_1_.refs_2_, ...), custom_call_target="tpu_custom_call" | custom-call | flops 4831838208 | bytes 16777216 | tf_op jit(solution)/shard_map/expert/pallas_call | solution.py:198
  73.6 0.0 copy-start.7
  73.6 3.1 %chain_sum_0.1 = (bf16[4,256,256]{2,1,0:T(8,128)(2,1)}, bf16[5,256,256]{2,1,0:T(8,128)(2,1)}) custom-call(s32[1]{0:T(128)} %bitcast.7._, bf16[512,4096]{1,0:T(8,128)(2,1)} %bitcast.3.rows_ref.grads_ref.refs_0_.refs_1_.refs_2_, bf16[512,4096]{1,0:T(8,128)(2,1)} %bitcast.3.rows_ref.grads_ref.refs_0_.refs_1_.refs_2_, ...), custom_call_target="tpu_custom_call" | custom-call | flops 20000000000 | bytes 62914560 | tf_op jit(solution)/shard_map/chain_sum_0/pallas_call | solution.py:220
  76.6 1.9 %collective-permute-start.2 = (bf16[4,256,256]{2,1,0:T(8,128)(2,1)}, bf16[4,256,256]{2,1,0:T(8,128)(2,1)}, u32[]{:S(2)}, u32[]{:S(2)}) collective-permute-start(bf16[4,256,256]{2,1,0:T(8,128)(2,1)} %get-tuple-element.43.refs_6_), channel_id=1, source_target_pairs={{0,1},{1,2},{2,3},{3,4},{4,5},{5,6},{6,7},{7,0},{8,9},{9,10},{10,1... | collective-permute-start | bytes 1572872 | tf_op jit(solution)/shard_map/ppermute | solution.py:266
  78.6 0.0 copy-start
  78.6 0.0 copy-start.1
  78.6 0.0 copy-start.2
  78.6 4.0 %collective-permute-start.3 = (bf16[5,256,256]{2,1,0:T(8,128)(2,1)}, bf16[5,256,256]{2,1,0:T(8,128)(2,1)}, u32[]{:S(2)}, u32[]{:S(2)}) collective-permute-start(bf16[5,256,256]{2,1,0:T(8,128)(2,1)} %get-tuple-element.50), channel_id=1, source_target_pairs={{0,7},{1,0},{2,1},{3,2},{4,3},{5,4},{6,5},{7,6},{8,15},{9,8},{10,9... | collective-permute-start | bytes 1966088 | tf_op jit(solution)/shard_map/ppermute | solution.py:266
  82.6 0.0 copy-done.7
  82.6 1.9 %chain_sum_1.1 = (bf16[4,256,256]{2,1,0:T(8,128)(2,1)S(1)}, bf16[5,256,256]{2,1,0:T(8,128)(2,1)S(1)}) custom-call(s32[1]{0:T(128)} %bitcast.7._, bf16[512,4096]{1,0:T(8,128)(2,1)} %bitcast.3.rows_ref.grads_ref.refs_0_.refs_1_.refs_2_, bf16[512,4096]{1,0:T(8,128)(2,1)} %bitcast.3.rows_ref.grads_ref.refs_0_.refs_1_.refs_2_, ...), custom_call_target="tpu_custom_call" | custom-call | flops 20000000000 | bytes 62914560 | tf_op jit(solution)/shard_map/chain_sum_1/pallas_call | solution.py:220
  84.5 2.7 %collective-permute-start = (bf16[4,256,256]{2,1,0:T(8,128)(2,1)S(1)}, bf16[4,256,256]{2,1,0:T(8,128)(2,1)}, u32[]{:S(2)}, u32[]{:S(2)}) collective-permute-start(bf16[4,256,256]{2,1,0:T(8,128)(2,1)S(1)} %get-tuple-element.44._), channel_id=1, source_target_pairs={{0,7},{1,0},{2,1},{3,2},{4,3},{5,4},{6,5},{7,6},{8,15},{9,8},{10,9... | collective-permute-start | bytes 1572872 | tf_op jit(solution)/shard_map/ppermute | solution.py:266
  87.3 0.0 collective-permute-start.1
  87.3 0.0 copy-done
  87.3 0.0 copy-done.1
  87.3 0.0 copy-done.2
  87.3 6.7 %rows_back.1 = (bf16[512,4096]{1,0:T(8,128)(2,1)}, f32[8,128]{1,0:T(8,128)S(1)}) custom-call(bf16[512,768]{1,0:T(8,128)(2,1)S(1)} %get-tuple-element.39.hidden_ref, bf16[512,768]{1,0:T(8,128)(2,1)S(1)} %get-tuple-element.40.refs_3_.gate_pre_ref, bf16[512,768]{1,0:T(8,128)(2,1)S(1)} %get-tuple-element.41.refs_4_.up_pre_ref, bf16[768,2048]{1,0:T(8,128)(2,1)S(1)} %bitcast.19, ...), custom_call_target="tpu_custom_call" | custom-call | flops 1 | bytes 1 | tf_op jit(solution)/shard_map/rows_back/pallas_call | solution.py:245
  94.0 6.9 %all-to-all-start.1 = ((bf16[32,16,4096]{2,1,0:T(8,128)(2,1)}), bf16[32,16,4096]{2,1,0:T(8,128)(2,1)}, u32[]{:S(2)}, u32[]{:S(2)}) async-start(bf16[32,16,4096]{2,1,0:T(8,128)(2,1)} %bitcast.24), calls=%async_computation.1 | async-start | bytes 8388608 | tf_op jit(solution)/shard_map/all_to_all | solution.py:195
  100.9 0.0 collective-permute-done.2.refs_6_
  100.9 0.0 collective-permute-done.3.refs_7_
  100.9 0.0 copy-start.8
  100.9 1.1 copy-done.8
  102.0 2.3 %chain_sum_2.1 = (bf16[4,256,256]{2,1,0:T(8,128)(2,1)S(1)}, bf16[5,256,256]{2,1,0:T(8,128)(2,1)S(1)}) custom-call(s32[1]{0:T(128)} %bitcast.7._, bf16[512,4096]{1,0:T(8,128)(2,1)} %bitcast.3.rows_ref.grads_ref.refs_0_.refs_1_.refs_2_, bf16[512,4096]{1,0:T(8,128)(2,1)} %bitcast.3.rows_ref.grads_ref.refs_0_.refs_1_.refs_2_, ...), custom_call_target="tpu_custom_call" | custom-call | flops 20000000000 | bytes 62914560 | tf_op jit(solution)/shard_map/chain_sum_2/pallas_call | solution.py:220
  104.4 0.1 collective-permute-start.6
  104.5 3.5 %collective-permute-start.7 = (bf16[5,256,256]{2,1,0:T(8,128)(2,1)S(1)}, bf16[5,256,256]{2,1,0:T(8,128)(2,1)S(1)}, u32[]{:S(2)}, u32[]{:S(2)}) collective-permute-start(bf16[5,256,256]{2,1,0:T(8,128)(2,1)S(1)} %get-tuple-element.55), channel_id=1, source_target_pairs={{0,7},{1,0},{2,1},{3,2},{4,3},{5,4},{6,5},{7,6},{8,15},{9,8},{10,9... | collective-permute-start | bytes 1966088 | tf_op jit(solution)/shard_map/ppermute | solution.py:266
  107.9 0.0 collective-permute-done.refs_6_
  107.9 0.5 collective-permute-done.1.refs_7_
  108.4 2.1 %chain_sum_3.1 = (bf16[4,256,256]{2,1,0:T(8,128)(2,1)S(1)}, bf16[5,256,256]{2,1,0:T(8,128)(2,1)S(1)}) custom-call(s32[1]{0:T(128)} %bitcast.7._, bf16[512,4096]{1,0:T(8,128)(2,1)} %bitcast.3.rows_ref.grads_ref.refs_0_.refs_1_.refs_2_, bf16[512,4096]{1,0:T(8,128)(2,1)} %bitcast.3.rows_ref.grads_ref.refs_0_.refs_1_.refs_2_, ...), custom_call_target="tpu_custom_call" | custom-call | flops 20000000000 | bytes 62914560 | tf_op jit(solution)/shard_map/chain_sum_3/pallas_call | solution.py:220
  110.5 3.2 %collective-permute-start.4 = (bf16[4,256,256]{2,1,0:T(8,128)(2,1)S(1)}, bf16[4,256,256]{2,1,0:T(8,128)(2,1)S(1)}, u32[]{:S(2)}, u32[]{:S(2)}) collective-permute-start(bf16[4,256,256]{2,1,0:T(8,128)(2,1)S(1)} %get-tuple-element.53.refs_8_), channel_id=1, source_target_pairs={{0,7},{1,0},{2,1},{3,2},{4,3},{5,4},{6,5},{7,6},{8,15},{9,8},{10,9... | collective-permute-start | bytes 1572872 | tf_op jit(solution)/shard_map/ppermute | solution.py:266
  113.8 0.0 collective-permute-start.5
  113.8 6.6 %collective-permute-done.6.refs_6_ = bf16[4,256,256]{2,1,0:T(8,128)(2,1)S(1)} collective-permute-done((bf16[4,256,256]{2,1,0:T(8,128)(2,1)S(1)}, bf16[4,256,256]{2,1,0:T(8,128)(2,1)S(1)}, u32[]{:S(2)}, u32[]{:S(2)}) %collective-permute-start.6) | collective-permute-done | bytes 524320 | tf_op jit(solution)/shard_map/ppermute | solution.py:266
  120.4 2.6 %collective-permute-done.7.refs_7_ = bf16[5,256,256]{2,1,0:T(8,128)(2,1)S(1)} collective-permute-done((bf16[5,256,256]{2,1,0:T(8,128)(2,1)S(1)}, bf16[5,256,256]{2,1,0:T(8,128)(2,1)S(1)}, u32[]{:S(2)}, u32[]{:S(2)}) %collective-permute-start.7) | collective-permute-done | bytes 655392 | tf_op jit(solution)/shard_map/ppermute | solution.py:266
  123.0 1.9 %chain_sum_4.1 = (bf16[4,256,256]{2,1,0:T(8,128)(2,1)S(1)}, bf16[5,256,256]{2,1,0:T(8,128)(2,1)S(1)}) custom-call(s32[1]{0:T(128)} %bitcast.7._, bf16[512,4096]{1,0:T(8,128)(2,1)} %bitcast.3.rows_ref.grads_ref.refs_0_.refs_1_.refs_2_, bf16[512,4096]{1,0:T(8,128)(2,1)} %bitcast.3.rows_ref.grads_ref.refs_0_.refs_1_.refs_2_, ...), custom_call_target="tpu_custom_call" | custom-call | flops 20000000000 | bytes 62914560 | tf_op jit(solution)/shard_map/chain_sum_4/pallas_call | solution.py:220
  125.0 1.2 collective-permute-start.10
  126.1 2.7 %collective-permute-start.11 = (bf16[5,256,256]{2,1,0:T(8,128)(2,1)S(1)}, bf16[5,256,256]{2,1,0:T(8,128)(2,1)S(1)}, u32[]{:S(2)}, u32[]{:S(2)}) collective-permute-start(bf16[5,256,256]{2,1,0:T(8,128)(2,1)S(1)} %get-tuple-element.59), channel_id=1, source_target_pairs={{0,7},{1,0},{2,1},{3,2},{4,3},{5,4},{6,5},{7,6},{8,15},{9,8},{10,9... | collective-permute-start | bytes 1966088 | tf_op jit(solution)/shard_map/ppermute | solution.py:266
  128.8 5.4 %collective-permute-done.4.refs_6_ = bf16[4,256,256]{2,1,0:T(8,128)(2,1)S(1)} collective-permute-done((bf16[4,256,256]{2,1,0:T(8,128)(2,1)S(1)}, bf16[4,256,256]{2,1,0:T(8,128)(2,1)S(1)}, u32[]{:S(2)}, u32[]{:S(2)}) %collective-permute-start.4) | collective-permute-done | bytes 524320 | tf_op jit(solution)/shard_map/ppermute | solution.py:266
  134.3 0.2 collective-permute-done.5.refs_7_
  134.4 2.8 %chain_sum_5.1 = (bf16[4,256,256]{2,1,0:T(8,128)(2,1)}, bf16[5,256,256]{2,1,0:T(8,128)(2,1)}) custom-call(s32[1]{0:T(128)} %bitcast.7._, bf16[512,4096]{1,0:T(8,128)(2,1)} %bitcast.3.rows_ref.grads_ref.refs_0_.refs_1_.refs_2_, bf16[512,4096]{1,0:T(8,128)(2,1)} %bitcast.3.rows_ref.grads_ref.refs_0_.refs_1_.refs_2_, ...), custom_call_target="tpu_custom_call" | custom-call | flops 20000000000 | bytes 62914560 | tf_op jit(solution)/shard_map/chain_sum_5/pallas_call | solution.py:220
  137.2 3.5 %collective-permute-start.8 = (bf16[4,256,256]{2,1,0:T(8,128)(2,1)}, bf16[4,256,256]{2,1,0:T(8,128)(2,1)}, u32[]{:S(2)}, u32[]{:S(2)}) collective-permute-start(bf16[4,256,256]{2,1,0:T(8,128)(2,1)} %get-tuple-element.57.refs_8_), channel_id=1, source_target_pairs={{0,7},{1,0},{2,1},{3,2},{4,3},{5,4},{6,5},{7,6},{8,15},{9,8},{10,9... | collective-permute-start | bytes 1572872 | tf_op jit(solution)/shard_map/ppermute | solution.py:266
  140.8 0.0 copy-start.3
  140.8 0.0 copy-start.4
  140.8 0.0 copy-start.5
  140.8 0.0 copy-start.6
  140.8 0.1 collective-permute-start.9
  140.9 4.8 %collective-permute-done.10.refs_6_ = bf16[4,256,256]{2,1,0:T(8,128)(2,1)S(1)} collective-permute-done((bf16[4,256,256]{2,1,0:T(8,128)(2,1)S(1)}, bf16[4,256,256]{2,1,0:T(8,128)(2,1)S(1)}, u32[]{:S(2)}, u32[]{:S(2)}) %collective-permute-start.10) | collective-permute-done | bytes 524320 | tf_op jit(solution)/shard_map/ppermute | solution.py:266
  145.7 2.6 %collective-permute-done.11.refs_7_ = bf16[5,256,256]{2,1,0:T(8,128)(2,1)S(1)} collective-permute-done((bf16[5,256,256]{2,1,0:T(8,128)(2,1)S(1)}, bf16[5,256,256]{2,1,0:T(8,128)(2,1)S(1)}, u32[]{:S(2)}, u32[]{:S(2)}) %collective-permute-start.11) | collective-permute-done | bytes 655392 | tf_op jit(solution)/shard_map/ppermute | solution.py:266
  148.3 2.8 %chain_sum_6.1 = (bf16[4,256,256]{2,1,0:T(8,128)(2,1)}, bf16[5,256,256]{2,1,0:T(8,128)(2,1)}) custom-call(s32[1]{0:T(128)} %bitcast.7._, bf16[512,4096]{1,0:T(8,128)(2,1)} %bitcast.3.rows_ref.grads_ref.refs_0_.refs_1_.refs_2_, bf16[512,4096]{1,0:T(8,128)(2,1)} %bitcast.3.rows_ref.grads_ref.refs_0_.refs_1_.refs_2_, ...), custom_call_target="tpu_custom_call" | custom-call | flops 20000000000 | bytes 62914560 | tf_op jit(solution)/shard_map/chain_sum_6/pallas_call | solution.py:220
  151.1 1.1 collective-permute-start.12
  152.2 2.6 %collective-permute-start.13 = (bf16[5,256,256]{2,1,0:T(8,128)(2,1)}, bf16[5,256,256]{2,1,0:T(8,128)(2,1)S(1)}, u32[]{:S(2)}, u32[]{:S(2)}) collective-permute-start(bf16[5,256,256]{2,1,0:T(8,128)(2,1)} %get-tuple-element.64), channel_id=1, source_target_pairs={{0,7},{1,0},{2,1},{3,2},{4,3},{5,4},{6,5},{7,6},{8,15},{9,8},{10,9... | collective-permute-start | bytes 1966088 | tf_op jit(solution)/shard_map/ppermute | solution.py:266
  154.8 0.0 all-to-all-done.1
  154.8 0.0 copy-done.3
  154.8 0.0 copy-done.4
  154.8 0.0 copy-done.5
  154.8 0.0 copy-done.6
  154.8 4.8 %combine.1 = (bf16[48,2048]{1,0:T(8,128)(2,1)}, bf16[48,2048]{1,0:T(8,128)(2,1)}, f32[8,48]{1,0:T(8,128)}, f32[8,128]{1,0:T(8,128)S(1)}) custom-call(s32[8,48]{1,0:T(8,128)S(1)} %bitcast.21, f32[8,48]{1,0:T(8,128)S(1)} %bitcast.23, bf16[512,48]{1,0:T(8,128)(2,1)S(1)} %copy-done.4, bf16[48,2048]{1,0:T(8,128)(2,1)S(1)} %copy-done.3, ...), custom_call_target="tpu_custom_call" | custom-call | flops 402653184 | bytes 4194304 | tf_op jit(solution)/shard_map/combine/pallas_call | solution.py:270
  159.6 0.0 collective-permute-done.8.refs_6_
  159.6 0.4 collective-permute-done.9.refs_7_
  160.0 0.0 copy-done.9
  160.1 2.3 %chain_sum_own.1 = (f32[4,256,256]{2,1,0:T(8,128)S(1)}, f32[5,256,256]{2,1,0:T(8,128)S(1)}) custom-call(s32[1]{0:T(128)} %bitcast.7._, bf16[512,4096]{1,0:T(8,128)(2,1)} %bitcast.3.rows_ref.grads_ref.refs_0_.refs_1_.refs_2_, bf16[512,4096]{1,0:T(8,128)(2,1)} %bitcast.3.rows_ref.grads_ref.refs_0_.refs_1_.refs_2_, ...), custom_call_target="tpu_custom_call" | custom-call | flops 20000000000 | bytes 62914560 | tf_op jit(solution)/shard_map/chain_sum_own/pallas_call | solution.py:220
  162.4 8.1 %collective-permute-done.12.a0 = bf16[4,256,256]{2,1,0:T(8,128)(2,1)S(1)} collective-permute-done((bf16[4,256,256]{2,1,0:T(8,128)(2,1)}, bf16[4,256,256]{2,1,0:T(8,128)(2,1)S(1)}, u32[]{:S(2)}, u32[]{:S(2)}) %collective-permute-start.12) | collective-permute-done | bytes 524320 | tf_op jit(solution)/shard_map/ppermute | solution.py:266
  170.5 2.4 %collective-permute-done.13.b0 = bf16[5,256,256]{2,1,0:T(8,128)(2,1)S(1)} collective-permute-done((bf16[5,256,256]{2,1,0:T(8,128)(2,1)}, bf16[5,256,256]{2,1,0:T(8,128)(2,1)S(1)}, u32[]{:S(2)}, u32[]{:S(2)}) %collective-permute-start.13) | collective-permute-done | bytes 655392 | tf_op jit(solution)/shard_map/ppermute | solution.py:266
  172.9 1.6 chain_sum_last.1
  (1 shorter events, 0.0 us)
Async XLA Ops:
  5.2 59.1 %all-to-all-start = ((bf16[32,16,4096]{2,1,0:T(8,128)(2,1)}), bf16[32,16,4096]{2,1,0:T(8,128)(2,1)}, u32[]{:S(2)}, u32[]{:S(2)}) async-start(bf16[32,16,4096]{2,1,0:T(8,128)(2,1)} %bitcast.25), calls=%async_computation | async-start | bytes 8388608 | tf_op jit(solution)/shard_map/all_to_all | solution.py:195
  73.6 9.0 %copy-start.7 = (bf16[768,512]{1,0:T(8,128)(2,1)}, bf16[768,512]{1,0:T(8,128)(2,1)S(1)}, u32[]{:S(2)}) copy-start(bf16[768,512]{1,0:T(8,128)(2,1)S(1)} %get-tuple-element.42.refs_5_) | copy-start | bytes 2359300
  76.6 24.2 %collective-permute-start.2 = (bf16[4,256,256]{2,1,0:T(8,128)(2,1)}, bf16[4,256,256]{2,1,0:T(8,128)(2,1)}, u32[]{:S(2)}, u32[]{:S(2)}) collective-permute-start(bf16[4,256,256]{2,1,0:T(8,128)(2,1)} %get-tuple-element.43.refs_6_), channel_id=1, source_target_pairs={{0,1},{1,2},{2,3},{3,4},{4,5},{5,6},{6,7},{7,0},{8,9},{9,10},{10,1... | collective-permute-start | bytes 1572872 | tf_op jit(solution)/shard_map/ppermute | solution.py:266
  78.6 8.7 %copy-start = (bf16[1,2048,768]{2,1,0:T(8,128)(2,1)S(1)}, bf16[1,2048,768]{2,1,0:T(8,128)(2,1)}, u32[]{:S(2)}) copy-start(bf16[1,2048,768]{2,1,0:T(8,128)(2,1)} %param.10) | copy-start | bytes 9437188
  78.6 8.7 %copy-start.1 = (bf16[1,2048,768]{2,1,0:T(8,128)(2,1)S(1)}, bf16[1,2048,768]{2,1,0:T(8,128)(2,1)}, u32[]{:S(2)}) copy-start(bf16[1,2048,768]{2,1,0:T(8,128)(2,1)} %param.11) | copy-start | bytes 9437188
  78.6 8.7 %copy-start.2 = (bf16[1,768,2048]{2,1,0:T(8,128)(2,1)S(1)}, bf16[1,768,2048]{2,1,0:T(8,128)(2,1)}, u32[]{:S(2)}) copy-start(bf16[1,768,2048]{2,1,0:T(8,128)(2,1)} %param.12) | copy-start | bytes 9437188
  78.6 22.3 %collective-permute-start.3 = (bf16[5,256,256]{2,1,0:T(8,128)(2,1)}, bf16[5,256,256]{2,1,0:T(8,128)(2,1)}, u32[]{:S(2)}, u32[]{:S(2)}) collective-permute-start(bf16[5,256,256]{2,1,0:T(8,128)(2,1)} %get-tuple-element.50), channel_id=1, source_target_pairs={{0,7},{1,0},{2,1},{3,2},{4,3},{5,4},{6,5},{7,6},{8,15},{9,8},{10,9... | collective-permute-start | bytes 1966088 | tf_op jit(solution)/shard_map/ppermute | solution.py:266
  84.5 23.4 %collective-permute-start = (bf16[4,256,256]{2,1,0:T(8,128)(2,1)S(1)}, bf16[4,256,256]{2,1,0:T(8,128)(2,1)}, u32[]{:S(2)}, u32[]{:S(2)}) collective-permute-start(bf16[4,256,256]{2,1,0:T(8,128)(2,1)S(1)} %get-tuple-element.44._), channel_id=1, source_target_pairs={{0,7},{1,0},{2,1},{3,2},{4,3},{5,4},{6,5},{7,6},{8,15},{9,8},{10,9... | collective-permute-start | bytes 1572872 | tf_op jit(solution)/shard_map/ppermute | solution.py:266
  87.3 21.1 %collective-permute-start.1 = (bf16[5,256,256]{2,1,0:T(8,128)(2,1)S(1)}, bf16[5,256,256]{2,1,0:T(8,128)(2,1)S(1)}, u32[]{:S(2)}, u32[]{:S(2)}) collective-permute-start(bf16[5,256,256]{2,1,0:T(8,128)(2,1)S(1)} %get-tuple-element.49), channel_id=1, source_target_pairs={{0,1},{1,2},{2,3},{3,4},{4,5},{5,6},{6,7},{7,0},{8,9},{9,10},{10,1... | collective-permute-start | bytes 1966088 | tf_op jit(solution)/shard_map/ppermute | solution.py:266
  94.0 60.8 %all-to-all-start.1 = ((bf16[32,16,4096]{2,1,0:T(8,128)(2,1)}), bf16[32,16,4096]{2,1,0:T(8,128)(2,1)}, u32[]{:S(2)}, u32[]{:S(2)}) async-start(bf16[32,16,4096]{2,1,0:T(8,128)(2,1)} %bitcast.24), calls=%async_computation.1 | async-start | bytes 8388608 | tf_op jit(solution)/shard_map/all_to_all | solution.py:195
  100.9 1.1 copy-start.8
  104.4 16.0 %collective-permute-start.6 = (bf16[4,256,256]{2,1,0:T(8,128)(2,1)S(1)}, bf16[4,256,256]{2,1,0:T(8,128)(2,1)S(1)}, u32[]{:S(2)}, u32[]{:S(2)}) collective-permute-start(bf16[4,256,256]{2,1,0:T(8,128)(2,1)S(1)} %get-tuple-element.52.refs_8_), channel_id=1, source_target_pairs={{0,1},{1,2},{2,3},{3,4},{4,5},{5,6},{6,7},{7,0},{8,9},{9,10},{10,1... | collective-permute-start | bytes 1572872 | tf_op jit(solution)/shard_map/ppermute | solution.py:266
  104.5 18.6 %collective-permute-start.7 = (bf16[5,256,256]{2,1,0:T(8,128)(2,1)S(1)}, bf16[5,256,256]{2,1,0:T(8,128)(2,1)S(1)}, u32[]{:S(2)}, u32[]{:S(2)}) collective-permute-start(bf16[5,256,256]{2,1,0:T(8,128)(2,1)S(1)} %get-tuple-element.55), channel_id=1, source_target_pairs={{0,7},{1,0},{2,1},{3,2},{4,3},{5,4},{6,5},{7,6},{8,15},{9,8},{10,9... | collective-permute-start | bytes 1966088 | tf_op jit(solution)/shard_map/ppermute | solution.py:266
  110.5 23.7 %collective-permute-start.4 = (bf16[4,256,256]{2,1,0:T(8,128)(2,1)S(1)}, bf16[4,256,256]{2,1,0:T(8,128)(2,1)S(1)}, u32[]{:S(2)}, u32[]{:S(2)}) collective-permute-start(bf16[4,256,256]{2,1,0:T(8,128)(2,1)S(1)} %get-tuple-element.53.refs_8_), channel_id=1, source_target_pairs={{0,7},{1,0},{2,1},{3,2},{4,3},{5,4},{6,5},{7,6},{8,15},{9,8},{10,9... | collective-permute-start | bytes 1572872 | tf_op jit(solution)/shard_map/ppermute | solution.py:266
  113.8 20.7 %collective-permute-start.5 = (bf16[5,256,256]{2,1,0:T(8,128)(2,1)S(1)}, bf16[5,256,256]{2,1,0:T(8,128)(2,1)S(1)}, u32[]{:S(2)}, u32[]{:S(2)}) collective-permute-start(bf16[5,256,256]{2,1,0:T(8,128)(2,1)S(1)} %get-tuple-element.54), channel_id=1, source_target_pairs={{0,1},{1,2},{2,3},{3,4},{4,5},{5,6},{6,7},{7,0},{8,9},{9,10},{10,1... | collective-permute-start | bytes 1966088 | tf_op jit(solution)/shard_map/ppermute | solution.py:266
  125.0 20.7 %collective-permute-start.10 = (bf16[4,256,256]{2,1,0:T(8,128)(2,1)S(1)}, bf16[4,256,256]{2,1,0:T(8,128)(2,1)S(1)}, u32[]{:S(2)}, u32[]{:S(2)}) collective-permute-start(bf16[4,256,256]{2,1,0:T(8,128)(2,1)S(1)} %get-tuple-element.56.refs_8_), channel_id=1, source_target_pairs={{0,1},{1,2},{2,3},{3,4},{4,5},{5,6},{6,7},{7,0},{8,9},{9,10},{10,1... | collective-permute-start | bytes 1572872 | tf_op jit(solution)/shard_map/ppermute | solution.py:266
  126.1 22.2 %collective-permute-start.11 = (bf16[5,256,256]{2,1,0:T(8,128)(2,1)S(1)}, bf16[5,256,256]{2,1,0:T(8,128)(2,1)S(1)}, u32[]{:S(2)}, u32[]{:S(2)}) collective-permute-start(bf16[5,256,256]{2,1,0:T(8,128)(2,1)S(1)} %get-tuple-element.59), channel_id=1, source_target_pairs={{0,7},{1,0},{2,1},{3,2},{4,3},{5,4},{6,5},{7,6},{8,15},{9,8},{10,9... | collective-permute-start | bytes 1966088 | tf_op jit(solution)/shard_map/ppermute | solution.py:266
  137.2 22.4 %collective-permute-start.8 = (bf16[4,256,256]{2,1,0:T(8,128)(2,1)}, bf16[4,256,256]{2,1,0:T(8,128)(2,1)}, u32[]{:S(2)}, u32[]{:S(2)}) collective-permute-start(bf16[4,256,256]{2,1,0:T(8,128)(2,1)} %get-tuple-element.57.refs_8_), channel_id=1, source_target_pairs={{0,7},{1,0},{2,1},{3,2},{4,3},{5,4},{6,5},{7,6},{8,15},{9,8},{10,9... | collective-permute-start | bytes 1572872 | tf_op jit(solution)/shard_map/ppermute | solution.py:266
  140.8 14.1 %copy-start.3 = (bf16[48,2048]{1,0:T(8,128)(2,1)S(1)}, bf16[48,2048]{1,0:T(8,128)(2,1)}, u32[]{:S(2)}) copy-start(bf16[48,2048]{1,0:T(8,128)(2,1)} %grads_ref.3) | copy-start | bytes 589828
  140.8 14.1 %copy-start.4 = (bf16[512,48]{1,0:T(8,128)(2,1)S(1)}, bf16[512,48]{1,0:T(8,128)(2,1)}, u32[]{:S(2)}) copy-start(bf16[512,48]{1,0:T(8,128)(2,1)} %get-tuple-element.37.place_ref) | copy-start | bytes 147460
  140.8 14.1 %copy-start.5 = (s32[48,8]{0,1:T(8,128)S(1)}, s32[48,8]{0,1:T(8,128)}, u32[]{:S(2)}) copy-start(s32[48,8]{0,1:T(8,128)} %param.8) | copy-start | bytes 4612
  140.8 14.1 %copy-start.6 = (f32[48,8]{0,1:T(8,128)S(1)}, f32[48,8]{0,1:T(8,128)}, u32[]{:S(2)}) copy-start(f32[48,8]{0,1:T(8,128)} %param.9) | copy-start | bytes 4612
  140.8 19.3 %collective-permute-start.9 = (bf16[5,256,256]{2,1,0:T(8,128)(2,1)}, bf16[5,256,256]{2,1,0:T(8,128)(2,1)}, u32[]{:S(2)}, u32[]{:S(2)}) collective-permute-start(bf16[5,256,256]{2,1,0:T(8,128)(2,1)} %get-tuple-element.58), channel_id=1, source_target_pairs={{0,1},{1,2},{2,3},{3,4},{4,5},{5,6},{6,7},{7,0},{8,9},{9,10},{10,1... | collective-permute-start | bytes 1966088 | tf_op jit(solution)/shard_map/ppermute | solution.py:266
  151.1 19.3 %collective-permute-start.12 = (bf16[4,256,256]{2,1,0:T(8,128)(2,1)}, bf16[4,256,256]{2,1,0:T(8,128)(2,1)S(1)}, u32[]{:S(2)}, u32[]{:S(2)}) collective-permute-start(bf16[4,256,256]{2,1,0:T(8,128)(2,1)} %get-tuple-element.60.refs_8_), channel_id=1, source_target_pairs={{0,1},{1,2},{2,3},{3,4},{4,5},{5,6},{6,7},{7,0},{8,9},{9,10},{10,1... | collective-permute-start | bytes 1572872 | tf_op jit(solution)/shard_map/ppermute | solution.py:266
  152.2 20.7 %collective-permute-start.13 = (bf16[5,256,256]{2,1,0:T(8,128)(2,1)}, bf16[5,256,256]{2,1,0:T(8,128)(2,1)S(1)}, u32[]{:S(2)}, u32[]{:S(2)}) collective-permute-start(bf16[5,256,256]{2,1,0:T(8,128)(2,1)} %get-tuple-element.64), channel_id=1, source_target_pairs={{0,7},{1,0},{2,1},{3,2},{4,3},{5,4},{6,5},{7,6},{8,15},{9,8},{10,9... | collective-permute-start | bytes 1966088 | tf_op jit(solution)/shard_map/ppermute | solution.py:266
  154.8 5.2 %copy-start.9 = (bf16[768,512]{1,0:T(8,128)(2,1)S(1)}, bf16[768,512]{1,0:T(8,128)(2,1)}, u32[]{:S(2)}) copy-start(bf16[768,512]{1,0:T(8,128)(2,1)} %copy-done.7) | copy-start | bytes 2359300
